TPU v7x, 256 devices: a whole 4x4x8 slice. The times are simulated.
256 devices in a mesh: row: 8 (over z_hi, x), col: 32 (over y, z_lo, core).
Axes of the slice: x: 4, y: 4, z: 8 (z_hi: 2, z_lo: 4; z = z_hi * 4 + z_lo), core: 2. Of those that a mesh axis runs over, the one named last changes fastest.
Arguments:
- tokens: bfloat16 [192, 256, 512], P('row', 'col'), may hold values from -6 to 6
- cotangent: bfloat16 [192, 256, 512], P('row', 'col'), may hold values from -6 to 6
- gains: float32 [2, 512], replicated, may hold values from 0.25 to 1.75
- w_qkv: bfloat16 [512, 1536], replicated, may hold values from -2 to 2
- w_out: bfloat16 [512, 512], replicated, may hold values from -0.25 to 0.25
- w_up: bfloat16 [512, 2048], replicated, may hold values from -0.25 to 0.25
- w_down: bfloat16 [2048, 512], replicated, may hold values from -0.125 to 0.125
- tile_mask: int32 [24, 32, 49], P('row', 'col'), may hold values from 0 to 1, as said below
Outputs:
- grad_tokens: bfloat16 [192, 256, 512], P('row', 'col')
- grad_qkv: float32 [786432], P(('row', 'col'))
- grad_out: float32 [262144], P(('row', 'col'))
- grad_up: float32 [1048576], P(('row', 'col'))
- grad_down: float32 [1048576], P(('row', 'col'))
- grad_gains: float32 [2, 512], replicated
Inputs may be any that keep to these rules, and one draw needn't show every extreme that they name: `tile_mask`: the middle entry, the token's own cell, is 1 for every tile.
All inputs are finite; a program needn't handle non-finite values.
Results may differ from a plain program's by a relative error of at most 0.02.
Values may be sent and summed in bfloat16 or wider, within the bound.
No kernel may reach another device: no remote copies, remote signals or barrier semaphores. Data moves between devices by JAX's collectives and lax.ppermute only.
A program may use at most 128 MiB of HBM per device.

v0:
```python
import math

import jax
import jax.numpy as jnp
import numpy as np
from jax import lax
from jax.sharding import PartitionSpec as P

HEADS = 8
WINDOW = 7
TILE = 8


epsilon = 1e-06
masked_value = -1e30


def padded_2(shard, sides, width):
    for axis, dim in sides:
        peers, length = (lax.axis_size(axis), shard.shape[dim])
        up = [(i, (i + 1) % peers) for i in range(peers - 1)]
        down = [(j, i) for i, j in up]
        last = lax.slice_in_dim(shard, length - width, length, axis=dim)
        leading = lax.slice_in_dim(shard, 0, width, axis=dim)
        before = lax.ppermute(last, axis, up)
        after = lax.ppermute(leading, axis, down)
        shard = jnp.concatenate([before, shard, after], axis=dim)
    return shard


def rms_forward(values_f):
    inverse = lax.rsqrt(jnp.mean(values_f * values_f, axis=-1, keepdims=True) + epsilon)
    return (values_f * inverse, inverse)


def rms_backward(unit, inverse, gain, incoming):
    scaled = incoming * gain
    inner_mean = jnp.mean(scaled * unit, axis=-1, keepdims=True)
    return (inverse * (scaled - unit * inner_mean), jnp.sum(incoming * unit, axis=0))


def times_transposed(left, right):
    return lax.dot_general(
        left, right, (((1,), (1,)), ((), ())), preferred_element_type=jnp.float32
    )


def transposed_times(left, right):
    return lax.dot_general(
        left, right, (((0,), (0,)), ((), ())), preferred_element_type=jnp.float32
    )


def project_front(flattened, gains, w_qkv):
    unit_in, inverse_in = rms_forward(flattened.astype(jnp.float32))
    normed_in = (unit_in * gains[0]).astype(jnp.bfloat16)
    projected = jnp.dot(normed_in, w_qkv, preferred_element_type=jnp.float32).astype(jnp.bfloat16)
    return (normed_in, unit_in, inverse_in, projected)


def middle_and_back(flattened, attention, grad_in, gains, w_out, w_up, w_down):
    mixed = (
        flattened.astype(jnp.float32)
        + jnp.dot(attention, w_out, preferred_element_type=jnp.float32)
    ).astype(jnp.bfloat16)
    unit_mid, inverse_mid = rms_forward(mixed.astype(jnp.float32))
    normed_mid = (unit_mid * gains[1]).astype(jnp.bfloat16)
    pre_act = jnp.dot(normed_mid, w_up, preferred_element_type=jnp.float32)
    activated, gelu_back = jax.vjp(jax.nn.gelu, pre_act)
    activated = activated.astype(jnp.bfloat16)
    grad_act = times_transposed(grad_in, w_down)
    grad_pre = gelu_back(grad_act)[0].astype(jnp.bfloat16)
    grad_normed = times_transposed(grad_pre, w_up)
    grad_inner, grad_gain = rms_backward(unit_mid, inverse_mid, gains[1], grad_normed)
    grad_mixed = (grad_in.astype(jnp.float32) + grad_inner).astype(jnp.bfloat16)
    return (normed_mid, activated, grad_pre, grad_mixed, grad_gain)


def cut_windows(array_in, count, span_width):
    tail = [(0, 0)] * (array_in.ndim - 1)
    shape_rest = array_in.shape[1:]
    padded = jnp.pad(array_in, [(0, 2 * TILE - span_width)] + tail)
    first = padded[: count * TILE].reshape((count, TILE) + shape_rest)
    second = padded[TILE:].reshape((count, TILE) + shape_rest)[:, : span_width - TILE]
    return jnp.concatenate([first, second], axis=1)


def join_windows(blocks, count, span_width):
    shape_rest = blocks.shape[2:]
    tail = [(0, 0)] * len(shape_rest)
    first = blocks[:, :TILE].reshape((count * TILE,) + shape_rest)
    second = jnp.pad(blocks[:, TILE:], [(0, 0), (0, 2 * TILE - span_width)] + tail).reshape(
        (count * TILE,) + shape_rest
    )
    total = jnp.pad(first, [(0, TILE)] + tail) + jnp.pad(second, [(TILE, 0)] + tail)
    return total[: count * TILE + span_width - TILE]


def key_tiles_of(extended, tile_rows, tile_cols, span_width):
    by_rows = cut_windows(extended, tile_rows, span_width)
    by_cols = cut_windows(jnp.moveaxis(by_rows, 2, 0), tile_cols, span_width)
    return by_cols.transpose(2, 0, 3, 1, 4).reshape(
        tile_rows * tile_cols, span_width * span_width, -1
    )


def key_tiles_back(blocks, tile_rows, tile_cols, span_width):
    features = blocks.shape[-1]
    by_cols = blocks.reshape(tile_rows, tile_cols, span_width, span_width, features).transpose(
        1, 3, 0, 2, 4
    )
    joined_cols = join_windows(by_cols, tile_cols, span_width)
    return join_windows(jnp.moveaxis(joined_cols, 0, 2), tile_rows, span_width)


def query_tiles_of(gridded, tile_rows, tile_cols):
    features = gridded.shape[-1]
    shaped = gridded.reshape(tile_rows, TILE, tile_cols, TILE, features).transpose(0, 2, 1, 3, 4)
    return shaped.reshape(tile_rows * tile_cols, TILE * TILE, features)


def query_tiles_back(tiled, tile_rows, tile_cols):
    features = tiled.shape[-1]
    shaped = tiled.reshape(tile_rows, tile_cols, TILE, TILE, features).transpose(0, 2, 1, 3, 4)
    return shaped.reshape(tile_rows * TILE, tile_cols * TILE, features)


def fold_rims(array_in, length, rim_width):
    tail = [(0, 0)] * (array_in.ndim - 1)
    middle = array_in[2 * rim_width : 2 * rim_width + length]
    upper = jnp.pad(array_in[:rim_width], [(0, length - rim_width)] + tail)
    lower = jnp.pad(array_in[length + 3 * rim_width :], [(length - rim_width, 0)] + tail)
    return middle + upper + lower


def offset_table(span_width):
    query_pos = np.arange(TILE * TILE)
    key_pos = np.arange(span_width * span_width)
    delta_row = (key_pos // span_width)[None, :] - (query_pos // TILE)[:, None]
    delta_col = (key_pos % span_width)[None, :] - (query_pos % TILE)[:, None]
    inside = (delta_row >= 0) & (delta_row < WINDOW) & (delta_col >= 0) & (delta_col < WINDOW)
    slot_index = delta_row * WINDOW + delta_col
    onehot = (slot_index[None] == np.arange(WINDOW * WINDOW)[:, None, None]) & inside[None]
    return jnp.asarray(onehot.reshape(WINDOW * WINDOW, -1).astype(np.float32))


def per_device(tokens, cotangent, gains, w_qkv, w_out, w_up, w_down, tile_mask):
    rows_dev, cols_dev, model_width = tokens.shape
    head_width = model_width // HEADS
    tok_count = rows_dev * cols_dev
    rim_width = WINDOW // 2
    span_width = TILE + 2 * rim_width
    span_cells = span_width * span_width
    tile_rows = rows_dev // TILE
    tile_cols = cols_dev // TILE
    tile_count = tile_rows * tile_cols
    scale_factor = head_width ** (-0.5)
    flattened = tokens.reshape(tok_count, model_width)
    grad_in = cotangent.reshape(tok_count, model_width)
    normed_in, unit_in, inverse_in, projected = project_front(flattened, gains, w_qkv)
    gridded = projected.reshape(rows_dev, cols_dev, 3 * model_width)
    key_value = gridded[..., model_width:]
    extended = padded_2(key_value, (("row", 0), ("col", 1)), rim_width)
    query_tiles = query_tiles_of(gridded[..., :model_width], tile_rows, tile_cols).reshape(
        tile_count, TILE * TILE, HEADS, head_width
    )
    kv_tiles = key_tiles_of(extended, tile_rows, tile_cols, span_width)
    key_tiles = kv_tiles[..., :model_width].reshape(tile_count, span_cells, HEADS, head_width)
    value_tiles = kv_tiles[..., model_width:].reshape(tile_count, span_cells, HEADS, head_width)
    mask_flat = tile_mask.reshape(tile_count, WINDOW * WINDOW).astype(jnp.float32)
    window_ok = (
        jnp.dot(mask_flat, offset_table(span_width), preferred_element_type=jnp.float32) > 0.5
    ).reshape(tile_count, TILE * TILE, span_cells)
    key_pos = np.arange(span_cells)
    tile_index = jnp.arange(tile_count)
    global_row = (
        lax.axis_index("row") * rows_dev
        - rim_width
        + (tile_index // tile_cols)[:, None] * TILE
        + (key_pos // span_width)[None, :]
    )
    global_col = (
        lax.axis_index("col") * cols_dev
        - rim_width
        + (tile_index % tile_cols)[:, None] * TILE
        + (key_pos % span_width)[None, :]
    )
    inside = (
        (global_row >= 0)
        & (global_row < rows_dev * lax.axis_size("row"))
        & (global_col >= 0)
        & (global_col < cols_dev * lax.axis_size("col"))
    )
    allowed = (window_ok & inside[:, None, :])[:, None]
    scores = (
        jnp.einsum("nqhd,nkhd->nhqk", query_tiles, key_tiles, preferred_element_type=jnp.float32)
        * scale_factor
    )
    masked = jnp.where(allowed, scores, masked_value)
    row_peak = jnp.max(masked, axis=-1, keepdims=True)
    exponent = jnp.where(allowed, jnp.exp(masked - row_peak), 0.0)
    probability = exponent / jnp.sum(exponent, axis=-1, keepdims=True)
    weights = probability.astype(jnp.bfloat16)
    attn_tiles = jnp.einsum(
        "nhqk,nkhd->nqhd", weights, value_tiles, preferred_element_type=jnp.float32
    ).astype(jnp.bfloat16)
    attention = query_tiles_back(
        attn_tiles.reshape(tile_count, TILE * TILE, model_width), tile_rows, tile_cols
    ).reshape(tok_count, model_width)
    normed_mid, activated, grad_pre, grad_mixed, gain_mid = middle_and_back(
        flattened, attention, grad_in, gains, w_out, w_up, w_down
    )
    grad_attn = times_transposed(grad_mixed, w_out).astype(jnp.bfloat16)
    grad_attn_tiles = query_tiles_of(
        grad_attn.reshape(rows_dev, cols_dev, model_width), tile_rows, tile_cols
    ).reshape(tile_count, TILE * TILE, HEADS, head_width)
    grad_prob = jnp.einsum(
        "nqhd,nkhd->nhqk", grad_attn_tiles, value_tiles, preferred_element_type=jnp.float32
    )
    row_inner = jnp.sum(probability * grad_prob, axis=-1, keepdims=True)
    grad_score = (probability * (grad_prob - row_inner) * scale_factor).astype(jnp.bfloat16)
    grad_query = jnp.einsum(
        "nhqk,nkhd->nqhd", grad_score, key_tiles, preferred_element_type=jnp.float32
    )
    grad_key = jnp.einsum(
        "nhqk,nqhd->nkhd", grad_score, query_tiles, preferred_element_type=jnp.float32
    )
    grad_value = jnp.einsum(
        "nhqk,nqhd->nkhd", weights, grad_attn_tiles, preferred_element_type=jnp.float32
    )
    grad_kv_tiles = jnp.concatenate(
        [
            grad_key.reshape(tile_count, span_cells, model_width),
            grad_value.reshape(tile_count, span_cells, model_width),
        ],
        axis=-1,
    )
    grad_kv_ext = key_tiles_back(grad_kv_tiles, tile_rows, tile_cols, span_width)
    returned = padded_2(grad_kv_ext, (("row", 0), ("col", 1)), rim_width)
    folded_rows = fold_rims(returned, rows_dev, rim_width)
    grad_kv = jnp.moveaxis(fold_rims(jnp.moveaxis(folded_rows, 1, 0), cols_dev, rim_width), 0, 1)
    grad_query_grid = query_tiles_back(
        grad_query.reshape(tile_count, TILE * TILE, model_width), tile_rows, tile_cols
    )
    grad_projected = (
        jnp.concatenate([grad_query_grid, grad_kv], axis=-1)
        .reshape(tok_count, 3 * model_width)
        .astype(jnp.bfloat16)
    )
    grad_normed = times_transposed(grad_projected, w_qkv)
    grad_front, gain_in = rms_backward(unit_in, inverse_in, gains[0], grad_normed)
    grad_tokens = (
        (grad_mixed.astype(jnp.float32) + grad_front)
        .astype(jnp.bfloat16)
        .reshape(rows_dev, cols_dev, model_width)
    )
    norm_scale = 1.0 / math.sqrt(tok_count * lax.axis_size("row") * lax.axis_size("col"))
    part_qkv = (transposed_times(normed_in, grad_projected) * norm_scale).reshape(-1)
    part_out = (transposed_times(attention, grad_mixed) * norm_scale).reshape(-1)
    part_up = (transposed_times(normed_mid, grad_pre) * norm_scale).reshape(-1)
    part_down = (transposed_times(activated, grad_in) * norm_scale).reshape(-1)
    grad_qkv, grad_out, grad_up, grad_down = (
        lax.psum_scatter(part_qkv, ("row", "col"), scatter_dimension=0, tiled=True),
        lax.psum_scatter(part_out, ("row", "col"), scatter_dimension=0, tiled=True),
        lax.psum_scatter(part_up, ("row", "col"), scatter_dimension=0, tiled=True),
        lax.psum_scatter(part_down, ("row", "col"), scatter_dimension=0, tiled=True),
    )
    grad_gains = lax.psum(jnp.stack([gain_in, gain_mid]) * norm_scale, ("row", "col"))
    return (grad_tokens, grad_qkv, grad_out, grad_up, grad_down, grad_gains)


def solution(mesh):
    in_specs = (
        P("row", "col", None),
        P("row", "col", None),
        P(),
        P(),
        P(),
        P(),
        P(),
        P("row", "col", None),
    )
    out_specs = (
        P("row", "col", None),
        P(("row", "col")),
        P(("row", "col")),
        P(("row", "col")),
        P(("row", "col")),
        P(),
    )
    return jax.shard_map(
        per_device, mesh=mesh, in_specs=in_specs, out_specs=out_specs, check_vma=False
    )
```

profile of v0, /device:TPU:8, one launch (start us, length us, event | category | flops | bytes accessed | tf_op | source)
XLA Modules:
  0.0 455.3 jit_solution(8617972745657086563)
XLA Ops:
  9.3 2.1 fusion.4
  12.7 4.5 collective-permute-start
  21.0 5.3 %collective-permute-start.3 = (bf16[30,3,1024]{2,1,0:T(4,128)(2,1)S(1)}, bf16[30,3,1024]{2,1,0:T(4,128)(2,1)S(1)}, u32[]{:S(2)}, u32[]{:S(2)}) collective-permute-start(bf16[30,3,1024]{2,1,0:T(4,128)(2,1)S(1)} %get-tuple-element.29), channel_id=1, source_target_pairs={{1,0},{2,1},{3,2},{4,3},{5,4},{6,5},{7,6},{8,7},{9,8},{10,9},{11,1... | collective-permute-start | bytes 552968 | tf_op jit(solution)/shard_map/ppermute | solution.py:26
  26.3 1.9 collective-permute-start.2
  28.9 3.6 collective-permute-done.3
  32.5 4.0 collective-permute-done.2
  39.3 2.2 fusion.95
  44.0 3.2 fusion.100
  47.2 2.7 fusion.40
  57.6 3.1 convolution_bitcast_fusion
  62.3 2.4 copy.55
  64.7 1.8 concatenate.41
  66.5 12.5 %fusion.30 = f32[3,196,8,64]{1,3,2,0:T(8,128)} fusion(bf16[3,64,8,64]{1,3,2,0:T(8,128)(2,1)} %copy.52, f32[3,8,64,196]{3,2,1,0:T(8,128)} %fusion.101, f32[3,8,64,196]{3,2,1,0:T(8,128)} %get-tuple-element.33, f32[3,8,64]{2,1,0:T(8,128)S(1)} %copy-done.28), kind=kOutput, calls=%fused_computation.44 | convolution fusion | flops 40644292 | bytes 3815424 | tf_op jit(solution)/shard_map/nhqk,nqhd->nkhd/dot_general | solution.py:225
  79.0 2.4 copy.53
  81.4 1.8 concatenate.40
  83.2 2.0 maximum_bitcast_fusion
  87.5 11.9 %fusion.37 = bf16[3,64,8,64]{1,3,2,0:T(8,128)(2,1)} fusion(bf16[3,196,8,64]{1,3,2,0:T(8,128)(2,1)S(1)} %bitcast.148, f32[3,8,64,196]{3,2,1,0:T(8,128)} %fusion.101, f32[3,8,64,196]{3,2,1,0:T(8,128)} %get-tuple-element.33, f32[3,8,64]{2,1,0:T(8,128)S(1)} %copy-done.28), kind=kOutput, calls=%fused_computation.57 | convolution fusion | flops 40742596 | bytes 3213312 | tf_op jit(solution)/shard_map/nhqk,nkhd->nqhd/dot_general | solution.py:222
  104.4 5.3 %collective-permute-start.4 = (f32[3,14,1024]{2,0,1:T(4,128)}, f32[3,14,1024]{2,0,1:T(4,128)}, u32[]{:S(2)}, u32[]{:S(2)}) collective-permute-start(f32[3,14,1024]{2,0,1:T(4,128)} %get-tuple-element.16), channel_id=1, source_target_pairs={{0,32},{32,64},{64,96},{96,128},{128,160},{160,192},{192,224},{1,3... | collective-permute-start | bytes 516104 | tf_op jit(solution)/shard_map/ppermute | solution.py:25
  110.9 2.0 copy.51
  112.9 1.9 concatenate.39
  114.8 2.5 copy.61
  118.7 2.1 collective-permute-start.7
  120.8 2.5 collective-permute-start.6
  124.1 2.9 copy.62
  127.9 3.0 copy.63
  130.9 3.0 collective-permute-done.7
  134.0 1.7 pad_maximum_fusion
  135.7 1.7 fusion.6
  139.3 1.9 reshape.209
  142.2 2.2 fusion.64
  144.5 87.7 %psum.7 = f32[2,512]{1,0:T(2,128)} all-reduce(f32[2,512]{1,0:T(2,128)S(1)} %maximum_multiply_fusion), channel_id=1, replica_groups=mesh['row'=8,'col'=32] {'row','col'}, use_global_device_ids=true, to_apply=%region_13.14 | all-reduce | flops 1024 | bytes 8192 | tf_op jit(solution)/shard_map/psum | solution.py:268
  233.1 210.1 %all-reduce.17.cloned.1.call-done = (f32[786432]{0:T(1024)}, f32[262144]{0:T(1024)}, f32[1048576]{0:T(1024)}, f32[1048576]{0:T(1024)}) async-done(((f32[786432]{0:T(1024)}, f32[262144]{0:T(1024)}, f32[1048576]{0:T(1024)}, f32[1048576]{0:T(1024)}), (f32[786432]{0:T(1024)}, f32[262144]{0:T(1024)}, f32[1048576]{0:T(1024)}, f32[1048576]{0:T(1024)})) %all-reduce.17.cloned.1.call-update) | async-done | bytes 12582928
  (132 shorter events, 42.7 us)
Async XLA Ops:
  7.2 44.7 %copy-start = (bf16[512,2048]{1,0:T(8,128)(2,1)S(1)}, bf16[512,2048]{1,0:T(8,128)(2,1)}, u32[]{:S(2)}) copy-start(bf16[512,2048]{1,0:T(8,128)(2,1)} %param.16) | copy-start | bytes 6291460
  7.2 10.1 %copy-start.21 = (s32[3,1,49]{2,1,0:T(1,128)S(1)}, s32[3,1,49]{2,1,0:T(1,128)}, u32[]{:S(2)}) copy-start(s32[3,1,49]{2,1,0:T(1,128)} %param.18) | copy-start | bytes 1768
  7.2 436.0 %all-reduce.17.cloned.1.call-start = ((), (), s32[]{:S(2)}) async-start(), calls=%async_computation | async-start | bytes 25165824
  9.3 9.7 %copy-start.23 = (s32[1,196]{1,0:T(1,128)S(1)}, s32[1,196]{1,0:T(1,128)}, u32[]{:S(2)}) copy-start(s32[1,196]{1,0:T(1,128)} %constant.98.clone) | copy-start | bytes 2356
  9.3 9.7 %copy-start.22 = (s32[196]{0:T(256)S(1)}, s32[196]{0:T(256)}, u32[]{:S(2)}) copy-start(s32[196]{0:T(256)} %constant.122) | copy-start | bytes 2356
  11.4 9.3 %collective-permute-start.1 = (bf16[3,8,1024]{2,1,0:T(8,128)(2,1)S(1)}, bf16[3,8,1024]{2,1,0:T(8,128)(2,1)S(1)}, u32[]{:S(2)}, u32[]{:S(2)}) collective-permute-start(bf16[3,8,1024]{2,1,0:T(8,128)(2,1)S(1)} %get-tuple-element.27), channel_id=1, source_target_pairs={{32,0},{64,32},{96,64},{128,96},{160,128},{192,160},{224,192},{33,... | collective-permute-start | bytes 147464 | tf_op jit(solution)/shard_map/ppermute | solution.py:26
  12.7 8.0 %collective-permute-start = (bf16[3,8,1024]{2,1,0:T(8,128)(2,1)S(1)}, bf16[3,8,1024]{2,1,0:T(8,128)(2,1)S(1)}, u32[]{:S(2)}, u32[]{:S(2)}) collective-permute-start(bf16[3,8,1024]{2,1,0:T(8,128)(2,1)S(1)} %get-tuple-element.26), channel_id=1, source_target_pairs={{0,32},{32,64},{64,96},{96,128},{128,160},{160,192},{192,224},{1,3... | collective-permute-start | bytes 147464 | tf_op jit(solution)/shard_map/ppermute | solution.py:25
  21.0 11.5 %collective-permute-start.3 = (bf16[30,3,1024]{2,1,0:T(4,128)(2,1)S(1)}, bf16[30,3,1024]{2,1,0:T(4,128)(2,1)S(1)}, u32[]{:S(2)}, u32[]{:S(2)}) collective-permute-start(bf16[30,3,1024]{2,1,0:T(4,128)(2,1)S(1)} %get-tuple-element.29), channel_id=1, source_target_pairs={{1,0},{2,1},{3,2},{4,3},{5,4},{6,5},{7,6},{8,7},{9,8},{10,9},{11,1... | collective-permute-start | bytes 552968 | tf_op jit(solution)/shard_map/ppermute | solution.py:26
  26.3 10.2 %collective-permute-start.2 = (bf16[30,3,1024]{2,1,0:T(4,128)(2,1)S(1)}, bf16[30,3,1024]{2,1,0:T(4,128)(2,1)S(1)}, u32[]{:S(2)}, u32[]{:S(2)}) collective-permute-start(bf16[30,3,1024]{2,1,0:T(4,128)(2,1)S(1)} %get-tuple-element.28), channel_id=1, source_target_pairs={{0,1},{1,2},{2,3},{3,4},{4,5},{5,6},{6,7},{7,8},{8,9},{9,10},{10,1... | collective-permute-start | bytes 552968 | tf_op jit(solution)/shard_map/ppermute | solution.py:25
  42.8 4.4 copy-start.6
  47.2 2.7 copy-start.27
  47.2 4.3 copy-start.3
  49.9 1.6 copy-start.8
  51.9 1.7 copy-start.26
  53.6 1.4 copy-start.11
  55.1 1.5 copy-start.4
  57.6 3.1 copy-start.7
  86.1 1.4 copy-start.17
  100.0 1.4 copy-start.2
  102.2 7.4 %copy-start.10 = (bf16[192,512]{1,0:T(8,128)(2,1)S(1)}, bf16[192,512]{1,0:T(8,128)(2,1)}, u32[]{:S(2)}) copy-start(bf16[192,512]{1,0:T(8,128)(2,1)} %copy-done.9) | copy-start | bytes 589828
  103.1 14.5 %collective-permute-start.5 = (f32[3,14,1024]{2,0,1:T(4,128)}, f32[3,14,1024]{2,0,1:T(4,128)}, u32[]{:S(2)}, u32[]{:S(2)}) collective-permute-start(f32[3,14,1024]{2,0,1:T(4,128)} %get-tuple-element.17), channel_id=1, source_target_pairs={{32,0},{64,32},{96,64},{128,96},{160,128},{192,160},{224,192},{33,... | collective-permute-start | bytes 516104 | tf_op jit(solution)/shard_map/ppermute | solution.py:26
  104.4 13.2 %collective-permute-start.4 = (f32[3,14,1024]{2,0,1:T(4,128)}, f32[3,14,1024]{2,0,1:T(4,128)}, u32[]{:S(2)}, u32[]{:S(2)}) collective-permute-start(f32[3,14,1024]{2,0,1:T(4,128)} %get-tuple-element.16), channel_id=1, source_target_pairs={{0,32},{32,64},{64,96},{96,128},{128,160},{160,192},{192,224},{1,3... | collective-permute-start | bytes 516104 | tf_op jit(solution)/shard_map/ppermute | solution.py:25
  117.5 5.7 %copy-start.5 = (bf16[192,2048]{1,0:T(8,128)(2,1)S(1)}, bf16[192,2048]{1,0:T(8,128)(2,1)}, u32[]{:S(2)}) copy-start(bf16[192,2048]{1,0:T(8,128)(2,1)} %copy-done.4) | copy-start | bytes 2359300
  118.7 15.3 %collective-permute-start.7 = (f32[36,3,1024]{2,0,1:T(8,128)S(1)}, f32[36,3,1024]{2,0,1:T(8,128)S(1)}, u32[]{:S(2)}, u32[]{:S(2)}) collective-permute-start(f32[36,3,1024]{2,0,1:T(8,128)S(1)} %get-tuple-element.19), channel_id=1, source_target_pairs={{1,0},{2,1},{3,2},{4,3},{5,4},{6,5},{7,6},{8,7},{9,8},{10,9},{11,1... | collective-permute-start | bytes 1327112 | tf_op jit(solution)/shard_map/ppermute | solution.py:26
  120.8 13.2 %collective-permute-start.6 = (f32[36,3,1024]{2,0,1:T(8,128)S(1)}, f32[36,3,1024]{2,0,1:T(8,128)S(1)}, u32[]{:S(2)}, u32[]{:S(2)}) collective-permute-start(f32[36,3,1024]{2,0,1:T(8,128)S(1)} %get-tuple-element.18), channel_id=1, source_target_pairs={{0,1},{1,2},{2,3},{3,4},{4,5},{5,6},{6,7},{7,8},{8,9},{9,10},{10,1... | collective-permute-start | bytes 1327112 | tf_op jit(solution)/shard_map/ppermute | solution.py:25
  124.1 2.9 copy-start.12
  124.1 2.9 copy-start.19
  130.9 4.7 %copy-start.25 = (pred[24]{0:T(512)(128)(4,1)S(1)}, pred[24]{0:T(512)(128)(4,1)}, u32[]{:S(2)}) copy-start(pred[24]{0:T(512)(128)(4,1)} %constant.93.clone.1) | copy-start | bytes 76
  135.6 1.8 copy-start.24
  137.4 1.2 copy-start.15
  141.2 307.2 %copy-start.1 = (bf16[512,2048]{1,0:T(8,128)(2,1)S(1)}, bf16[512,2048]{1,0:T(8,128)(2,1)}, u32[]{:S(2)}) copy-start(bf16[512,2048]{1,0:T(8,128)(2,1)} %param.16) | copy-start | bytes 6291460
  142.2 2.2 copy-start.20
  (6 other events, 5.8 us)
Sparse Core Ops, SparseCore 0:
  141.3 301.8 all-reduce.16
where the time goes:
time: 457 us; the launch traced here: 455 us
  waiting for transfers between devices  221 us (48%)
  blocking collectives  87.7 us (19%)
  matrix products  48.7 us (11%)
  local copies, waits for them, and re-layouts  47 us (10%)
  starting transfers between devices  24.2 us (5%)
  between operations  14.7 us (3%)
  other arithmetic  12.1 us (3%)
    unnamed x2, waiting for transfers between devices  210 us
    psum x1, blocking collectives, per_device(): lax.psum(jnp.stack([gain_in, gain_mid]) * norm_scale, ('row', 'col'))  87.7 us
    unnamed x66, local copies, waits for them, and re-layouts  18.6 us
    ppermute x4, starting transfers between devices, padded_2(): before = lax.ppermute(last, axis, up)  14.2 us
    dot_general x1, matrix products, per_device(): jnp.einsum('nhqk,nqhd->nkhd', grad_score, query_tiles, preferred_element_...  12.5 us
    dot_general x1, matrix products, per_device(): jnp.einsum('nhqk,nkhd->nqhd', grad_score, key_tiles, preferred_element_ty...  11.9 us
    ppermute x4, starting transfers between devices, padded_2(): after = lax.ppermute(leading, axis, down)  9.93 us
  transfers between devices with their start and end apart: 9, of which 4 were waited for; matrix products, arithmetic and copies ran while one was open for 5% of the time, Pallas kernels for 0%

commit v1 on v0

v1 whole, which is shorter than its diff:
```python
import functools
import math

import jax
import jax.numpy as jnp
import numpy as np
from jax import lax
from jax.experimental import pallas as pl
from jax.experimental.pallas import tpu as pltpu
from jax.sharding import PartitionSpec as P

D = 512
FF = 2048
HEADS = 8
WINDOW = 7
TILE = 8
RIM = WINDOW // 2
EPS = 1e-06
AXES = ("row", "col")
N_COL = 32
GRID_ROWS = 192
GRID_COLS = 256
ROWS = 24
COLS = 8
TOK = ROWS * COLS
TILES = ROWS // TILE
ER = 32
EC = 16
EXT = ER * EC
QT = TILE * TILE
KT = 256
F32 = jnp.float32
BF16 = jnp.bfloat16
GELU_C = math.sqrt(2.0 / math.pi)


def nn(a, b):
    return lax.dot_general(a, b, (((1,), (0,)), ((), ())), preferred_element_type=F32)


def nt(a, b):
    return lax.dot_general(a, b, (((1,), (1,)), ((), ())), preferred_element_type=F32)


def tn(a, b):
    return lax.dot_general(a, b, (((0,), (0,)), ((), ())), preferred_element_type=F32)


def unit_of(x):
    inv = lax.rsqrt(jnp.mean(x * x, axis=-1, keepdims=True) + EPS)
    return x * inv, inv


def head_mask(rows, h):
    lane = lax.broadcasted_iota(jnp.int32, (rows, 256), 1)
    return (lane // 64) == h


def stack_heads(x):
    zero = jnp.zeros_like(x)
    return jnp.concatenate([jnp.where(head_mask(x.shape[0], h), x, zero) for h in range(4)], axis=0)


def unstack_heads(x):
    rows = x.shape[0] // 4
    out = jnp.where(head_mask(rows, 0), x[:rows], 0.0)
    for h in range(1, 4):
        out = out + jnp.where(head_mask(rows, h), x[h * rows : (h + 1) * rows], 0.0)
    return out


def prep_kernel(coord, mask, cot, w_down, gact, bias, pt_a, pt_b, pt_d):
    for c in range(4):
        gact[:, c * 512 : (c + 1) * 512] = nt(cot[...], w_down[c * 512 : (c + 1) * 512, :])
    q = lax.broadcasted_iota(jnp.int32, (QT, KT), 0)
    k = lax.broadcasted_iota(jnp.int32, (QT, KT), 1)
    ki = k // EC
    kj = k % EC
    da = ki - q // TILE
    db = kj - q % TILE
    slot = jnp.where((da >= 0) & (da < WINDOW) & (db >= 0) & (db < WINDOW), da * WINDOW + db, -1)
    allowed = [jnp.zeros((QT, KT), jnp.int32) for _ in range(TILES)]
    for s in range(WINDOW * WINDOW):
        here = slot == s
        for t in range(TILES):
            allowed[t] = jnp.where(here, mask[t, s], allowed[t])
    gc = coord[1] * COLS + kj - RIM
    for t in range(TILES):
        gr = coord[0] * ROWS + t * TILE + ki - RIM
        ok = (allowed[t] == 1) & (gr >= 0) & (gr < GRID_ROWS) & (gc >= 0) & (gc < GRID_COLS)
        bias[t] = jnp.where(ok, 0.0, -1e30)
    me = coord[2]
    lane = lax.broadcasted_iota(jnp.int32, (512, 512), 1)
    p = lax.broadcasted_iota(jnp.int32, (512, 512), 0)
    s1 = p & 1
    z = (p >> 1) & 7
    mid1 = (p >> 4) & 3
    mid2 = (p >> 6) & 3
    co = p >> 8
    zpart = (z >> 2) * 128 + (z & 3) * 2 + co
    ka = (zpart + mid2 * 32 + mid1 * 8) ^ me
    pt_a[...] = jnp.where(lane == ka * 2 + s1, 1.0, 0.0).astype(BF16)
    kb = (zpart + mid1 * 32 + mid2 * 8) ^ me
    pt_b[...] = jnp.where(lane == kb * 2 + s1, 1.0, 0.0).astype(BF16)
    s8 = p & 7
    zl = (p >> 3) & 3
    xl = (p >> 5) & 1
    y = (p >> 6) & 3
    kd = (xl * 32 + y * 8 + zl * 2 + co) ^ (me & 63)
    pt_d[...] = jnp.where(lane == kd * 8 + s8, 1.0, 0.0).astype(BF16)


def forward_kernel(
    coord, text, tok, cot, gains, w_qkv, w_out, w_up, gact, bias, pt_a, pt_d,
    u_keep, u_send, d_keep, d_send, gm_o, q_o, kv_o, p_o, ne_o, no_o, gain_o, attn_s,
):
    unit_e, _ = unit_of(text[...].astype(F32))
    ne = (unit_e * gains[0:1, :]).astype(BF16)
    ne_o[...] = ne
    kv_o[...] = nn(ne, w_qkv[:, D:]).astype(BF16)
    xt = tok[...].astype(F32)
    unit_o, _ = unit_of(xt)
    no = (unit_o * gains[0:1, :]).astype(BF16)
    no_o[...] = no
    q_o[...] = nn(no, w_qkv[:, :D]).astype(BF16)
    for t in range(TILES):
        b4 = jnp.concatenate([bias[t]] * 4, axis=0)
        for g in range(2):
            cols = slice(g * 256, (g + 1) * 256)
            vcols = slice(D + g * 256, D + (g + 1) * 256)
            keys = kv_o[t * 128 : t * 128 + KT, cols]
            vals = kv_o[t * 128 : t * 128 + KT, vcols]
            qs = stack_heads(q_o[t * QT : (t + 1) * QT, cols])
            s = nt(qs, keys) * 0.125 + b4
            e = jnp.exp(s - jnp.max(s, axis=-1, keepdims=True))
            prob = e / jnp.sum(e, axis=-1, keepdims=True)
            p_o[t * 2 + g] = prob
            o = nn(prob.astype(BF16), vals)
            attn_s[t * QT : (t + 1) * QT, cols] = unstack_heads(o).astype(BF16)
    attn = attn_s[...]
    mixed = (xt + nn(attn, w_out[...])).astype(BF16)
    um, inv_m = unit_of(mixed.astype(F32))
    nm = (um * gains[1:2, :]).astype(BF16)
    nmt = nt(pt_a[...], nm).astype(BF16)
    c_me = (coord[2] >> 6) & 3
    gn = jnp.zeros((TOK, D), F32)
    for c in range(4):
        cols = slice(c * 512, (c + 1) * 512)
        pre = nn(nm, w_up[:, cols])
        th = jnp.tanh(GELU_C * (pre + 0.044715 * (pre * pre * pre)))
        half = 0.5 * (1.0 + th)
        act = (pre * half).astype(BF16)
        slope = half + 0.5 * pre * (1.0 - th * th) * (GELU_C * (1.0 + 0.134145 * (pre * pre)))
        gp = (gact[:, cols] * slope).astype(BF16)
        gn = gn + nt(gp, w_up[:, cols])
        gu = nn(nmt, gp).astype(BF16)
        u_keep[:, cols] = gu[:256]
        u_send[:, cols] = gu[256:]
        act_t = nt(pt_d[...], act).astype(BF16)
        gd = nn(act_t, cot[...]).astype(BF16)
        c_rel = c ^ c_me
        zh = c_rel >> 1
        xh = c_rel & 1
        for y in range(4):
            for xl in range(2):
                base = (y * 2 + xl) * 32
                d_keep[y, xh, xl, zh] = gd[base : base + 32]
                d_send[y, xh, xl, zh] = gd[256 + base : 256 + base + 32]
    g = gn * gains[1:2, :]
    gm = (cot[...].astype(F32) + inv_m * (g - um * jnp.mean(g * um, axis=-1, keepdims=True))).astype(BF16)
    gm_o[...] = gm
    gain_o[...] = jnp.sum(gn * um, axis=0, keepdims=True)
    go = nn(nt(pt_a[...], attn).astype(BF16), gm).astype(BF16)
    u_keep[:, FF:] = go[:256]
    u_send[:, FF:] = go[256:]


def backward_kernel(
    gm, w_out, w_qkv, q, kv, p_in, ne, no, text, tok, gain_mid, pt,
    k_keep, k_send, gne_o, gnq_o, dq_s, dkv_s,
):
    ga = nt(gm[...], w_out[...]).astype(BF16)
    dkv_s[...] = jnp.zeros_like(dkv_s)
    for t in range(TILES):
        for g in range(2):
            cols = slice(g * 256, (g + 1) * 256)
            vcols = slice(D + g * 256, D + (g + 1) * 256)
            rows = slice(t * 128, t * 128 + KT)
            prob = p_in[t * 2 + g]
            gas = stack_heads(ga[t * QT : (t + 1) * QT, cols])
            qs = stack_heads(q[t * QT : (t + 1) * QT, cols])
            gp = nt(gas, kv[rows, vcols])
            inner = jnp.sum(prob * gp, axis=-1, keepdims=True)
            ds = (prob * (gp - inner) * 0.125).astype(BF16)
            dq_s[t * QT : (t + 1) * QT, cols] = unstack_heads(nn(ds, kv[rows, cols])).astype(BF16)
            dkv_s[rows, cols] += tn(ds, qs)
            dkv_s[rows, vcols] += tn(prob.astype(BF16), gas)
    dkv = dkv_s[...].astype(BF16)
    dq = dq_s[...]
    gk = nn(nt(pt[...], ne[...]).astype(BF16), dkv).astype(BF16)
    gq = nn(nt(pt[...], no[...]).astype(BF16), dq).astype(BF16)
    k_keep[:256, :D] = gq[:256]
    k_send[:256, :D] = gq[256:]
    k_keep[:256, D:] = gk[:256]
    k_send[:256, D:] = gk[256:]
    gne = nt(dkv, w_qkv[:, D:])
    gnq = nt(dq, w_qkv[:, :D])
    gne_o[...] = gne
    gnq_o[...] = gnq
    unit_e, _ = unit_of(text[...].astype(F32))
    unit_o, _ = unit_of(tok[...].astype(F32))
    gain_in = jnp.sum(gne * unit_e, axis=0, keepdims=True) + jnp.sum(gnq * unit_o, axis=0, keepdims=True)
    row = jnp.concatenate([gain_in, gain_mid[...], jnp.zeros((1, D), F32)], axis=1)
    block = jnp.broadcast_to(row, (16, 3 * D)).astype(BF16)
    k_keep[256:, :] = block
    k_send[256:, :] = block


def call(body, outs, scratch, n_smem, n_in, flops, nbytes):
    smem = pl.BlockSpec(memory_space=pltpu.SMEM)
    vmem = pl.BlockSpec(memory_space=pltpu.VMEM)
    return pl.pallas_call(
        body,
        out_shape=[jax.ShapeDtypeStruct(s, d) for s, d in outs],
        in_specs=[smem] * n_smem + [vmem] * n_in,
        out_specs=[vmem] * len(outs),
        scratch_shapes=scratch,
        compiler_params=pltpu.CompilerParams(vmem_limit_bytes=50 * 1024 * 1024),
        cost_estimate=pl.CostEstimate(flops=flops, bytes_accessed=nbytes, transcendentals=0),
    )


def perm_xor(bits):
    return [(k, k ^ bits) for k in range(256)]


def shift(step):
    pairs = []
    for k in range(256):
        r, c = divmod(k, N_COL)
        if step in (1, -1):
            if 0 <= c + step < N_COL:
                pairs.append((k, k + step))
        elif 0 <= k + step < 256:
            pairs.append((k, k + step))
    return pairs


def send(x, perm):
    return lax.ppermute(x, AXES, perm)


X_BIT = 32
Y_BIT = 8


def z_bits(d):
    return (d >> 2) * 128 + (d & 3) * 2


def total(parts):
    f = [v.astype(F32) for v in parts]
    while len(f) > 1:
        f = [f[i] + f[i + 1] for i in range(0, len(f), 2)]
    return f[0]


def quarter(chunks, bit):
    got = [send(chunks[d], perm_xor(bit * d)) for d in range(1, 4)]
    return [chunks[0]] + got


def chain(keep, sent, bits, gain_rows):
    rows = keep.shape[0] - gain_rows
    recv = send(sent, perm_xor(1))
    extra = None
    step = rows // 4

    def piece(a, lo, size):
        return lax.slice_in_dim(a, lo, lo + size, axis=0)

    chunks = [total([piece(keep, d * step, step), piece(recv, d * step, step)]).astype(BF16) for d in range(4)]
    if gain_rows:
        extra = total([piece(keep, rows, 8), piece(recv, rows, 8)]).astype(BF16)
    for level, bit in enumerate(bits):
        msgs = chunks if extra is None else [jnp.concatenate([c, extra], axis=0) for c in chunks]
        got = quarter(msgs, bit)
        summed = total(got).astype(BF16)
        if extra is not None:
            extra = piece(summed, step, 8)
        if level + 1 < len(bits):
            step //= 4
            chunks = [piece(summed, d * step, step) for d in range(4)]
    return (piece(summed, 0, step), extra)


def per_device(tokens, cotangent, gains, w_qkv, w_out, w_up, w_down, tile_mask):
    row = lax.axis_index("row")
    col = lax.axis_index("col")
    coord = jnp.stack([row, col, row * N_COL + col]).astype(jnp.int32)
    tok = tokens.reshape(TOK, D)
    cot = cotangent.reshape(TOK, D)

    above = send(tokens[ROWS - RIM :], shift(N_COL))
    below = send(tokens[:RIM], shift(-N_COL))
    tall = jnp.concatenate([above, tokens, below], axis=0)
    left = send(tall[:, COLS - RIM :], shift(1))
    right = send(tall[:, :RIM], shift(-1))
    wide = jnp.concatenate([left, tall, right, jnp.zeros((ROWS + 2 * RIM, 2, D), BF16)], axis=1)
    text = jnp.concatenate([wide, jnp.zeros((2, EC, D), BF16)], axis=0).reshape(EXT, D)

    gact, bias, pt_a, pt_b, pt_d = call(
        prep_kernel,
        [((TOK, FF), F32), ((TILES, QT, KT), F32), ((D, D), BF16), ((D, D), BF16), ((D, D), BF16)],
        [], 2, 2, 2 * TOK * D * FF, 6_000_000,
    )(coord, tile_mask.reshape(TILES, WINDOW * WINDOW), cot, w_down)

    u_keep, u_send, d_keep, d_send, gm, q, kv, prob, ne, no, gain_mid = call(
        forward_kernel,
        [
            ((256, FF + D), BF16), ((256, FF + D), BF16),
            ((4, 2, 2, 2, 32, D), BF16), ((4, 2, 2, 2, 32, D), BF16),
            ((TOK, D), BF16), ((TOK, D), BF16), ((EXT, 2 * D), BF16), ((6, 256, KT), F32),
            ((EXT, D), BF16), ((TOK, D), BF16), ((1, D), F32),
        ],
        [pltpu.VMEM((TOK, D), BF16)], 1, 11, 5_000_000_000, 20_000_000,
    )(coord, text, tok, cot, gains, w_qkv, w_out, w_up, gact, bias, pt_a, pt_d)

    k_keep, k_send, gne, gnq = call(
        backward_kernel,
        [((272, 3 * D), BF16), ((272, 3 * D), BF16), ((EXT, D), F32), ((TOK, D), F32)],
        [pltpu.VMEM((TOK, D), BF16), pltpu.VMEM((EXT, 2 * D), F32)], 0, 12, 3_000_000_000, 12_000_000,
    )(gm, w_out, w_qkv, q, kv, prob, ne, no, text, tok, gain_mid, pt_b)

    su, _ = chain(u_keep, u_send, (X_BIT, Y_BIT), 0)
    sd, _ = chain(d_keep.reshape(1024, D), d_send.reshape(1024, D), (Y_BIT, X_BIT), 0)
    sk, sg = chain(k_keep, k_send, (Y_BIT, X_BIT), 16)
    su = su.reshape(8, 2, FF + D)
    sd = sd.reshape(8, 8, D)
    sk = sk.reshape(8, 2, 3 * D)
    flat = jnp.concatenate(
        [
            su[..., :FF].reshape(8, 2 * FF), sd.reshape(8, 8 * D), su[..., FF:].reshape(8, 2 * D),
            sk.reshape(8, 6 * D), jnp.broadcast_to(sg[:1, : 2 * D], (8, 2 * D)),
        ],
        axis=1,
    )
    got = [flat[0:1]] + [send(flat[d : d + 1], perm_xor(z_bits(d))) for d in range(1, 8)]
    norm_scale = 1.0 / math.sqrt(GRID_ROWS * GRID_COLS)
    summed = total(got)[0] * norm_scale
    cuts = np.cumsum([0, 2 * FF, 8 * D, 2 * D, 6 * D, 2 * D])
    g_up, g_down, g_out, g_qkv, g_gains = [summed[a:b] for a, b in zip(cuts[:-1], cuts[1:])]

    gne3 = gne.reshape(ER, EC, D)[: ROWS + 2 * RIM]
    to_left = send(gne3[:, :RIM].astype(BF16), shift(-1)).astype(F32)
    to_right = send(gne3[:, RIM + COLS : 2 * RIM + COLS].astype(BF16), shift(1)).astype(F32)
    mid = gne3[:, RIM : RIM + COLS]
    gap = COLS - RIM
    mid = mid + jnp.pad(to_right, ((0, 0), (0, gap), (0, 0))) + jnp.pad(to_left, ((0, 0), (gap, 0), (0, 0)))
    to_up = send(mid[:RIM].astype(BF16), shift(-N_COL)).astype(F32)
    to_down = send(mid[RIM + ROWS :].astype(BF16), shift(N_COL)).astype(F32)
    gap = ROWS - RIM
    gn = mid[RIM : RIM + ROWS] + jnp.pad(to_down, ((0, gap), (0, 0), (0, 0))) + jnp.pad(to_up, ((gap, 0), (0, 0), (0, 0)))
    gn = gn + gnq.reshape(ROWS, COLS, D)
    unit, inv = unit_of(tokens.astype(F32))
    g1 = gn * gains[0]
    front = inv * (g1 - unit * jnp.mean(g1 * unit, axis=-1, keepdims=True))
    grad_tokens = (gm.reshape(ROWS, COLS, D).astype(F32) + front).astype(BF16)
    return (grad_tokens, g_qkv, g_out, g_up, g_down, g_gains.reshape(2, D))


def solution(mesh):
    block = P("row", "col", None)
    flat = P(("row", "col"))
    return jax.shard_map(
        per_device,
        mesh=mesh,
        in_specs=(block, block, P(), P(), P(), P(), P(), block),
        out_specs=(block, flat, flat, flat, flat, P()),
        check_vma=False,
    )
```

time: 457 us -> 158 us (0.35)
  waiting for transfers between devices: 221 us -> 30 us
  blocking collectives: 87.7 us -> 0 us
  starting transfers between devices: 24.2 us -> 84.5 us
  matrix products: 48.7 us -> 0 us
  local copies, waits for them, and re-layouts: 47 us -> 8.44 us
  Pallas kernels: 0 us -> 24 us
  between operations: 14.7 us -> 1.3 us
    unnamed x2 -> x0, waiting for transfers between devices: 210 us -> none
    psum x1 -> x0, blocking collectives: 87.7 us -> none  [per_device(): lax.psum(jnp.stack([gain_in, gain_mid]) * norm_scale, ('row', 'col'))]
    ppermute x8 -> x36, starting transfers between devices: 24.1 us -> 84.5 us  [send(): return lax.ppermute(x, AXES, perm)]
    dot_general x17 -> x0, matrix products: 45.5 us -> none  [the longest x1 12.5 us: per_device(): jnp.einsum('nhqk,nqhd->nkhd', grad_score, query_tiles, preferred_element_...]
    pallas_call x0 -> x3, Pallas kernels: none -> 24 us  [the longest x1 12 us: per_device(): call(forward_kernel, [((256, FF + D), BF16), ((256, FF + D), BF16), ((4,...]
    ppermute x8 -> x36, waiting for transfers between devices: 10.7 us -> 30 us  [send(): return lax.ppermute(x, AXES, perm)]
    unnamed x66 -> x45, local copies, waits for them, and re-layouts: 18.6 us -> 3.05 us
    transpose x4 -> x0, local copies, waits for them, and re-layouts: 6.94 us -> none  [the longest x1 2.38 us: per_device(): jnp.einsum('nhqk,nqhd->nkhd', weights, grad_attn_tiles, preferred_element...]
  transfers between devices with their start and end apart: 9 -> 36, of which waited for: 4 -> 19; matrix products, arithmetic and copies ran while one was open for 5% -> 6% of each run, Pallas kernels for 0% -> 2%
where the time goes in v1:
time: 158 us; the launch traced here: 156 us
  starting transfers between devices  84.5 us (53%)
  waiting for transfers between devices  30 us (19%)
  Pallas kernels  24 us (15%)
  local copies, waits for them, and re-layouts  8.44 us (5%)
  other arithmetic  8.15 us (5%)
    ppermute x36, starting transfers between devices, send(): return lax.ppermute(x, AXES, perm)  84.5 us
    ppermute x36, waiting for transfers between devices, send(): return lax.ppermute(x, AXES, perm)  30 us
    pallas_call x1, Pallas kernels, per_device(): call(forward_kernel, [((256, FF + D), BF16), ((256, FF + D), BF16), ((4,...  12 us
    pallas_call x1, Pallas kernels, per_device(): call(backward_kernel, [((272, 3 * D), BF16), ((272, 3 * D), BF16), ((EXT,...  8.1 us
    pallas_call x1, Pallas kernels, per_device(): call(prep_kernel, [((TOK, FF), F32), ((TILES, QT, KT), F32), ((D, D), BF1...  3.87 us
  transfers between devices with their start and end apart: 36, of which 19 were waited for; matrix products, arithmetic and copies ran while one was open for 6% of the time, Pallas kernels for 2%

profile of v1, /device:TPU:8, one launch (start us, length us, event | category | flops | bytes accessed | tf_op | source)
XLA Modules:
  0.0 156.4 jit_solution(8162030045902005602)
XLA Ops:
  1.4 3.4 %collective-permute-start = (bf16[3,8,512]{2,1,0:T(8,128)(2,1)S(1)}, bf16[3,8,512]{2,1,0:T(8,128)(2,1)S(1)}, u32[]{:S(2)}, u32[]{:S(2)}) collective-permute-start(bf16[3,8,512]{2,1,0:T(8,128)(2,1)S(1)} %get-tuple-element.85), channel_id=1, source_target_pairs={{0,32},{1,33},{2,34},{3,35},{4,36},{5,37},{6,38},{7,39},{8,40},{9,... | collective-permute-start | bytes 73736 | tf_op jit(solution)/shard_map/ppermute | solution.py:250
  4.8 1.3 collective-permute-start.1
  7.9 3.9 %shard_map.127 = (f32[192,2048]{1,0:T(8,128)S(1)}, f32[3,64,256]{2,1,0:T(8,128)S(1)}, bf16[512,512]{1,0:T(8,128)(2,1)S(1)}, bf16[512,512]{1,0:T(8,128)(2,1)S(1)}, bf16[512,512]{1,0:T(8,128)(2,1)S(1)}) custom-call(s32[3]{0:T(128)S(1)} %pad_add_fusion.coord, s32[3,49]{1,0:T(4,128)S(1)} %bitcast.49, bf16[192,512]{1,0:T(8,128)(2,1)S(1)} %bitcast.47, ...), custom_call_target="tpu_custom_call" | custom-call | flops 402653184 | bytes 6000000 | tf_op jit(solution)/shard_map/pallas_call | solution.py:312
  13.2 2.1 %collective-permute-start.2 = (bf16[30,3,512]{2,1,0:T(4,128)(2,1)S(1)}, bf16[30,3,512]{2,1,0:T(4,128)(2,1)S(1)}, u32[]{:S(2)}, u32[]{:S(2)}) collective-permute-start(bf16[30,3,512]{2,1,0:T(4,128)(2,1)S(1)} %get-tuple-element.72), channel_id=1, source_target_pairs={{0,1},{1,2},{2,3},{3,4},{4,5},{5,6},{6,7},{7,8},{8,9},{9,10},{10,1... | collective-permute-start | bytes 276488 | tf_op jit(solution)/shard_map/ppermute | solution.py:250
  15.3 6.5 %collective-permute-start.3 = (bf16[30,3,512]{2,1,0:T(4,128)(2,1)S(1)}, bf16[30,3,512]{2,1,0:T(4,128)(2,1)S(1)}, u32[]{:S(2)}, u32[]{:S(2)}) collective-permute-start(bf16[30,3,512]{2,1,0:T(4,128)(2,1)S(1)} %get-tuple-element.73), channel_id=1, source_target_pairs={{1,0},{2,1},{3,2},{4,3},{5,4},{6,5},{7,6},{8,7},{9,8},{10,9},{11,1... | collective-permute-start | bytes 276488 | tf_op jit(solution)/shard_map/ppermute | solution.py:250
  24.4 12.0 %shard_map.128 = (bf16[256,2560]{1,0:T(8,128)(2,1)}, bf16[256,2560]{1,0:T(8,128)(2,1)}, bf16[4,2,2,2,32,512]{5,4,3,2,1,0:T(8,128)(2,1)}, bf16[4,2,2,2,32,512]{5,...) custom-call(s32[3]{0:T(128)S(1)} %pad_add_fusion.coord, ...), custom_call_target="tpu_custom_call" | custom-call | flops 5000000000 | bytes 20000000 | tf_op jit(solution)/shard_map/pallas_call | solution.py:318
  36.5 8.1 %shard_map.129 = (bf16[272,1536]{1,0:T(8,128)(2,1)S(1)}, bf16[272,1536]{1,0:T(8,128)(2,1)}, f32[512,512]{1,0:T(8,128)}, f32[192,512]{1,0:T(8,128)S(1)}) custom-call(bf16[192,512]{1,0:T(8,128)(2,1)S(1)} %get-tuple-element.30.gm, bf16[512,512]{1,0:T(8,128)(2,1)S(1)} %copy-done.5, bf16[512,1536]{1,0:T(8,128)(2,1)} %w_qkv.3, ...), custom_call_target="tpu_custom_call" | custom-call | flops 3000000000 | bytes 12000000 | tf_op jit(solution)/shard_map/pallas_call | solution.py:329
  46.0 2.4 %collective-permute-start.4 = (bf16[30,3,512]{2,1,0:T(4,128)(2,1)S(1)}, bf16[30,3,512]{2,1,0:T(4,128)(2,1)S(1)}, u32[]{:S(2)}, u32[]{:S(2)}) collective-permute-start(bf16[30,3,512]{2,1,0:T(4,128)(2,1)S(1)} %get-tuple-element.62), channel_id=1, source_target_pairs={{0,1},{1,2},{2,3},{3,4},{4,5},{5,6},{6,7},{7,8},{8,9},{9,10},{10,1... | collective-permute-start | bytes 276488 | tf_op jit(solution)/shard_map/ppermute | solution.py:250
  48.4 6.0 %collective-permute-start.5 = (bf16[30,3,512]{2,1,0:T(4,128)(2,1)S(1)}, bf16[30,3,512]{2,1,0:T(4,128)(2,1)S(1)}, u32[]{:S(2)}, u32[]{:S(2)}) collective-permute-start(bf16[30,3,512]{2,1,0:T(4,128)(2,1)S(1)} %get-tuple-element.63), channel_id=1, source_target_pairs={{1,0},{2,1},{3,2},{4,3},{5,4},{6,5},{7,6},{8,7},{9,8},{10,9},{11,1... | collective-permute-start | bytes 276488 | tf_op jit(solution)/shard_map/ppermute | solution.py:250
  55.1 1.7 %collective-permute-done.5 = bf16[30,3,512]{2,1,0:T(4,128)(2,1)S(1)} collective-permute-done((bf16[30,3,512]{2,1,0:T(4,128)(2,1)S(1)}, bf16[30,3,512]{2,1,0:T(4,128)(2,1)S(1)}, u32[]{:S(2)}, u32[]{:S(2)}) %collective-permute-start.5) | collective-permute-done | bytes 92192 | tf_op jit(solution)/shard_map/ppermute | solution.py:250
  57.0 4.5 %collective-permute-start.6 = (bf16[3,8,512]{2,1,0:T(8,128)(2,1)S(1)}, bf16[3,8,512]{2,1,0:T(8,128)(2,1)S(1)}, u32[]{:S(2)}, u32[]{:S(2)}) collective-permute-start(bf16[3,8,512]{2,1,0:T(8,128)(2,1)S(1)} %get-tuple-element.70), channel_id=1, source_target_pairs={{0,32},{1,33},{2,34},{3,35},{4,36},{5,37},{6,38},{7,39},{8,40},{9,... | collective-permute-start | bytes 73736 | tf_op jit(solution)/shard_map/ppermute | solution.py:250
  61.6 1.3 collective-permute-start.7
  63.5 3.0 %collective-permute-start.24 = (bf16[72,1536]{1,0:T(8,128)(2,1)S(1)}, bf16[72,1536]{1,0:T(8,128)(2,1)S(1)}, u32[]{:S(2)}, u32[]{:S(2)}) collective-permute-start(bf16[72,1536]{1,0:T(8,128)(2,1)S(1)} %get-tuple-element.93), channel_id=1, source_target_pairs={{0,16},{1,17},{2,18},{3,19},{4,20},{5,21},{6,22},{7,23},{8,24},{9,... | collective-permute-start | bytes 663560 | tf_op jit(solution)/shard_map/ppermute | solution.py:250
  68.7 3.2 %collective-permute-done.23 = bf16[72,1536]{1,0:T(8,128)(2,1)S(1)} collective-permute-done((bf16[72,1536]{1,0:T(8,128)(2,1)S(1)}, bf16[72,1536]{1,0:T(8,128)(2,1)S(1)}, u32[]{:S(2)}, u32[]{:S(2)}) %collective-permute-start.23) | collective-permute-done | bytes 221216 | tf_op jit(solution)/shard_map/ppermute | solution.py:250
  71.9 3.7 %collective-permute-done.24 = bf16[72,1536]{1,0:T(8,128)(2,1)S(1)} collective-permute-done((bf16[72,1536]{1,0:T(8,128)(2,1)S(1)}, bf16[72,1536]{1,0:T(8,128)(2,1)S(1)}, u32[]{:S(2)}, u32[]{:S(2)}) %collective-permute-start.24) | collective-permute-done | bytes 221216 | tf_op jit(solution)/shard_map/ppermute | solution.py:250
  75.6 1.4 collective-permute-done.25
  77.2 3.3 %collective-permute-start.26 = (bf16[24,1536]{1,0:T(8,128)(2,1)S(1)}, bf16[24,1536]{1,0:T(8,128)(2,1)S(1)}, u32[]{:S(2)}, u32[]{:S(2)}) collective-permute-start(bf16[24,1536]{1,0:T(8,128)(2,1)S(1)} %get-tuple-element.90), channel_id=1, source_target_pairs={{0,32},{1,33},{2,34},{3,35},{4,36},{5,37},{6,38},{7,39},{8,40},{9,... | collective-permute-start | bytes 221192 | tf_op jit(solution)/shard_map/ppermute | solution.py:250
  80.4 13.3 %collective-permute-start.27 = (bf16[24,1536]{1,0:T(8,128)(2,1)S(1)}, bf16[24,1536]{1,0:T(8,128)(2,1)S(1)}, u32[]{:S(2)}, u32[]{:S(2)}) collective-permute-start(bf16[24,1536]{1,0:T(8,128)(2,1)S(1)} %get-tuple-element.91), channel_id=1, source_target_pairs={{0,64},{1,65},{2,66},{3,67},{4,68},{5,69},{6,70},{7,71},{8,72},{9,... | collective-permute-start | bytes 221192 | tf_op jit(solution)/shard_map/ppermute | solution.py:250
  94.7 1.8 %collective-permute-start.16 = (bf16[256,512]{1,0:T(8,128)(2,1)}, bf16[256,512]{1,0:T(8,128)(2,1)}, u32[]{:S(2)}, u32[]{:S(2)}) collective-permute-start(bf16[256,512]{1,0:T(8,128)(2,1)} %get-tuple-element.59), channel_id=1, source_target_pairs={{0,8},{1,9},{2,10},{3,11},{4,12},{5,13},{6,14},{7,15},{8,0},{9,1},... | collective-permute-start | bytes 786440 | tf_op jit(solution)/shard_map/ppermute | solution.py:250
  96.8 1.4 collective-permute-start.18
  99.4 1.4 add_convert_fusion.3
  101.6 1.5 collective-permute-start.11
  104.4 3.1 %collective-permute-done.17 = bf16[256,512]{1,0:T(8,128)(2,1)} collective-permute-done((bf16[256,512]{1,0:T(8,128)(2,1)S(1)}, bf16[256,512]{1,0:T(8,128)(2,1)}, u32[]{:S(2)}, u32[]{:S(2)}) %collective-permute-start.17) | collective-permute-done | bytes 262176 | tf_op jit(solution)/shard_map/ppermute | solution.py:250
  108.6 1.4 add_convert_fusion.5
  110.1 4.4 %collective-permute-start.20 = (bf16[64,512]{1,0:T(8,128)(2,1)S(1)}, bf16[64,512]{1,0:T(8,128)(2,1)S(1)}, u32[]{:S(2)}, u32[]{:S(2)}) collective-permute-start(bf16[64,512]{1,0:T(8,128)(2,1)S(1)} %get-tuple-element.69), channel_id=1, source_target_pairs={{0,64},{1,65},{2,66},{3,67},{4,68},{5,69},{6,70},{7,71},{8,72},{9,... | collective-permute-start | bytes 196616 | tf_op jit(solution)/shard_map/ppermute | solution.py:250
  118.0 3.0 %collective-permute-start.12 = (bf16[16,2560]{1,0:T(8,128)(2,1)S(1)}, bf16[16,2560]{1,0:T(8,128)(2,1)S(1)}, u32[]{:S(2)}, u32[]{:S(2)}) collective-permute-start(bf16[16,2560]{1,0:T(8,128)(2,1)S(1)} %get-tuple-element.64), channel_id=1, source_target_pairs={{0,8},{1,9},{2,10},{3,11},{4,12},{5,13},{6,14},{7,15},{8,0},{9,1},... | collective-permute-start | bytes 245768 | tf_op jit(solution)/shard_map/ppermute | solution.py:250
  122.7 1.6 %collective-permute-done.12 = bf16[16,2560]{1,0:T(8,128)(2,1)S(1)} collective-permute-done((bf16[16,2560]{1,0:T(8,128)(2,1)S(1)}, bf16[16,2560]{1,0:T(8,128)(2,1)S(1)}, u32[]{:S(2)}, u32[]{:S(2)}) %collective-permute-start.12) | collective-permute-done | bytes 81952 | tf_op jit(solution)/shard_map/ppermute | solution.py:250
  124.3 2.8 %collective-permute-done.13 = bf16[16,2560]{1,0:T(8,128)(2,1)S(1)} collective-permute-done((bf16[16,2560]{1,0:T(8,128)(2,1)S(1)}, bf16[16,2560]{1,0:T(8,128)(2,1)S(1)}, u32[]{:S(2)}, u32[]{:S(2)}) %collective-permute-start.13) | collective-permute-done | bytes 81952 | tf_op jit(solution)/shard_map/ppermute | solution.py:250
  128.9 5.4 %collective-permute-start.30 = (bf16[1,13312]{1,0:T(2,128)(2,1)S(1)}, bf16[1,13312]{1,0:T(2,128)(2,1)S(1)}, u32[]{:S(2)}, u32[]{:S(2)}) collective-permute-start(bf16[1,13312]{1,0:T(2,128)(2,1)S(1)} %get-tuple-element.83), channel_id=1, source_target_pairs={{0,4},{1,5},{2,6},{3,7},{4,0},{5,1},{6,2},{7,3},{8,12},{9,13},{10,... | collective-permute-start | bytes 79880 | tf_op jit(solution)/shard_map/ppermute | solution.py:250
  134.4 7.5 %collective-permute-start.32 = (bf16[1,13312]{1,0:T(2,128)(2,1)S(1)}, bf16[1,13312]{1,0:T(2,128)(2,1)S(1)}, u32[]{:S(2)}, u32[]{:S(2)}) collective-permute-start(bf16[1,13312]{1,0:T(2,128)(2,1)S(1)} %get-tuple-element.81), channel_id=1, source_target_pairs={{0,128},{1,129},{2,130},{3,131},{4,132},{5,133},{6,134},{7,135},{8... | collective-permute-start | bytes 79880 | tf_op jit(solution)/shard_map/ppermute | solution.py:250
  141.9 6.4 %collective-permute-start.34 = (bf16[1,13312]{1,0:T(2,128)(2,1)S(1)}, bf16[1,13312]{1,0:T(2,128)(2,1)S(1)}, u32[]{:S(2)}, u32[]{:S(2)}) collective-permute-start(bf16[1,13312]{1,0:T(2,128)(2,1)S(1)} %get-tuple-element.79), channel_id=1, source_target_pairs={{0,132},{1,133},{2,134},{3,135},{4,128},{5,129},{6,130},{7,131},{8... | collective-permute-start | bytes 79880 | tf_op jit(solution)/shard_map/ppermute | solution.py:250
  150.4 3.3 %collective-permute-done.35 = bf16[1,13312]{1,0:T(2,128)(2,1)S(1)} collective-permute-done((bf16[1,13312]{1,0:T(2,128)(2,1)S(1)}, bf16[1,13312]{1,0:T(2,128)(2,1)S(1)}, u32[]{:S(2)}, u32[]{:S(2)}) %collective-permute-start.35) | collective-permute-done | bytes 26656 | tf_op jit(solution)/shard_map/ppermute | solution.py:250
  (137 shorter events, 29.1 us)
Async XLA Ops:
  1.4 11.6 %collective-permute-start = (bf16[3,8,512]{2,1,0:T(8,128)(2,1)S(1)}, bf16[3,8,512]{2,1,0:T(8,128)(2,1)S(1)}, u32[]{:S(2)}, u32[]{:S(2)}) collective-permute-start(bf16[3,8,512]{2,1,0:T(8,128)(2,1)S(1)} %get-tuple-element.85), channel_id=1, source_target_pairs={{0,32},{1,33},{2,34},{3,35},{4,36},{5,37},{6,38},{7,39},{8,40},{9,... | collective-permute-start | bytes 73736 | tf_op jit(solution)/shard_map/ppermute | solution.py:250
  4.8 8.2 %collective-permute-start.1 = (bf16[3,8,512]{2,1,0:T(8,128)(2,1)S(1)}, bf16[3,8,512]{2,1,0:T(8,128)(2,1)S(1)}, u32[]{:S(2)}, u32[]{:S(2)}) collective-permute-start(bf16[3,8,512]{2,1,0:T(8,128)(2,1)S(1)} %get-tuple-element.84), channel_id=1, source_target_pairs={{32,0},{33,1},{34,2},{35,3},{36,4},{37,5},{38,6},{39,7},{40,8},{41... | collective-permute-start | bytes 73736 | tf_op jit(solution)/shard_map/ppermute | solution.py:250
  13.2 9.6 %collective-permute-start.2 = (bf16[30,3,512]{2,1,0:T(4,128)(2,1)S(1)}, bf16[30,3,512]{2,1,0:T(4,128)(2,1)S(1)}, u32[]{:S(2)}, u32[]{:S(2)}) collective-permute-start(bf16[30,3,512]{2,1,0:T(4,128)(2,1)S(1)} %get-tuple-element.72), channel_id=1, source_target_pairs={{0,1},{1,2},{2,3},{3,4},{4,5},{5,6},{6,7},{7,8},{8,9},{9,10},{10,1... | collective-permute-start | bytes 276488 | tf_op jit(solution)/shard_map/ppermute | solution.py:250
  15.3 8.8 %collective-permute-start.3 = (bf16[30,3,512]{2,1,0:T(4,128)(2,1)S(1)}, bf16[30,3,512]{2,1,0:T(4,128)(2,1)S(1)}, u32[]{:S(2)}, u32[]{:S(2)}) collective-permute-start(bf16[30,3,512]{2,1,0:T(4,128)(2,1)S(1)} %get-tuple-element.73), channel_id=1, source_target_pairs={{1,0},{2,1},{3,2},{4,3},{5,4},{6,5},{7,6},{8,7},{9,8},{10,9},{11,1... | collective-permute-start | bytes 276488 | tf_op jit(solution)/shard_map/ppermute | solution.py:250
  44.6 18.3 %collective-permute-start.22 = (bf16[272,1536]{1,0:T(8,128)(2,1)}, bf16[272,1536]{1,0:T(8,128)(2,1)S(1)}, u32[]{:S(2)}, u32[]{:S(2)}) collective-permute-start(bf16[272,1536]{1,0:T(8,128)(2,1)} %get-tuple-element.45), channel_id=1, source_target_pairs={{0,1},{1,0},{2,3},{3,2},{4,5},{5,4},{6,7},{7,6},{8,9},{9,8},{10,11... | collective-permute-start | bytes 2506760 | tf_op jit(solution)/shard_map/ppermute | solution.py:250
  46.0 9.1 %collective-permute-start.4 = (bf16[30,3,512]{2,1,0:T(4,128)(2,1)S(1)}, bf16[30,3,512]{2,1,0:T(4,128)(2,1)S(1)}, u32[]{:S(2)}, u32[]{:S(2)}) collective-permute-start(bf16[30,3,512]{2,1,0:T(4,128)(2,1)S(1)} %get-tuple-element.62), channel_id=1, source_target_pairs={{0,1},{1,2},{2,3},{3,4},{4,5},{5,6},{6,7},{7,8},{8,9},{9,10},{10,1... | collective-permute-start | bytes 276488 | tf_op jit(solution)/shard_map/ppermute | solution.py:250
  48.4 8.4 %collective-permute-start.5 = (bf16[30,3,512]{2,1,0:T(4,128)(2,1)S(1)}, bf16[30,3,512]{2,1,0:T(4,128)(2,1)S(1)}, u32[]{:S(2)}, u32[]{:S(2)}) collective-permute-start(bf16[30,3,512]{2,1,0:T(4,128)(2,1)S(1)} %get-tuple-element.63), channel_id=1, source_target_pairs={{1,0},{2,1},{3,2},{4,3},{5,4},{6,5},{7,6},{8,7},{9,8},{10,9},{11,1... | collective-permute-start | bytes 276488 | tf_op jit(solution)/shard_map/ppermute | solution.py:250
  57.0 10.0 %collective-permute-start.6 = (bf16[3,8,512]{2,1,0:T(8,128)(2,1)S(1)}, bf16[3,8,512]{2,1,0:T(8,128)(2,1)S(1)}, u32[]{:S(2)}, u32[]{:S(2)}) collective-permute-start(bf16[3,8,512]{2,1,0:T(8,128)(2,1)S(1)} %get-tuple-element.70), channel_id=1, source_target_pairs={{0,32},{1,33},{2,34},{3,35},{4,36},{5,37},{6,38},{7,39},{8,40},{9,... | collective-permute-start | bytes 73736 | tf_op jit(solution)/shard_map/ppermute | solution.py:250
  61.6 6.3 %collective-permute-start.7 = (bf16[3,8,512]{2,1,0:T(8,128)(2,1)S(1)}, bf16[3,8,512]{2,1,0:T(8,128)(2,1)S(1)}, u32[]{:S(2)}, u32[]{:S(2)}) collective-permute-start(bf16[3,8,512]{2,1,0:T(8,128)(2,1)S(1)} %get-tuple-element.71), channel_id=1, source_target_pairs={{32,0},{33,1},{34,2},{35,3},{36,4},{37,5},{38,6},{39,7},{40,8},{41... | collective-permute-start | bytes 73736 | tf_op jit(solution)/shard_map/ppermute | solution.py:250
  63.2 8.7 %collective-permute-start.23 = (bf16[72,1536]{1,0:T(8,128)(2,1)S(1)}, bf16[72,1536]{1,0:T(8,128)(2,1)S(1)}, u32[]{:S(2)}, u32[]{:S(2)}) collective-permute-start(bf16[72,1536]{1,0:T(8,128)(2,1)S(1)} %get-tuple-element.92), channel_id=1, source_target_pairs={{0,8},{1,9},{2,10},{3,11},{4,12},{5,13},{6,14},{7,15},{8,0},{9,1},... | collective-permute-start | bytes 663560 | tf_op jit(solution)/shard_map/ppermute | solution.py:250
  63.5 12.1 %collective-permute-start.24 = (bf16[72,1536]{1,0:T(8,128)(2,1)S(1)}, bf16[72,1536]{1,0:T(8,128)(2,1)S(1)}, u32[]{:S(2)}, u32[]{:S(2)}) collective-permute-start(bf16[72,1536]{1,0:T(8,128)(2,1)S(1)} %get-tuple-element.93), channel_id=1, source_target_pairs={{0,16},{1,17},{2,18},{3,19},{4,20},{5,21},{6,22},{7,23},{8,24},{9,... | collective-permute-start | bytes 663560 | tf_op jit(solution)/shard_map/ppermute | solution.py:250
  66.5 10.4 %collective-permute-start.25 = (bf16[72,1536]{1,0:T(8,128)(2,1)S(1)}, bf16[72,1536]{1,0:T(8,128)(2,1)S(1)}, u32[]{:S(2)}, u32[]{:S(2)}) collective-permute-start(bf16[72,1536]{1,0:T(8,128)(2,1)S(1)} %get-tuple-element.94), channel_id=1, source_target_pairs={{0,24},{1,25},{2,26},{3,27},{4,28},{5,29},{6,30},{7,31},{8,16},{9,... | collective-permute-start | bytes 663560 | tf_op jit(solution)/shard_map/ppermute | solution.py:250
  67.1 26.6 %collective-permute-start.15 = (bf16[1024,512]{1,0:T(8,128)(2,1)S(1)}, bf16[1024,512]{1,0:T(8,128)(2,1)S(1)}, u32[]{:S(2)}, u32[]{:S(2)}) collective-permute-start(bf16[1024,512]{1,0:T(8,128)(2,1)S(1)} %bitcast.60), channel_id=1, source_target_pairs={{0,1},{1,0},{2,3},{3,2},{4,5},{5,4},{6,7},{7,6},{8,9},{9,8},{10,11... | collective-permute-start | bytes 3145736 | tf_op jit(solution)/shard_map/ppermute | solution.py:250
  67.9 31.5 %collective-permute-start.8 = (bf16[256,2560]{1,0:T(8,128)(2,1)}, bf16[256,2560]{1,0:T(8,128)(2,1)}, u32[]{:S(2)}, u32[]{:S(2)}) collective-permute-start(bf16[256,2560]{1,0:T(8,128)(2,1)} %get-tuple-element.41), channel_id=1, source_target_pairs={{0,1},{1,0},{2,3},{3,2},{4,5},{5,4},{6,7},{7,6},{8,9},{9,8},{10,11... | collective-permute-start | bytes 3932168 | tf_op jit(solution)/shard_map/ppermute | solution.py:250
  77.2 19.3 %collective-permute-start.26 = (bf16[24,1536]{1,0:T(8,128)(2,1)S(1)}, bf16[24,1536]{1,0:T(8,128)(2,1)S(1)}, u32[]{:S(2)}, u32[]{:S(2)}) collective-permute-start(bf16[24,1536]{1,0:T(8,128)(2,1)S(1)} %get-tuple-element.90), channel_id=1, source_target_pairs={{0,32},{1,33},{2,34},{3,35},{4,36},{5,37},{6,38},{7,39},{8,40},{9,... | collective-permute-start | bytes 221192 | tf_op jit(solution)/shard_map/ppermute | solution.py:250
  80.4 16.4 %collective-permute-start.27 = (bf16[24,1536]{1,0:T(8,128)(2,1)S(1)}, bf16[24,1536]{1,0:T(8,128)(2,1)S(1)}, u32[]{:S(2)}, u32[]{:S(2)}) collective-permute-start(bf16[24,1536]{1,0:T(8,128)(2,1)S(1)} %get-tuple-element.91), channel_id=1, source_target_pairs={{0,64},{1,65},{2,66},{3,67},{4,68},{5,69},{6,70},{7,71},{8,72},{9,... | collective-permute-start | bytes 221192 | tf_op jit(solution)/shard_map/ppermute | solution.py:250
  94.7 9.3 %collective-permute-start.16 = (bf16[256,512]{1,0:T(8,128)(2,1)}, bf16[256,512]{1,0:T(8,128)(2,1)}, u32[]{:S(2)}, u32[]{:S(2)}) collective-permute-start(bf16[256,512]{1,0:T(8,128)(2,1)} %get-tuple-element.59), channel_id=1, source_target_pairs={{0,8},{1,9},{2,10},{3,11},{4,12},{5,13},{6,14},{7,15},{8,0},{9,1},... | collective-permute-start | bytes 786440 | tf_op jit(solution)/shard_map/ppermute | solution.py:250
  96.5 11.0 %collective-permute-start.17 = (bf16[256,512]{1,0:T(8,128)(2,1)S(1)}, bf16[256,512]{1,0:T(8,128)(2,1)}, u32[]{:S(2)}, u32[]{:S(2)}) collective-permute-start(bf16[256,512]{1,0:T(8,128)(2,1)S(1)} %get-tuple-element.61), channel_id=1, source_target_pairs={{0,16},{1,17},{2,18},{3,19},{4,20},{5,21},{6,22},{7,23},{8,24},{9,... | collective-permute-start | bytes 786440 | tf_op jit(solution)/shard_map/ppermute | solution.py:250
  96.8 11.8 %collective-permute-start.18 = (bf16[256,512]{1,0:T(8,128)(2,1)S(1)}, bf16[256,512]{1,0:T(8,128)(2,1)}, u32[]{:S(2)}, u32[]{:S(2)}) collective-permute-start(bf16[256,512]{1,0:T(8,128)(2,1)S(1)} %get-tuple-element.60), channel_id=1, source_target_pairs={{0,24},{1,25},{2,26},{3,27},{4,28},{5,29},{6,30},{7,31},{8,16},{9,... | collective-permute-start | bytes 786440 | tf_op jit(solution)/shard_map/ppermute | solution.py:250
  100.8 13.7 %collective-permute-start.10 = (bf16[64,2560]{1,0:T(8,128)(2,1)S(1)}, bf16[64,2560]{1,0:T(8,128)(2,1)S(1)}, u32[]{:S(2)}, u32[]{:S(2)}) collective-permute-start(bf16[64,2560]{1,0:T(8,128)(2,1)S(1)} %get-tuple-element.50), channel_id=1, source_target_pairs={{0,64},{1,65},{2,66},{3,67},{4,68},{5,69},{6,70},{7,71},{8,72},{9,... | collective-permute-start | bytes 983048 | tf_op jit(solution)/shard_map/ppermute | solution.py:250
  101.6 14.8 %collective-permute-start.11 = (bf16[64,2560]{1,0:T(8,128)(2,1)S(1)}, bf16[64,2560]{1,0:T(8,128)(2,1)S(1)}, u32[]{:S(2)}, u32[]{:S(2)}) collective-permute-start(bf16[64,2560]{1,0:T(8,128)(2,1)S(1)} %get-tuple-element.49), channel_id=1, source_target_pairs={{0,96},{1,97},{2,98},{3,99},{4,100},{5,101},{6,102},{7,103},{8,104... | collective-permute-start | bytes 983048 | tf_op jit(solution)/shard_map/ppermute | solution.py:250
  104.0 12.8 %collective-permute-start.9 = (bf16[64,2560]{1,0:T(8,128)(2,1)S(1)}, bf16[64,2560]{1,0:T(8,128)(2,1)S(1)}, u32[]{:S(2)}, u32[]{:S(2)}) collective-permute-start(bf16[64,2560]{1,0:T(8,128)(2,1)S(1)} %get-tuple-element.48), channel_id=1, source_target_pairs={{0,32},{1,33},{2,34},{3,35},{4,36},{5,37},{6,38},{7,39},{8,40},{9,... | collective-permute-start | bytes 983048 | tf_op jit(solution)/shard_map/ppermute | solution.py:250
  110.0 11.8 %collective-permute-start.19 = (bf16[64,512]{1,0:T(8,128)(2,1)S(1)}, bf16[64,512]{1,0:T(8,128)(2,1)S(1)}, u32[]{:S(2)}, u32[]{:S(2)}) collective-permute-start(bf16[64,512]{1,0:T(8,128)(2,1)S(1)} %get-tuple-element.67), channel_id=1, source_target_pairs={{0,32},{1,33},{2,34},{3,35},{4,36},{5,37},{6,38},{7,39},{8,40},{9,... | collective-permute-start | bytes 196616 | tf_op jit(solution)/shard_map/ppermute | solution.py:250
  110.1 12.5 %collective-permute-start.20 = (bf16[64,512]{1,0:T(8,128)(2,1)S(1)}, bf16[64,512]{1,0:T(8,128)(2,1)S(1)}, u32[]{:S(2)}, u32[]{:S(2)}) collective-permute-start(bf16[64,512]{1,0:T(8,128)(2,1)S(1)} %get-tuple-element.69), channel_id=1, source_target_pairs={{0,64},{1,65},{2,66},{3,67},{4,68},{5,69},{6,70},{7,71},{8,72},{9,... | collective-permute-start | bytes 196616 | tf_op jit(solution)/shard_map/ppermute | solution.py:250
  114.5 8.1 %collective-permute-start.21 = (bf16[64,512]{1,0:T(8,128)(2,1)S(1)}, bf16[64,512]{1,0:T(8,128)(2,1)S(1)}, u32[]{:S(2)}, u32[]{:S(2)}) collective-permute-start(bf16[64,512]{1,0:T(8,128)(2,1)S(1)} %get-tuple-element.68), channel_id=1, source_target_pairs={{0,96},{1,97},{2,98},{3,99},{4,100},{5,101},{6,102},{7,103},{8,104... | collective-permute-start | bytes 196616 | tf_op jit(solution)/shard_map/ppermute | solution.py:250
  118.0 6.3 %collective-permute-start.12 = (bf16[16,2560]{1,0:T(8,128)(2,1)S(1)}, bf16[16,2560]{1,0:T(8,128)(2,1)S(1)}, u32[]{:S(2)}, u32[]{:S(2)}) collective-permute-start(bf16[16,2560]{1,0:T(8,128)(2,1)S(1)} %get-tuple-element.64), channel_id=1, source_target_pairs={{0,8},{1,9},{2,10},{3,11},{4,12},{5,13},{6,14},{7,15},{8,0},{9,1},... | collective-permute-start | bytes 245768 | tf_op jit(solution)/shard_map/ppermute | solution.py:250
  127.7 14.2 %collective-permute-start.29 = (bf16[1,13312]{1,0:T(2,128)(2,1)S(1)}, bf16[1,13312]{1,0:T(2,128)(2,1)S(1)}, u32[]{:S(2)}, u32[]{:S(2)}) collective-permute-start(bf16[1,13312]{1,0:T(2,128)(2,1)S(1)} %get-tuple-element.77), channel_id=1, source_target_pairs={{0,2},{1,3},{2,0},{3,1},{4,6},{5,7},{6,4},{7,5},{8,10},{9,11},{10,... | collective-permute-start | bytes 79880 | tf_op jit(solution)/shard_map/ppermute | solution.py:250
  128.9 19.4 %collective-permute-start.30 = (bf16[1,13312]{1,0:T(2,128)(2,1)S(1)}, bf16[1,13312]{1,0:T(2,128)(2,1)S(1)}, u32[]{:S(2)}, u32[]{:S(2)}) collective-permute-start(bf16[1,13312]{1,0:T(2,128)(2,1)S(1)} %get-tuple-element.83), channel_id=1, source_target_pairs={{0,4},{1,5},{2,6},{3,7},{4,0},{5,1},{6,2},{7,3},{8,12},{9,13},{10,... | collective-permute-start | bytes 79880 | tf_op jit(solution)/shard_map/ppermute | solution.py:250
  134.4 14.9 %collective-permute-start.31 = (bf16[1,13312]{1,0:T(2,128)(2,1)S(1)}, bf16[1,13312]{1,0:T(2,128)(2,1)S(1)}, u32[]{:S(2)}, u32[]{:S(2)}) collective-permute-start(bf16[1,13312]{1,0:T(2,128)(2,1)S(1)} %get-tuple-element.82), channel_id=1, source_target_pairs={{0,6},{1,7},{2,4},{3,5},{4,2},{5,3},{6,0},{7,1},{8,14},{9,15},{10,... | collective-permute-start | bytes 79880 | tf_op jit(solution)/shard_map/ppermute | solution.py:250
  134.4 14.9 %collective-permute-start.32 = (bf16[1,13312]{1,0:T(2,128)(2,1)S(1)}, bf16[1,13312]{1,0:T(2,128)(2,1)S(1)}, u32[]{:S(2)}, u32[]{:S(2)}) collective-permute-start(bf16[1,13312]{1,0:T(2,128)(2,1)S(1)} %get-tuple-element.81), channel_id=1, source_target_pairs={{0,128},{1,129},{2,130},{3,131},{4,132},{5,133},{6,134},{7,135},{8... | collective-permute-start | bytes 79880 | tf_op jit(solution)/shard_map/ppermute | solution.py:250
  141.9 7.5 %collective-permute-start.33 = (bf16[1,13312]{1,0:T(2,128)(2,1)S(1)}, bf16[1,13312]{1,0:T(2,128)(2,1)S(1)}, u32[]{:S(2)}, u32[]{:S(2)}) collective-permute-start(bf16[1,13312]{1,0:T(2,128)(2,1)S(1)} %get-tuple-element.80), channel_id=1, source_target_pairs={{0,130},{1,131},{2,128},{3,129},{4,134},{5,135},{6,132},{7,133},{8... | collective-permute-start | bytes 79880 | tf_op jit(solution)/shard_map/ppermute | solution.py:250
  141.9 8.5 %collective-permute-start.34 = (bf16[1,13312]{1,0:T(2,128)(2,1)S(1)}, bf16[1,13312]{1,0:T(2,128)(2,1)S(1)}, u32[]{:S(2)}, u32[]{:S(2)}) collective-permute-start(bf16[1,13312]{1,0:T(2,128)(2,1)S(1)} %get-tuple-element.79), channel_id=1, source_target_pairs={{0,132},{1,133},{2,134},{3,135},{4,128},{5,129},{6,130},{7,131},{8... | collective-permute-start | bytes 79880 | tf_op jit(solution)/shard_map/ppermute | solution.py:250
  (21 other events, 230.3 us)

commit v2 on v1

v2 whole, which is shorter than its diff:
```python
import math

import jax
import jax.numpy as jnp
from jax import lax
from jax.experimental import pallas as pl
from jax.experimental.pallas import tpu as pltpu
from jax.sharding import PartitionSpec as P

D = 512
FF = 2048
HEADS = 8
WINDOW = 7
TILE = 8
RIM = WINDOW // 2
EPS = 1e-06
AXES = ("row", "col")
N_COL = 32
GRID_ROWS = 192
GRID_COLS = 256
ROWS = 24
COLS = 8
TOK = ROWS * COLS
TILES = ROWS // TILE
ER = 32
EC = 16
EXT = ER * EC
QT = TILE * TILE
KT = 256
F32 = jnp.float32
BF16 = jnp.bfloat16
GELU_C = math.sqrt(2.0 / math.pi)


def nn(a, b):
    return lax.dot_general(a, b, (((1,), (0,)), ((), ())), preferred_element_type=F32)


def nt(a, b):
    return lax.dot_general(a, b, (((1,), (1,)), ((), ())), preferred_element_type=F32)


def tn(a, b):
    return lax.dot_general(a, b, (((0,), (0,)), ((), ())), preferred_element_type=F32)


def unit_of(x):
    inv = lax.rsqrt(jnp.mean(x * x, axis=-1, keepdims=True) + EPS)
    return x * inv, inv


def head_mask(rows, h):
    lane = lax.broadcasted_iota(jnp.int32, (rows, 256), 1)
    return (lane // 64) == h


def stack_heads(x):
    zero = jnp.zeros_like(x)
    return jnp.concatenate([jnp.where(head_mask(x.shape[0], h), x, zero) for h in range(4)], axis=0)


def unstack_heads(x):
    rows = x.shape[0] // 4
    out = jnp.where(head_mask(rows, 0), x[:rows], 0.0)
    for h in range(1, 4):
        out = out + jnp.where(head_mask(rows, h), x[h * rows : (h + 1) * rows], 0.0)
    return out


def prep_front_kernel(cot, w_down, gact):
    for c in range(4):
        gact[:, c * 512 : (c + 1) * 512] = nt(cot[...], w_down[c * 512 : (c + 1) * 512, :])


def prep_mask_kernel(coord, mask, bias, pt_u, pt_d):
    q = lax.broadcasted_iota(jnp.int32, (QT, KT), 0)
    k = lax.broadcasted_iota(jnp.int32, (QT, KT), 1)
    ki = k // EC
    kc = k % EC
    kj = jnp.where(kc < COLS, kc + RIM, jnp.where(kc < COLS + RIM, kc - COLS, kc))
    da = ki - q // TILE
    db = kj - q % TILE
    slot = jnp.where((da >= 0) & (da < WINDOW) & (db >= 0) & (db < WINDOW), da * WINDOW + db, -1)
    allowed = [jnp.zeros((QT, KT), jnp.int32) for _ in range(TILES)]
    for s in range(WINDOW * WINDOW):
        here = slot == s
        for t in range(TILES):
            allowed[t] = jnp.where(here, mask[t, s], allowed[t])
    gc = coord[1] * COLS + kj - RIM
    for t in range(TILES):
        gr = coord[0] * ROWS + t * TILE + ki - RIM
        ok = (allowed[t] == 1) & (gr >= 0) & (gr < GRID_ROWS) & (gc >= 0) & (gc < GRID_COLS)
        bias[t] = jnp.where(ok, 0.0, -1e30)
    me = coord[2] & 1
    lane = lax.broadcasted_iota(jnp.int32, (512, 512), 1)
    p = lax.broadcasted_iota(jnp.int32, (512, 512), 0)
    co = (p >> 8) ^ me
    k_u = ((p >> 3) & 1) * 128 + ((p >> 4) & 15) * 8 + ((p >> 1) & 3) * 2 + co
    pt_u[...] = jnp.where(lane == k_u * 2 + (p & 1), 1.0, 0.0).astype(BF16)
    k_d = ((p >> 5) & 7) * 8 + ((p >> 3) & 3) * 2 + co
    pt_d[...] = jnp.where(lane == k_d * 8 + (p & 7), 1.0, 0.0).astype(BF16)


def forward_kernel(
    mid, top, low, tok, cot, gains, w_qkv, w_out, w_up, gact, bias, pt_u, pt_d,
    u_keep, u_send, d_keep, d_send, gm_o, q_o, kv_o, p_o, ne_o, no_o, gain_o, text_s, attn_s,
):
    text_s[:RIM] = top[...]
    text_s[RIM : RIM + ROWS] = mid[...]
    text_s[RIM + ROWS : ROWS + 2 * RIM] = low[...]
    text_s[ROWS + 2 * RIM :] = jnp.zeros((ER - ROWS - 2 * RIM, EC, D), BF16)
    unit_e, _ = unit_of(text_s[...].reshape(EXT, D).astype(F32))
    ne = (unit_e * gains[0:1, :]).astype(BF16)
    ne_o[...] = ne
    kv_o[...] = nn(ne, w_qkv[:, D:]).astype(BF16)
    xt = tok[...].astype(F32)
    unit_o, _ = unit_of(xt)
    no = (unit_o * gains[0:1, :]).astype(BF16)
    no_o[...] = no
    q_o[...] = nn(no, w_qkv[:, :D]).astype(BF16)
    for t in range(TILES):
        b4 = jnp.concatenate([bias[t]] * 4, axis=0)
        for g in range(2):
            cols = slice(g * 256, (g + 1) * 256)
            vcols = slice(D + g * 256, D + (g + 1) * 256)
            keys = kv_o[t * 128 : t * 128 + KT, cols]
            vals = kv_o[t * 128 : t * 128 + KT, vcols]
            qs = stack_heads(q_o[t * QT : (t + 1) * QT, cols])
            s = nt(qs, keys) * 0.125 + b4
            e = jnp.exp(s - jnp.max(s, axis=-1, keepdims=True))
            prob = e / jnp.sum(e, axis=-1, keepdims=True)
            p_o[t * 2 + g] = prob
            o = nn(prob.astype(BF16), vals)
            attn_s[t * QT : (t + 1) * QT, cols] = unstack_heads(o).astype(BF16)
    attn = attn_s[...]
    mixed = (xt + nn(attn, w_out[...])).astype(BF16)
    um, inv_m = unit_of(mixed.astype(F32))
    nm = (um * gains[1:2, :]).astype(BF16)
    nmt = nt(pt_u[...], nm).astype(BF16)
    gn = jnp.zeros((TOK, D), F32)
    for c in range(4):
        cols = slice(c * 512, (c + 1) * 512)
        pre = nn(nm, w_up[:, cols])
        th = jnp.tanh(GELU_C * (pre + 0.044715 * (pre * pre * pre)))
        half = 0.5 * (1.0 + th)
        act = (pre * half).astype(BF16)
        slope = half + 0.5 * pre * (1.0 - th * th) * (GELU_C * (1.0 + 0.134145 * (pre * pre)))
        gp = (gact[:, cols] * slope).astype(BF16)
        gn = gn + nt(gp, w_up[:, cols])
        gu = nn(nmt, gp).astype(BF16)
        u_keep[:, c] = gu[:256].reshape(16, 16, D)
        u_send[:, c] = gu[256:].reshape(16, 16, D)
        act_t = nt(pt_d[...], act).astype(BF16)
        gd = nn(act_t, cot[...]).astype(BF16)
        for x in range(2):
            lo = (2 * (c & 1) + x) * 4
            d_keep[lo : lo + 4, c >> 1] = gd[x * 128 : x * 128 + 128].reshape(4, 32, D)
            d_send[lo : lo + 4, c >> 1] = gd[256 + x * 128 : 256 + x * 128 + 128].reshape(4, 32, D)
    g = gn * gains[1:2, :]
    gm = (cot[...].astype(F32) + inv_m * (g - um * jnp.mean(g * um, axis=-1, keepdims=True))).astype(BF16)
    gm_o[...] = gm
    gain_o[...] = jnp.sum(gn * um, axis=0, keepdims=True)
    go = nn(nt(pt_u[...], attn).astype(BF16), gm).astype(BF16)
    u_keep[:, 4] = go[:256].reshape(16, 16, D)
    u_send[:, 4] = go[256:].reshape(16, 16, D)


def backward_kernel(
    gm, w_out, w_qkv, q, kv, p_in, ne, no, mid, top, low, tok, gain_mid, pt,
    k_keep, k_send, g_keep, g_send, gne_o, gnq_o, dq_s, dkv_s,
):
    ga = nt(gm[...], w_out[...]).astype(BF16)
    dkv_s[...] = jnp.zeros_like(dkv_s)
    for t in range(TILES):
        for g in range(2):
            cols = slice(g * 256, (g + 1) * 256)
            vcols = slice(D + g * 256, D + (g + 1) * 256)
            rows = slice(t * 128, t * 128 + KT)
            prob = p_in[t * 2 + g]
            gas = stack_heads(ga[t * QT : (t + 1) * QT, cols])
            qs = stack_heads(q[t * QT : (t + 1) * QT, cols])
            gp = nt(gas, kv[rows, vcols])
            inner = jnp.sum(prob * gp, axis=-1, keepdims=True)
            ds = (prob * (gp - inner) * 0.125).astype(BF16)
            dq_s[t * QT : (t + 1) * QT, cols] = unstack_heads(nn(ds, kv[rows, cols])).astype(BF16)
            dkv_s[rows, cols] += tn(ds, qs)
            dkv_s[rows, vcols] += tn(prob.astype(BF16), gas)
    dkv = dkv_s[...].astype(BF16)
    dq = dq_s[...]
    gk = nn(nt(pt[...], ne[...]).astype(BF16), dkv).astype(BF16)
    gq = nn(nt(pt[...], no[...]).astype(BF16), dq).astype(BF16)
    for i, part in enumerate([gq, gk[:, :D], gk[:, D:]]):
        k_keep[:, i] = part[:256].reshape(16, 16, D)
        k_send[:, i] = part[256:].reshape(16, 16, D)
    gne = nt(dkv, w_qkv[:, D:])
    gnq = nt(dq, w_qkv[:, :D])
    gne_o[...] = gne
    gnq_o[...] = gnq
    gain_in = jnp.sum(gnq * unit_of(tok[...].astype(F32))[0], axis=0, keepdims=True)
    at = 0
    for ref in (top, mid, low):
        size = ref.shape[0] * EC
        unit, _ = unit_of(ref[...].reshape(size, D).astype(F32))
        gain_in = gain_in + jnp.sum(gne[at : at + size] * unit, axis=0, keepdims=True)
        at += size
    spread = jnp.concatenate([gain_in, gain_mid[...], jnp.zeros((14, D), F32)], axis=0).astype(BF16)
    g_keep[...] = spread
    g_send[...] = spread


def join_kernel(uk, ur, dk, dr, kk, kr, gk, gr, out):
    at = 0
    for a, b in ((uk, ur), (dk, dr), (kk, kr)):
        n = a.shape[1]
        out[:, at : at + n] = (a[...].astype(F32) + b[...].astype(F32)).astype(BF16)
        at += n
    gain = (gk[...].astype(F32) + gr[...].astype(F32)).astype(BF16)
    for j in range(16):
        out[j, at] = gain


def reduce_xy_kernel(got, out):
    rows = 13 * 16
    acc = got[0].reshape(rows, D).astype(F32)
    for j in range(1, 16):
        acc = acc + got[j].reshape(rows, D).astype(F32)
    acc = acc.astype(BF16)
    i = lax.broadcasted_iota(jnp.int32, (256, rows), 0)
    lane = lax.broadcasted_iota(jnp.int32, (256, rows), 1)
    z = i // 32
    r = i % 32
    up = (r % 4) * 16 + z * 2 + r // 4
    down = 80 + z * 8 + (r - 8)
    o = 64 + z * 2 + (r - 16)
    qkv = 144 + ((r - 18) % 3) * 16 + z * 2 + (r - 18) // 3
    gain = 192 + (r - 24)
    src = jnp.where(r < 8, up, jnp.where(r < 16, down, jnp.where(r < 18, o, jnp.where(r < 24, qkv, gain))))
    pick = jnp.where((lane == src) & (r < 26), 1.0, 0.0).astype(BF16)
    out[...] = nn(pick, acc).astype(BF16).reshape(8, 32, D)


def reduce_z_kernel(got, up, down, o, qkv, gain, acc_s):
    acc = got[0].astype(F32)
    for j in range(1, 8):
        acc = acc + got[j].astype(F32)
    acc_s[...] = acc * (1.0 / math.sqrt(GRID_ROWS * GRID_COLS))
    at = 0
    for ref, rows in ((up, 8), (down, 8), (o, 2), (qkv, 6)):
        for r in range(rows):
            for j in range(4):
                ref[4 * r + j : 4 * r + j + 1, :] = acc_s[at + r : at + r + 1, j * 128 : (j + 1) * 128]
        at += rows
    gain[...] = acc_s[at : at + 2, :]


def call(body, outs, scratch, n_smem, n_in, flops, nbytes, mib):
    smem = pl.BlockSpec(memory_space=pltpu.SMEM)
    vmem = pl.BlockSpec(memory_space=pltpu.VMEM)
    return pl.pallas_call(
        body,
        out_shape=[jax.ShapeDtypeStruct(s, d) for s, d in outs],
        in_specs=[smem] * n_smem + [vmem] * n_in,
        out_specs=[vmem] * len(outs),
        scratch_shapes=scratch,
        compiler_params=pltpu.CompilerParams(vmem_limit_bytes=mib * 1024 * 1024),
        cost_estimate=pl.CostEstimate(flops=flops, bytes_accessed=nbytes, transcendentals=0),
    )


def shift(step):
    pairs = []
    for k in range(256):
        c = k % N_COL
        if step in (1, -1):
            if 0 <= c + step < N_COL:
                pairs.append((k, k + step))
        elif 0 <= k + step < 256:
            pairs.append((k, k + step))
    return pairs


CORE_SWAP = [(k, k ^ 1) for k in range(256)]
XY_GROUPS = [[zh * 128 + x * 32 + y * 8 + zl * 2 + c for x in range(4) for y in range(4)] for zh in range(2) for zl in range(4) for c in range(2)]
Z_GROUPS = [[zh * 128 + x * 32 + y * 8 + zl * 2 + c for zh in range(2) for zl in range(4)] for x in range(4) for y in range(4) for c in range(2)]


def send(x, perm):
    return lax.ppermute(x, AXES, perm)


def exchange(x, groups):
    return lax.all_to_all(x, AXES, 0, 0, axis_index_groups=groups, tiled=True)


def per_device(tokens, cotangent, gains, w_qkv, w_out, w_up, w_down, tile_mask):
    row = lax.axis_index("row")
    col = lax.axis_index("col")
    coord = jnp.stack([row, col, row * N_COL + col]).astype(jnp.int32)
    tok = tokens.reshape(TOK, D)
    cot = cotangent.reshape(TOK, D)
    mask = tile_mask.reshape(TILES, WINDOW * WINDOW)

    left = send(tokens[:, COLS - RIM :], shift(1))
    right = send(tokens[:, :RIM], shift(-1))
    (gact,) = call(
        prep_front_kernel, [((TOK, FF), F32)], [], 0, 2, 2 * TOK * D * FF, 4_000_000, 16,
    )(cot, w_down)
    left, right, gact, mask = lax.optimization_barrier((left, right, gact, mask))
    mid = jnp.concatenate([tokens, left, right, jnp.zeros((ROWS, EC - COLS - 2 * RIM, D), BF16)], axis=1)
    top = send(mid[ROWS - RIM :], shift(N_COL))
    low = send(mid[:RIM], shift(-N_COL))
    bias, pt_u, pt_d = call(
        prep_mask_kernel, [((TILES, QT, KT), F32), ((D, D), BF16), ((D, D), BF16)],
        [], 2, 0, 2 * TOK * D * FF, 4_000_000, 16,
    )(coord, mask)

    half_u, half_d, half_k = ((16, 5, 16, D), BF16), ((16, 2, 32, D), BF16), ((16, 3, 16, D), BF16)
    u_keep, u_send, d_keep, d_send, gm, q, kv, prob, ne, no, gain_mid = call(
        forward_kernel,
        [
            half_u, half_u, half_d, half_d,
            ((TOK, D), BF16), ((TOK, D), BF16), ((EXT, 2 * D), BF16), ((6, 256, KT), F32),
            ((EXT, D), BF16), ((TOK, D), BF16), ((1, D), F32),
        ],
        [pltpu.VMEM((ER, EC, D), BF16), pltpu.VMEM((TOK, D), BF16)], 0, 13, 5_000_000_000, 20_000_000, 30,
    )(mid, top, low, tok, cot, gains, w_qkv, w_out, w_up, gact, bias, pt_u, pt_d)

    u_got = send(u_send, CORE_SWAP)
    d_got = send(d_send, CORE_SWAP)
    k_keep, k_send, g_keep, g_send, gne, gnq = call(
        backward_kernel,
        [half_k, half_k, ((16, D), BF16), ((16, D), BF16), ((EXT, D), F32), ((TOK, D), F32)],
        [pltpu.VMEM((TOK, D), BF16), pltpu.VMEM((EXT, 2 * D), F32)], 0, 14, 3_000_000_000, 12_000_000, 30,
    )(gm, w_out, w_qkv, q, kv, prob, ne, no, mid, top, low, tok, gain_mid, pt_u)
    u_got, d_got, k_send, g_send, gne = lax.optimization_barrier((u_got, d_got, k_send, g_send, gne))

    k_got = send(k_send, CORE_SWAP)
    g_got = send(g_send, CORE_SWAP)
    gne3 = gne.reshape(ER, EC, D)[: ROWS + 2 * RIM]
    to_left = send(gne3[:, COLS : COLS + RIM].astype(BF16), shift(-1)).astype(F32)
    to_right = send(gne3[:, COLS + RIM : COLS + 2 * RIM].astype(BF16), shift(1)).astype(F32)
    gap = COLS - RIM
    own = gne3[:, :COLS]
    own = own + jnp.pad(to_right, ((0, 0), (0, gap), (0, 0))) + jnp.pad(to_left, ((0, 0), (gap, 0), (0, 0)))
    (packed,) = call(
        join_kernel, [((16, 13, 16, D), BF16)], [], 0, 8, 4_000_000, 10_000_000, 30,
    )(u_keep, u_got, d_keep.reshape(16, 4, 16, D), d_got.reshape(16, 4, 16, D), k_keep, k_got, g_keep, g_got)
    packed, own = lax.optimization_barrier((packed, own))
    to_up = send(own[:RIM].astype(BF16), shift(-N_COL)).astype(F32)
    to_down = send(own[RIM + ROWS :].astype(BF16), shift(N_COL)).astype(F32)
    got = exchange(packed, XY_GROUPS)
    (spread,) = call(
        reduce_xy_kernel, [((8, 32, D), BF16)], [], 0, 1, 60_000_000, 4_000_000, 16,
    )(got)
    spread, to_up, to_down = lax.optimization_barrier((spread, to_up, to_down))
    got_z = exchange(spread, Z_GROUPS)
    g_up, g_down, g_out, g_qkv, g_gains = call(
        reduce_z_kernel,
        [((32, 128), F32), ((32, 128), F32), ((8, 128), F32), ((24, 128), F32), ((2, D), F32)],
        [pltpu.VMEM((32, D), F32)], 0, 1, 1_000_000, 400_000, 8,
    )(got_z)

    gap = ROWS - RIM
    gn = own[RIM : RIM + ROWS] + jnp.pad(to_down, ((0, gap), (0, 0), (0, 0))) + jnp.pad(to_up, ((gap, 0), (0, 0), (0, 0)))
    gn = gn + gnq.reshape(ROWS, COLS, D)
    unit, inv = unit_of(tokens.astype(F32))
    g1 = gn * gains[0]
    front = inv * (g1 - unit * jnp.mean(g1 * unit, axis=-1, keepdims=True))
    grad_tokens = (gm.reshape(ROWS, COLS, D).astype(F32) + front).astype(BF16)
    return (grad_tokens, g_qkv.reshape(-1), g_out.reshape(-1), g_up.reshape(-1), g_down.reshape(-1), g_gains)


def solution(mesh):
    block = P("row", "col", None)
    flat = P(("row", "col"))
    return jax.shard_map(
        per_device,
        mesh=mesh,
        in_specs=(block, block, P(), P(), P(), P(), P(), block),
        out_specs=(block, flat, flat, flat, flat, P()),
        check_vma=False,
    )
```

time: 158 us -> 131 us (0.83)
  starting transfers between devices: 84.5 us -> 50.6 us
  waiting for transfers between devices: 30 us -> 49.4 us
  Pallas kernels: 24 us -> 16.5 us
  other arithmetic: 8.15 us -> 5.69 us
    ppermute x36 -> x12, starting transfers between devices: 84.5 us -> 28.2 us  [send(): return lax.ppermute(x, AXES, perm)]
    all_to_all x0 -> x2, starting transfers between devices: none -> 22.3 us  [exchange(): return lax.all_to_all(x, AXES, 0, 0, axis_index_groups=groups, tiled=True)]
    all_to_all x0 -> x2, waiting for transfers between devices: none -> 13.4 us  [exchange(): return lax.all_to_all(x, AXES, 0, 0, axis_index_groups=groups, tiled=True)]
    pallas_call x3 -> x7, Pallas kernels: 24 us -> 16.5 us  [the longest x1 7.16 us: per_device(): call(forward_kernel, [half_u, half_u, half_d, half_d, ((TOK, D), BF16), (...]
    ppermute x36 -> x12, waiting for transfers between devices: 30 us -> 36 us  [send(): return lax.ppermute(x, AXES, perm)]
    convert_element_type x10 -> x2, other arithmetic: 5.37 us -> 0.01 us  [the longest x1 0.01 us: per_device(): to_up = send(own[:RIM].astype(BF16), shift(-N_COL)).astype(F32)]
    unnamed x45 -> x33, local copies, waits for them, and re-layouts: 3.05 us -> 5.87 us
    slice x16 -> x4, local copies, waits for them, and re-layouts: 3.89 us -> 1.2 us  [the longest x1 1.1 us: per_device(): right = send(tokens[:, :RIM], shift(-1))]
  transfers between devices with their start and end apart: 36 -> 14, of which waited for: 19 -> 7; matrix products, arithmetic and copies ran while one was open for 6% -> 5% of each run, Pallas kernels for 2% -> 6%
where the time goes in v2:
time: 131 us; the launch traced here: 130 us
  starting transfers between devices  50.6 us (39%)
  waiting for transfers between devices  49.4 us (38%)
  Pallas kernels  16.5 us (13%)
  local copies, waits for them, and re-layouts  7.22 us (6%)
  other arithmetic  5.69 us (4%)
    ppermute x12, waiting for transfers between devices, send(): return lax.ppermute(x, AXES, perm)  36 us
    ppermute x12, starting transfers between devices, send(): return lax.ppermute(x, AXES, perm)  28.2 us
    all_to_all x2, starting transfers between devices, exchange(): return lax.all_to_all(x, AXES, 0, 0, axis_index_groups=groups, tiled=True)  22.3 us
    all_to_all x2, waiting for transfers between devices, exchange(): return lax.all_to_all(x, AXES, 0, 0, axis_index_groups=groups, tiled=True)  13.4 us
    pallas_call x1, Pallas kernels, per_device(): call(forward_kernel, [half_u, half_u, half_d, half_d, ((TOK, D), BF16), (...  7.16 us
    unnamed x33, local copies, waits for them, and re-layouts  5.87 us
    pallas_call x1, Pallas kernels, per_device(): call(backward_kernel, [half_k, half_k, ((16, D), BF16), ((16, D), BF16),...  4.73 us
  transfers between devices with their start and end apart: 14, of which 7 were waited for; matrix products, arithmetic and copies ran while one was open for 5% of the time, Pallas kernels for 6%

profile of v2, /device:TPU:8, one launch (start us, length us, event | category | flops | bytes accessed | tf_op | source)
XLA Modules:
  0.0 130.3 jit_solution(2943000891659212581)
XLA Ops:
  0.6 1.1 fusion.13
  1.7 1.9 %collective-permute-start = (bf16[24,3,512]{2,1,0:T(4,128)(2,1)S(1)}, bf16[24,3,512]{2,1,0:T(4,128)(2,1)S(1)}, u32[]{:S(2)}, u32[]{:S(2)}) collective-permute-start(bf16[24,3,512]{2,1,0:T(4,128)(2,1)S(1)} %get-tuple-element.91), channel_id=1, source_target_pairs={{0,1},{1,2},{2,3},{3,4},{4,5},{5,6},{6,7},{7,8},{8,9},{9,10},{10,1... | collective-permute-start | bytes 221192 | tf_op jit(solution)/shard_map/ppermute | solution.py:288
  3.7 6.3 %collective-permute-start.1 = (bf16[24,3,512]{2,1,0:T(4,128)(2,1)S(1)}, bf16[24,3,512]{2,1,0:T(4,128)(2,1)S(1)}, u32[]{:S(2)}, u32[]{:S(2)}) collective-permute-start(bf16[24,3,512]{2,1,0:T(4,128)(2,1)S(1)} %get-tuple-element.90), channel_id=1, source_target_pairs={{1,0},{2,1},{3,2},{4,3},{5,4},{6,5},{7,6},{8,7},{9,8},{10,9},{11,1... | collective-permute-start | bytes 221192 | tf_op jit(solution)/shard_map/ppermute | solution.py:288
  10.0 0.7 copy.16
  10.8 1.6 %copy-done.3 = bf16[2048,512]{1,0:T(8,128)(2,1)S(1)} copy-done((bf16[2048,512]{1,0:T(8,128)(2,1)S(1)}, bf16[2048,512]{1,0:T(8,128)(2,1)}, u32[]{:S(2)}) %copy-start.3) | copy-done | bytes 2097176
  12.4 0.9 copy-done.9
  13.3 0.8 shard_map.127.gact
  14.4 3.5 %collective-permute-start.2 = (bf16[3,16,512]{2,1,0:T(8,128)(2,1)S(1)}, bf16[3,16,512]{2,1,0:T(8,128)(2,1)S(1)}, u32[]{:S(2)}, u32[]{:S(2)}) collective-permute-start(bf16[3,16,512]{2,1,0:T(8,128)(2,1)S(1)} %get-tuple-element.87), channel_id=1, source_target_pairs={{0,32},{1,33},{2,34},{3,35},{4,36},{5,37},{6,38},{7,39},{8,40},{9,... | collective-permute-start | bytes 147464 | tf_op jit(solution)/shard_map/ppermute | solution.py:288
  18.0 1.3 collective-permute-start.3
  19.3 1.7 %shard_map.128 = (f32[3,64,256]{2,1,0:T(8,128)S(1)}, bf16[512,512]{1,0:T(8,128)(2,1)S(1)}, bf16[512,512]{1,0:T(8,128)(2,1)S(1)}) custom-call(s32[3]{0:T(128)S(1)} %pad_add_fusion.coord, s32[3,49]{1,0:T(4,128)S(1)} %bitcast.33), custom_call_target="tpu_custom_call" | custom-call | flops 402653184 | bytes 4000000 | tf_op jit(solution)/shard_map/pallas_call | solution.py:312
  21.1 2.9 %collective-permute-done.3.low = bf16[3,16,512]{2,1,0:T(8,128)(2,1)S(1)} collective-permute-done((bf16[3,16,512]{2,1,0:T(8,128)(2,1)S(1)}, bf16[3,16,512]{2,1,0:T(8,128)(2,1)S(1)}, u32[]{:S(2)}, u32[]{:S(2)}) %collective-permute-start.3) | collective-permute-done | bytes 49184 | tf_op jit(solution)/shard_map/ppermute | solution.py:288
  24.0 7.2 %shard_map.129 = (bf16[16,5,16,512]{3,2,1,0:T(8,128)(2,1)S(1)}, bf16[16,5,16,512]{3,2,1,0:T(8,128)(2,1)S(1)}, bf16[16,2,32,512]{3,2,1,0:T(8,128)(2,1)S(1)}, bf16...) custom-call(bf16[24,16,512]{2,1,0:T(8,128)(2,1)S(1)} %maximum_maximu, ...), custom_call_target="tpu_custom_call" | custom-call | flops 5000000000 | bytes 20000000 | tf_op jit(solution)/shard_map/pallas_call | solution.py:318
  31.8 4.7 %shard_map.130 = (bf16[16,3,16,512]{3,2,1,0:T(8,128)(2,1)S(1)}, bf16[16,3,16,512]{3,2,1,0:T(8,128)(2,1)S(1)}, bf16[16,512]{1,0:T(8,128)(2,1)S(1)}, bf16[16,512]{...) custom-call(bf16[192,512]{1,0:T(8,128)(2,1)S(1)} %get-tuple-element.52.gm, ...), custom_call_target="tpu_custom_call" | custom-call | flops 3000000000 | bytes 12000000 | tf_op jit(solution)/shard_map/pallas_call | solution.py:330
  37.4 2.2 %collective-permute-start.8 = (bf16[30,3,512]{2,1,0:T(4,128)(2,1)S(1)}, bf16[30,3,512]{2,1,0:T(4,128)(2,1)S(1)}, u32[]{:S(2)}, u32[]{:S(2)}) collective-permute-start(bf16[30,3,512]{2,1,0:T(4,128)(2,1)S(1)} %get-tuple-element.84), channel_id=1, source_target_pairs={{0,1},{1,2},{2,3},{3,4},{4,5},{5,6},{6,7},{7,8},{8,9},{9,10},{10,1... | collective-permute-start | bytes 276488 | tf_op jit(solution)/shard_map/ppermute | solution.py:288
  39.6 6.1 %collective-permute-start.9 = (bf16[30,3,512]{2,1,0:T(4,128)(2,1)S(1)}, bf16[30,3,512]{2,1,0:T(4,128)(2,1)S(1)}, u32[]{:S(2)}, u32[]{:S(2)}) collective-permute-start(bf16[30,3,512]{2,1,0:T(4,128)(2,1)S(1)} %get-tuple-element.85), channel_id=1, source_target_pairs={{1,0},{2,1},{3,2},{4,3},{5,4},{6,5},{7,6},{8,7},{9,8},{10,9},{11,1... | collective-permute-start | bytes 276488 | tf_op jit(solution)/shard_map/ppermute | solution.py:288
  46.4 1.7 %collective-permute-done.9 = bf16[30,3,512]{2,1,0:T(4,128)(2,1)S(1)} collective-permute-done((bf16[30,3,512]{2,1,0:T(4,128)(2,1)S(1)}, bf16[30,3,512]{2,1,0:T(4,128)(2,1)S(1)}, u32[]{:S(2)}, u32[]{:S(2)}) %collective-permute-start.9) | collective-permute-done | bytes 92192 | tf_op jit(solution)/shard_map/ppermute | solution.py:288
  48.1 0.9 fusion
  49.0 0.7 shard_map.131
  49.8 1.7 %copy-done = bf16[16,13,16,512]{3,2,1,0:T(8,128)(2,1)} copy-done((bf16[16,13,16,512]{3,2,1,0:T(8,128)(2,1)}, bf16[16,13,16,512]{3,2,1,0:T(8,128)(2,1)S(1)}, u32[]{:S(2)}) %copy-start) | copy-done | bytes 3407896
  51.5 18.8 %all-to-all-start = ((bf16[16,13,16,512]{3,2,1,0:T(8,128)(2,1)}), bf16[16,13,16,512]{3,2,1,0:T(8,128)(2,1)S(1)}, u32[]{:S(2)}, u32[]{:S(2)}) async-start(bf16[16,13,16,512]{3,2,1,0:T(8,128)(2,1)} %copy-done), calls=%async_computation | async-start | bytes 6815744 | tf_op jit(solution)/shard_map/all_to_all | solution.py:292
  70.2 1.0 fusion.8
  71.3 1.1 convert.14
  72.3 1.3 collective-permute-start.10
  73.6 4.5 %collective-permute-start.11 = (bf16[3,8,512]{2,1,0:T(8,128)(2,1)S(1)}, bf16[3,8,512]{2,1,0:T(8,128)(2,1)S(1)}, u32[]{:S(2)}, u32[]{:S(2)}) collective-permute-start(bf16[3,8,512]{2,1,0:T(8,128)(2,1)S(1)} %get-tuple-element.88), channel_id=1, source_target_pairs={{0,32},{1,33},{2,34},{3,35},{4,36},{5,37},{6,38},{7,39},{8,40},{9,... | collective-permute-start | bytes 73736 | tf_op jit(solution)/shard_map/ppermute | solution.py:288
  78.2 30.7 %collective-permute-done.10 = bf16[3,8,512]{2,1,0:T(8,128)(2,1)S(1)} collective-permute-done((bf16[3,8,512]{2,1,0:T(8,128)(2,1)S(1)}, bf16[3,8,512]{2,1,0:T(8,128)(2,1)S(1)}, u32[]{:S(2)}, u32[]{:S(2)}) %collective-permute-start.10) | collective-permute-done | bytes 24608 | tf_op jit(solution)/shard_map/ppermute | solution.py:288
  109.0 5.3 %all-to-all-done.got = bf16[16,13,16,512]{3,2,1,0:T(8,128)(2,1)S(1)} async-done(((bf16[16,13,16,512]{3,2,1,0:T(8,128)(2,1)}), bf16[16,13,16,512]{3,2,1,0:T(8,128)(2,1)S(1)}, u32[]{:S(2)}, u32[]{:S(2)}) %all-to-all-start) | async-done | bytes 3407904 | tf_op jit(solution)/shard_map/all_to_all | solution.py:292
  115.0 0.7 copy-done.6
  115.7 3.6 %all-to-all-start.1 = ((bf16[8,32,512]{2,1,0:T(8,128)(2,1)}), bf16[8,32,512]{2,1,0:T(8,128)(2,1)S(1)}, u32[]{:S(2)}, u32[]{:S(2)}) async-start(bf16[8,32,512]{2,1,0:T(8,128)(2,1)} %copy-done.6), calls=%async_computation.1 | async-start | bytes 524288 | tf_op jit(solution)/shard_map/all_to_all | solution.py:292
  119.3 1.4 %fusion.3 = f32[24,8]{1,0:T(8,128)S(1)} fusion(bf16[24,8,512]{2,1,0:T(8,128)(2,1)} %param.8, f32[24,8]{1,0:T(8,128)S(1)} %add_rsqrt_fusion, f32[512]{0:T(512)S(1)} %bitcast.36, f32[192,512]{1,0:T(8,128)} %copy-done.4, f32[3,8,512]{2,1,0:T(8,128)S(1)} %convert_element_type.35, f32[3,8,512]{2,1,0:T(8,128)S(1)} %convert_element_type.36, f32[30,8,512]{2,1,0:T(8,128)} %fusion), kind=kLoop, calls=%fused_computation.6 | loop fusion | flops 786240 | bytes 1084928 | tf_op jit(solution)/shard_map/reduce_sum | solution.py:368
  120.7 0.9 fusion.7
  121.6 8.0 %all-to-all-done.1.got = bf16[8,32,512]{2,1,0:T(8,128)(2,1)S(1)} async-done(((bf16[8,32,512]{2,1,0:T(8,128)(2,1)}), bf16[8,32,512]{2,1,0:T(8,128)(2,1)S(1)}, u32[]{:S(2)}, u32[]{:S(2)}) %all-to-all-start.1) | async-done | bytes 262176 | tf_op jit(solution)/shard_map/all_to_all | solution.py:292
  129.7 0.7 shard_map.133
  (56 shorter events, 3.4 us)
Async XLA Ops:
  1.7 12.4 %collective-permute-start = (bf16[24,3,512]{2,1,0:T(4,128)(2,1)S(1)}, bf16[24,3,512]{2,1,0:T(4,128)(2,1)S(1)}, u32[]{:S(2)}, u32[]{:S(2)}) collective-permute-start(bf16[24,3,512]{2,1,0:T(4,128)(2,1)S(1)} %get-tuple-element.91), channel_id=1, source_target_pairs={{0,1},{1,2},{2,3},{3,4},{4,5},{5,6},{6,7},{7,8},{8,9},{9,10},{10,1... | collective-permute-start | bytes 221192 | tf_op jit(solution)/shard_map/ppermute | solution.py:288
  3.7 10.5 %collective-permute-start.1 = (bf16[24,3,512]{2,1,0:T(4,128)(2,1)S(1)}, bf16[24,3,512]{2,1,0:T(4,128)(2,1)S(1)}, u32[]{:S(2)}, u32[]{:S(2)}) collective-permute-start(bf16[24,3,512]{2,1,0:T(4,128)(2,1)S(1)} %get-tuple-element.90), channel_id=1, source_target_pairs={{1,0},{2,1},{3,2},{4,3},{5,4},{6,5},{7,6},{8,7},{9,8},{10,9},{11,1... | collective-permute-start | bytes 221192 | tf_op jit(solution)/shard_map/ppermute | solution.py:288
  10.8 1.6 %copy-start.3 = (bf16[2048,512]{1,0:T(8,128)(2,1)S(1)}, bf16[2048,512]{1,0:T(8,128)(2,1)}, u32[]{:S(2)}) copy-start(bf16[2048,512]{1,0:T(8,128)(2,1)} %w_down.1) | copy-start | bytes 6291460
  12.4 0.9 copy-start.9
  13.3 0.9 copy-start.1
  13.3 10.6 %copy-start.13 = (bf16[512,1536]{1,0:T(8,128)(2,1)S(1)}, bf16[512,1536]{1,0:T(8,128)(2,1)}, u32[]{:S(2)}) copy-start(bf16[512,1536]{1,0:T(8,128)(2,1)} %w_qkv.3) | copy-start | bytes 4718596
  13.3 10.6 %copy-start.14 = (bf16[512,512]{1,0:T(8,128)(2,1)S(1)}, bf16[512,512]{1,0:T(8,128)(2,1)}, u32[]{:S(2)}) copy-start(bf16[512,512]{1,0:T(8,128)(2,1)} %w_out.3) | copy-start | bytes 1572868
  14.1 9.8 %copy-start.10 = (bf16[24,8,512]{2,1,0:T(8,128)(2,1)S(1)}, bf16[24,8,512]{2,1,0:T(8,128)(2,1)}, u32[]{:S(2)}) copy-start(bf16[24,8,512]{2,1,0:T(8,128)(2,1)} %param.9) | copy-start | bytes 589828
  14.2 9.8 %copy-start.11 = (f32[2,512]{1,0:T(2,128)S(1)}, f32[2,512]{1,0:T(2,128)}, u32[]{:S(2)}) copy-start(f32[2,512]{1,0:T(2,128)} %gains.1) | copy-start | bytes 12292
  14.2 9.8 %copy-start.12 = (bf16[512,2048]{1,0:T(8,128)(2,1)S(1)}, bf16[512,2048]{1,0:T(8,128)(2,1)}, u32[]{:S(2)}) copy-start(bf16[512,2048]{1,0:T(8,128)(2,1)} %w_up.1) | copy-start | bytes 6291460
  14.4 6.7 %collective-permute-start.2 = (bf16[3,16,512]{2,1,0:T(8,128)(2,1)S(1)}, bf16[3,16,512]{2,1,0:T(8,128)(2,1)S(1)}, u32[]{:S(2)}, u32[]{:S(2)}) collective-permute-start(bf16[3,16,512]{2,1,0:T(8,128)(2,1)S(1)} %get-tuple-element.87), channel_id=1, source_target_pairs={{0,32},{1,33},{2,34},{3,35},{4,36},{5,37},{6,38},{7,39},{8,40},{9,... | collective-permute-start | bytes 147464 | tf_op jit(solution)/shard_map/ppermute | solution.py:288
  18.0 6.0 %collective-permute-start.3 = (bf16[3,16,512]{2,1,0:T(8,128)(2,1)S(1)}, bf16[3,16,512]{2,1,0:T(8,128)(2,1)S(1)}, u32[]{:S(2)}, u32[]{:S(2)}) collective-permute-start(bf16[3,16,512]{2,1,0:T(8,128)(2,1)S(1)} %get-tuple-element.86), channel_id=1, source_target_pairs={{32,0},{33,1},{34,2},{35,3},{36,4},{37,5},{38,6},{39,7},{40,8},{41... | collective-permute-start | bytes 147464 | tf_op jit(solution)/shard_map/ppermute | solution.py:288
  31.2 5.3 %copy-start.7 = (bf16[192,512]{1,0:T(8,128)(2,1)}, bf16[192,512]{1,0:T(8,128)(2,1)S(1)}, u32[]{:S(2)}) copy-start(bf16[192,512]{1,0:T(8,128)(2,1)S(1)} %get-tuple-element.52.gm) | copy-start | bytes 589828
  31.2 5.4 %collective-permute-start.4 = (bf16[16,5,16,512]{3,2,1,0:T(8,128)(2,1)S(1)}, bf16[16,5,16,512]{3,2,1,0:T(8,128)(2,1)S(1)}, u32[]{:S(2)}, u32[]{:S(2)}) collective-permute-start(bf16[16,5,16,512]{3,2,1,0:T(8,128)(2,1)S(1)} %get-tuple-element.54), channel_id=1, source_target_pairs={{0,1},{1,0},{2,3},{3,2},{4,5},{5,4},{6,7},{7,6},{8,9},{9,8},{10,11... | collective-permute-start | bytes 3932168 | tf_op jit(solution)/shard_map/ppermute | solution.py:288
  31.3 5.3 %collective-permute-start.5 = (bf16[16,2,32,512]{3,2,1,0:T(8,128)(2,1)S(1)}, bf16[16,2,32,512]{3,2,1,0:T(8,128)(2,1)S(1)}, u32[]{:S(2)}, u32[]{:S(2)}) collective-permute-start(bf16[16,2,32,512]{3,2,1,0:T(8,128)(2,1)S(1)} %get-tuple-element.55), channel_id=1, source_target_pairs={{0,1},{1,0},{2,3},{3,2},{4,5},{5,4},{6,7},{7,6},{8,9},{9,8},{10,11... | collective-permute-start | bytes 3145736 | tf_op jit(solution)/shard_map/ppermute | solution.py:288
  36.5 0.8 copy-start.4
  36.5 12.5 %collective-permute-start.6 = (bf16[16,3,16,512]{3,2,1,0:T(8,128)(2,1)S(1)}, bf16[16,3,16,512]{3,2,1,0:T(8,128)(2,1)S(1)}, u32[]{:S(2)}, u32[]{:S(2)}) collective-permute-start(bf16[16,3,16,512]{3,2,1,0:T(8,128)(2,1)S(1)} %get-tuple-element.69), channel_id=1, source_target_pairs={{0,1},{1,0},{2,3},{3,2},{4,5},{5,4},{6,7},{7,6},{8,9},{9,8},{10,11... | collective-permute-start | bytes 2359304 | tf_op jit(solution)/shard_map/ppermute | solution.py:288
  37.4 9.0 %collective-permute-start.8 = (bf16[30,3,512]{2,1,0:T(4,128)(2,1)S(1)}, bf16[30,3,512]{2,1,0:T(4,128)(2,1)S(1)}, u32[]{:S(2)}, u32[]{:S(2)}) collective-permute-start(bf16[30,3,512]{2,1,0:T(4,128)(2,1)S(1)} %get-tuple-element.84), channel_id=1, source_target_pairs={{0,1},{1,2},{2,3},{3,4},{4,5},{5,6},{6,7},{7,8},{8,9},{9,10},{10,1... | collective-permute-start | bytes 276488 | tf_op jit(solution)/shard_map/ppermute | solution.py:288
  39.6 8.5 %collective-permute-start.9 = (bf16[30,3,512]{2,1,0:T(4,128)(2,1)S(1)}, bf16[30,3,512]{2,1,0:T(4,128)(2,1)S(1)}, u32[]{:S(2)}, u32[]{:S(2)}) collective-permute-start(bf16[30,3,512]{2,1,0:T(4,128)(2,1)S(1)} %get-tuple-element.85), channel_id=1, source_target_pairs={{1,0},{2,1},{3,2},{4,3},{5,4},{6,5},{7,6},{8,7},{9,8},{10,9},{11,1... | collective-permute-start | bytes 276488 | tf_op jit(solution)/shard_map/ppermute | solution.py:288
  45.6 3.4 %collective-permute-start.7 = (bf16[16,512]{1,0:T(8,128)(2,1)S(1)}, bf16[16,512]{1,0:T(8,128)(2,1)S(1)}, u32[]{:S(2)}, u32[]{:S(2)}) collective-permute-start(bf16[16,512]{1,0:T(8,128)(2,1)S(1)} %get-tuple-element.71), channel_id=1, source_target_pairs={{0,1},{1,0},{2,3},{3,2},{4,5},{5,4},{6,7},{7,6},{8,9},{9,8},{10,11... | collective-permute-start | bytes 49160 | tf_op jit(solution)/shard_map/ppermute | solution.py:288
  49.7 1.7 %copy-start = (bf16[16,13,16,512]{3,2,1,0:T(8,128)(2,1)}, bf16[16,13,16,512]{3,2,1,0:T(8,128)(2,1)S(1)}, u32[]{:S(2)}) copy-start(bf16[16,13,16,512]{3,2,1,0:T(8,128)(2,1)S(1)} %shard_map.131) | copy-start | bytes 10223620
  51.5 62.9 %all-to-all-start = ((bf16[16,13,16,512]{3,2,1,0:T(8,128)(2,1)}), bf16[16,13,16,512]{3,2,1,0:T(8,128)(2,1)S(1)}, u32[]{:S(2)}, u32[]{:S(2)}) async-start(bf16[16,13,16,512]{3,2,1,0:T(8,128)(2,1)} %copy-done), calls=%async_computation | async-start | bytes 6815744 | tf_op jit(solution)/shard_map/all_to_all | solution.py:292
  72.3 36.5 %collective-permute-start.10 = (bf16[3,8,512]{2,1,0:T(8,128)(2,1)S(1)}, bf16[3,8,512]{2,1,0:T(8,128)(2,1)S(1)}, u32[]{:S(2)}, u32[]{:S(2)}) collective-permute-start(bf16[3,8,512]{2,1,0:T(8,128)(2,1)S(1)} %get-tuple-element.89), channel_id=1, source_target_pairs={{32,0},{33,1},{34,2},{35,3},{36,4},{37,5},{38,6},{39,7},{40,8},{41... | collective-permute-start | bytes 73736 | tf_op jit(solution)/shard_map/ppermute | solution.py:288
  73.6 35.4 %collective-permute-start.11 = (bf16[3,8,512]{2,1,0:T(8,128)(2,1)S(1)}, bf16[3,8,512]{2,1,0:T(8,128)(2,1)S(1)}, u32[]{:S(2)}, u32[]{:S(2)}) collective-permute-start(bf16[3,8,512]{2,1,0:T(8,128)(2,1)S(1)} %get-tuple-element.88), channel_id=1, source_target_pairs={{0,32},{1,33},{2,34},{3,35},{4,36},{5,37},{6,38},{7,39},{8,40},{9,... | collective-permute-start | bytes 73736 | tf_op jit(solution)/shard_map/ppermute | solution.py:288
  115.0 0.7 copy-start.6
  115.7 5.0 %copy-start.2 = (bf16[24,8,512]{2,1,0:T(8,128)(2,1)S(1)}, bf16[24,8,512]{2,1,0:T(8,128)(2,1)}, u32[]{:S(2)}) copy-start(bf16[24,8,512]{2,1,0:T(8,128)(2,1)} %param.8) | copy-start | bytes 589828
  115.7 5.0 %copy-start.5 = (f32[192,512]{1,0:T(8,128)S(1)}, f32[192,512]{1,0:T(8,128)}, u32[]{:S(2)}) copy-start(f32[192,512]{1,0:T(8,128)} %copy-done.4) | copy-start | bytes 1179652
  115.7 5.0 %copy-start.8 = (bf16[192,512]{1,0:T(8,128)(2,1)S(1)}, bf16[192,512]{1,0:T(8,128)(2,1)}, u32[]{:S(2)}) copy-start(bf16[192,512]{1,0:T(8,128)(2,1)} %copy-done.7) | copy-start | bytes 589828
  115.7 5.0 %copy-start.15 = (f32[30,8,512]{2,1,0:T(8,128)S(1)}, f32[30,8,512]{2,1,0:T(8,128)}, u32[]{:S(2)}) copy-start(f32[30,8,512]{2,1,0:T(8,128)} %fusion) | copy-start | bytes 1474564
  115.7 13.9 %all-to-all-start.1 = ((bf16[8,32,512]{2,1,0:T(8,128)(2,1)}), bf16[8,32,512]{2,1,0:T(8,128)(2,1)S(1)}, u32[]{:S(2)}, u32[]{:S(2)}) async-start(bf16[8,32,512]{2,1,0:T(8,128)(2,1)} %copy-done.6), calls=%async_computation.1 | async-start | bytes 524288 | tf_op jit(solution)/shard_map/all_to_all | solution.py:292

commit v3 on v2

--- a/solution.py
+++ b/solution.py
@@ -77,7 +77,10 @@
     k = lax.broadcasted_iota(jnp.int32, (QT, KT), 1)
     ki = k // EC
     kc = k % EC
-    kj = jnp.where(kc < COLS, kc + RIM, jnp.where(kc < COLS + RIM, kc - COLS, kc))
+    odd = coord[1] & 1
+    near = kc - COLS + odd * (COLS + RIM)
+    far = kc - COLS - RIM + (1 - odd) * (COLS + RIM)
+    kj = jnp.where(kc < COLS, kc + RIM, jnp.where(kc < COLS + RIM, near, jnp.where(kc < COLS + 2 * RIM, far, -99)))
     da = ki - q // TILE
     db = kj - q % TILE
     slot = jnp.where((da >= 0) & (da < WINDOW) & (db >= 0) & (db < WINDOW), da * WINDOW + db, -1)
@@ -102,12 +105,13 @@
 
 
 def forward_kernel(
-    mid, top, low, tok, cot, gains, w_qkv, w_out, w_up, gact, bias, pt_u, pt_d,
+    coord, mid, rim_a, rim_b, tok, cot, gains, w_qkv, w_out, w_up, gact, bias, pt_u, pt_d,
     u_keep, u_send, d_keep, d_send, gm_o, q_o, kv_o, p_o, ne_o, no_o, gain_o, text_s, attn_s,
 ):
-    text_s[:RIM] = top[...]
+    odd = coord[0] & 1
+    text_s[pl.ds(odd * (RIM + ROWS), RIM)] = rim_a[...]
     text_s[RIM : RIM + ROWS] = mid[...]
-    text_s[RIM + ROWS : ROWS + 2 * RIM] = low[...]
+    text_s[pl.ds((1 - odd) * (RIM + ROWS), RIM)] = rim_b[...]
     text_s[ROWS + 2 * RIM :] = jnp.zeros((ER - ROWS - 2 * RIM, EC, D), BF16)
     unit_e, _ = unit_of(text_s[...].reshape(EXT, D).astype(F32))
     ne = (unit_e * gains[0:1, :]).astype(BF16)
@@ -166,7 +170,7 @@
 
 
 def backward_kernel(
-    gm, w_out, w_qkv, q, kv, p_in, ne, no, mid, top, low, tok, gain_mid, pt,
+    coord, gm, w_out, w_qkv, q, kv, p_in, ne, no, mid, rim_a, rim_b, tok, gain_mid, pt,
     k_keep, k_send, g_keep, g_send, gne_o, gnq_o, dq_s, dkv_s,
 ):
     ga = nt(gm[...], w_out[...]).astype(BF16)
@@ -197,12 +201,12 @@
     gne_o[...] = gne
     gnq_o[...] = gnq
     gain_in = jnp.sum(gnq * unit_of(tok[...].astype(F32))[0], axis=0, keepdims=True)
-    at = 0
-    for ref in (top, mid, low):
+    odd = coord[0] & 1
+    for ref, at in ((rim_a, odd * (RIM + ROWS)), (mid, RIM), (rim_b, (1 - odd) * (RIM + ROWS))):
         size = ref.shape[0] * EC
         unit, _ = unit_of(ref[...].reshape(size, D).astype(F32))
-        gain_in = gain_in + jnp.sum(gne[at : at + size] * unit, axis=0, keepdims=True)
-        at += size
+        part = gne_o[pl.ds(pl.multiple_of(at * EC, EC), size), :]
+        gain_in = gain_in + jnp.sum(part * unit, axis=0, keepdims=True)
     spread = jnp.concatenate([gain_in, gain_mid[...], jnp.zeros((14, D), F32)], axis=0).astype(BF16)
     g_keep[...] = spread
     g_send[...] = spread
@@ -267,18 +271,18 @@
     )
 
 
-def shift(step):
-    pairs = []
+def pairs(stride, count, first):
+    out = []
     for k in range(256):
-        c = k % N_COL
-        if step in (1, -1):
-            if 0 <= c + step < N_COL:
-                pairs.append((k, k + step))
-        elif 0 <= k + step < 256:
-            pairs.append((k, k + step))
-    return pairs
-
-
+        at = (k // stride) % count
+        other = at + 1 if (at - first) % 2 == 0 else at - 1
+        if 0 <= other < count:
+            out.append((k, k + (other - at) * stride))
+    return out
+
+
+ROW_A, ROW_B = pairs(N_COL, 8, 1), pairs(N_COL, 8, 0)
+COL_A, COL_B = pairs(1, N_COL, 1), pairs(1, N_COL, 0)
 CORE_SWAP = [(k, k ^ 1) for k in range(256)]
 XY_GROUPS = [[zh * 128 + x * 32 + y * 8 + zl * 2 + c for x in range(4) for y in range(4)] for zh in range(2) for zl in range(4) for c in range(2)]
 Z_GROUPS = [[zh * 128 + x * 32 + y * 8 + zl * 2 + c for zh in range(2) for zl in range(4)] for x in range(4) for y in range(4) for c in range(2)]
@@ -300,15 +304,18 @@
     cot = cotangent.reshape(TOK, D)
     mask = tile_mask.reshape(TILES, WINDOW * WINDOW)
 
-    left = send(tokens[:, COLS - RIM :], shift(1))
-    right = send(tokens[:, :RIM], shift(-1))
+    row_odd = (row & 1) == 1
+    col_odd = (col & 1) == 1
+    first, last = tokens[:, :RIM], tokens[:, COLS - RIM :]
+    side_b = send(jnp.where(col_odd, first, last), COL_B)
+    side_a = send(jnp.where(col_odd, last, first), COL_A)
     (gact,) = call(
         prep_front_kernel, [((TOK, FF), F32)], [], 0, 2, 2 * TOK * D * FF, 4_000_000, 16,
     )(cot, w_down)
-    left, right, gact, mask = lax.optimization_barrier((left, right, gact, mask))
-    mid = jnp.concatenate([tokens, left, right, jnp.zeros((ROWS, EC - COLS - 2 * RIM, D), BF16)], axis=1)
-    top = send(mid[ROWS - RIM :], shift(N_COL))
-    low = send(mid[:RIM], shift(-N_COL))
+    side_a, side_b, gact, mask = lax.optimization_barrier((side_a, side_b, gact, mask))
+    mid = jnp.concatenate([tokens, side_a, side_b, jnp.zeros((ROWS, EC - COLS - 2 * RIM, D), BF16)], axis=1)
+    rim_b = send(jnp.where(row_odd, mid[:RIM], mid[ROWS - RIM :]), ROW_B)
+    rim_a = send(jnp.where(row_odd, mid[ROWS - RIM :], mid[:RIM]), ROW_A)
     bias, pt_u, pt_d = call(
         prep_mask_kernel, [((TILES, QT, KT), F32), ((D, D), BF16), ((D, D), BF16)],
         [], 2, 0, 2 * TOK * D * FF, 4_000_000, 16,
@@ -322,37 +329,28 @@
             ((TOK, D), BF16), ((TOK, D), BF16), ((EXT, 2 * D), BF16), ((6, 256, KT), F32),
             ((EXT, D), BF16), ((TOK, D), BF16), ((1, D), F32),
         ],
-        [pltpu.VMEM((ER, EC, D), BF16), pltpu.VMEM((TOK, D), BF16)], 0, 13, 5_000_000_000, 20_000_000, 30,
-    )(mid, top, low, tok, cot, gains, w_qkv, w_out, w_up, gact, bias, pt_u, pt_d)
+        [pltpu.VMEM((ER, EC, D), BF16), pltpu.VMEM((TOK, D), BF16)], 1, 13, 5_000_000_000, 20_000_000, 30,
+    )(coord, mid, rim_a, rim_b, tok, cot, gains, w_qkv, w_out, w_up, gact, bias, pt_u, pt_d)
 
     u_got = send(u_send, CORE_SWAP)
     d_got = send(d_send, CORE_SWAP)
     k_keep, k_send, g_keep, g_send, gne, gnq = call(
         backward_kernel,
         [half_k, half_k, ((16, D), BF16), ((16, D), BF16), ((EXT, D), F32), ((TOK, D), F32)],
-        [pltpu.VMEM((TOK, D), BF16), pltpu.VMEM((EXT, 2 * D), F32)], 0, 14, 3_000_000_000, 12_000_000, 30,
-    )(gm, w_out, w_qkv, q, kv, prob, ne, no, mid, top, low, tok, gain_mid, pt_u)
-    u_got, d_got, k_send, g_send, gne = lax.optimization_barrier((u_got, d_got, k_send, g_send, gne))
+        [pltpu.VMEM((TOK, D), BF16), pltpu.VMEM((EXT, 2 * D), F32)], 1, 14, 3_000_000_000, 12_000_000, 30,
+    )(coord, gm, w_out, w_qkv, q, kv, prob, ne, no, mid, rim_a, rim_b, tok, gain_mid, pt_u)
+    u_got, d_got, k_send, g_send = lax.optimization_barrier((u_got, d_got, k_send, g_send))
 
     k_got = send(k_send, CORE_SWAP)
     g_got = send(g_send, CORE_SWAP)
-    gne3 = gne.reshape(ER, EC, D)[: ROWS + 2 * RIM]
-    to_left = send(gne3[:, COLS : COLS + RIM].astype(BF16), shift(-1)).astype(F32)
-    to_right = send(gne3[:, COLS + RIM : COLS + 2 * RIM].astype(BF16), shift(1)).astype(F32)
-    gap = COLS - RIM
-    own = gne3[:, :COLS]
-    own = own + jnp.pad(to_right, ((0, 0), (0, gap), (0, 0))) + jnp.pad(to_left, ((0, 0), (gap, 0), (0, 0)))
     (packed,) = call(
         join_kernel, [((16, 13, 16, D), BF16)], [], 0, 8, 4_000_000, 10_000_000, 30,
     )(u_keep, u_got, d_keep.reshape(16, 4, 16, D), d_got.reshape(16, 4, 16, D), k_keep, k_got, g_keep, g_got)
-    packed, own = lax.optimization_barrier((packed, own))
-    to_up = send(own[:RIM].astype(BF16), shift(-N_COL)).astype(F32)
-    to_down = send(own[RIM + ROWS :].astype(BF16), shift(N_COL)).astype(F32)
+    packed, gne = lax.optimization_barrier((packed, gne))
     got = exchange(packed, XY_GROUPS)
     (spread,) = call(
         reduce_xy_kernel, [((8, 32, D), BF16)], [], 0, 1, 60_000_000, 4_000_000, 16,
     )(got)
-    spread, to_up, to_down = lax.optimization_barrier((spread, to_up, to_down))
     got_z = exchange(spread, Z_GROUPS)
     g_up, g_down, g_out, g_qkv, g_gains = call(
         reduce_z_kernel,
@@ -360,8 +358,22 @@
         [pltpu.VMEM((32, D), F32)], 0, 1, 1_000_000, 400_000, 8,
     )(got_z)
 
-    gap = ROWS - RIM
-    gn = own[RIM : RIM + ROWS] + jnp.pad(to_down, ((0, gap), (0, 0), (0, 0))) + jnp.pad(to_up, ((gap, 0), (0, 0), (0, 0)))
+    def place(x, axis, at_end, size):
+        gap = size - RIM
+        after = [(0, 0)] * 3
+        before = [(0, 0)] * 3
+        after[axis], before[axis] = (0, gap), (gap, 0)
+        x = x.astype(F32)
+        return jnp.where(at_end, jnp.pad(x, before), jnp.pad(x, after))
+
+    gne3 = gne.reshape(ER, EC, D)[: ROWS + 2 * RIM]
+    back_b = send(gne3[:, COLS + RIM : COLS + 2 * RIM].astype(BF16), COL_B)
+    back_a = send(gne3[:, COLS : COLS + RIM].astype(BF16), COL_A)
+    own = gne3[:, :COLS] + place(back_a, 1, col_odd, COLS) + place(back_b, 1, ~col_odd, COLS)
+    head, tail = own[:RIM].astype(BF16), own[RIM + ROWS :].astype(BF16)
+    up_b = send(jnp.where(row_odd, head, tail), ROW_B)
+    up_a = send(jnp.where(row_odd, tail, head), ROW_A)
+    gn = own[RIM : RIM + ROWS] + place(up_a, 0, row_odd, ROWS) + place(up_b, 0, ~row_odd, ROWS)
     gn = gn + gnq.reshape(ROWS, COLS, D)
     unit, inv = unit_of(tokens.astype(F32))
     g1 = gn * gains[0]

time: 131 us -> 122 us (0.931)
  the two profiles are of different devices: /device:TPU:8 before, /device:TPU:4 now
where the time goes in v3:
time: 122 us; the launch traced here: 121 us
  waiting for transfers between devices  49.4 us (40%)
  starting transfers between devices  38.5 us (32%)
  Pallas kernels  17.6 us (14%)
  local copies, waits for them, and re-layouts  7.87 us (6%)
  other arithmetic  6.96 us (6%)
    ppermute x12, waiting for transfers between devices, send(): return lax.ppermute(x, AXES, perm)  40.7 us
    ppermute x12, starting transfers between devices, send(): return lax.ppermute(x, AXES, perm)  23.2 us
    all_to_all x2, starting transfers between devices, exchange(): return lax.all_to_all(x, AXES, 0, 0, axis_index_groups=groups, tiled=True)  15.3 us
    all_to_all x2, waiting for transfers between devices, exchange(): return lax.all_to_all(x, AXES, 0, 0, axis_index_groups=groups, tiled=True)  8.7 us
    pallas_call x1, Pallas kernels, per_device(): call(forward_kernel, [half_u, half_u, half_d, half_d, ((TOK, D), BF16), (...  7.72 us
    unnamed x29, local copies, waits for them, and re-layouts  6.4 us
    pallas_call x1, Pallas kernels, per_device(): call(backward_kernel, [half_k, half_k, ((16, D), BF16), ((16, D), BF16),...  5.28 us
  transfers between devices with their start and end apart: 14, of which 6 were waited for; matrix products, arithmetic and copies ran while one was open for 6% of the time, Pallas kernels for 6%

profile of v3, /device:TPU:4, one launch (start us, length us, event | category | flops | bytes accessed | tf_op | source)
XLA Modules:
  0.0 121.3 jit_solution(1086012214638463579)
XLA Ops:
  0.6 1.1 broadcast_select_fusion
  2.5 3.4 %collective-permute-start.1 = (bf16[24,3,512]{2,1,0:T(4,128)(2,1)S(1)}, bf16[24,3,512]{2,1,0:T(4,128)(2,1)S(1)}, u32[]{:S(2)}, u32[]{:S(2)}) collective-permute-start(bf16[24,3,512]{2,1,0:T(4,128)(2,1)S(1)} %get-tuple-element.84), channel_id=1, source_target_pairs={{0,1},{1,0},{2,3},{3,2},{4,5},{5,4},{6,7},{7,6},{8,9},{9,8},{10,11... | collective-permute-start | bytes 221192 | tf_op jit(solution)/shard_map/ppermute | solution.py:292
  5.8 0.7 copy.16
  6.6 1.6 %copy-done.3 = bf16[2048,512]{1,0:T(8,128)(2,1)S(1)} copy-done((bf16[2048,512]{1,0:T(8,128)(2,1)S(1)}, bf16[2048,512]{1,0:T(8,128)(2,1)}, u32[]{:S(2)}) %copy-start.3) | copy-done | bytes 2097176
  8.2 0.9 copy-done.8
  9.1 0.8 shard_map.127.gact
  10.2 2.6 %collective-permute-start.2 = (bf16[3,16,512]{2,1,0:T(8,128)(2,1)S(1)}, bf16[3,16,512]{2,1,0:T(8,128)(2,1)S(1)}, u32[]{:S(2)}, u32[]{:S(2)}) collective-permute-start(bf16[3,16,512]{2,1,0:T(8,128)(2,1)S(1)} %get-tuple-element.81), channel_id=1, source_target_pairs={{32,64},{33,65},{34,66},{35,67},{36,68},{37,69},{38,70},{39,71},{4... | collective-permute-start | bytes 147464 | tf_op jit(solution)/shard_map/ppermute | solution.py:292
  12.8 7.0 %collective-permute-start.3 = (bf16[3,16,512]{2,1,0:T(8,128)(2,1)S(1)}, bf16[3,16,512]{2,1,0:T(8,128)(2,1)S(1)}, u32[]{:S(2)}, u32[]{:S(2)}) collective-permute-start(bf16[3,16,512]{2,1,0:T(8,128)(2,1)S(1)} %get-tuple-element.80), channel_id=1, source_target_pairs={{0,32},{1,33},{2,34},{3,35},{4,36},{5,37},{6,38},{7,39},{8,40},{9,... | collective-permute-start | bytes 147464 | tf_op jit(solution)/shard_map/ppermute | solution.py:292
  19.8 1.7 %shard_map.128 = (f32[3,64,256]{2,1,0:T(8,128)S(1)}, bf16[512,512]{1,0:T(8,128)(2,1)S(1)}, bf16[512,512]{1,0:T(8,128)(2,1)S(1)}) custom-call(s32[3]{0:T(128)S(1)} %pad_add_fusion.coord, s32[3,49]{1,0:T(4,128)S(1)} %bitcast.31), custom_call_target="tpu_custom_call" | custom-call | flops 402653184 | bytes 4000000 | tf_op jit(solution)/shard_map/pallas_call | solution.py:319
  21.9 7.7 %shard_map.129 = (bf16[16,5,16,512]{3,2,1,0:T(8,128)(2,1)S(1)}, bf16[16,5,16,512]{3,2,1,0:T(8,128)(2,1)S(1)}, bf16[16,2,32,512]{3,2,1,0:T(8,128)(2,1)S(1)}, bf16...) custom-call(s32[3]{0:T(128)S(1)} %pad_add_fusion.coord, ...), custom_call_target="tpu_custom_call" | custom-call | flops 5000000000 | bytes 20000000 | tf_op jit(solution)/shard_map/pallas_call | solution.py:325
  30.2 5.3 %shard_map.130 = (bf16[16,3,16,512]{3,2,1,0:T(8,128)(2,1)S(1)}, bf16[16,3,16,512]{3,2,1,0:T(8,128)(2,1)S(1)}, bf16[16,512]{1,0:T(8,128)(2,1)S(1)}, bf16[16,512]{...) custom-call(s32[3]{0:T(128)S(1)} %pad_add_fusion.coord, ...), custom_call_target="tpu_custom_call" | custom-call | flops 3000000000 | bytes 12000000 | tf_op jit(solution)/shard_map/pallas_call | solution.py:337
  35.5 0.7 copy-done.4
  36.8 1.8 %collective-permute-done.7.gr = bf16[16,512]{1,0:T(8,128)(2,1)S(1)} collective-permute-done((bf16[16,512]{1,0:T(8,128)(2,1)S(1)}, bf16[16,512]{1,0:T(8,128)(2,1)S(1)}, u32[]{:S(2)}, u32[]{:S(2)}) %collective-permute-start.7) | collective-permute-done | bytes 16416 | tf_op jit(solution)/shard_map/ppermute | solution.py:292
  38.6 0.7 shard_map.131
  39.4 1.7 %copy-done = bf16[16,13,16,512]{3,2,1,0:T(8,128)(2,1)} copy-done((bf16[16,13,16,512]{3,2,1,0:T(8,128)(2,1)}, bf16[16,13,16,512]{3,2,1,0:T(8,128)(2,1)S(1)}, u32[]{:S(2)}) %copy-start) | copy-done | bytes 3407896
  41.1 9.8 %all-to-all-start = ((bf16[16,13,16,512]{3,2,1,0:T(8,128)(2,1)}), bf16[16,13,16,512]{3,2,1,0:T(8,128)(2,1)S(1)}, u32[]{:S(2)}, u32[]{:S(2)}) async-start(bf16[16,13,16,512]{3,2,1,0:T(8,128)(2,1)} %copy-done), calls=%async_computation | async-start | bytes 6815744 | tf_op jit(solution)/shard_map/all_to_all | solution.py:296
  50.9 1.3 %slice.49 = f32[480,512]{1,0:T(8,128)S(1)} slice(f32[512,512]{1,0:T(8,128)} %copy-done.6), slice={[0:480], [0:512]} | slice | bytes 1966080 | tf_op jit(solution)/shard_map/slice | solution.py:369
  52.4 0.7 collective-permute-start.8
  53.1 2.1 %collective-permute-start.9 = (bf16[30,3,512]{2,1,0:T(4,128)(2,1)S(1)}, bf16[30,3,512]{2,1,0:T(4,128)(2,1)S(1)}, u32[]{:S(2)}, u32[]{:S(2)}) collective-permute-start(bf16[30,3,512]{2,1,0:T(4,128)(2,1)S(1)} %get-tuple-element.79), channel_id=1, source_target_pairs={{0,1},{1,0},{2,3},{3,2},{4,5},{5,4},{6,7},{7,6},{8,9},{9,8},{10,11... | collective-permute-start | bytes 276488 | tf_op jit(solution)/shard_map/ppermute | solution.py:292
  55.4 0.8 collective-permute-done.9
  56.2 1.0 fusion.12
  57.2 2.5 %collective-permute-start.10 = (bf16[3,8,512]{2,1,0:T(8,128)(2,1)S(1)}, bf16[3,8,512]{2,1,0:T(8,128)(2,1)}, u32[]{:S(2)}, u32[]{:S(2)}) collective-permute-start(bf16[3,8,512]{2,1,0:T(8,128)(2,1)S(1)} %get-tuple-element.82), channel_id=1, source_target_pairs={{32,64},{33,65},{34,66},{35,67},{36,68},{37,69},{38,70},{39,71},{4... | collective-permute-start | bytes 73736 | tf_op jit(solution)/shard_map/ppermute | solution.py:292
  59.7 3.2 %collective-permute-start.11 = (bf16[3,8,512]{2,1,0:T(8,128)(2,1)S(1)}, bf16[3,8,512]{2,1,0:T(8,128)(2,1)S(1)}, u32[]{:S(2)}, u32[]{:S(2)}) collective-permute-start(bf16[3,8,512]{2,1,0:T(8,128)(2,1)S(1)} %get-tuple-element.83), channel_id=1, source_target_pairs={{0,32},{1,33},{2,34},{3,35},{4,36},{5,37},{6,38},{7,39},{8,40},{9,... | collective-permute-start | bytes 73736 | tf_op jit(solution)/shard_map/ppermute | solution.py:292
  62.9 23.0 %collective-permute-done.10 = bf16[3,8,512]{2,1,0:T(8,128)(2,1)} collective-permute-done((bf16[3,8,512]{2,1,0:T(8,128)(2,1)S(1)}, bf16[3,8,512]{2,1,0:T(8,128)(2,1)}, u32[]{:S(2)}, u32[]{:S(2)}) %collective-permute-start.10) | collective-permute-done | bytes 24608 | tf_op jit(solution)/shard_map/ppermute | solution.py:292
  85.9 0.7 convert_element_type.45
  86.6 14.8 %collective-permute-done.11 = bf16[3,8,512]{2,1,0:T(8,128)(2,1)S(1)} collective-permute-done((bf16[3,8,512]{2,1,0:T(8,128)(2,1)S(1)}, bf16[3,8,512]{2,1,0:T(8,128)(2,1)S(1)}, u32[]{:S(2)}, u32[]{:S(2)}) %collective-permute-start.11) | collective-permute-done | bytes 24608 | tf_op jit(solution)/shard_map/ppermute | solution.py:292
  101.4 1.4 %fusion.3 = f32[24,8]{1,0:T(8,128)S(1)} fusion(bf16[24,8,512]{2,1,0:T(8,128)(2,1)} %param.8, f32[24,8]{1,0:T(8,128)S(1)} %add_rsqrt_fusion, f32[512]{0:T(512)S(1)} %bitcast.34, f32[192,512]{1,0:T(8,128)} %copy-done.4, f32[3,8,512]{2,1,0:T(8,128)S(1)} %convert_element_type.46, pred[]{:T(512)S(6)} %not.7, f32[3,8,512]{2,1,0:T(8,128)S(1)} %convert_element_type.45, ...), kind=kLoop, calls=%fused_computation.6 | loop fusion | flops 982848 | bytes 1084930 | tf_op jit(solution)/shard_map/reduce_sum | solution.py:380
  103.5 0.7 copy-done.5
  104.2 5.5 %all-to-all-start.1 = ((bf16[8,32,512]{2,1,0:T(8,128)(2,1)}), bf16[8,32,512]{2,1,0:T(8,128)(2,1)S(1)}, u32[]{:S(2)}, u32[]{:S(2)}) async-start(bf16[8,32,512]{2,1,0:T(8,128)(2,1)} %copy-done.5), calls=%async_computation.1 | async-start | bytes 524288 | tf_op jit(solution)/shard_map/all_to_all | solution.py:296
  109.7 2.2 %fusion.7 = bf16[24,8,512]{2,1,0:T(8,128)(2,1)} fusion(bf16[24,8,512]{2,1,0:T(8,128)(2,1)} %param.8, bf16[192,512]{1,0:T(8,128)(2,1)} %copy-done.7, f32[24,8]{1,0:T(8,128)S(1)} %broadcast_multiply_fusion, f32[24,8]{1,0:T(8,128)S(1)} %add_rsqrt_fusion, f32[512]{0:T(512)S(1)} %bitcast.35, f32[192,512]{1,0:T(8,128)} %copy-done.4, ...), kind=kLoop, calls=%fused_computation.10 | loop fusion | flops 1376256 | bytes 1478146 | tf_op jit(solution)/shard_map/convert_element_type | solution.py:381
  111.9 8.7 %all-to-all-done.1.got = bf16[8,32,512]{2,1,0:T(8,128)(2,1)S(1)} async-done(((bf16[8,32,512]{2,1,0:T(8,128)(2,1)}), bf16[8,32,512]{2,1,0:T(8,128)(2,1)S(1)}, u32[]{:S(2)}, u32[]{:S(2)}) %all-to-all-start.1) | async-done | bytes 262176 | tf_op jit(solution)/shard_map/all_to_all | solution.py:296
  120.6 0.7 shard_map.133
  (53 shorter events, 3.5 us)
Async XLA Ops:
  1.8 8.2 %collective-permute-start = (bf16[24,3,512]{2,1,0:T(4,128)(2,1)S(1)}, bf16[24,3,512]{2,1,0:T(4,128)(2,1)S(1)}, u32[]{:S(2)}, u32[]{:S(2)}) collective-permute-start(bf16[24,3,512]{2,1,0:T(4,128)(2,1)S(1)} %get-tuple-element.85), channel_id=1, source_target_pairs={{1,2},{2,1},{3,4},{4,3},{5,6},{6,5},{7,8},{8,7},{9,10},{10,9},{11,... | collective-permute-start | bytes 221192 | tf_op jit(solution)/shard_map/ppermute | solution.py:292
  2.5 7.5 %collective-permute-start.1 = (bf16[24,3,512]{2,1,0:T(4,128)(2,1)S(1)}, bf16[24,3,512]{2,1,0:T(4,128)(2,1)S(1)}, u32[]{:S(2)}, u32[]{:S(2)}) collective-permute-start(bf16[24,3,512]{2,1,0:T(4,128)(2,1)S(1)} %get-tuple-element.84), channel_id=1, source_target_pairs={{0,1},{1,0},{2,3},{3,2},{4,5},{5,4},{6,7},{7,6},{8,9},{9,8},{10,11... | collective-permute-start | bytes 221192 | tf_op jit(solution)/shard_map/ppermute | solution.py:292
  6.6 1.6 %copy-start.3 = (bf16[2048,512]{1,0:T(8,128)(2,1)S(1)}, bf16[2048,512]{1,0:T(8,128)(2,1)}, u32[]{:S(2)}) copy-start(bf16[2048,512]{1,0:T(8,128)(2,1)} %w_down.1) | copy-start | bytes 6291460
  8.2 0.9 copy-start.8
  9.1 0.9 copy-start.1
  9.1 12.7 %copy-start.12 = (bf16[512,1536]{1,0:T(8,128)(2,1)S(1)}, bf16[512,1536]{1,0:T(8,128)(2,1)}, u32[]{:S(2)}) copy-start(bf16[512,1536]{1,0:T(8,128)(2,1)} %w_qkv.3) | copy-start | bytes 4718596
  9.1 12.7 %copy-start.13 = (bf16[512,512]{1,0:T(8,128)(2,1)S(1)}, bf16[512,512]{1,0:T(8,128)(2,1)}, u32[]{:S(2)}) copy-start(bf16[512,512]{1,0:T(8,128)(2,1)} %w_out.3) | copy-start | bytes 1572868
  9.9 11.9 %copy-start.9 = (bf16[24,8,512]{2,1,0:T(8,128)(2,1)S(1)}, bf16[24,8,512]{2,1,0:T(8,128)(2,1)}, u32[]{:S(2)}) copy-start(bf16[24,8,512]{2,1,0:T(8,128)(2,1)} %param.9) | copy-start | bytes 589828
  9.9 11.9 %copy-start.10 = (f32[2,512]{1,0:T(2,128)S(1)}, f32[2,512]{1,0:T(2,128)}, u32[]{:S(2)}) copy-start(f32[2,512]{1,0:T(2,128)} %gains.1) | copy-start | bytes 12292
  10.0 11.9 %copy-start.11 = (bf16[512,2048]{1,0:T(8,128)(2,1)S(1)}, bf16[512,2048]{1,0:T(8,128)(2,1)}, u32[]{:S(2)}) copy-start(bf16[512,2048]{1,0:T(8,128)(2,1)} %w_up.1) | copy-start | bytes 6291460
  10.2 11.3 %collective-permute-start.2 = (bf16[3,16,512]{2,1,0:T(8,128)(2,1)S(1)}, bf16[3,16,512]{2,1,0:T(8,128)(2,1)S(1)}, u32[]{:S(2)}, u32[]{:S(2)}) collective-permute-start(bf16[3,16,512]{2,1,0:T(8,128)(2,1)S(1)} %get-tuple-element.81), channel_id=1, source_target_pairs={{32,64},{33,65},{34,66},{35,67},{36,68},{37,69},{38,70},{39,71},{4... | collective-permute-start | bytes 147464 | tf_op jit(solution)/shard_map/ppermute | solution.py:292
  12.8 9.0 %collective-permute-start.3 = (bf16[3,16,512]{2,1,0:T(8,128)(2,1)S(1)}, bf16[3,16,512]{2,1,0:T(8,128)(2,1)S(1)}, u32[]{:S(2)}, u32[]{:S(2)}) collective-permute-start(bf16[3,16,512]{2,1,0:T(8,128)(2,1)S(1)} %get-tuple-element.80), channel_id=1, source_target_pairs={{0,32},{1,33},{2,34},{3,35},{4,36},{5,37},{6,38},{7,39},{8,40},{9,... | collective-permute-start | bytes 147464 | tf_op jit(solution)/shard_map/ppermute | solution.py:292
  29.6 5.9 %copy-start.7 = (bf16[192,512]{1,0:T(8,128)(2,1)}, bf16[192,512]{1,0:T(8,128)(2,1)S(1)}, u32[]{:S(2)}) copy-start(bf16[192,512]{1,0:T(8,128)(2,1)S(1)} %get-tuple-element.48.gm) | copy-start | bytes 589828
  29.6 6.6 %collective-permute-start.4 = (bf16[16,5,16,512]{3,2,1,0:T(8,128)(2,1)S(1)}, bf16[16,5,16,512]{3,2,1,0:T(8,128)(2,1)S(1)}, u32[]{:S(2)}, u32[]{:S(2)}) collective-permute-start(bf16[16,5,16,512]{3,2,1,0:T(8,128)(2,1)S(1)} %get-tuple-element.50), channel_id=1, source_target_pairs={{0,1},{1,0},{2,3},{3,2},{4,5},{5,4},{6,7},{7,6},{8,9},{9,8},{10,11... | collective-permute-start | bytes 3932168 | tf_op jit(solution)/shard_map/ppermute | solution.py:292
  29.7 6.5 %collective-permute-start.5 = (bf16[16,2,32,512]{3,2,1,0:T(8,128)(2,1)S(1)}, bf16[16,2,32,512]{3,2,1,0:T(8,128)(2,1)S(1)}, u32[]{:S(2)}, u32[]{:S(2)}) collective-permute-start(bf16[16,2,32,512]{3,2,1,0:T(8,128)(2,1)S(1)} %get-tuple-element.51), channel_id=1, source_target_pairs={{0,1},{1,0},{2,3},{3,2},{4,5},{5,4},{6,7},{7,6},{8,9},{9,8},{10,11... | collective-permute-start | bytes 3145736 | tf_op jit(solution)/shard_map/ppermute | solution.py:292
  35.5 0.7 copy-start.4
  36.2 3.1 %copy-start.6 = (f32[512,512]{1,0:T(8,128)}, f32[512,512]{1,0:T(8,128)S(1)}, u32[]{:S(2)}) copy-start(f32[512,512]{1,0:T(8,128)S(1)} %get-tuple-element.68) | copy-start | bytes 3145732
  36.2 2.4 %collective-permute-start.6 = (bf16[16,3,16,512]{3,2,1,0:T(8,128)(2,1)S(1)}, bf16[16,3,16,512]{3,2,1,0:T(8,128)(2,1)S(1)}, u32[]{:S(2)}, u32[]{:S(2)}) collective-permute-start(bf16[16,3,16,512]{3,2,1,0:T(8,128)(2,1)S(1)} %get-tuple-element.64), channel_id=1, source_target_pairs={{0,1},{1,0},{2,3},{3,2},{4,5},{5,4},{6,7},{7,6},{8,9},{9,8},{10,11... | collective-permute-start | bytes 2359304 | tf_op jit(solution)/shard_map/ppermute | solution.py:292
  36.6 2.0 %collective-permute-start.7 = (bf16[16,512]{1,0:T(8,128)(2,1)S(1)}, bf16[16,512]{1,0:T(8,128)(2,1)S(1)}, u32[]{:S(2)}, u32[]{:S(2)}) collective-permute-start(bf16[16,512]{1,0:T(8,128)(2,1)S(1)} %get-tuple-element.66), channel_id=1, source_target_pairs={{0,1},{1,0},{2,3},{3,2},{4,5},{5,4},{6,7},{7,6},{8,9},{9,8},{10,11... | collective-permute-start | bytes 49160 | tf_op jit(solution)/shard_map/ppermute | solution.py:292
  39.4 1.7 %copy-start = (bf16[16,13,16,512]{3,2,1,0:T(8,128)(2,1)}, bf16[16,13,16,512]{3,2,1,0:T(8,128)(2,1)S(1)}, u32[]{:S(2)}) copy-start(bf16[16,13,16,512]{3,2,1,0:T(8,128)(2,1)S(1)} %shard_map.131) | copy-start | bytes 10223620
  41.1 61.7 %all-to-all-start = ((bf16[16,13,16,512]{3,2,1,0:T(8,128)(2,1)}), bf16[16,13,16,512]{3,2,1,0:T(8,128)(2,1)S(1)}, u32[]{:S(2)}, u32[]{:S(2)}) async-start(bf16[16,13,16,512]{3,2,1,0:T(8,128)(2,1)} %copy-done), calls=%async_computation | async-start | bytes 6815744 | tf_op jit(solution)/shard_map/all_to_all | solution.py:296
  50.9 4.3 %copy-start.2 = (bf16[24,8,512]{2,1,0:T(8,128)(2,1)S(1)}, bf16[24,8,512]{2,1,0:T(8,128)(2,1)}, u32[]{:S(2)}) copy-start(bf16[24,8,512]{2,1,0:T(8,128)(2,1)} %param.8) | copy-start | bytes 589828
  52.4 2.9 %collective-permute-start.8 = (bf16[30,3,512]{2,1,0:T(4,128)(2,1)S(1)}, bf16[30,3,512]{2,1,0:T(4,128)(2,1)S(1)}, u32[]{:S(2)}, u32[]{:S(2)}) collective-permute-start(bf16[30,3,512]{2,1,0:T(4,128)(2,1)S(1)} %get-tuple-element.78), channel_id=1, source_target_pairs={{1,2},{2,1},{3,4},{4,3},{5,6},{6,5},{7,8},{8,7},{9,10},{10,9},{11,... | collective-permute-start | bytes 276488 | tf_op jit(solution)/shard_map/ppermute | solution.py:292
  53.1 3.1 %collective-permute-start.9 = (bf16[30,3,512]{2,1,0:T(4,128)(2,1)S(1)}, bf16[30,3,512]{2,1,0:T(4,128)(2,1)S(1)}, u32[]{:S(2)}, u32[]{:S(2)}) collective-permute-start(bf16[30,3,512]{2,1,0:T(4,128)(2,1)S(1)} %get-tuple-element.79), channel_id=1, source_target_pairs={{0,1},{1,0},{2,3},{3,2},{4,5},{5,4},{6,7},{7,6},{8,9},{9,8},{10,11... | collective-permute-start | bytes 276488 | tf_op jit(solution)/shard_map/ppermute | solution.py:292
  57.2 28.7 %collective-permute-start.10 = (bf16[3,8,512]{2,1,0:T(8,128)(2,1)S(1)}, bf16[3,8,512]{2,1,0:T(8,128)(2,1)}, u32[]{:S(2)}, u32[]{:S(2)}) collective-permute-start(bf16[3,8,512]{2,1,0:T(8,128)(2,1)S(1)} %get-tuple-element.82), channel_id=1, source_target_pairs={{32,64},{33,65},{34,66},{35,67},{36,68},{37,69},{38,70},{39,71},{4... | collective-permute-start | bytes 73736 | tf_op jit(solution)/shard_map/ppermute | solution.py:292
  59.7 41.8 %collective-permute-start.11 = (bf16[3,8,512]{2,1,0:T(8,128)(2,1)S(1)}, bf16[3,8,512]{2,1,0:T(8,128)(2,1)S(1)}, u32[]{:S(2)}, u32[]{:S(2)}) collective-permute-start(bf16[3,8,512]{2,1,0:T(8,128)(2,1)S(1)} %get-tuple-element.83), channel_id=1, source_target_pairs={{0,32},{1,33},{2,34},{3,35},{4,36},{5,37},{6,38},{7,39},{8,40},{9,... | collective-permute-start | bytes 73736 | tf_op jit(solution)/shard_map/ppermute | solution.py:292
  103.5 0.7 copy-start.5
  104.2 16.4 %all-to-all-start.1 = ((bf16[8,32,512]{2,1,0:T(8,128)(2,1)}), bf16[8,32,512]{2,1,0:T(8,128)(2,1)S(1)}, u32[]{:S(2)}, u32[]{:S(2)}) async-start(bf16[8,32,512]{2,1,0:T(8,128)(2,1)} %copy-done.5), calls=%async_computation.1 | async-start | bytes 524288 | tf_op jit(solution)/shard_map/all_to_all | solution.py:296

commit v4 on v3

--- a/solution.py
+++ b/solution.py
@@ -72,7 +72,7 @@
         gact[:, c * 512 : (c + 1) * 512] = nt(cot[...], w_down[c * 512 : (c + 1) * 512, :])
 
 
-def prep_mask_kernel(coord, mask, bias, pt_u, pt_d):
+def prep_mask_kernel(coord, mask, bias, pt_u, pt_k, pt_d):
     q = lax.broadcasted_iota(jnp.int32, (QT, KT), 0)
     k = lax.broadcasted_iota(jnp.int32, (QT, KT), 1)
     ki = k // EC
@@ -94,13 +94,15 @@
         gr = coord[0] * ROWS + t * TILE + ki - RIM
         ok = (allowed[t] == 1) & (gr >= 0) & (gr < GRID_ROWS) & (gc >= 0) & (gc < GRID_COLS)
         bias[t] = jnp.where(ok, 0.0, -1e30)
-    me = coord[2] & 1
+    me = coord[2]
     lane = lax.broadcasted_iota(jnp.int32, (512, 512), 1)
     p = lax.broadcasted_iota(jnp.int32, (512, 512), 0)
-    co = (p >> 8) ^ me
-    k_u = ((p >> 3) & 1) * 128 + ((p >> 4) & 15) * 8 + ((p >> 1) & 3) * 2 + co
-    pt_u[...] = jnp.where(lane == k_u * 2 + (p & 1), 1.0, 0.0).astype(BF16)
-    k_d = ((p >> 5) & 7) * 8 + ((p >> 3) & 3) * 2 + co
+    core_z = ((p >> 3) & 1) * 128 + ((p >> 1) & 3) * 2 + (p >> 8)
+    hi, lo = (p >> 6) & 3, (p >> 4) & 3
+    here = me & 121
+    pt_u[...] = jnp.where(lane == ((core_z + hi * 32 + lo * 8) ^ here) * 2 + (p & 1), 1.0, 0.0).astype(BF16)
+    pt_k[...] = jnp.where(lane == ((core_z + hi * 8 + lo * 32) ^ here) * 2 + (p & 1), 1.0, 0.0).astype(BF16)
+    k_d = (((p >> 5) & 1) * 32 + ((p >> 6) & 3) * 8 + ((p >> 3) & 3) * 2 + (p >> 8)) ^ (me & 57)
     pt_d[...] = jnp.where(lane == k_d * 8 + (p & 7), 1.0, 0.0).astype(BF16)
 
 
@@ -156,10 +158,12 @@
         u_send[:, c] = gu[256:].reshape(16, 16, D)
         act_t = nt(pt_d[...], act).astype(BF16)
         gd = nn(act_t, cot[...]).astype(BF16)
-        for x in range(2):
-            lo = (2 * (c & 1) + x) * 4
-            d_keep[lo : lo + 4, c >> 1] = gd[x * 128 : x * 128 + 128].reshape(4, 32, D)
-            d_send[lo : lo + 4, c >> 1] = gd[256 + x * 128 : 256 + x * 128 + 128].reshape(4, 32, D)
+        xh = (c & 1) ^ ((coord[2] >> 6) & 1)
+        for y in range(4):
+            for xl in range(2):
+                at = (y * 2 + xl) * 32
+                d_keep[y, xh * 2 + xl, c >> 1] = gd[at : at + 32]
+                d_send[y, xh * 2 + xl, c >> 1] = gd[256 + at : 256 + at + 32]
     g = gn * gains[1:2, :]
     gm = (cot[...].astype(F32) + inv_m * (g - um * jnp.mean(g * um, axis=-1, keepdims=True))).astype(BF16)
     gm_o[...] = gm
@@ -171,7 +175,7 @@
 
 def backward_kernel(
     coord, gm, w_out, w_qkv, q, kv, p_in, ne, no, mid, rim_a, rim_b, tok, gain_mid, pt,
-    k_keep, k_send, g_keep, g_send, gne_o, gnq_o, dq_s, dkv_s,
+    k_keep, k_send, gne_o, gnq_o, dq_s, dkv_s,
 ):
     ga = nt(gm[...], w_out[...]).astype(BF16)
     dkv_s[...] = jnp.zeros_like(dkv_s)
@@ -194,8 +198,9 @@
     gk = nn(nt(pt[...], ne[...]).astype(BF16), dkv).astype(BF16)
     gq = nn(nt(pt[...], no[...]).astype(BF16), dq).astype(BF16)
     for i, part in enumerate([gq, gk[:, :D], gk[:, D:]]):
-        k_keep[:, i] = part[:256].reshape(16, 16, D)
-        k_send[:, i] = part[256:].reshape(16, 16, D)
+        for j in range(16):
+            k_keep[j * 3 + i] = part[j * 16 : j * 16 + 16]
+            k_send[j * 3 + i] = part[256 + j * 16 : 256 + j * 16 + 16]
     gne = nt(dkv, w_qkv[:, D:])
     gnq = nt(dq, w_qkv[:, :D])
     gne_o[...] = gne
@@ -208,27 +213,52 @@
         part = gne_o[pl.ds(pl.multiple_of(at * EC, EC), size), :]
         gain_in = gain_in + jnp.sum(part * unit, axis=0, keepdims=True)
     spread = jnp.concatenate([gain_in, gain_mid[...], jnp.zeros((14, D), F32)], axis=0).astype(BF16)
-    g_keep[...] = spread
-    g_send[...] = spread
-
-
-def join_kernel(uk, ur, dk, dr, kk, kr, gk, gr, out):
-    at = 0
-    for a, b in ((uk, ur), (dk, dr), (kk, kr)):
-        n = a.shape[1]
-        out[:, at : at + n] = (a[...].astype(F32) + b[...].astype(F32)).astype(BF16)
-        at += n
-    gain = (gk[...].astype(F32) + gr[...].astype(F32)).astype(BF16)
-    for j in range(16):
-        out[j, at] = gain
-
-
-def reduce_xy_kernel(got, out):
-    rows = 13 * 16
-    acc = got[0].reshape(rows, D).astype(F32)
-    for j in range(1, 16):
-        acc = acc + got[j].reshape(rows, D).astype(F32)
-    acc = acc.astype(BF16)
+    k_keep[48] = spread
+    k_send[48] = spread
+
+
+def add2(a, b):
+    return (a.astype(F32) + b.astype(F32)).astype(BF16)
+
+
+def add4(parts):
+    a, b, c, d = [v.astype(F32) for v in parts]
+    return ((a + b) + (c + d)).astype(BF16)
+
+
+def join_pair_kernel(keep, got, *outs):
+    n = keep.shape[0] // 4
+    for d in range(4):
+        outs[d][...] = add2(keep[d * n : (d + 1) * n], got[d * n : (d + 1) * n])
+
+
+def join_qkv_kernel(keep, got, *outs):
+    gain = add2(keep[48], got[48])
+    for d in range(4):
+        outs[d][:12] = add2(keep[d * 12 : (d + 1) * 12], got[d * 12 : (d + 1) * 12])
+        outs[d][12] = gain
+
+
+def join_four_kernel(*refs):
+    parts, outs = refs[:4], refs[4:]
+    n = outs[0].shape[0]
+    for d in range(4):
+        outs[d][...] = add4([r[d * n : (d + 1) * n] for r in parts])
+
+
+def join_four_qkv_kernel(*refs):
+    parts, outs = refs[:4], refs[4:]
+    gain = add4([r[12] for r in parts])
+    for d in range(4):
+        outs[d][:3] = add4([r[d * 3 : (d + 1) * 3] for r in parts])
+        outs[d][3] = gain
+
+
+def reduce_xy_kernel(*refs):
+    out = refs[12]
+    sums = [add4([r[...] for r in refs[i : i + 4]]).reshape(-1, D) for i in (0, 4, 8)]
+    acc = jnp.concatenate(sums, axis=0)
+    rows = acc.shape[0]
     i = lax.broadcasted_iota(jnp.int32, (256, rows), 0)
     lane = lax.broadcasted_iota(jnp.int32, (256, rows), 1)
     z = i // 32
@@ -284,12 +314,17 @@
 ROW_A, ROW_B = pairs(N_COL, 8, 1), pairs(N_COL, 8, 0)
 COL_A, COL_B = pairs(1, N_COL, 1), pairs(1, N_COL, 0)
 CORE_SWAP = [(k, k ^ 1) for k in range(256)]
-XY_GROUPS = [[zh * 128 + x * 32 + y * 8 + zl * 2 + c for x in range(4) for y in range(4)] for zh in range(2) for zl in range(4) for c in range(2)]
+X_BIT = 32
+Y_BIT = 8
 Z_GROUPS = [[zh * 128 + x * 32 + y * 8 + zl * 2 + c for zh in range(2) for zl in range(4)] for x in range(4) for y in range(4) for c in range(2)]
 
 
 def send(x, perm):
     return lax.ppermute(x, AXES, perm)
+
+
+def to_three(chunks, bit):
+    return [chunks[0]] + [send(chunks[d], [(k, k ^ (bit * d)) for k in range(256)]) for d in (1, 3, 2)]
 
 
 def exchange(x, groups):
@@ -309,19 +344,19 @@
     first, last = tokens[:, :RIM], tokens[:, COLS - RIM :]
     side_b = send(jnp.where(col_odd, first, last), COL_B)
     side_a = send(jnp.where(col_odd, last, first), COL_A)
+    bias, pt_u, pt_k, pt_d = call(
+        prep_mask_kernel, [((TILES, QT, KT), F32), ((D, D), BF16), ((D, D), BF16), ((D, D), BF16)],
+        [], 2, 0, 2 * TOK * D * FF, 4_000_000, 16,
+    )(coord, mask)
+    side_a, side_b, cot, bias = lax.optimization_barrier((side_a, side_b, cot, bias))
+    mid = jnp.concatenate([tokens, side_a, side_b, jnp.zeros((ROWS, EC - COLS - 2 * RIM, D), BF16)], axis=1)
+    rim_b = send(jnp.where(row_odd, mid[:RIM], mid[ROWS - RIM :]), ROW_B)
+    rim_a = send(jnp.where(row_odd, mid[ROWS - RIM :], mid[:RIM]), ROW_A)
     (gact,) = call(
         prep_front_kernel, [((TOK, FF), F32)], [], 0, 2, 2 * TOK * D * FF, 4_000_000, 16,
     )(cot, w_down)
-    side_a, side_b, gact, mask = lax.optimization_barrier((side_a, side_b, gact, mask))
-    mid = jnp.concatenate([tokens, side_a, side_b, jnp.zeros((ROWS, EC - COLS - 2 * RIM, D), BF16)], axis=1)
-    rim_b = send(jnp.where(row_odd, mid[:RIM], mid[ROWS - RIM :]), ROW_B)
-    rim_a = send(jnp.where(row_odd, mid[ROWS - RIM :], mid[:RIM]), ROW_A)
-    bias, pt_u, pt_d = call(
-        prep_mask_kernel, [((TILES, QT, KT), F32), ((D, D), BF16), ((D, D), BF16)],
-        [], 2, 0, 2 * TOK * D * FF, 4_000_000, 16,
-    )(coord, mask)
-
-    half_u, half_d, half_k = ((16, 5, 16, D), BF16), ((16, 2, 32, D), BF16), ((16, 3, 16, D), BF16)
+
+    half_u, half_d, half_k = ((16, 5, 16, D), BF16), ((4, 4, 2, 32, D), BF16), ((49, 16, D), BF16)
     u_keep, u_send, d_keep, d_send, gm, q, kv, prob, ne, no, gain_mid = call(
         forward_kernel,
         [
@@ -334,23 +369,37 @@
 
     u_got = send(u_send, CORE_SWAP)
     d_got = send(d_send, CORE_SWAP)
-    k_keep, k_send, g_keep, g_send, gne, gnq = call(
+    k_keep, k_send, gne, gnq = call(
         backward_kernel,
-        [half_k, half_k, ((16, D), BF16), ((16, D), BF16), ((EXT, D), F32), ((TOK, D), F32)],
+        [half_k, half_k, ((EXT, D), F32), ((TOK, D), F32)],
         [pltpu.VMEM((TOK, D), BF16), pltpu.VMEM((EXT, 2 * D), F32)], 1, 14, 3_000_000_000, 12_000_000, 30,
-    )(coord, gm, w_out, w_qkv, q, kv, prob, ne, no, mid, rim_a, rim_b, tok, gain_mid, pt_u)
-    u_got, d_got, k_send, g_send = lax.optimization_barrier((u_got, d_got, k_send, g_send))
+    )(coord, gm, w_out, w_qkv, q, kv, prob, ne, no, mid, rim_a, rim_b, tok, gain_mid, pt_k)
+    u_got, d_got, k_send = lax.optimization_barrier((u_got, d_got, k_send))
+
+    def join(body, ins, blocks):
+        outs = [((blocks, 16, D), BF16)] * 4
+        return list(call(body, outs, [], 0, len(ins), 1_000_000, 4_000_000, 12)(*ins))
 
     k_got = send(k_send, CORE_SWAP)
-    g_got = send(g_send, CORE_SWAP)
-    (packed,) = call(
-        join_kernel, [((16, 13, 16, D), BF16)], [], 0, 8, 4_000_000, 10_000_000, 30,
-    )(u_keep, u_got, d_keep.reshape(16, 4, 16, D), d_got.reshape(16, 4, 16, D), k_keep, k_got, g_keep, g_got)
-    packed, gne = lax.optimization_barrier((packed, gne))
-    got = exchange(packed, XY_GROUPS)
+    u = join(join_pair_kernel, [u_keep.reshape(80, 16, D), u_got.reshape(80, 16, D)], 20)
+    d = join(join_pair_kernel, [d_keep.reshape(64, 16, D), d_got.reshape(64, 16, D)], 16)
+    u1 = to_three(u, X_BIT)
+    d1 = to_three(d, Y_BIT)
+    k_got, u[0], d[0] = lax.optimization_barrier((k_got, u[0], d[0]))
+    kc = join(join_qkv_kernel, [k_keep, k_got], 13)
+    kc[0], gne = lax.optimization_barrier((kc[0], gne))
+    k1 = to_three(kc, Y_BIT)
+    u1[0], d1[0] = u[0], d[0]
+    u = join(join_four_kernel, u1, 5)
+    d = join(join_four_kernel, d1, 4)
+    u2 = to_three(u, Y_BIT)
+    d2 = to_three(d, X_BIT)
+    k1[0], u2[0], d2[0] = lax.optimization_barrier((k1[0], u2[0], d2[0]))
+    kc = join(join_four_qkv_kernel, k1, 4)
+    k2 = to_three(kc, X_BIT)
     (spread,) = call(
-        reduce_xy_kernel, [((8, 32, D), BF16)], [], 0, 1, 60_000_000, 4_000_000, 16,
-    )(got)
+        reduce_xy_kernel, [((8, 32, D), BF16)], [], 0, 12, 60_000_000, 4_000_000, 12,
+    )(*u2, *d2, *k2)
     got_z = exchange(spread, Z_GROUPS)
     g_up, g_down, g_out, g_qkv, g_gains = call(
         reduce_z_kernel,

time: 122 us -> 113 us (0.926)
  the two profiles are of different devices: /device:TPU:4 before, /device:TPU:8 now
where the time goes in v4:
time: 113 us; the launch traced here: 112 us
  starting transfers between devices  58.6 us (52%)
  waiting for transfers between devices  22.6 us (20%)
  Pallas kernels  20.7 us (18%)
  other arithmetic  6.8 us (6%)
  local copies, waits for them, and re-layouts  2.27 us (2%)
    ppermute x29, starting transfers between devices, send(): return lax.ppermute(x, AXES, perm)  55.2 us
    ppermute x29, waiting for transfers between devices, send(): return lax.ppermute(x, AXES, perm)  13.1 us
    all_to_all x1, waiting for transfers between devices, exchange(): return lax.all_to_all(x, AXES, 0, 0, axis_index_groups=groups, tiled=True)  9.48 us
    pallas_call x1, Pallas kernels, per_device(): call(forward_kernel, [half_u, half_u, half_d, half_d, ((TOK, D), BF16), (...  7.77 us
    pallas_call x1, Pallas kernels, per_device(): call(backward_kernel, [half_k, half_k, ((EXT, D), F32), ((TOK, D), F32)],...  5.29 us
    all_to_all x1, starting transfers between devices, exchange(): return lax.all_to_all(x, AXES, 0, 0, axis_index_groups=groups, tiled=True)  3.41 us
    pallas_call x6, Pallas kernels, join(): return list(call(body, outs, [], 0, len(ins), 1000000, 4000000, 12)(*ins))  3.11 us
  transfers between devices with their start and end apart: 30, of which 9 were waited for; matrix products, arithmetic and copies ran while one was open for 5% of the time, Pallas kernels for 9%

profile of v4, /device:TPU:8, one launch (start us, length us, event | category | flops | bytes accessed | tf_op | source)
XLA Modules:
  0.0 112.0 jit_solution(16740082260453208350)
XLA Ops:
  0.7 1.3 %broadcast_select_fusion = (bf16[24,3,512]{2,1,0:T(4,128)(2,1)S(1)}, bf16[24,3,512]{2,1,0:T(4,128)(2,1)S(1)}) fusion(pred[]{:T(512)S(6)} %eq.6, bf16[24,8,512]{2,1,0:T(8,128)(2,1)} %param.8), kind=kLoop, calls=%fused_computation.17 | loop fusion | flops 73728 | bytes 294913 | tf_op jit(solution)/shard_map/jit(_where)/select_n | solution.py:345
  2.0 5.9 %collective-permute-start = (bf16[24,3,512]{2,1,0:T(4,128)(2,1)S(1)}, bf16[24,3,512]{2,1,0:T(4,128)(2,1)S(1)}, u32[]{:S(2)}, u32[]{:S(2)}) collective-permute-start(bf16[24,3,512]{2,1,0:T(4,128)(2,1)S(1)} %get-tuple-element.141), channel_id=1, source_target_pairs={{1,2},{2,1},{3,4},{4,3},{5,6},{6,5},{7,8},{8,7},{9,10},{10,9},{11,... | collective-permute-start | bytes 221192 | tf_op jit(solution)/shard_map/ppermute | solution.py:323
  8.8 2.0 %shard_map.127 = (f32[3,64,256]{2,1,0:T(8,128)S(1)}, bf16[512,512]{1,0:T(8,128)(2,1)S(1)}, bf16[512,512]{1,0:T(8,128)(2,1)S(1)}, bf16[512,512]{1,0:T(8,128)(2,1)S(1)}) custom-call(s32[3]{0:T(128)S(1)} %pad_add_fusion.coord, s32[3,49]{1,0:T(4,128)S(1)} %bitcast.35), custom_call_target="tpu_custom_call" | custom-call | flops 402653184 | bytes 4000000 | tf_op jit(solution)/shard_map/pallas_call | solution.py:347
  12.3 4.3 %collective-permute-start.3 = (bf16[3,16,512]{2,1,0:T(8,128)(2,1)S(1)}, bf16[3,16,512]{2,1,0:T(8,128)(2,1)S(1)}, u32[]{:S(2)}, u32[]{:S(2)}) collective-permute-start(bf16[3,16,512]{2,1,0:T(8,128)(2,1)S(1)} %get-tuple-element.136), channel_id=1, source_target_pairs={{0,32},{1,33},{2,34},{3,35},{4,36},{5,37},{6,38},{7,39},{8,40},{9,... | collective-permute-start | bytes 147464 | tf_op jit(solution)/shard_map/ppermute | solution.py:323
  17.4 1.2 %collective-permute-done.3.rim_b = bf16[3,16,512]{2,1,0:T(8,128)(2,1)S(1)} collective-permute-done((bf16[3,16,512]{2,1,0:T(8,128)(2,1)S(1)}, bf16[3,16,512]{2,1,0:T(8,128)(2,1)S(1)}, u32[]{:S(2)}, u32[]{:S(2)}) %collective-permute-start.3) | collective-permute-done | bytes 49184 | tf_op jit(solution)/shard_map/ppermute | solution.py:323
  18.7 7.8 %shard_map.129 = (bf16[16,5,16,512]{3,2,1,0:T(8,128)(2,1)S(1)}, bf16[16,5,16,512]{3,2,1,0:T(8,128)(2,1)S(1)}, bf16[4,4,2,32,512]{4,3,2,1,0:T(8,128)(2,1)S(1)}, b...) custom-call(s32[3]{0:T(128)S(1)} %pad_add_fusion.coord, ...), custom_call_target="tpu_custom_call" | custom-call | flops 5000000000 | bytes 20000000 | tf_op jit(solution)/shard_map/pallas_call | solution.py:360
  27.1 5.3 %shard_map.130 = (bf16[49,16,512]{2,1,0:T(8,128)(2,1)S(1)}, bf16[49,16,512]{2,1,0:T(8,128)(2,1)S(1)}, f32[512,512]{1,0:T(8,128)S(1)}, f32[192,512]{1,0:T(8,128)S(1)}) custom-call(s32[3]{0:T(128)S(1)} %pad_add_fusion.coord, bf16[192,512]{1,0:T(8,128)(2,1)S(1)} %get-tuple-element.76.gm, bf16[512,512]{1,0:T(8,128)(2,1)S(1)} %copy-done.6, ...), custom_call_target="tpu_custom_call" | custom-call | flops 3000000000 | bytes 12000000 | tf_op jit(solution)/shard_map/pallas_call | solution.py:372
  32.7 1.0 shard_map.132
  33.7 0.9 shard_map.131
  37.1 3.9 %collective-permute-start.7 = (bf16[30,3,512]{2,1,0:T(4,128)(2,1)}, bf16[30,3,512]{2,1,0:T(4,128)(2,1)}, u32[]{:S(2)}, u32[]{:S(2)}) collective-permute-start(bf16[30,3,512]{2,1,0:T(4,128)(2,1)} %get-tuple-element.134), channel_id=1, source_target_pairs={{1,2},{2,1},{3,4},{4,3},{5,6},{6,5},{7,8},{8,7},{9,10},{10,9},{11,... | collective-permute-start | bytes 276488 | tf_op jit(solution)/shard_map/ppermute | solution.py:323
  41.3 3.1 %collective-permute-start.15 = (bf16[16,16,512]{2,1,0:T(8,128)(2,1)S(1)}, bf16[16,16,512]{2,1,0:T(8,128)(2,1)S(1)}, u32[]{:S(2)}, u32[]{:S(2)}) collective-permute-start(bf16[16,16,512]{2,1,0:T(8,128)(2,1)S(1)} %get-tuple-element.108), channel_id=1, source_target_pairs={{0,24},{1,25},{2,26},{3,27},{4,28},{5,29},{6,30},{7,31},{8,16},{9,... | collective-permute-start | bytes 786440 | tf_op jit(solution)/shard_map/ppermute | solution.py:323
  44.4 0.9 collective-permute-start.16
  45.3 1.1 collective-permute-done.7
  46.4 2.0 %collective-permute-start.11 = (bf16[20,16,512]{2,1,0:T(8,128)(2,1)}, bf16[20,16,512]{2,1,0:T(8,128)(2,1)S(1)}, u32[]{:S(2)}, u32[]{:S(2)}) collective-permute-start(bf16[20,16,512]{2,1,0:T(8,128)(2,1)} %get-tuple-element.102), channel_id=1, source_target_pairs={{0,32},{1,33},{2,34},{3,35},{4,36},{5,37},{6,38},{7,39},{8,40},{9,... | collective-permute-start | bytes 983048 | tf_op jit(solution)/shard_map/ppermute | solution.py:323
  48.4 0.9 convert_element_type.43
  49.4 6.2 %collective-permute-start.12 = (bf16[20,16,512]{2,1,0:T(8,128)(2,1)S(1)}, bf16[20,16,512]{2,1,0:T(8,128)(2,1)S(1)}, u32[]{:S(2)}, u32[]{:S(2)}) collective-permute-start(bf16[20,16,512]{2,1,0:T(8,128)(2,1)S(1)} %get-tuple-element.103), channel_id=1, source_target_pairs={{0,96},{1,97},{2,98},{3,99},{4,100},{5,101},{6,102},{7,103},{8,104... | collective-permute-start | bytes 983048 | tf_op jit(solution)/shard_map/ppermute | solution.py:323
  55.6 2.0 %fusion.12 = (bf16[30,8,512]{2,1,0:T(8,128)(2,1)S(1)}, f32[30,8,512]{2,1,0:T(8,128)}) fusion(f32[30,3,512]{2,1,0:T(4,128)S(1)} %convert_element_type.44, pred[]{:T(512)S(6)} %not.6, f32[30,3,512]{2,1,0:T(4,128)S(1)} %convert_element_type.43, pred[]{:T(512)S(6)} %eq.6, f32[30,16,512]{2,1,0:T(8,128)} %bitcast.37), kind=kLoop, calls=%fused_computation.27 | loop fusion | flops 614400 | bytes 1597442 | tf_op jit(solution)/shard_map/convert.2
  57.6 1.5 %collective-permute-start.13 = (bf16[20,16,512]{2,1,0:T(8,128)(2,1)S(1)}, bf16[20,16,512]{2,1,0:T(8,128)(2,1)S(1)}, u32[]{:S(2)}, u32[]{:S(2)}) collective-permute-start(bf16[20,16,512]{2,1,0:T(8,128)(2,1)S(1)} %get-tuple-element.104), channel_id=1, source_target_pairs={{0,64},{1,65},{2,66},{3,67},{4,68},{5,69},{6,70},{7,71},{8,72},{9,... | collective-permute-start | bytes 983048 | tf_op jit(solution)/shard_map/ppermute | solution.py:323
  59.1 2.8 %collective-permute-start.24 = (bf16[13,16,512]{2,1,0:T(8,128)(2,1)S(1)}, bf16[13,16,512]{2,1,0:T(8,128)(2,1)S(1)}, u32[]{:S(2)}, u32[]{:S(2)}) collective-permute-start(bf16[13,16,512]{2,1,0:T(8,128)(2,1)S(1)} %copy-done.8), channel_id=1, source_target_pairs={{0,24},{1,25},{2,26},{3,27},{4,28},{5,29},{6,30},{7,31},{8,16},{9,... | collective-permute-start | bytes 638984 | tf_op jit(solution)/shard_map/ppermute | solution.py:323
  62.6 5.2 %collective-permute-done.12.refs_2_ = bf16[20,16,512]{2,1,0:T(8,128)(2,1)S(1)} collective-permute-done((bf16[20,16,512]{2,1,0:T(8,128)(2,1)S(1)}, bf16[20,16,512]{2,1,0:T(8,128)(2,1)S(1)}, u32[]{:S(2)}, u32[]{:S(2)}) %collective-permute-start.12) | collective-permute-done | bytes 327712 | tf_op jit(solution)/shard_map/ppermute | solution.py:323
  67.8 2.1 %collective-permute-start.10 = (bf16[3,8,512]{2,1,0:T(8,128)(2,1)S(1)}, bf16[3,8,512]{2,1,0:T(8,128)(2,1)S(1)}, u32[]{:S(2)}, u32[]{:S(2)}) collective-permute-start(bf16[3,8,512]{2,1,0:T(8,128)(2,1)S(1)} %get-tuple-element.139), channel_id=1, source_target_pairs={{0,32},{1,33},{2,34},{3,35},{4,36},{5,37},{6,38},{7,39},{8,40},{9,... | collective-permute-start | bytes 73736 | tf_op jit(solution)/shard_map/ppermute | solution.py:323
  70.2 2.9 %collective-permute-start.25 = (bf16[13,16,512]{2,1,0:T(8,128)(2,1)}, bf16[13,16,512]{2,1,0:T(8,128)(2,1)S(1)}, u32[]{:S(2)}, u32[]{:S(2)}) collective-permute-start(bf16[13,16,512]{2,1,0:T(8,128)(2,1)} %get-tuple-element.122), channel_id=1, source_target_pairs={{0,16},{1,17},{2,18},{3,19},{4,20},{5,21},{6,22},{7,23},{8,24},{9,... | collective-permute-start | bytes 638984 | tf_op jit(solution)/shard_map/ppermute | solution.py:323
  73.4 6.9 %collective-permute-start.21 = (bf16[4,16,512]{2,1,0:T(8,128)(2,1)S(1)}, bf16[4,16,512]{2,1,0:T(8,128)(2,1)S(1)}, u32[]{:S(2)}, u32[]{:S(2)}) collective-permute-start(bf16[4,16,512]{2,1,0:T(8,128)(2,1)S(1)} %get-tuple-element.117), channel_id=1, source_target_pairs={{0,96},{1,97},{2,98},{3,99},{4,100},{5,101},{6,102},{7,103},{8,104... | collective-permute-start | bytes 196616 | tf_op jit(solution)/shard_map/ppermute | solution.py:323
  81.0 2.1 %collective-permute-start.17 = (bf16[5,16,512]{2,1,0:T(8,128)(2,1)S(1)}, bf16[5,16,512]{2,1,0:T(8,128)(2,1)S(1)}, u32[]{:S(2)}, u32[]{:S(2)}) collective-permute-start(bf16[5,16,512]{2,1,0:T(8,128)(2,1)S(1)} %get-tuple-element.112), channel_id=1, source_target_pairs={{0,8},{1,9},{2,10},{3,11},{4,12},{5,13},{6,14},{7,15},{8,0},{9,1},... | collective-permute-start | bytes 245768 | tf_op jit(solution)/shard_map/ppermute | solution.py:323
  84.1 1.4 %collective-permute-start.19 = (bf16[5,16,512]{2,1,0:T(8,128)(2,1)S(1)}, bf16[5,16,512]{2,1,0:T(8,128)(2,1)S(1)}, u32[]{:S(2)}, u32[]{:S(2)}) collective-permute-start(bf16[5,16,512]{2,1,0:T(8,128)(2,1)S(1)} %get-tuple-element.114), channel_id=1, source_target_pairs={{0,16},{1,17},{2,18},{3,19},{4,20},{5,21},{6,22},{7,23},{8,24},{9,... | collective-permute-start | bytes 245768 | tf_op jit(solution)/shard_map/ppermute | solution.py:323
  86.0 4.7 %collective-permute-start.27 = (bf16[4,16,512]{2,1,0:T(8,128)(2,1)S(1)}, bf16[4,16,512]{2,1,0:T(8,128)(2,1)S(1)}, u32[]{:S(2)}, u32[]{:S(2)}) collective-permute-start(bf16[4,16,512]{2,1,0:T(8,128)(2,1)S(1)} %get-tuple-element.125), channel_id=1, source_target_pairs={{0,96},{1,97},{2,98},{3,99},{4,100},{5,101},{6,102},{7,103},{8,104... | collective-permute-start | bytes 196616 | tf_op jit(solution)/shard_map/ppermute | solution.py:323
  90.7 1.2 %fusion.3 = f32[24,8]{1,0:T(8,128)S(1)} fusion(bf16[24,8,512]{2,1,0:T(8,128)(2,1)S(1)} %copy-done, f32[24,8]{1,0:T(8,128)S(1)} %add_rsqrt_fusion, f32[512]{0:T(512)S(1)} %bitcast.38, f32[192,512]{1,0:T(8,128)S(1)} %get-tuple-element.99, f32[3,8,512]{2,1,0:T(8,128)S(1)} %convert_element_type.46, pred[]{:T(512)S(6)} %not.7, ...), kind=kLoop, calls=%fused_computation.6 | loop fusion | flops 982848 | bytes 1084930 | tf_op jit(solution)/shard_map/reduce_sum | solution.py:429
  92.0 1.3 %collective-permute-done.27.refs_10_ = bf16[4,16,512]{2,1,0:T(8,128)(2,1)S(1)} collective-permute-done((bf16[4,16,512]{2,1,0:T(8,128)(2,1)S(1)}, bf16[4,16,512]{2,1,0:T(8,128)(2,1)S(1)}, u32[]{:S(2)}, u32[]{:S(2)}) %collective-permute-start.27) | collective-permute-done | bytes 65568 | tf_op jit(solution)/shard_map/ppermute | solution.py:323
  93.3 3.3 %collective-permute-done.28.refs_11_ = bf16[4,16,512]{2,1,0:T(8,128)(2,1)S(1)} collective-permute-done((bf16[4,16,512]{2,1,0:T(8,128)(2,1)S(1)}, bf16[4,16,512]{2,1,0:T(8,128)(2,1)S(1)}, u32[]{:S(2)}, u32[]{:S(2)}) %collective-permute-start.28) | collective-permute-done | bytes 65568 | tf_op jit(solution)/shard_map/ppermute | solution.py:323
  96.5 1.0 shard_map.137
  97.5 3.4 %all-to-all-start = ((bf16[8,32,512]{2,1,0:T(8,128)(2,1)}), bf16[8,32,512]{2,1,0:T(8,128)(2,1)S(1)}, u32[]{:S(2)}, u32[]{:S(2)}) async-start(bf16[8,32,512]{2,1,0:T(8,128)(2,1)} %shard_map.137), calls=%async_computation | async-start | bytes 524288 | tf_op jit(solution)/shard_map/all_to_all | solution.py:331
  101.9 9.5 %all-to-all-done.got = bf16[8,32,512]{2,1,0:T(8,128)(2,1)S(1)} async-done(((bf16[8,32,512]{2,1,0:T(8,128)(2,1)}), bf16[8,32,512]{2,1,0:T(8,128)(2,1)S(1)}, u32[]{:S(2)}, u32[]{:S(2)}) %all-to-all-start) | async-done | bytes 262176 | tf_op jit(solution)/shard_map/all_to_all | solution.py:331
  (88 shorter events, 11.8 us)
Async XLA Ops:
  0.6 15.9 %copy-start.2 = (bf16[24,8,512]{2,1,0:T(8,128)(2,1)S(1)}, bf16[24,8,512]{2,1,0:T(8,128)(2,1)}, u32[]{:S(2)}) copy-start(bf16[24,8,512]{2,1,0:T(8,128)(2,1)} %param.9) | copy-start | bytes 589828
  2.0 9.4 %collective-permute-start = (bf16[24,3,512]{2,1,0:T(4,128)(2,1)S(1)}, bf16[24,3,512]{2,1,0:T(4,128)(2,1)S(1)}, u32[]{:S(2)}, u32[]{:S(2)}) collective-permute-start(bf16[24,3,512]{2,1,0:T(4,128)(2,1)S(1)} %get-tuple-element.141), channel_id=1, source_target_pairs={{1,2},{2,1},{3,4},{4,3},{5,6},{6,5},{7,8},{8,7},{9,10},{10,9},{11,... | collective-permute-start | bytes 221192 | tf_op jit(solution)/shard_map/ppermute | solution.py:323
  7.8 3.5 %collective-permute-start.1 = (bf16[24,3,512]{2,1,0:T(4,128)(2,1)S(1)}, bf16[24,3,512]{2,1,0:T(4,128)(2,1)S(1)}, u32[]{:S(2)}, u32[]{:S(2)}) collective-permute-start(bf16[24,3,512]{2,1,0:T(4,128)(2,1)S(1)} %get-tuple-element.140), channel_id=1, source_target_pairs={{0,1},{1,0},{2,3},{3,2},{4,5},{5,4},{6,7},{7,6},{8,9},{9,8},{10,11... | collective-permute-start | bytes 221192 | tf_op jit(solution)/shard_map/ppermute | solution.py:323
  11.6 5.9 %collective-permute-start.2 = (bf16[3,16,512]{2,1,0:T(8,128)(2,1)S(1)}, bf16[3,16,512]{2,1,0:T(8,128)(2,1)S(1)}, u32[]{:S(2)}, u32[]{:S(2)}) collective-permute-start(bf16[3,16,512]{2,1,0:T(8,128)(2,1)S(1)} %get-tuple-element.137), channel_id=1, source_target_pairs={{32,64},{33,65},{34,66},{35,67},{36,68},{37,69},{38,70},{39,71},{4... | collective-permute-start | bytes 147464 | tf_op jit(solution)/shard_map/ppermute | solution.py:323
  12.3 6.4 %collective-permute-start.3 = (bf16[3,16,512]{2,1,0:T(8,128)(2,1)S(1)}, bf16[3,16,512]{2,1,0:T(8,128)(2,1)S(1)}, u32[]{:S(2)}, u32[]{:S(2)}) collective-permute-start(bf16[3,16,512]{2,1,0:T(8,128)(2,1)S(1)} %get-tuple-element.136), channel_id=1, source_target_pairs={{0,32},{1,33},{2,34},{3,35},{4,36},{5,37},{6,38},{7,39},{8,40},{9,... | collective-permute-start | bytes 147464 | tf_op jit(solution)/shard_map/ppermute | solution.py:323
  26.5 5.9 %collective-permute-start.4 = (bf16[16,5,16,512]{3,2,1,0:T(8,128)(2,1)S(1)}, bf16[16,5,16,512]{3,2,1,0:T(8,128)(2,1)S(1)}, u32[]{:S(2)}, u32[]{:S(2)}) collective-permute-start(bf16[16,5,16,512]{3,2,1,0:T(8,128)(2,1)S(1)} %get-tuple-element.85), channel_id=1, source_target_pairs={{0,1},{1,0},{2,3},{3,2},{4,5},{5,4},{6,7},{7,6},{8,9},{9,8},{10,11... | collective-permute-start | bytes 3932168 | tf_op jit(solution)/shard_map/ppermute | solution.py:323
  26.6 5.8 %collective-permute-start.5 = (bf16[4,4,2,32,512]{4,3,2,1,0:T(8,128)(2,1)S(1)}, bf16[4,4,2,32,512]{4,3,2,1,0:T(8,128)(2,1)S(1)}, u32[]{:S(2)}, u32[]{:S(2)}) collective-permute-start(bf16[4,4,2,32,512]{4,3,2,1,0:T(8,128)(2,1)S(1)} %get-tuple-element.86), channel_id=1, source_target_pairs={{0,1},{1,0},{2,3},{3,2},{4,5},{5,4},{6,7},{7,6},{8,9},{9,8},{10,11... | collective-permute-start | bytes 3145736 | tf_op jit(solution)/shard_map/ppermute | solution.py:323
  32.4 2.4 %collective-permute-start.6 = (bf16[49,16,512]{2,1,0:T(8,128)(2,1)S(1)}, bf16[49,16,512]{2,1,0:T(8,128)(2,1)S(1)}, u32[]{:S(2)}, u32[]{:S(2)}) collective-permute-start(bf16[49,16,512]{2,1,0:T(8,128)(2,1)S(1)} %get-tuple-element.88), channel_id=1, source_target_pairs={{0,1},{1,0},{2,3},{3,2},{4,5},{5,4},{6,7},{7,6},{8,9},{9,8},{10,11... | collective-permute-start | bytes 2408456 | tf_op jit(solution)/shard_map/ppermute | solution.py:323
  37.1 9.3 %collective-permute-start.7 = (bf16[30,3,512]{2,1,0:T(4,128)(2,1)}, bf16[30,3,512]{2,1,0:T(4,128)(2,1)}, u32[]{:S(2)}, u32[]{:S(2)}) collective-permute-start(bf16[30,3,512]{2,1,0:T(4,128)(2,1)} %get-tuple-element.134), channel_id=1, source_target_pairs={{1,2},{2,1},{3,4},{4,3},{5,6},{6,5},{7,8},{8,7},{9,10},{10,9},{11,... | collective-permute-start | bytes 276488 | tf_op jit(solution)/shard_map/ppermute | solution.py:323
  41.1 8.3 %collective-permute-start.8 = (bf16[30,3,512]{2,1,0:T(4,128)(2,1)}, bf16[30,3,512]{2,1,0:T(4,128)(2,1)S(1)}, u32[]{:S(2)}, u32[]{:S(2)}) collective-permute-start(bf16[30,3,512]{2,1,0:T(4,128)(2,1)} %get-tuple-element.135), channel_id=1, source_target_pairs={{0,1},{1,0},{2,3},{3,2},{4,5},{5,4},{6,7},{7,6},{8,9},{9,8},{10,11... | collective-permute-start | bytes 276488 | tf_op jit(solution)/shard_map/ppermute | solution.py:323
  41.2 16.5 %collective-permute-start.14 = (bf16[16,16,512]{2,1,0:T(8,128)(2,1)}, bf16[16,16,512]{2,1,0:T(8,128)(2,1)S(1)}, u32[]{:S(2)}, u32[]{:S(2)}) collective-permute-start(bf16[16,16,512]{2,1,0:T(8,128)(2,1)} %get-tuple-element.107), channel_id=1, source_target_pairs={{0,8},{1,9},{2,10},{3,11},{4,12},{5,13},{6,14},{7,15},{8,0},{9,1},... | collective-permute-start | bytes 786440 | tf_op jit(solution)/shard_map/ppermute | solution.py:323
  41.3 17.8 %collective-permute-start.15 = (bf16[16,16,512]{2,1,0:T(8,128)(2,1)S(1)}, bf16[16,16,512]{2,1,0:T(8,128)(2,1)S(1)}, u32[]{:S(2)}, u32[]{:S(2)}) collective-permute-start(bf16[16,16,512]{2,1,0:T(8,128)(2,1)S(1)} %get-tuple-element.108), channel_id=1, source_target_pairs={{0,24},{1,25},{2,26},{3,27},{4,28},{5,29},{6,30},{7,31},{8,16},{9,... | collective-permute-start | bytes 786440 | tf_op jit(solution)/shard_map/ppermute | solution.py:323
  44.4 14.7 %collective-permute-start.16 = (bf16[16,16,512]{2,1,0:T(8,128)(2,1)}, bf16[16,16,512]{2,1,0:T(8,128)(2,1)S(1)}, u32[]{:S(2)}, u32[]{:S(2)}) collective-permute-start(bf16[16,16,512]{2,1,0:T(8,128)(2,1)} %get-tuple-element.109), channel_id=1, source_target_pairs={{0,16},{1,17},{2,18},{3,19},{4,20},{5,21},{6,22},{7,23},{8,24},{9,... | collective-permute-start | bytes 786440 | tf_op jit(solution)/shard_map/ppermute | solution.py:323
  46.4 15.6 %collective-permute-start.11 = (bf16[20,16,512]{2,1,0:T(8,128)(2,1)}, bf16[20,16,512]{2,1,0:T(8,128)(2,1)S(1)}, u32[]{:S(2)}, u32[]{:S(2)}) collective-permute-start(bf16[20,16,512]{2,1,0:T(8,128)(2,1)} %get-tuple-element.102), channel_id=1, source_target_pairs={{0,32},{1,33},{2,34},{3,35},{4,36},{5,37},{6,38},{7,39},{8,40},{9,... | collective-permute-start | bytes 983048 | tf_op jit(solution)/shard_map/ppermute | solution.py:323
  49.4 18.5 %collective-permute-start.12 = (bf16[20,16,512]{2,1,0:T(8,128)(2,1)S(1)}, bf16[20,16,512]{2,1,0:T(8,128)(2,1)S(1)}, u32[]{:S(2)}, u32[]{:S(2)}) collective-permute-start(bf16[20,16,512]{2,1,0:T(8,128)(2,1)S(1)} %get-tuple-element.103), channel_id=1, source_target_pairs={{0,96},{1,97},{2,98},{3,99},{4,100},{5,101},{6,102},{7,103},{8,104... | collective-permute-start | bytes 983048 | tf_op jit(solution)/shard_map/ppermute | solution.py:323
  57.6 12.6 %collective-permute-start.13 = (bf16[20,16,512]{2,1,0:T(8,128)(2,1)S(1)}, bf16[20,16,512]{2,1,0:T(8,128)(2,1)S(1)}, u32[]{:S(2)}, u32[]{:S(2)}) collective-permute-start(bf16[20,16,512]{2,1,0:T(8,128)(2,1)S(1)} %get-tuple-element.104), channel_id=1, source_target_pairs={{0,64},{1,65},{2,66},{3,67},{4,68},{5,69},{6,70},{7,71},{8,72},{9,... | collective-permute-start | bytes 983048 | tf_op jit(solution)/shard_map/ppermute | solution.py:323
  59.1 21.2 %collective-permute-start.23 = (bf16[13,16,512]{2,1,0:T(8,128)(2,1)S(1)}, bf16[13,16,512]{2,1,0:T(8,128)(2,1)S(1)}, u32[]{:S(2)}, u32[]{:S(2)}) collective-permute-start(bf16[13,16,512]{2,1,0:T(8,128)(2,1)S(1)} %copy-done.10), channel_id=1, source_target_pairs={{0,8},{1,9},{2,10},{3,11},{4,12},{5,13},{6,14},{7,15},{8,0},{9,1},... | collective-permute-start | bytes 638984 | tf_op jit(solution)/shard_map/ppermute | solution.py:323
  59.1 21.9 %collective-permute-start.24 = (bf16[13,16,512]{2,1,0:T(8,128)(2,1)S(1)}, bf16[13,16,512]{2,1,0:T(8,128)(2,1)S(1)}, u32[]{:S(2)}, u32[]{:S(2)}) collective-permute-start(bf16[13,16,512]{2,1,0:T(8,128)(2,1)S(1)} %copy-done.8), channel_id=1, source_target_pairs={{0,24},{1,25},{2,26},{3,27},{4,28},{5,29},{6,30},{7,31},{8,16},{9,... | collective-permute-start | bytes 638984 | tf_op jit(solution)/shard_map/ppermute | solution.py:323
  62.0 11.3 %collective-permute-start.9 = (bf16[3,8,512]{2,1,0:T(8,128)(2,1)S(1)}, bf16[3,8,512]{2,1,0:T(8,128)(2,1)S(1)}, u32[]{:S(2)}, u32[]{:S(2)}) collective-permute-start(bf16[3,8,512]{2,1,0:T(8,128)(2,1)S(1)} %get-tuple-element.138), channel_id=1, source_target_pairs={{32,64},{33,65},{34,66},{35,67},{36,68},{37,69},{38,70},{39,71},{4... | collective-permute-start | bytes 73736 | tf_op jit(solution)/shard_map/ppermute | solution.py:323
  67.8 5.5 %collective-permute-start.10 = (bf16[3,8,512]{2,1,0:T(8,128)(2,1)S(1)}, bf16[3,8,512]{2,1,0:T(8,128)(2,1)S(1)}, u32[]{:S(2)}, u32[]{:S(2)}) collective-permute-start(bf16[3,8,512]{2,1,0:T(8,128)(2,1)S(1)} %get-tuple-element.139), channel_id=1, source_target_pairs={{0,32},{1,33},{2,34},{3,35},{4,36},{5,37},{6,38},{7,39},{8,40},{9,... | collective-permute-start | bytes 73736 | tf_op jit(solution)/shard_map/ppermute | solution.py:323
  70.2 13.0 %collective-permute-start.25 = (bf16[13,16,512]{2,1,0:T(8,128)(2,1)}, bf16[13,16,512]{2,1,0:T(8,128)(2,1)S(1)}, u32[]{:S(2)}, u32[]{:S(2)}) collective-permute-start(bf16[13,16,512]{2,1,0:T(8,128)(2,1)} %get-tuple-element.122), channel_id=1, source_target_pairs={{0,16},{1,17},{2,18},{3,19},{4,20},{5,21},{6,22},{7,23},{8,24},{9,... | collective-permute-start | bytes 638984 | tf_op jit(solution)/shard_map/ppermute | solution.py:323
  73.3 10.8 %collective-permute-start.20 = (bf16[4,16,512]{2,1,0:T(8,128)(2,1)S(1)}, bf16[4,16,512]{2,1,0:T(8,128)(2,1)S(1)}, u32[]{:S(2)}, u32[]{:S(2)}) collective-permute-start(bf16[4,16,512]{2,1,0:T(8,128)(2,1)S(1)} %get-tuple-element.116), channel_id=1, source_target_pairs={{0,32},{1,33},{2,34},{3,35},{4,36},{5,37},{6,38},{7,39},{8,40},{9,... | collective-permute-start | bytes 196616 | tf_op jit(solution)/shard_map/ppermute | solution.py:323
  73.4 12.2 %collective-permute-start.21 = (bf16[4,16,512]{2,1,0:T(8,128)(2,1)S(1)}, bf16[4,16,512]{2,1,0:T(8,128)(2,1)S(1)}, u32[]{:S(2)}, u32[]{:S(2)}) collective-permute-start(bf16[4,16,512]{2,1,0:T(8,128)(2,1)S(1)} %get-tuple-element.117), channel_id=1, source_target_pairs={{0,96},{1,97},{2,98},{3,99},{4,100},{5,101},{6,102},{7,103},{8,104... | collective-permute-start | bytes 196616 | tf_op jit(solution)/shard_map/ppermute | solution.py:323
  80.3 5.8 %collective-permute-start.22 = (bf16[4,16,512]{2,1,0:T(8,128)(2,1)S(1)}, bf16[4,16,512]{2,1,0:T(8,128)(2,1)S(1)}, u32[]{:S(2)}, u32[]{:S(2)}) collective-permute-start(bf16[4,16,512]{2,1,0:T(8,128)(2,1)S(1)} %get-tuple-element.118), channel_id=1, source_target_pairs={{0,64},{1,65},{2,66},{3,67},{4,68},{5,69},{6,70},{7,71},{8,72},{9,... | collective-permute-start | bytes 196616 | tf_op jit(solution)/shard_map/ppermute | solution.py:323
  81.0 9.7 %collective-permute-start.17 = (bf16[5,16,512]{2,1,0:T(8,128)(2,1)S(1)}, bf16[5,16,512]{2,1,0:T(8,128)(2,1)S(1)}, u32[]{:S(2)}, u32[]{:S(2)}) collective-permute-start(bf16[5,16,512]{2,1,0:T(8,128)(2,1)S(1)} %get-tuple-element.112), channel_id=1, source_target_pairs={{0,8},{1,9},{2,10},{3,11},{4,12},{5,13},{6,14},{7,15},{8,0},{9,1},... | collective-permute-start | bytes 245768 | tf_op jit(solution)/shard_map/ppermute | solution.py:323
  83.2 8.8 %collective-permute-start.18 = (bf16[5,16,512]{2,1,0:T(8,128)(2,1)S(1)}, bf16[5,16,512]{2,1,0:T(8,128)(2,1)S(1)}, u32[]{:S(2)}, u32[]{:S(2)}) collective-permute-start(bf16[5,16,512]{2,1,0:T(8,128)(2,1)S(1)} %get-tuple-element.113), channel_id=1, source_target_pairs={{0,24},{1,25},{2,26},{3,27},{4,28},{5,29},{6,30},{7,31},{8,16},{9,... | collective-permute-start | bytes 245768 | tf_op jit(solution)/shard_map/ppermute | solution.py:323
  84.1 16.9 %copy-start.12 = (f32[30,8,512]{2,1,0:T(8,128)S(1)}, f32[30,8,512]{2,1,0:T(8,128)}, u32[]{:S(2)}) copy-start(f32[30,8,512]{2,1,0:T(8,128)} %get-tuple-element.133) | copy-start | bytes 1474564
  84.1 7.8 %collective-permute-start.19 = (bf16[5,16,512]{2,1,0:T(8,128)(2,1)S(1)}, bf16[5,16,512]{2,1,0:T(8,128)(2,1)S(1)}, u32[]{:S(2)}, u32[]{:S(2)}) collective-permute-start(bf16[5,16,512]{2,1,0:T(8,128)(2,1)S(1)} %get-tuple-element.114), channel_id=1, source_target_pairs={{0,16},{1,17},{2,18},{3,19},{4,20},{5,21},{6,22},{7,23},{8,24},{9,... | collective-permute-start | bytes 245768 | tf_op jit(solution)/shard_map/ppermute | solution.py:323
  85.6 6.4 %collective-permute-start.26 = (bf16[4,16,512]{2,1,0:T(8,128)(2,1)S(1)}, bf16[4,16,512]{2,1,0:T(8,128)(2,1)S(1)}, u32[]{:S(2)}, u32[]{:S(2)}) collective-permute-start(bf16[4,16,512]{2,1,0:T(8,128)(2,1)S(1)} %get-tuple-element.124), channel_id=1, source_target_pairs={{0,32},{1,33},{2,34},{3,35},{4,36},{5,37},{6,38},{7,39},{8,40},{9,... | collective-permute-start | bytes 196616 | tf_op jit(solution)/shard_map/ppermute | solution.py:323
  86.0 7.2 %collective-permute-start.27 = (bf16[4,16,512]{2,1,0:T(8,128)(2,1)S(1)}, bf16[4,16,512]{2,1,0:T(8,128)(2,1)S(1)}, u32[]{:S(2)}, u32[]{:S(2)}) collective-permute-start(bf16[4,16,512]{2,1,0:T(8,128)(2,1)S(1)} %get-tuple-element.125), channel_id=1, source_target_pairs={{0,96},{1,97},{2,98},{3,99},{4,100},{5,101},{6,102},{7,103},{8,104... | collective-permute-start | bytes 196616 | tf_op jit(solution)/shard_map/ppermute | solution.py:323
  90.7 5.8 %collective-permute-start.28 = (bf16[4,16,512]{2,1,0:T(8,128)(2,1)S(1)}, bf16[4,16,512]{2,1,0:T(8,128)(2,1)S(1)}, u32[]{:S(2)}, u32[]{:S(2)}) collective-permute-start(bf16[4,16,512]{2,1,0:T(8,128)(2,1)S(1)} %get-tuple-element.126), channel_id=1, source_target_pairs={{0,64},{1,65},{2,66},{3,67},{4,68},{5,69},{6,70},{7,71},{8,72},{9,... | collective-permute-start | bytes 196616 | tf_op jit(solution)/shard_map/ppermute | solution.py:323
  97.5 13.8 %all-to-all-start = ((bf16[8,32,512]{2,1,0:T(8,128)(2,1)}), bf16[8,32,512]{2,1,0:T(8,128)(2,1)S(1)}, u32[]{:S(2)}, u32[]{:S(2)}) async-start(bf16[8,32,512]{2,1,0:T(8,128)(2,1)} %shard_map.137), calls=%async_computation | async-start | bytes 524288 | tf_op jit(solution)/shard_map/all_to_all | solution.py:331
  (11 other events, 91.0 us)

commit v5 on v4

--- a/solution.py
+++ b/solution.py
@@ -100,7 +100,7 @@
     core_z = ((p >> 3) & 1) * 128 + ((p >> 1) & 3) * 2 + (p >> 8)
     hi, lo = (p >> 6) & 3, (p >> 4) & 3
     here = me & 121
-    pt_u[...] = jnp.where(lane == ((core_z + hi * 32 + lo * 8) ^ here) * 2 + (p & 1), 1.0, 0.0).astype(BF16)
+    pt_u[...] = jnp.where(lane == ((core_z + hi * 32 + lo * 8) ^ (me & 1)) * 2 + (p & 1), 1.0, 0.0).astype(BF16)
     pt_k[...] = jnp.where(lane == ((core_z + hi * 8 + lo * 32) ^ here) * 2 + (p & 1), 1.0, 0.0).astype(BF16)
     k_d = (((p >> 5) & 1) * 32 + ((p >> 6) & 3) * 8 + ((p >> 3) & 3) * 2 + (p >> 8)) ^ (me & 57)
     pt_d[...] = jnp.where(lane == k_d * 8 + (p & 7), 1.0, 0.0).astype(BF16)
@@ -226,37 +226,34 @@
     return ((a + b) + (c + d)).astype(BF16)
 
 
-def join_pair_kernel(keep, got, *outs):
-    n = keep.shape[0] // 4
+def join_pair_kernel(keep, got, out):
+    out[...] = add2(keep[...], got[...])
+
+
+def join_down_qkv_kernel(dk, dg, kk, kg, *outs):
+    gain = add2(kk[48], kg[48])
     for d in range(4):
-        outs[d][...] = add2(keep[d * n : (d + 1) * n], got[d * n : (d + 1) * n])
-
-
-def join_qkv_kernel(keep, got, *outs):
-    gain = add2(keep[48], got[48])
+        outs[d][:16] = add2(dk[d * 16 : (d + 1) * 16], dg[d * 16 : (d + 1) * 16])
+        outs[d][16:28] = add2(kk[d * 12 : (d + 1) * 12], kg[d * 12 : (d + 1) * 12])
+        outs[d][28] = gain
+
+
+def sum_up_kernel(got, out):
+    out[...] = add4([got[d] for d in range(4)])
+
+
+def sum_down_qkv_kernel(*refs):
+    parts, outs = refs[:4], refs[4:]
+    gain = add4([r[28] for r in parts])
     for d in range(4):
-        outs[d][:12] = add2(keep[d * 12 : (d + 1) * 12], got[d * 12 : (d + 1) * 12])
-        outs[d][12] = gain
-
-
-def join_four_kernel(*refs):
-    parts, outs = refs[:4], refs[4:]
-    n = outs[0].shape[0]
-    for d in range(4):
-        outs[d][...] = add4([r[d * n : (d + 1) * n] for r in parts])
-
-
-def join_four_qkv_kernel(*refs):
-    parts, outs = refs[:4], refs[4:]
-    gain = add4([r[12] for r in parts])
-    for d in range(4):
-        outs[d][:3] = add4([r[d * 3 : (d + 1) * 3] for r in parts])
-        outs[d][3] = gain
+        outs[d][:4] = add4([r[d * 4 : (d + 1) * 4] for r in parts])
+        outs[d][4:7] = add4([r[16 + d * 3 : 16 + (d + 1) * 3] for r in parts])
+        outs[d][7] = gain
 
 
 def reduce_xy_kernel(*refs):
-    out = refs[12]
-    sums = [add4([r[...] for r in refs[i : i + 4]]).reshape(-1, D) for i in (0, 4, 8)]
+    u_got, out = refs[0], refs[5]
+    sums = [add4([u_got[d] for d in range(4)]).reshape(-1, D), add4([r[...] for r in refs[1:5]]).reshape(-1, D)]
     acc = jnp.concatenate(sums, axis=0)
     rows = acc.shape[0]
     i = lax.broadcasted_iota(jnp.int32, (256, rows), 0)
@@ -316,6 +313,8 @@
 CORE_SWAP = [(k, k ^ 1) for k in range(256)]
 X_BIT = 32
 Y_BIT = 8
+X_GROUPS = [[zh * 128 + x * 32 + c for x in range(4)] for zh in range(2) for c in range(32)]
+Y_GROUPS = [[r * 32 + y * 8 + c for y in range(4)] for r in range(8) for c in range(8)]
 Z_GROUPS = [[zh * 128 + x * 32 + y * 8 + zl * 2 + c for zh in range(2) for zl in range(4)] for x in range(4) for y in range(4) for c in range(2)]
 
 
@@ -346,14 +345,14 @@
     side_a = send(jnp.where(col_odd, last, first), COL_A)
     bias, pt_u, pt_k, pt_d = call(
         prep_mask_kernel, [((TILES, QT, KT), F32), ((D, D), BF16), ((D, D), BF16), ((D, D), BF16)],
-        [], 2, 0, 2 * TOK * D * FF, 4_000_000, 16,
+        [], 2, 0, 2 * TOK * D * FF, 4_000_000, 8,
     )(coord, mask)
     side_a, side_b, cot, bias = lax.optimization_barrier((side_a, side_b, cot, bias))
     mid = jnp.concatenate([tokens, side_a, side_b, jnp.zeros((ROWS, EC - COLS - 2 * RIM, D), BF16)], axis=1)
     rim_b = send(jnp.where(row_odd, mid[:RIM], mid[ROWS - RIM :]), ROW_B)
     rim_a = send(jnp.where(row_odd, mid[ROWS - RIM :], mid[:RIM]), ROW_A)
     (gact,) = call(
-        prep_front_kernel, [((TOK, FF), F32)], [], 0, 2, 2 * TOK * D * FF, 4_000_000, 16,
+        prep_front_kernel, [((TOK, FF), F32)], [], 0, 2, 2 * TOK * D * FF, 4_000_000, 8,
     )(cot, w_down)
 
     half_u, half_d, half_k = ((16, 5, 16, D), BF16), ((4, 4, 2, 32, D), BF16), ((49, 16, D), BF16)
@@ -364,7 +363,7 @@
             ((TOK, D), BF16), ((TOK, D), BF16), ((EXT, 2 * D), BF16), ((6, 256, KT), F32),
             ((EXT, D), BF16), ((TOK, D), BF16), ((1, D), F32),
         ],
-        [pltpu.VMEM((ER, EC, D), BF16), pltpu.VMEM((TOK, D), BF16)], 1, 13, 5_000_000_000, 20_000_000, 30,
+        [pltpu.VMEM((ER, EC, D), BF16), pltpu.VMEM((TOK, D), BF16)], 1, 13, 5_000_000_000, 20_000_000, 24,
     )(coord, mid, rim_a, rim_b, tok, cot, gains, w_qkv, w_out, w_up, gact, bias, pt_u, pt_d)
 
     u_got = send(u_send, CORE_SWAP)
@@ -372,40 +371,9 @@
     k_keep, k_send, gne, gnq = call(
         backward_kernel,
         [half_k, half_k, ((EXT, D), F32), ((TOK, D), F32)],
-        [pltpu.VMEM((TOK, D), BF16), pltpu.VMEM((EXT, 2 * D), F32)], 1, 14, 3_000_000_000, 12_000_000, 30,
+        [pltpu.VMEM((TOK, D), BF16), pltpu.VMEM((EXT, 2 * D), F32)], 1, 14, 3_000_000_000, 12_000_000, 20,
     )(coord, gm, w_out, w_qkv, q, kv, prob, ne, no, mid, rim_a, rim_b, tok, gain_mid, pt_k)
     u_got, d_got, k_send = lax.optimization_barrier((u_got, d_got, k_send))
-
-    def join(body, ins, blocks):
-        outs = [((blocks, 16, D), BF16)] * 4
-        return list(call(body, outs, [], 0, len(ins), 1_000_000, 4_000_000, 12)(*ins))
-
-    k_got = send(k_send, CORE_SWAP)
-    u = join(join_pair_kernel, [u_keep.reshape(80, 16, D), u_got.reshape(80, 16, D)], 20)
-    d = join(join_pair_kernel, [d_keep.reshape(64, 16, D), d_got.reshape(64, 16, D)], 16)
-    u1 = to_three(u, X_BIT)
-    d1 = to_three(d, Y_BIT)
-    k_got, u[0], d[0] = lax.optimization_barrier((k_got, u[0], d[0]))
-    kc = join(join_qkv_kernel, [k_keep, k_got], 13)
-    kc[0], gne = lax.optimization_barrier((kc[0], gne))
-    k1 = to_three(kc, Y_BIT)
-    u1[0], d1[0] = u[0], d[0]
-    u = join(join_four_kernel, u1, 5)
-    d = join(join_four_kernel, d1, 4)
-    u2 = to_three(u, Y_BIT)
-    d2 = to_three(d, X_BIT)
-    k1[0], u2[0], d2[0] = lax.optimization_barrier((k1[0], u2[0], d2[0]))
-    kc = join(join_four_qkv_kernel, k1, 4)
-    k2 = to_three(kc, X_BIT)
-    (spread,) = call(
-        reduce_xy_kernel, [((8, 32, D), BF16)], [], 0, 12, 60_000_000, 4_000_000, 12,
-    )(*u2, *d2, *k2)
-    got_z = exchange(spread, Z_GROUPS)
-    g_up, g_down, g_out, g_qkv, g_gains = call(
-        reduce_z_kernel,
-        [((32, 128), F32), ((32, 128), F32), ((8, 128), F32), ((24, 128), F32), ((2, D), F32)],
-        [pltpu.VMEM((32, D), F32)], 0, 1, 1_000_000, 400_000, 8,
-    )(got_z)
 
     def place(x, axis, at_end, size):
         gap = size - RIM
@@ -419,6 +387,34 @@
     back_b = send(gne3[:, COLS + RIM : COLS + 2 * RIM].astype(BF16), COL_B)
     back_a = send(gne3[:, COLS : COLS + RIM].astype(BF16), COL_A)
     own = gne3[:, :COLS] + place(back_a, 1, col_odd, COLS) + place(back_b, 1, ~col_odd, COLS)
+
+    def join(body, ins, outs):
+        return list(call(body, [(o, BF16) for o in outs], [], 0, len(ins), 1_000_000, 4_000_000, 12)(*ins))
+
+    k_got = send(k_send, CORE_SWAP)
+    (u,) = join(join_pair_kernel, [u_keep.reshape(80, 16, D), u_got.reshape(80, 16, D)], [(80, 16, D)])
+    u, k_got = lax.optimization_barrier((u, k_got))
+    u_x = exchange(u.reshape(4, 20, 16, D), X_GROUPS)
+    b = join(
+        join_down_qkv_kernel, [d_keep.reshape(64, 16, D), d_got.reshape(64, 16, D), k_keep, k_got], [(29, 16, D)] * 4,
+    )
+    b = to_three(b, Y_BIT)
+    u_x, *b = lax.optimization_barrier((u_x, *b))
+    (u,) = join(sum_up_kernel, [u_x], [(20, 16, D)])
+    b = join(sum_down_qkv_kernel, b, [(8, 16, D)] * 4)
+    u, own, *b = lax.optimization_barrier((u, own, *b))
+    u_y = exchange(u.reshape(4, 5, 16, D), Y_GROUPS)
+    b = to_three(b, X_BIT)
+    (spread,) = call(
+        reduce_xy_kernel, [((8, 32, D), BF16)], [], 0, 5, 60_000_000, 4_000_000, 12,
+    )(u_y, *b)
+    got_z = exchange(spread, Z_GROUPS)
+    g_up, g_down, g_out, g_qkv, g_gains = call(
+        reduce_z_kernel,
+        [((32, 128), F32), ((32, 128), F32), ((8, 128), F32), ((24, 128), F32), ((2, D), F32)],
+        [pltpu.VMEM((32, D), F32)], 0, 1, 1_000_000, 400_000, 8,
+    )(got_z)
+
     head, tail = own[:RIM].astype(BF16), own[RIM + ROWS :].astype(BF16)
     up_b = send(jnp.where(row_odd, head, tail), ROW_B)
     up_a = send(jnp.where(row_odd, tail, head), ROW_A)

time: 113 us -> 115 us (1.018)
  waiting for transfers between devices: 22.6 us -> 34.6 us
  starting transfers between devices: 58.6 us -> 50.2 us
  other arithmetic: 6.8 us -> 3.77 us
  local copies, waits for them, and re-layouts: 2.27 us -> 4.64 us
    ppermute x29 -> x17, starting transfers between devices: 55.2 us -> 31.2 us  [send(): return lax.ppermute(x, AXES, perm)]
    all_to_all x1 -> x3, starting transfers between devices: 3.41 us -> 19 us  [exchange(): return lax.all_to_all(x, AXES, 0, 0, axis_index_groups=groups, tiled=True)]
    ppermute x29 -> x17, waiting for transfers between devices: 13.1 us -> 25.1 us  [send(): return lax.ppermute(x, AXES, perm)]
    another operation x2, other arithmetic: 2.08 us -> 0.1 us
    unnamed x27 -> x39, local copies, waits for them, and re-layouts: 1.35 us -> 3.06 us
    slice x1, local copies, waits for them, and re-layouts: 0.06 us -> 1.42 us  [per_device(): gne3 = gne.reshape(ER, EC, D)[:ROWS + 2 * RIM]]
    all_to_all x1 -> x3, waiting for transfers between devices: 9.48 us -> 9.5 us  [exchange(): return lax.all_to_all(x, AXES, 0, 0, axis_index_groups=groups, tiled=True)]
    pallas_call x7 -> x5, Pallas kernels: 4.14 us -> 4.15 us  [the longest x4 3.11 us: join(): call(body, [(o, BF16) for o in outs], [], 0, len(ins), 1000000, 4000000, 12)]
  transfers between devices with their start and end apart: 30 -> 20, of which waited for: 9 -> 9; matrix products, arithmetic and copies ran while one was open for 5% -> 4% of each run, Pallas kernels for 9% -> 9%
where the time goes in v5:
time: 115 us
  starting transfers between devices  50.2 us (44%)
  waiting for transfers between devices  34.6 us (30%)
  Pallas kernels  20.7 us (18%)
  local copies, waits for them, and re-layouts  4.64 us (4%)
  other arithmetic  3.77 us (3%)
    ppermute x17, starting transfers between devices, send(): return lax.ppermute(x, AXES, perm)  31.2 us
    ppermute x17, waiting for transfers between devices, send(): return lax.ppermute(x, AXES, perm)  25.1 us
    all_to_all x3, starting transfers between devices, exchange(): return lax.all_to_all(x, AXES, 0, 0, axis_index_groups=groups, tiled=True)  19 us
    all_to_all x3, waiting for transfers between devices, exchange(): return lax.all_to_all(x, AXES, 0, 0, axis_index_groups=groups, tiled=True)  9.5 us
    pallas_call x1, Pallas kernels, per_device(): call(forward_kernel, [half_u, half_u, half_d, half_d, ((TOK, D), BF16), (...  7.73 us
    pallas_call x1, Pallas kernels, per_device(): call(backward_kernel, [half_k, half_k, ((EXT, D), F32), ((TOK, D), F32)],...  5.3 us
    pallas_call x4, Pallas kernels, join(): call(body, [(o, BF16) for o in outs], [], 0, len(ins), 1000000, 4000000, 12)  3.11 us
    unnamed x39, local copies, waits for them, and re-layouts  3.06 us
  transfers between devices with their start and end apart: 20, of which 9 were waited for; matrix products, arithmetic and copies ran while one was open for 4% of the time, Pallas kernels for 9%

profile of v5, /device:TPU:8, one launch (start us, length us, event | category | flops | bytes accessed | tf_op | source)
XLA Modules:
  0.0 114.9 jit_solution(11253594419719980519)
XLA Ops:
  0.7 1.2 %broadcast_select_fusion = (bf16[24,3,512]{2,1,0:T(4,128)(2,1)S(1)}, bf16[24,3,512]{2,1,0:T(4,128)(2,1)S(1)}) fusion(pred[]{:T(512)S(6)} %eq.6, bf16[24,8,512]{2,1,0:T(8,128)(2,1)} %param.8), kind=kLoop, calls=%fused_computation.15 | loop fusion | flops 73728 | bytes 294913 | tf_op jit(solution)/shard_map/jit(_where)/select_n | solution.py:344
  1.8 5.9 %collective-permute-start = (bf16[24,3,512]{2,1,0:T(4,128)(2,1)S(1)}, bf16[24,3,512]{2,1,0:T(4,128)(2,1)S(1)}, u32[]{:S(2)}, u32[]{:S(2)}) collective-permute-start(bf16[24,3,512]{2,1,0:T(4,128)(2,1)S(1)} %get-tuple-element.117), channel_id=1, source_target_pairs={{1,2},{2,1},{3,4},{4,3},{5,6},{6,5},{7,8},{8,7},{9,10},{10,9},{11,... | collective-permute-start | bytes 221192 | tf_op jit(solution)/shard_map/ppermute | solution.py:322
  7.9 0.7 copy.16
  8.7 2.0 %shard_map.127 = (f32[3,64,256]{2,1,0:T(8,128)S(1)}, bf16[512,512]{1,0:T(8,128)(2,1)S(1)}, bf16[512,512]{1,0:T(8,128)(2,1)S(1)}, bf16[512,512]{1,0:T(8,128)(2,1)S(1)}) custom-call(s32[3]{0:T(128)S(1)} %pad_add_fusion.coord, s32[3,49]{1,0:T(4,128)S(1)} %bitcast.39), custom_call_target="tpu_custom_call" | custom-call | flops 402653184 | bytes 4000000 | tf_op jit(solution)/shard_map/pallas_call | solution.py:346
  12.2 4.3 %collective-permute-start.3 = (bf16[3,16,512]{2,1,0:T(8,128)(2,1)S(1)}, bf16[3,16,512]{2,1,0:T(8,128)(2,1)S(1)}, u32[]{:S(2)}, u32[]{:S(2)}) collective-permute-start(bf16[3,16,512]{2,1,0:T(8,128)(2,1)S(1)} %get-tuple-element.112), channel_id=1, source_target_pairs={{0,32},{1,33},{2,34},{3,35},{4,36},{5,37},{6,38},{7,39},{8,40},{9,... | collective-permute-start | bytes 147464 | tf_op jit(solution)/shard_map/ppermute | solution.py:322
  16.5 0.8 shard_map.128.gact
  17.3 1.2 %collective-permute-done.3.rim_b = bf16[3,16,512]{2,1,0:T(8,128)(2,1)S(1)} collective-permute-done((bf16[3,16,512]{2,1,0:T(8,128)(2,1)S(1)}, bf16[3,16,512]{2,1,0:T(8,128)(2,1)S(1)}, u32[]{:S(2)}, u32[]{:S(2)}) %collective-permute-start.3) | collective-permute-done | bytes 49184 | tf_op jit(solution)/shard_map/ppermute | solution.py:322
  18.6 7.7 %shard_map.129 = (bf16[16,5,16,512]{3,2,1,0:T(8,128)(2,1)S(1)}, bf16[16,5,16,512]{3,2,1,0:T(8,128)(2,1)S(1)}, bf16[4,4,2,32,512]{4,3,2,1,0:T(8,128)(2,1)S(1)}, b...) custom-call(s32[3]{0:T(128)S(1)} %pad_add_fusion.coord, ...), custom_call_target="tpu_custom_call" | custom-call | flops 5000000000 | bytes 20000000 | tf_op jit(solution)/shard_map/pallas_call | solution.py:359
  26.9 5.3 %shard_map.130 = (bf16[49,16,512]{2,1,0:T(8,128)(2,1)S(1)}, bf16[49,16,512]{2,1,0:T(8,128)(2,1)S(1)}, f32[512,512]{1,0:T(8,128)S(1)}, f32[192,512]{1,0:T(8,128)S(1)}) custom-call(s32[3]{0:T(128)S(1)} %pad_add_fusion.coord, bf16[192,512]{1,0:T(8,128)(2,1)S(1)} %get-tuple-element.65.gm, bf16[512,512]{1,0:T(8,128)(2,1)S(1)} %copy-done.17, ...), custom_call_target="tpu_custom_call" | custom-call | flops 3000000000 | bytes 12000000 | tf_op jit(solution)/shard_map/pallas_call | solution.py:371
  32.6 1.6 %shard_map.131 = bf16[80,16,512]{2,1,0:T(8,128)(2,1)} custom-call(bf16[80,16,512]{2,1,0:T(8,128)(2,1)S(1)} %bitcast.33, bf16[80,16,512]{2,1,0:T(8,128)(2,1)S(1)} %bitcast.34), custom_call_target="tpu_custom_call" | custom-call | flops 1000000 | bytes 4000000 | tf_op jit(solution)/shard_map/pallas_call | solution.py:392
  34.7 0.9 copy-done.7
  35.6 9.4 %all-to-all-start = ((bf16[4,20,16,512]{3,2,1,0:T(8,128)(2,1)}), bf16[4,20,16,512]{3,2,1,0:T(8,128)(2,1)S(1)}, u32[]{:S(2)}, u32[]{:S(2)}) async-start(bf16[4,20,16,512]{3,2,1,0:T(8,128)(2,1)} %bitcast.8), calls=%async_computation | async-start | bytes 2621440 | tf_op jit(solution)/shard_map/all_to_all | solution.py:330
  45.0 1.4 %slice.49 = f32[480,512]{1,0:T(8,128)S(1)} slice(f32[512,512]{1,0:T(8,128)} %copy-done.4), slice={[0:480], [0:512]} | slice | bytes 1966080 | tf_op jit(solution)/shard_map/slice | solution.py:386
  47.5 2.8 %collective-permute-start.8 = (bf16[29,16,512]{2,1,0:T(8,128)(2,1)S(1)}, bf16[29,16,512]{2,1,0:T(8,128)(2,1)S(1)}, u32[]{:S(2)}, u32[]{:S(2)}) collective-permute-start(bf16[29,16,512]{2,1,0:T(8,128)(2,1)S(1)} %get-tuple-element.86), channel_id=1, source_target_pairs={{0,24},{1,25},{2,26},{3,27},{4,28},{5,29},{6,30},{7,31},{8,16},{9,... | collective-permute-start | bytes 1425416 | tf_op jit(solution)/shard_map/ppermute | solution.py:322
  50.3 1.2 %collective-permute-start.9 = (bf16[29,16,512]{2,1,0:T(8,128)(2,1)S(1)}, bf16[29,16,512]{2,1,0:T(8,128)(2,1)S(1)}, u32[]{:S(2)}, u32[]{:S(2)}) collective-permute-start(bf16[29,16,512]{2,1,0:T(8,128)(2,1)S(1)} %get-tuple-element.87), channel_id=1, source_target_pairs={{0,16},{1,17},{2,18},{3,19},{4,20},{5,21},{6,22},{7,23},{8,24},{9,... | collective-permute-start | bytes 1425416 | tf_op jit(solution)/shard_map/ppermute | solution.py:322
  51.7 2.4 %collective-permute-start.10 = (bf16[30,3,512]{2,1,0:T(4,128)(2,1)S(1)}, bf16[30,3,512]{2,1,0:T(4,128)(2,1)S(1)}, u32[]{:S(2)}, u32[]{:S(2)}) collective-permute-start(bf16[30,3,512]{2,1,0:T(4,128)(2,1)S(1)} %get-tuple-element.110), channel_id=1, source_target_pairs={{1,2},{2,1},{3,4},{4,3},{5,6},{6,5},{7,8},{8,7},{9,10},{10,9},{11,... | collective-permute-start | bytes 276488 | tf_op jit(solution)/shard_map/ppermute | solution.py:322
  54.2 6.4 %collective-permute-done.10 = bf16[30,3,512]{2,1,0:T(4,128)(2,1)S(1)} collective-permute-done((bf16[30,3,512]{2,1,0:T(4,128)(2,1)S(1)}, bf16[30,3,512]{2,1,0:T(4,128)(2,1)S(1)}, u32[]{:S(2)}, u32[]{:S(2)}) %collective-permute-start.10) | collective-permute-done | bytes 92192 | tf_op jit(solution)/shard_map/ppermute | solution.py:322
  60.7 0.9 fusion
  61.7 0.9 collective-permute-done.7.refs_1_
  62.5 9.3 %collective-permute-done.8.refs_2_ = bf16[29,16,512]{2,1,0:T(8,128)(2,1)S(1)} collective-permute-done((bf16[29,16,512]{2,1,0:T(8,128)(2,1)S(1)}, bf16[29,16,512]{2,1,0:T(8,128)(2,1)S(1)}, u32[]{:S(2)}, u32[]{:S(2)}) %collective-permute-start.8) | collective-permute-done | bytes 475168 | tf_op jit(solution)/shard_map/ppermute | solution.py:322
  71.8 0.8 copy-done.9
  72.6 0.9 shard_map.133
  73.9 6.2 %all-to-all-start.1 = ((bf16[4,5,16,512]{3,2,1,0:T(8,128)(2,1)}), bf16[4,5,16,512]{3,2,1,0:T(8,128)(2,1)S(1)}, u32[]{:S(2)}, u32[]{:S(2)}) async-start(bf16[4,5,16,512]{3,2,1,0:T(8,128)(2,1)} %bitcast.14), calls=%async_computation.1 | async-start | bytes 655360 | tf_op jit(solution)/shard_map/all_to_all | solution.py:330
  80.2 0.8 collective-permute-start.12
  81.0 4.5 %collective-permute-start.13 = (bf16[3,8,512]{2,1,0:T(8,128)(2,1)S(1)}, bf16[3,8,512]{2,1,0:T(8,128)(2,1)S(1)}, u32[]{:S(2)}, u32[]{:S(2)}) collective-permute-start(bf16[3,8,512]{2,1,0:T(8,128)(2,1)S(1)} %get-tuple-element.115), channel_id=1, source_target_pairs={{0,32},{1,33},{2,34},{3,35},{4,36},{5,37},{6,38},{7,39},{8,40},{9,... | collective-permute-start | bytes 73736 | tf_op jit(solution)/shard_map/ppermute | solution.py:322
  85.7 7.2 %collective-permute-start.15 = (bf16[8,16,512]{2,1,0:T(8,128)(2,1)S(1)}, bf16[8,16,512]{2,1,0:T(8,128)(2,1)S(1)}, u32[]{:S(2)}, u32[]{:S(2)}) collective-permute-start(bf16[8,16,512]{2,1,0:T(8,128)(2,1)S(1)} %get-tuple-element.103), channel_id=1, source_target_pairs={{0,96},{1,97},{2,98},{3,99},{4,100},{5,101},{6,102},{7,103},{8,104... | collective-permute-start | bytes 393224 | tf_op jit(solution)/shard_map/ppermute | solution.py:322
  93.2 4.1 %collective-permute-done.15.refs_3_ = bf16[8,16,512]{2,1,0:T(8,128)(2,1)S(1)} collective-permute-done((bf16[8,16,512]{2,1,0:T(8,128)(2,1)S(1)}, bf16[8,16,512]{2,1,0:T(8,128)(2,1)S(1)}, u32[]{:S(2)}, u32[]{:S(2)}) %collective-permute-start.15) | collective-permute-done | bytes 131104 | tf_op jit(solution)/shard_map/ppermute | solution.py:322
  97.3 2.1 %collective-permute-done.16.refs_4_ = bf16[8,16,512]{2,1,0:T(8,128)(2,1)S(1)} collective-permute-done((bf16[8,16,512]{2,1,0:T(8,128)(2,1)S(1)}, bf16[8,16,512]{2,1,0:T(8,128)(2,1)S(1)}, u32[]{:S(2)}, u32[]{:S(2)}) %collective-permute-start.16) | collective-permute-done | bytes 131104 | tf_op jit(solution)/shard_map/ppermute | solution.py:322
  99.4 1.0 shard_map.135
  100.4 3.4 %all-to-all-start.2 = ((bf16[8,32,512]{2,1,0:T(8,128)(2,1)}), bf16[8,32,512]{2,1,0:T(8,128)(2,1)S(1)}, u32[]{:S(2)}, u32[]{:S(2)}) async-start(bf16[8,32,512]{2,1,0:T(8,128)(2,1)} %shard_map.135), calls=%async_computation.2 | async-start | bytes 524288 | tf_op jit(solution)/shard_map/all_to_all | solution.py:330
  103.9 0.9 fusion.7
  104.7 9.5 %all-to-all-done.2.got = bf16[8,32,512]{2,1,0:T(8,128)(2,1)S(1)} async-done(((bf16[8,32,512]{2,1,0:T(8,128)(2,1)}), bf16[8,32,512]{2,1,0:T(8,128)(2,1)S(1)}, u32[]{:S(2)}, u32[]{:S(2)}) %all-to-all-start.2) | async-done | bytes 262176 | tf_op jit(solution)/shard_map/all_to_all | solution.py:330
  (79 shorter events, 6.0 us)
Async XLA Ops:
  0.6 10.6 %copy-start = (bf16[24,8,512]{2,1,0:T(8,128)(2,1)S(1)}, bf16[24,8,512]{2,1,0:T(8,128)(2,1)}, u32[]{:S(2)}) copy-start(bf16[24,8,512]{2,1,0:T(8,128)(2,1)} %param.8) | copy-start | bytes 589828
  0.6 15.8 %copy-start.13 = (bf16[24,8,512]{2,1,0:T(8,128)(2,1)S(1)}, bf16[24,8,512]{2,1,0:T(8,128)(2,1)}, u32[]{:S(2)}) copy-start(bf16[24,8,512]{2,1,0:T(8,128)(2,1)} %param.9) | copy-start | bytes 589828
  1.8 9.4 %collective-permute-start = (bf16[24,3,512]{2,1,0:T(4,128)(2,1)S(1)}, bf16[24,3,512]{2,1,0:T(4,128)(2,1)S(1)}, u32[]{:S(2)}, u32[]{:S(2)}) collective-permute-start(bf16[24,3,512]{2,1,0:T(4,128)(2,1)S(1)} %get-tuple-element.117), channel_id=1, source_target_pairs={{1,2},{2,1},{3,4},{4,3},{5,6},{6,5},{7,8},{8,7},{9,10},{10,9},{11,... | collective-permute-start | bytes 221192 | tf_op jit(solution)/shard_map/ppermute | solution.py:322
  7.7 3.5 %collective-permute-start.1 = (bf16[24,3,512]{2,1,0:T(4,128)(2,1)S(1)}, bf16[24,3,512]{2,1,0:T(4,128)(2,1)S(1)}, u32[]{:S(2)}, u32[]{:S(2)}) collective-permute-start(bf16[24,3,512]{2,1,0:T(4,128)(2,1)S(1)} %get-tuple-element.116), channel_id=1, source_target_pairs={{0,1},{1,0},{2,3},{3,2},{4,5},{5,4},{6,7},{7,6},{8,9},{9,8},{10,11... | collective-permute-start | bytes 221192 | tf_op jit(solution)/shard_map/ppermute | solution.py:322
  8.6 7.9 %copy-start.1 = (bf16[2048,512]{1,0:T(8,128)(2,1)S(1)}, bf16[2048,512]{1,0:T(8,128)(2,1)}, u32[]{:S(2)}) copy-start(bf16[2048,512]{1,0:T(8,128)(2,1)} %w_down.1) | copy-start | bytes 6291460
  11.2 7.3 %copy-start.17 = (bf16[512,512]{1,0:T(8,128)(2,1)S(1)}, bf16[512,512]{1,0:T(8,128)(2,1)}, u32[]{:S(2)}) copy-start(bf16[512,512]{1,0:T(8,128)(2,1)} %w_out.3) | copy-start | bytes 1572868
  11.4 5.9 %collective-permute-start.2 = (bf16[3,16,512]{2,1,0:T(8,128)(2,1)S(1)}, bf16[3,16,512]{2,1,0:T(8,128)(2,1)S(1)}, u32[]{:S(2)}, u32[]{:S(2)}) collective-permute-start(bf16[3,16,512]{2,1,0:T(8,128)(2,1)S(1)} %get-tuple-element.113), channel_id=1, source_target_pairs={{32,64},{33,65},{34,66},{35,67},{36,68},{37,69},{38,70},{39,71},{4... | collective-permute-start | bytes 147464 | tf_op jit(solution)/shard_map/ppermute | solution.py:322
  12.1 6.4 %copy-start.14 = (f32[2,512]{1,0:T(2,128)S(1)}, f32[2,512]{1,0:T(2,128)}, u32[]{:S(2)}) copy-start(f32[2,512]{1,0:T(2,128)} %gains.1) | copy-start | bytes 12292
  12.1 6.4 %copy-start.15 = (bf16[512,2048]{1,0:T(8,128)(2,1)S(1)}, bf16[512,2048]{1,0:T(8,128)(2,1)}, u32[]{:S(2)}) copy-start(bf16[512,2048]{1,0:T(8,128)(2,1)} %w_up.1) | copy-start | bytes 6291460
  12.1 6.4 %copy-start.16 = (bf16[512,1536]{1,0:T(8,128)(2,1)S(1)}, bf16[512,1536]{1,0:T(8,128)(2,1)}, u32[]{:S(2)}) copy-start(bf16[512,1536]{1,0:T(8,128)(2,1)} %w_qkv.3) | copy-start | bytes 4718596
  12.2 6.4 %collective-permute-start.3 = (bf16[3,16,512]{2,1,0:T(8,128)(2,1)S(1)}, bf16[3,16,512]{2,1,0:T(8,128)(2,1)S(1)}, u32[]{:S(2)}, u32[]{:S(2)}) collective-permute-start(bf16[3,16,512]{2,1,0:T(8,128)(2,1)S(1)} %get-tuple-element.112), channel_id=1, source_target_pairs={{0,32},{1,33},{2,34},{3,35},{4,36},{5,37},{6,38},{7,39},{8,40},{9,... | collective-permute-start | bytes 147464 | tf_op jit(solution)/shard_map/ppermute | solution.py:322
  26.3 5.9 %copy-start.11 = (bf16[192,512]{1,0:T(8,128)(2,1)}, bf16[192,512]{1,0:T(8,128)(2,1)S(1)}, u32[]{:S(2)}) copy-start(bf16[192,512]{1,0:T(8,128)(2,1)S(1)} %get-tuple-element.65.gm) | copy-start | bytes 589828
  26.3 6.0 %collective-permute-start.4 = (bf16[16,5,16,512]{3,2,1,0:T(8,128)(2,1)S(1)}, bf16[16,5,16,512]{3,2,1,0:T(8,128)(2,1)S(1)}, u32[]{:S(2)}, u32[]{:S(2)}) collective-permute-start(bf16[16,5,16,512]{3,2,1,0:T(8,128)(2,1)S(1)} %get-tuple-element.67), channel_id=1, source_target_pairs={{0,1},{1,0},{2,3},{3,2},{4,5},{5,4},{6,7},{7,6},{8,9},{9,8},{10,11... | collective-permute-start | bytes 3932168 | tf_op jit(solution)/shard_map/ppermute | solution.py:322
  26.4 5.8 %collective-permute-start.5 = (bf16[4,4,2,32,512]{4,3,2,1,0:T(8,128)(2,1)S(1)}, bf16[4,4,2,32,512]{4,3,2,1,0:T(8,128)(2,1)S(1)}, u32[]{:S(2)}, u32[]{:S(2)}) collective-permute-start(bf16[4,4,2,32,512]{4,3,2,1,0:T(8,128)(2,1)S(1)} %get-tuple-element.68), channel_id=1, source_target_pairs={{0,1},{1,0},{2,3},{3,2},{4,5},{5,4},{6,7},{7,6},{8,9},{9,8},{10,11... | collective-permute-start | bytes 3145736 | tf_op jit(solution)/shard_map/ppermute | solution.py:322
  32.2 2.0 %copy-start.4 = (f32[512,512]{1,0:T(8,128)}, f32[512,512]{1,0:T(8,128)S(1)}, u32[]{:S(2)}) copy-start(f32[512,512]{1,0:T(8,128)S(1)} %get-tuple-element.89) | copy-start | bytes 3145732
  32.3 2.4 %collective-permute-start.6 = (bf16[49,16,512]{2,1,0:T(8,128)(2,1)S(1)}, bf16[49,16,512]{2,1,0:T(8,128)(2,1)S(1)}, u32[]{:S(2)}, u32[]{:S(2)}) collective-permute-start(bf16[49,16,512]{2,1,0:T(8,128)(2,1)S(1)} %get-tuple-element.78), channel_id=1, source_target_pairs={{0,1},{1,0},{2,3},{3,2},{4,5},{5,4},{6,7},{7,6},{8,9},{9,8},{10,11... | collective-permute-start | bytes 2408456 | tf_op jit(solution)/shard_map/ppermute | solution.py:322
  35.6 37.0 %all-to-all-start = ((bf16[4,20,16,512]{3,2,1,0:T(8,128)(2,1)}), bf16[4,20,16,512]{3,2,1,0:T(8,128)(2,1)S(1)}, u32[]{:S(2)}, u32[]{:S(2)}) async-start(bf16[4,20,16,512]{3,2,1,0:T(8,128)(2,1)} %bitcast.8), calls=%async_computation | async-start | bytes 2621440 | tf_op jit(solution)/shard_map/all_to_all | solution.py:330
  45.0 2.0 %copy-start.8 = (bf16[49,16,512]{2,1,0:T(8,128)(2,1)S(1)}, bf16[49,16,512]{2,1,0:T(8,128)(2,1)}, u32[]{:S(2)}) copy-start(bf16[49,16,512]{2,1,0:T(8,128)(2,1)} %copy-done.7) | copy-start | bytes 2408452
  47.4 15.1 %collective-permute-start.7 = (bf16[29,16,512]{2,1,0:T(8,128)(2,1)S(1)}, bf16[29,16,512]{2,1,0:T(8,128)(2,1)S(1)}, u32[]{:S(2)}, u32[]{:S(2)}) collective-permute-start(bf16[29,16,512]{2,1,0:T(8,128)(2,1)S(1)} %get-tuple-element.85), channel_id=1, source_target_pairs={{0,8},{1,9},{2,10},{3,11},{4,12},{5,13},{6,14},{7,15},{8,0},{9,1},... | collective-permute-start | bytes 1425416 | tf_op jit(solution)/shard_map/ppermute | solution.py:322
  47.5 24.3 %collective-permute-start.8 = (bf16[29,16,512]{2,1,0:T(8,128)(2,1)S(1)}, bf16[29,16,512]{2,1,0:T(8,128)(2,1)S(1)}, u32[]{:S(2)}, u32[]{:S(2)}) collective-permute-start(bf16[29,16,512]{2,1,0:T(8,128)(2,1)S(1)} %get-tuple-element.86), channel_id=1, source_target_pairs={{0,24},{1,25},{2,26},{3,27},{4,28},{5,29},{6,30},{7,31},{8,16},{9,... | collective-permute-start | bytes 1425416 | tf_op jit(solution)/shard_map/ppermute | solution.py:322
  50.3 21.5 %collective-permute-start.9 = (bf16[29,16,512]{2,1,0:T(8,128)(2,1)S(1)}, bf16[29,16,512]{2,1,0:T(8,128)(2,1)S(1)}, u32[]{:S(2)}, u32[]{:S(2)}) collective-permute-start(bf16[29,16,512]{2,1,0:T(8,128)(2,1)S(1)} %get-tuple-element.87), channel_id=1, source_target_pairs={{0,16},{1,17},{2,18},{3,19},{4,20},{5,21},{6,22},{7,23},{8,24},{9,... | collective-permute-start | bytes 1425416 | tf_op jit(solution)/shard_map/ppermute | solution.py:322
  51.7 9.0 %collective-permute-start.10 = (bf16[30,3,512]{2,1,0:T(4,128)(2,1)S(1)}, bf16[30,3,512]{2,1,0:T(4,128)(2,1)S(1)}, u32[]{:S(2)}, u32[]{:S(2)}) collective-permute-start(bf16[30,3,512]{2,1,0:T(4,128)(2,1)S(1)} %get-tuple-element.110), channel_id=1, source_target_pairs={{1,2},{2,1},{3,4},{4,3},{5,6},{6,5},{7,8},{8,7},{9,10},{10,9},{11,... | collective-permute-start | bytes 276488 | tf_op jit(solution)/shard_map/ppermute | solution.py:322
  54.0 6.7 %collective-permute-start.11 = (bf16[30,3,512]{2,1,0:T(4,128)(2,1)S(1)}, bf16[30,3,512]{2,1,0:T(4,128)(2,1)S(1)}, u32[]{:S(2)}, u32[]{:S(2)}) collective-permute-start(bf16[30,3,512]{2,1,0:T(4,128)(2,1)S(1)} %get-tuple-element.111), channel_id=1, source_target_pairs={{0,1},{1,0},{2,3},{3,2},{4,5},{5,4},{6,7},{7,6},{8,9},{9,8},{10,11... | collective-permute-start | bytes 276488 | tf_op jit(solution)/shard_map/ppermute | solution.py:322
  73.7 6.5 %copy-start.18 = (f32[30,8,512]{2,1,0:T(8,128)S(1)}, f32[30,8,512]{2,1,0:T(8,128)}, u32[]{:S(2)}) copy-start(f32[30,8,512]{2,1,0:T(8,128)} %fusion) | copy-start | bytes 1474564
  73.9 25.5 %all-to-all-start.1 = ((bf16[4,5,16,512]{3,2,1,0:T(8,128)(2,1)}), bf16[4,5,16,512]{3,2,1,0:T(8,128)(2,1)S(1)}, u32[]{:S(2)}, u32[]{:S(2)}) async-start(bf16[4,5,16,512]{3,2,1,0:T(8,128)(2,1)} %bitcast.14), calls=%async_computation.1 | async-start | bytes 655360 | tf_op jit(solution)/shard_map/all_to_all | solution.py:330
  80.2 23.7 %copy-start.12 = (bf16[192,512]{1,0:T(8,128)(2,1)S(1)}, bf16[192,512]{1,0:T(8,128)(2,1)}, u32[]{:S(2)}) copy-start(bf16[192,512]{1,0:T(8,128)(2,1)} %copy-done.11) | copy-start | bytes 589828
  80.2 12.7 %collective-permute-start.12 = (bf16[3,8,512]{2,1,0:T(8,128)(2,1)S(1)}, bf16[3,8,512]{2,1,0:T(8,128)(2,1)S(1)}, u32[]{:S(2)}, u32[]{:S(2)}) collective-permute-start(bf16[3,8,512]{2,1,0:T(8,128)(2,1)S(1)} %get-tuple-element.114), channel_id=1, source_target_pairs={{32,64},{33,65},{34,66},{35,67},{36,68},{37,69},{38,70},{39,71},{4... | collective-permute-start | bytes 73736 | tf_op jit(solution)/shard_map/ppermute | solution.py:322
  81.0 11.9 %collective-permute-start.13 = (bf16[3,8,512]{2,1,0:T(8,128)(2,1)S(1)}, bf16[3,8,512]{2,1,0:T(8,128)(2,1)S(1)}, u32[]{:S(2)}, u32[]{:S(2)}) collective-permute-start(bf16[3,8,512]{2,1,0:T(8,128)(2,1)S(1)} %get-tuple-element.115), channel_id=1, source_target_pairs={{0,32},{1,33},{2,34},{3,35},{4,36},{5,37},{6,38},{7,39},{8,40},{9,... | collective-permute-start | bytes 73736 | tf_op jit(solution)/shard_map/ppermute | solution.py:322
  85.5 7.6 %collective-permute-start.14 = (bf16[8,16,512]{2,1,0:T(8,128)(2,1)S(1)}, bf16[8,16,512]{2,1,0:T(8,128)(2,1)S(1)}, u32[]{:S(2)}, u32[]{:S(2)}) collective-permute-start(bf16[8,16,512]{2,1,0:T(8,128)(2,1)S(1)} %get-tuple-element.102), channel_id=1, source_target_pairs={{0,32},{1,33},{2,34},{3,35},{4,36},{5,37},{6,38},{7,39},{8,40},{9,... | collective-permute-start | bytes 393224 | tf_op jit(solution)/shard_map/ppermute | solution.py:322
  85.7 11.6 %collective-permute-start.15 = (bf16[8,16,512]{2,1,0:T(8,128)(2,1)S(1)}, bf16[8,16,512]{2,1,0:T(8,128)(2,1)S(1)}, u32[]{:S(2)}, u32[]{:S(2)}) collective-permute-start(bf16[8,16,512]{2,1,0:T(8,128)(2,1)S(1)} %get-tuple-element.103), channel_id=1, source_target_pairs={{0,96},{1,97},{2,98},{3,99},{4,100},{5,101},{6,102},{7,103},{8,104... | collective-permute-start | bytes 393224 | tf_op jit(solution)/shard_map/ppermute | solution.py:322
  92.9 6.5 %collective-permute-start.16 = (bf16[8,16,512]{2,1,0:T(8,128)(2,1)S(1)}, bf16[8,16,512]{2,1,0:T(8,128)(2,1)S(1)}, u32[]{:S(2)}, u32[]{:S(2)}) collective-permute-start(bf16[8,16,512]{2,1,0:T(8,128)(2,1)S(1)} %get-tuple-element.104), channel_id=1, source_target_pairs={{0,64},{1,65},{2,66},{3,67},{4,68},{5,69},{6,70},{7,71},{8,72},{9,... | collective-permute-start | bytes 393224 | tf_op jit(solution)/shard_map/ppermute | solution.py:322
  100.4 13.8 %all-to-all-start.2 = ((bf16[8,32,512]{2,1,0:T(8,128)(2,1)}), bf16[8,32,512]{2,1,0:T(8,128)(2,1)S(1)}, u32[]{:S(2)}, u32[]{:S(2)}) async-start(bf16[8,32,512]{2,1,0:T(8,128)(2,1)} %shard_map.135), calls=%async_computation.2 | async-start | bytes 524288 | tf_op jit(solution)/shard_map/all_to_all | solution.py:330
  (7 other events, 9.9 us)

commit v6 on v5

--- a/solution.py
+++ b/solution.py
@@ -100,44 +100,65 @@
     core_z = ((p >> 3) & 1) * 128 + ((p >> 1) & 3) * 2 + (p >> 8)
     hi, lo = (p >> 6) & 3, (p >> 4) & 3
     here = me & 121
-    pt_u[...] = jnp.where(lane == ((core_z + hi * 32 + lo * 8) ^ (me & 1)) * 2 + (p & 1), 1.0, 0.0).astype(BF16)
+    pt_u[...] = jnp.where(lane == ((core_z + hi * 32 + lo * 8) ^ here) * 2 + (p & 1), 1.0, 0.0).astype(BF16)
     pt_k[...] = jnp.where(lane == ((core_z + hi * 8 + lo * 32) ^ here) * 2 + (p & 1), 1.0, 0.0).astype(BF16)
     k_d = (((p >> 5) & 1) * 32 + ((p >> 6) & 3) * 8 + ((p >> 3) & 3) * 2 + (p >> 8)) ^ (me & 57)
     pt_d[...] = jnp.where(lane == k_d * 8 + (p & 7), 1.0, 0.0).astype(BF16)
 
 
-def forward_kernel(
-    coord, mid, rim_a, rim_b, tok, cot, gains, w_qkv, w_out, w_up, gact, bias, pt_u, pt_d,
-    u_keep, u_send, d_keep, d_send, gm_o, q_o, kv_o, p_o, ne_o, no_o, gain_o, text_s, attn_s,
-):
-    odd = coord[0] & 1
-    text_s[pl.ds(odd * (RIM + ROWS), RIM)] = rim_a[...]
-    text_s[RIM : RIM + ROWS] = mid[...]
-    text_s[pl.ds((1 - odd) * (RIM + ROWS), RIM)] = rim_b[...]
-    text_s[ROWS + 2 * RIM :] = jnp.zeros((ER - ROWS - 2 * RIM, EC, D), BF16)
-    unit_e, _ = unit_of(text_s[...].reshape(EXT, D).astype(F32))
+def attend(qt, keys, vals, bias_t):
+    s = nt(stack_heads(qt), keys) * 0.125 + jnp.concatenate([bias_t] * 4, axis=0)
+    e = jnp.exp(s - jnp.max(s, axis=-1, keepdims=True))
+    prob = e / jnp.sum(e, axis=-1, keepdims=True)
+    return prob, unstack_heads(nn(prob.astype(BF16), vals)).astype(BF16)
+
+
+def middle_kernel(mid, tok, gains, w_qkv, bias, q_o, no_o, ne_o, kv_o, p_o, attn_o):
+    unit_e, _ = unit_of(mid[...].reshape(ROWS * EC, D).astype(F32))
     ne = (unit_e * gains[0:1, :]).astype(BF16)
     ne_o[...] = ne
     kv_o[...] = nn(ne, w_qkv[:, D:]).astype(BF16)
-    xt = tok[...].astype(F32)
-    unit_o, _ = unit_of(xt)
+    unit_o, _ = unit_of(tok[...].astype(F32))
     no = (unit_o * gains[0:1, :]).astype(BF16)
     no_o[...] = no
     q_o[...] = nn(no, w_qkv[:, :D]).astype(BF16)
-    for t in range(TILES):
-        b4 = jnp.concatenate([bias[t]] * 4, axis=0)
+    at = 128 - RIM * EC
+    for g in range(2):
+        cols = slice(g * 256, (g + 1) * 256)
+        vcols = slice(D + g * 256, D + (g + 1) * 256)
+        prob, o = attend(q_o[QT : 2 * QT, cols], kv_o[at : at + KT, cols], kv_o[at : at + KT, vcols], bias[1])
+        p_o[g] = prob
+        attn_o[:, cols] = o
+
+
+def forward_kernel(
+    coord, rim_a, rim_b, tok, cot, gains, w_qkv, w_out, w_up, gact, bias, pt_u, pt_d, q_i, ne_i, kv_i, attn_i,
+    u_keep, u_send, d_keep, d_send, gm_o, kv_o, p_o, ne_o, gain_o, attn_s,
+):
+    odd = coord[0] & 1
+    edge = RIM * EC
+    at_a = pl.multiple_of(odd * (RIM + ROWS) * EC, EC)
+    at_b = pl.multiple_of((1 - odd) * (RIM + ROWS) * EC, EC)
+    end = (RIM + ROWS) * EC
+    both = jnp.concatenate([rim_a[...].reshape(edge, D), rim_b[...].reshape(edge, D)], axis=0)
+    unit_r, _ = unit_of(both.astype(F32))
+    ne_r = (unit_r * gains[0:1, :]).astype(BF16)
+    kv_r = nn(ne_r, w_qkv[:, D:]).astype(BF16)
+    for ref, mid, rims in ((ne_o, ne_i, ne_r), (kv_o, kv_i, kv_r)):
+        ref[edge:end, :] = mid[...]
+        ref[pl.ds(at_a, edge), :] = rims[:edge]
+        ref[pl.ds(at_b, edge), :] = rims[edge:]
+        ref[end + edge :, :] = jnp.zeros((EXT - end - edge, ref.shape[1]), BF16)
+    xt = tok[...].astype(F32)
+    attn_s[QT : 2 * QT, :] = attn_i[...]
+    for i, t in enumerate((0, 2)):
+        rows = slice(t * 128, t * 128 + KT)
         for g in range(2):
             cols = slice(g * 256, (g + 1) * 256)
             vcols = slice(D + g * 256, D + (g + 1) * 256)
-            keys = kv_o[t * 128 : t * 128 + KT, cols]
-            vals = kv_o[t * 128 : t * 128 + KT, vcols]
-            qs = stack_heads(q_o[t * QT : (t + 1) * QT, cols])
-            s = nt(qs, keys) * 0.125 + b4
-            e = jnp.exp(s - jnp.max(s, axis=-1, keepdims=True))
-            prob = e / jnp.sum(e, axis=-1, keepdims=True)
-            p_o[t * 2 + g] = prob
-            o = nn(prob.astype(BF16), vals)
-            attn_s[t * QT : (t + 1) * QT, cols] = unstack_heads(o).astype(BF16)
+            prob, o = attend(q_i[t * QT : (t + 1) * QT, cols], kv_o[rows, cols], kv_o[rows, vcols], bias[t])
+            p_o[i * 2 + g] = prob
+            attn_s[t * QT : (t + 1) * QT, cols] = o
     attn = attn_s[...]
     mixed = (xt + nn(attn, w_out[...])).astype(BF16)
     um, inv_m = unit_of(mixed.astype(F32))
@@ -174,7 +195,7 @@
 
 
 def backward_kernel(
-    coord, gm, w_out, w_qkv, q, kv, p_in, ne, no, mid, rim_a, rim_b, tok, gain_mid, pt,
+    coord, gm, w_out, w_qkv, q, kv, p_mid, p_out, ne, no, mid, rim_a, rim_b, tok, gain_mid, pt,
     k_keep, k_send, gne_o, gnq_o, dq_s, dkv_s,
 ):
     ga = nt(gm[...], w_out[...]).astype(BF16)
@@ -184,7 +205,7 @@
             cols = slice(g * 256, (g + 1) * 256)
             vcols = slice(D + g * 256, D + (g + 1) * 256)
             rows = slice(t * 128, t * 128 + KT)
-            prob = p_in[t * 2 + g]
+            prob = p_mid[g] if t == 1 else p_out[t + g]
             gas = stack_heads(ga[t * QT : (t + 1) * QT, cols])
             qs = stack_heads(q[t * QT : (t + 1) * QT, cols])
             gp = nt(gas, kv[rows, vcols])
@@ -203,7 +224,9 @@
             k_send[j * 3 + i] = part[256 + j * 16 : 256 + j * 16 + 16]
     gne = nt(dkv, w_qkv[:, D:])
     gnq = nt(dq, w_qkv[:, :D])
-    gne_o[...] = gne
+    gne_o[...] = gne[: (ROWS + 2 * RIM) * EC]
+    sides = gne.reshape(ER, EC, D)[: ROWS + 2 * RIM, COLS:]
+    k_send[49:] = sides.reshape((ROWS + 2 * RIM) * COLS, D).astype(BF16).reshape(15, 16, D)
     gnq_o[...] = gnq
     gain_in = jnp.sum(gnq * unit_of(tok[...].astype(F32))[0], axis=0, keepdims=True)
     odd = coord[0] & 1
@@ -226,10 +249,6 @@
     return ((a + b) + (c + d)).astype(BF16)
 
 
-def join_pair_kernel(keep, got, out):
-    out[...] = add2(keep[...], got[...])
-
-
 def join_down_qkv_kernel(dk, dg, kk, kg, *outs):
     gain = add2(kk[48], kg[48])
     for d in range(4):
@@ -238,22 +257,30 @@
         outs[d][28] = gain
 
 
-def sum_up_kernel(got, out):
-    out[...] = add4([got[d] for d in range(4)])
+def join_up_kernel(keep, got, *outs):
+    for d in range(4):
+        outs[d][...] = add2(keep[d * 20 : (d + 1) * 20], got[d * 20 : (d + 1) * 20])
+
+
+def sum_up_kernel(*refs):
+    parts, outs = refs[:4], refs[4:]
+    for d in range(4):
+        outs[d][...] = add4([r[d * 5 : (d + 1) * 5] for r in parts])
 
 
 def sum_down_qkv_kernel(*refs):
-    parts, outs = refs[:4], refs[4:]
+    parts, ride, outs = refs[:4], refs[4], refs[5:]
     gain = add4([r[28] for r in parts])
     for d in range(4):
         outs[d][:4] = add4([r[d * 4 : (d + 1) * 4] for r in parts])
         outs[d][4:7] = add4([r[16 + d * 3 : 16 + (d + 1) * 3] for r in parts])
         outs[d][7] = gain
+    outs[1][8:10] = ride[...]
 
 
 def reduce_xy_kernel(*refs):
-    u_got, out = refs[0], refs[5]
-    sums = [add4([u_got[d] for d in range(4)]).reshape(-1, D), add4([r[...] for r in refs[1:5]]).reshape(-1, D)]
+    out = refs[8]
+    sums = [add4([r[...] for r in refs[:4]]).reshape(-1, D), add4([r[:8] for r in refs[4:8]]).reshape(-1, D)]
     acc = jnp.concatenate(sums, axis=0)
     rows = acc.shape[0]
     i = lax.broadcasted_iota(jnp.int32, (256, rows), 0)
@@ -313,8 +340,6 @@
 CORE_SWAP = [(k, k ^ 1) for k in range(256)]
 X_BIT = 32
 Y_BIT = 8
-X_GROUPS = [[zh * 128 + x * 32 + c for x in range(4)] for zh in range(2) for c in range(32)]
-Y_GROUPS = [[r * 32 + y * 8 + c for y in range(4)] for r in range(8) for c in range(8)]
 Z_GROUPS = [[zh * 128 + x * 32 + y * 8 + zl * 2 + c for zh in range(2) for zl in range(4)] for x in range(4) for y in range(4) for c in range(2)]
 
 
@@ -355,24 +380,32 @@
         prep_front_kernel, [((TOK, FF), F32)], [], 0, 2, 2 * TOK * D * FF, 4_000_000, 8,
     )(cot, w_down)
 
+    q, no, ne_mid, kv_mid, p_mid, attn_mid = call(
+        middle_kernel,
+        [
+            ((TOK, D), BF16), ((TOK, D), BF16), ((ROWS * EC, D), BF16), ((ROWS * EC, 2 * D), BF16),
+            ((2, 256, KT), F32), ((QT, D), BF16),
+        ],
+        [], 0, 5, 600_000_000, 5_000_000, 16,
+    )(mid, tok, gains, w_qkv, bias)
+
     half_u, half_d, half_k = ((16, 5, 16, D), BF16), ((4, 4, 2, 32, D), BF16), ((49, 16, D), BF16)
-    u_keep, u_send, d_keep, d_send, gm, q, kv, prob, ne, no, gain_mid = call(
+    u_keep, u_send, d_keep, d_send, gm, kv, p_out, ne, gain_mid = call(
         forward_kernel,
         [
-            half_u, half_u, half_d, half_d,
-            ((TOK, D), BF16), ((TOK, D), BF16), ((EXT, 2 * D), BF16), ((6, 256, KT), F32),
-            ((EXT, D), BF16), ((TOK, D), BF16), ((1, D), F32),
+            half_u, half_u, half_d, half_d, ((TOK, D), BF16), ((EXT, 2 * D), BF16), ((4, 256, KT), F32),
+            ((EXT, D), BF16), ((1, D), F32),
         ],
-        [pltpu.VMEM((ER, EC, D), BF16), pltpu.VMEM((TOK, D), BF16)], 1, 13, 5_000_000_000, 20_000_000, 24,
-    )(coord, mid, rim_a, rim_b, tok, cot, gains, w_qkv, w_out, w_up, gact, bias, pt_u, pt_d)
+        [pltpu.VMEM((TOK, D), BF16)], 1, 16, 4_000_000_000, 20_000_000, 24,
+    )(coord, rim_a, rim_b, tok, cot, gains, w_qkv, w_out, w_up, gact, bias, pt_u, pt_d, q, ne_mid, kv_mid, attn_mid)
 
     u_got = send(u_send, CORE_SWAP)
     d_got = send(d_send, CORE_SWAP)
     k_keep, k_send, gne, gnq = call(
         backward_kernel,
-        [half_k, half_k, ((EXT, D), F32), ((TOK, D), F32)],
-        [pltpu.VMEM((TOK, D), BF16), pltpu.VMEM((EXT, 2 * D), F32)], 1, 14, 3_000_000_000, 12_000_000, 20,
-    )(coord, gm, w_out, w_qkv, q, kv, prob, ne, no, mid, rim_a, rim_b, tok, gain_mid, pt_k)
+        [half_k, ((64, 16, D), BF16), (((ROWS + 2 * RIM) * EC, D), F32), ((TOK, D), F32)],
+        [pltpu.VMEM((TOK, D), BF16), pltpu.VMEM((EXT, 2 * D), F32)], 1, 15, 3_000_000_000, 12_000_000, 20,
+    )(coord, gm, w_out, w_qkv, q, kv, p_mid, p_out, ne, no, mid, rim_a, rim_b, tok, gain_mid, pt_k)
     u_got, d_got, k_send = lax.optimization_barrier((u_got, d_got, k_send))
 
     def place(x, axis, at_end, size):
@@ -383,31 +416,32 @@
         x = x.astype(F32)
         return jnp.where(at_end, jnp.pad(x, before), jnp.pad(x, after))
 
-    gne3 = gne.reshape(ER, EC, D)[: ROWS + 2 * RIM]
-    back_b = send(gne3[:, COLS + RIM : COLS + 2 * RIM].astype(BF16), COL_B)
-    back_a = send(gne3[:, COLS : COLS + RIM].astype(BF16), COL_A)
-    own = gne3[:, :COLS] + place(back_a, 1, col_odd, COLS) + place(back_b, 1, ~col_odd, COLS)
-
     def join(body, ins, outs):
         return list(call(body, [(o, BF16) for o in outs], [], 0, len(ins), 1_000_000, 4_000_000, 12)(*ins))
 
     k_got = send(k_send, CORE_SWAP)
-    (u,) = join(join_pair_kernel, [u_keep.reshape(80, 16, D), u_got.reshape(80, 16, D)], [(80, 16, D)])
-    u, k_got = lax.optimization_barrier((u, k_got))
-    u_x = exchange(u.reshape(4, 20, 16, D), X_GROUPS)
+    gne3 = gne.reshape(ROWS + 2 * RIM, EC, D)
+    back_a = send(gne3[:, COLS : COLS + RIM].astype(BF16), COL_A)
     b = join(
         join_down_qkv_kernel, [d_keep.reshape(64, 16, D), d_got.reshape(64, 16, D), k_keep, k_got], [(29, 16, D)] * 4,
     )
+    u_got, *b = lax.optimization_barrier((u_got, *b))
     b = to_three(b, Y_BIT)
-    u_x, *b = lax.optimization_barrier((u_x, *b))
-    (u,) = join(sum_up_kernel, [u_x], [(20, 16, D)])
-    b = join(sum_down_qkv_kernel, b, [(8, 16, D)] * 4)
-    u, own, *b = lax.optimization_barrier((u, own, *b))
-    u_y = exchange(u.reshape(4, 5, 16, D), Y_GROUPS)
+    u = join(join_up_kernel, [u_keep.reshape(80, 16, D), u_got.reshape(80, 16, D)], [(20, 16, D)] * 4)
+    u = to_three(u, X_BIT)
+    back_b = k_got[49:].reshape(ROWS + 2 * RIM, COLS, D)[:, RIM : 2 * RIM]
+    own = gne3[:, :COLS] + place(back_a, 1, col_odd, COLS) + place(back_b, 1, ~col_odd, COLS)
+    head, tail = own[:RIM].astype(BF16), own[RIM + ROWS :].astype(BF16)
+    ride = jnp.pad(jnp.where(row_odd, head, tail), ((0, 1), (0, 0), (0, 0))).reshape(2, 16, D)
+    u, b, ride = lax.optimization_barrier((u, b, ride))
+    b = join(sum_down_qkv_kernel, [*b, ride], [(8, 16, D), (10, 16, D), (8, 16, D), (8, 16, D)])
     b = to_three(b, X_BIT)
+    u = join(sum_up_kernel, u, [(5, 16, D)] * 4)
+    u = to_three(u, Y_BIT)
+    up_b = b[1][8:].reshape(4, COLS, D)[:RIM]
     (spread,) = call(
-        reduce_xy_kernel, [((8, 32, D), BF16)], [], 0, 5, 60_000_000, 4_000_000, 12,
-    )(u_y, *b)
+        reduce_xy_kernel, [((8, 32, D), BF16)], [], 0, 8, 60_000_000, 4_000_000, 12,
+    )(*u, *b)
     got_z = exchange(spread, Z_GROUPS)
     g_up, g_down, g_out, g_qkv, g_gains = call(
         reduce_z_kernel,
@@ -415,8 +449,6 @@
         [pltpu.VMEM((32, D), F32)], 0, 1, 1_000_000, 400_000, 8,
     )(got_z)
 
-    head, tail = own[:RIM].astype(BF16), own[RIM + ROWS :].astype(BF16)
-    up_b = send(jnp.where(row_odd, head, tail), ROW_B)
     up_a = send(jnp.where(row_odd, tail, head), ROW_A)
     gn = own[RIM : RIM + ROWS] + place(up_a, 0, row_odd, ROWS) + place(up_b, 0, ~row_odd, ROWS)
     gn = gn + gnq.reshape(ROWS, COLS, D)

time: 115 us -> 109 us (0.948)
  waiting for transfers between devices: 34.6 us -> 31.6 us
  starting transfers between devices: 50.2 us -> 48.5 us
  local copies, waits for them, and re-layouts: 4.64 us -> 2.97 us
    all_to_all x3 -> x1, starting transfers between devices: 19 us -> 6.39 us  [exchange(): return lax.all_to_all(x, AXES, 0, 0, axis_index_groups=groups, tiled=True)]
    ppermute x17 -> x21, starting transfers between devices: 31.2 us -> 42.1 us  [send(): return lax.ppermute(x, AXES, perm)]
    ppermute x17 -> x21, waiting for transfers between devices: 25.1 us -> 21.5 us  [send(): return lax.ppermute(x, AXES, perm)]
    pallas_call x2 -> x3, Pallas kernels: 6.34 us -> 7.88 us  [the longest x1 5.24 us: per_device(): call(backward_kernel, [half_k, ((64, 16, D), BF16), (((ROWS + 2 * RIM) *...]
    slice x1 -> x2, local copies, waits for them, and re-layouts: 1.42 us -> 0.02 us  [the longest x1 0.02 us: per_device(): back_b = k_got[49:].reshape(ROWS + 2 * RIM, COLS, D)[:, RIM:2 * RIM]]
    unnamed x39 -> x29, local copies, waits for them, and re-layouts: 3.06 us -> 2.19 us
    all_to_all x3 -> x1, waiting for transfers between devices: 9.5 us -> 10 us  [exchange(): return lax.all_to_all(x, AXES, 0, 0, axis_index_groups=groups, tiled=True)]
  transfers between devices with their start and end apart: 20 -> 22, of which waited for: 9 -> 6; matrix products, arithmetic and copies ran while one was open for 4% -> 3% of each run, Pallas kernels for 9% -> 12%
where the time goes in v6:
time: 109 us
  starting transfers between devices  48.5 us (44%)
  waiting for transfers between devices  31.6 us (29%)
  Pallas kernels  21.4 us (20%)
  other arithmetic  3.05 us (3%)
  local copies, waits for them, and re-layouts  2.97 us (3%)
    ppermute x21, starting transfers between devices, send(): return lax.ppermute(x, AXES, perm)  42.1 us
    ppermute x21, waiting for transfers between devices, send(): return lax.ppermute(x, AXES, perm)  21.5 us
    all_to_all x1, waiting for transfers between devices, exchange(): return lax.all_to_all(x, AXES, 0, 0, axis_index_groups=groups, tiled=True)  10 us
    pallas_call x1, Pallas kernels, per_device(): call(forward_kernel, [half_u, half_u, half_d, half_d, ((TOK, D), BF16), (...  6.95 us
    all_to_all x1, starting transfers between devices, exchange(): return lax.all_to_all(x, AXES, 0, 0, axis_index_groups=groups, tiled=True)  6.39 us
    pallas_call x1, Pallas kernels, per_device(): call(backward_kernel, [half_k, ((64, 16, D), BF16), (((ROWS + 2 * RIM) *...  5.24 us
    pallas_call x4, Pallas kernels, join(): call(body, [(o, BF16) for o in outs], [], 0, len(ins), 1000000, 4000000, 12)  3.05 us
    unnamed x29, local copies, waits for them, and re-layouts  2.19 us
  transfers between devices with their start and end apart: 22, of which 6 were waited for; matrix products, arithmetic and copies ran while one was open for 3% of the time, Pallas kernels for 12%

profile of v6, /device:TPU:8, one launch (start us, length us, event | category | flops | bytes accessed | tf_op | source)
XLA Modules:
  0.0 108.5 jit_solution(14099115046991449010)
XLA Ops:
  0.7 1.3 %broadcast_select_fusion = (bf16[24,3,512]{2,1,0:T(4,128)(2,1)S(1)}, bf16[24,3,512]{2,1,0:T(4,128)(2,1)S(1)}) fusion(pred[]{:T(512)S(6)} %eq.7, bf16[24,8,512]{2,1,0:T(8,128)(2,1)} %param.8), kind=kLoop, calls=%fused_computation.19 | loop fusion | flops 73728 | bytes 294913 | tf_op jit(solution)/shard_map/jit(_where)/select_n | solution.py:369
  2.0 5.9 %collective-permute-start = (bf16[24,3,512]{2,1,0:T(4,128)(2,1)S(1)}, bf16[24,3,512]{2,1,0:T(4,128)(2,1)S(1)}, u32[]{:S(2)}, u32[]{:S(2)}) collective-permute-start(bf16[24,3,512]{2,1,0:T(4,128)(2,1)S(1)} %get-tuple-element.143), channel_id=1, source_target_pairs={{1,2},{2,1},{3,4},{4,3},{5,6},{6,5},{7,8},{8,7},{9,10},{10,9},{11,... | collective-permute-start | bytes 221192 | tf_op jit(solution)/shard_map/ppermute | solution.py:347
  8.8 2.0 %shard_map.127 = (f32[3,64,256]{2,1,0:T(8,128)S(1)}, bf16[512,512]{1,0:T(8,128)(2,1)S(1)}, bf16[512,512]{1,0:T(8,128)(2,1)S(1)}, bf16[512,512]{1,0:T(8,128)(2,1)S(1)}) custom-call(s32[3]{0:T(128)S(1)} %pad_add_fusion.coord, s32[3,49]{1,0:T(4,128)S(1)} %bitcast.42), custom_call_target="tpu_custom_call" | custom-call | flops 402653184 | bytes 4000000 | tf_op jit(solution)/shard_map/pallas_call | solution.py:371
  12.3 4.3 %collective-permute-start.3 = (bf16[3,16,512]{2,1,0:T(8,128)(2,1)S(1)}, bf16[3,16,512]{2,1,0:T(8,128)(2,1)S(1)}, u32[]{:S(2)}, u32[]{:S(2)}) collective-permute-start(bf16[3,16,512]{2,1,0:T(8,128)(2,1)S(1)} %get-tuple-element.138), channel_id=1, source_target_pairs={{0,32},{1,33},{2,34},{3,35},{4,36},{5,37},{6,38},{7,39},{8,40},{9,... | collective-permute-start | bytes 147464 | tf_op jit(solution)/shard_map/ppermute | solution.py:347
  16.6 0.8 shard_map.128.gact
  17.5 1.6 %shard_map.129 = (bf16[192,512]{1,0:T(8,128)(2,1)S(1)}, bf16[192,512]{1,0:T(8,128)(2,1)S(1)}, bf16[384,512]{1,0:T(8,128)(2,1)S(1)}, bf16[384,1024]{1,0:T(8,128)(...) custom-call(bf16[24,16,512]{2,1,0:T(8,128)(2,1)S(1)} %maximum_maximum_fusion.mid, ...), custom_call_target="tpu_custom_call" | custom-call | flops 600000000 | bytes 5000000 | tf_op jit(solution)/shard_map/pallas_call | solution.py:383
  19.1 7.0 %shard_map.130 = (bf16[16,5,16,512]{3,2,1,0:T(8,128)(2,1)S(1)}, bf16[16,5,16,512]{3,2,1,0:T(8,128)(2,1)S(1)}, bf16[4,4,2,32,512]{4,3,2,1,0:T(8,128)(2,1)S(1)}, b...) custom-call(s32[3]{0:T(128)S(1)} %pad_add_fusion.coord, ...), custom_call_target="tpu_custom_call" | custom-call | flops 4000000000 | bytes 20000000 | tf_op jit(solution)/shard_map/pallas_call | solution.py:393
  26.7 5.2 %shard_map.131 = (bf16[49,16,512]{2,1,0:T(8,128)(2,1)S(1)}, bf16[64,16,512]{2,1,0:T(8,128)(2,1)S(1)}, f32[480,512]{1,0:T(8,128)S(1)}, f32[192,512]{1,0:T(8,128)S(1)}) custom-call(s32[3]{0:T(128)S(1)} %pad_add_fusion.coord, bf16[192,512]{1,0:T(8,128)(2,1)S(1)} %get-tuple-element.82.gm, bf16[512,512]{1,0:T(8,128)(2,1)S(1)} %copy-done.8, ...), custom_call_target="tpu_custom_call" | custom-call | flops 3000000000 | bytes 12000000 | tf_op jit(solution)/shard_map/pallas_call | solution.py:404
  33.0 4.5 %collective-permute-start.4 = (bf16[30,3,512]{2,1,0:T(4,128)(2,1)}, bf16[30,3,512]{2,1,0:T(4,128)(2,1)S(1)}, u32[]{:S(2)}, u32[]{:S(2)}) collective-permute-start(bf16[30,3,512]{2,1,0:T(4,128)(2,1)} %slice.101), channel_id=1, source_target_pairs={{1,2},{2,1},{3,4},{4,3},{5,6},{6,5},{7,8},{8,7},{9,10},{10,9},{11,... | collective-permute-start | bytes 276488 | tf_op jit(solution)/shard_map/ppermute | solution.py:347
  38.0 1.2 %shard_map.133 = (bf16[20,16,512]{2,1,0:T(8,128)(2,1)S(1)}, bf16[20,16,512]{2,1,0:T(8,128)(2,1)S(1)}, bf16[20,16,512]{2,1,0:T(8,128)(2,1)S(1)}, bf16[20,16,512]{2,1,0:T(8,128)(2,1)}) custom-call(bf16[80,16,512]{2,1,0:T(8,128)(2,1)S(1)} %bitcast.33, bf16[80,16,512]{2,1,0:T(8,128)(2,1)S(1)} %bitcast.34), custom_call_target="tpu_custom_call" | custom-call | flops 1000000 | bytes 4000000 | tf_op jit(solution)/shard_map/pallas_call | solution.py:420
  39.3 0.7 copy-done.12
  40.0 0.7 copy-done.13
  40.7 6.6 %collective-permute-start.10 = (bf16[20,16,512]{2,1,0:T(8,128)(2,1)}, bf16[20,16,512]{2,1,0:T(8,128)(2,1)}, u32[]{:S(2)}, u32[]{:S(2)}) collective-permute-start(bf16[20,16,512]{2,1,0:T(8,128)(2,1)} %get-tuple-element.107), channel_id=1, source_target_pairs={{0,96},{1,97},{2,98},{3,99},{4,100},{5,101},{6,102},{7,103},{8,104... | collective-permute-start | bytes 983048 | tf_op jit(solution)/shard_map/ppermute | solution.py:347
  47.4 2.4 %collective-permute-start.11 = (bf16[20,16,512]{2,1,0:T(8,128)(2,1)}, bf16[20,16,512]{2,1,0:T(8,128)(2,1)S(1)}, u32[]{:S(2)}, u32[]{:S(2)}) collective-permute-start(bf16[20,16,512]{2,1,0:T(8,128)(2,1)} %copy-done.13), channel_id=1, source_target_pairs={{0,64},{1,65},{2,66},{3,67},{4,68},{5,69},{6,70},{7,71},{8,72},{9,... | collective-permute-start | bytes 983048 | tf_op jit(solution)/shard_map/ppermute | solution.py:347
  49.8 0.9 collective-permute-start.9
  50.7 2.9 %collective-permute-start.13 = (bf16[29,16,512]{2,1,0:T(8,128)(2,1)}, bf16[29,16,512]{2,1,0:T(8,128)(2,1)S(1)}, u32[]{:S(2)}, u32[]{:S(2)}) collective-permute-start(bf16[29,16,512]{2,1,0:T(8,128)(2,1)} %copy-done.10), channel_id=1, source_target_pairs={{0,24},{1,25},{2,26},{3,27},{4,28},{5,29},{6,30},{7,31},{8,16},{9,... | collective-permute-start | bytes 1425416 | tf_op jit(solution)/shard_map/ppermute | solution.py:347
  53.7 7.5 %collective-permute-done.10.refs_2_ = bf16[20,16,512]{2,1,0:T(8,128)(2,1)} collective-permute-done((bf16[20,16,512]{2,1,0:T(8,128)(2,1)}, bf16[20,16,512]{2,1,0:T(8,128)(2,1)}, u32[]{:S(2)}, u32[]{:S(2)}) %collective-permute-start.10) | collective-permute-done | bytes 327712 | tf_op jit(solution)/shard_map/ppermute | solution.py:347
  61.2 2.3 %collective-permute-start.14 = (bf16[29,16,512]{2,1,0:T(8,128)(2,1)}, bf16[29,16,512]{2,1,0:T(8,128)(2,1)S(1)}, u32[]{:S(2)}, u32[]{:S(2)}) collective-permute-start(bf16[29,16,512]{2,1,0:T(8,128)(2,1)} %copy-done.9), channel_id=1, source_target_pairs={{0,16},{1,17},{2,18},{3,19},{4,20},{5,21},{6,22},{7,23},{8,24},{9,... | collective-permute-start | bytes 1425416 | tf_op jit(solution)/shard_map/ppermute | solution.py:347
  64.4 8.4 %collective-permute-done.14.refs_3_ = bf16[29,16,512]{2,1,0:T(8,128)(2,1)S(1)} collective-permute-done((bf16[29,16,512]{2,1,0:T(8,128)(2,1)}, bf16[29,16,512]{2,1,0:T(8,128)(2,1)S(1)}, u32[]{:S(2)}, u32[]{:S(2)}) %collective-permute-start.14) | collective-permute-done | bytes 475168 | tf_op jit(solution)/shard_map/ppermute | solution.py:347
  72.8 1.1 %shard_map.135 = (bf16[5,16,512]{2,1,0:T(8,128)(2,1)S(1)}, bf16[5,16,512]{2,1,0:T(8,128)(2,1)S(1)}, bf16[5,16,512]{2,1,0:T(8,128)(2,1)S(1)}, bf16[5,16,512]{2,1,0:T(8,128)(2,1)S(1)}) custom-call(bf16[20,16,512]{2,1,0:T(8,128)(2,1)S(1)} %get-tuple-element.120.refs_0_, bf16[20,16,512]{2,1,0:T(8,128)(2,1)S(1)} %collective-permute-done.9.refs_1_, ...), custom_call_target="tpu_custom_call" | custom-call | flops 1000000 | bytes 4000000 | tf_op jit(solution)/shard_map/pallas_call | solution.py:420
  74.0 1.1 %collective-permute-start.16 = (bf16[5,16,512]{2,1,0:T(8,128)(2,1)S(1)}, bf16[5,16,512]{2,1,0:T(8,128)(2,1)S(1)}, u32[]{:S(2)}, u32[]{:S(2)}) collective-permute-start(bf16[5,16,512]{2,1,0:T(8,128)(2,1)S(1)} %get-tuple-element.125), channel_id=1, source_target_pairs={{0,8},{1,9},{2,10},{3,11},{4,12},{5,13},{6,14},{7,15},{8,0},{9,1},... | collective-permute-start | bytes 245768 | tf_op jit(solution)/shard_map/ppermute | solution.py:347
  75.2 1.8 %collective-permute-start.17 = (bf16[5,16,512]{2,1,0:T(8,128)(2,1)S(1)}, bf16[5,16,512]{2,1,0:T(8,128)(2,1)S(1)}, u32[]{:S(2)}, u32[]{:S(2)}) collective-permute-start(bf16[5,16,512]{2,1,0:T(8,128)(2,1)S(1)} %get-tuple-element.126), channel_id=1, source_target_pairs={{0,24},{1,25},{2,26},{3,27},{4,28},{5,29},{6,30},{7,31},{8,16},{9,... | collective-permute-start | bytes 245768 | tf_op jit(solution)/shard_map/ppermute | solution.py:347
  76.9 1.4 %collective-permute-start.18 = (bf16[5,16,512]{2,1,0:T(8,128)(2,1)S(1)}, bf16[5,16,512]{2,1,0:T(8,128)(2,1)S(1)}, u32[]{:S(2)}, u32[]{:S(2)}) collective-permute-start(bf16[5,16,512]{2,1,0:T(8,128)(2,1)S(1)} %get-tuple-element.127), channel_id=1, source_target_pairs={{0,16},{1,17},{2,18},{3,19},{4,20},{5,21},{6,22},{7,23},{8,24},{9,... | collective-permute-start | bytes 245768 | tf_op jit(solution)/shard_map/ppermute | solution.py:347
  78.6 1.5 %collective-permute-start.15 = (bf16[10,16,512]{2,1,0:T(8,128)(2,1)S(1)}, bf16[10,16,512]{2,1,0:T(8,128)(2,1)S(1)}, u32[]{:S(2)}, u32[]{:S(2)}) collective-permute-start(bf16[10,16,512]{2,1,0:T(8,128)(2,1)S(1)} %get-tuple-element.118), channel_id=1, source_target_pairs={{0,32},{1,33},{2,34},{3,35},{4,36},{5,37},{6,38},{7,39},{8,40},{9,... | collective-permute-start | bytes 491528 | tf_op jit(solution)/shard_map/ppermute | solution.py:347
  80.1 2.7 %collective-permute-start.19 = (bf16[8,16,512]{2,1,0:T(8,128)(2,1)S(1)}, bf16[8,16,512]{2,1,0:T(8,128)(2,1)S(1)}, u32[]{:S(2)}, u32[]{:S(2)}) collective-permute-start(bf16[8,16,512]{2,1,0:T(8,128)(2,1)S(1)} %get-tuple-element.129), channel_id=1, source_target_pairs={{0,96},{1,97},{2,98},{3,99},{4,100},{5,101},{6,102},{7,103},{8,104... | collective-permute-start | bytes 393224 | tf_op jit(solution)/shard_map/ppermute | solution.py:347
  82.8 1.4 %collective-permute-start.20 = (bf16[8,16,512]{2,1,0:T(8,128)(2,1)S(1)}, bf16[8,16,512]{2,1,0:T(8,128)(2,1)S(1)}, u32[]{:S(2)}, u32[]{:S(2)}) collective-permute-start(bf16[8,16,512]{2,1,0:T(8,128)(2,1)S(1)} %get-tuple-element.130), channel_id=1, source_target_pairs={{0,64},{1,65},{2,66},{3,67},{4,68},{5,69},{6,70},{7,71},{8,72},{9,... | collective-permute-start | bytes 393224 | tf_op jit(solution)/shard_map/ppermute | solution.py:347
  84.3 2.4 %collective-permute-done.19.refs_6_ = bf16[8,16,512]{2,1,0:T(8,128)(2,1)S(1)} collective-permute-done((bf16[8,16,512]{2,1,0:T(8,128)(2,1)S(1)}, bf16[8,16,512]{2,1,0:T(8,128)(2,1)S(1)}, u32[]{:S(2)}, u32[]{:S(2)}) %collective-permute-start.19) | collective-permute-done | bytes 131104 | tf_op jit(solution)/shard_map/ppermute | solution.py:347
  86.7 2.6 %collective-permute-done.20.refs_7_ = bf16[8,16,512]{2,1,0:T(8,128)(2,1)S(1)} collective-permute-done((bf16[8,16,512]{2,1,0:T(8,128)(2,1)S(1)}, bf16[8,16,512]{2,1,0:T(8,128)(2,1)S(1)}, u32[]{:S(2)}, u32[]{:S(2)}) %collective-permute-start.20) | collective-permute-done | bytes 131104 | tf_op jit(solution)/shard_map/ppermute | solution.py:347
  89.3 1.0 shard_map.136
  90.3 6.4 %all-to-all-start = ((bf16[8,32,512]{2,1,0:T(8,128)(2,1)}), bf16[8,32,512]{2,1,0:T(8,128)(2,1)S(1)}, u32[]{:S(2)}, u32[]{:S(2)}) async-start(bf16[8,32,512]{2,1,0:T(8,128)(2,1)} %shard_map.136), calls=%async_computation | async-start | bytes 524288 | tf_op jit(solution)/shard_map/all_to_all | solution.py:355
  96.9 0.9 fusion.7
  97.8 10.0 %all-to-all-done.got = bf16[8,32,512]{2,1,0:T(8,128)(2,1)S(1)} async-done(((bf16[8,32,512]{2,1,0:T(8,128)(2,1)}), bf16[8,32,512]{2,1,0:T(8,128)(2,1)S(1)}, u32[]{:S(2)}, u32[]{:S(2)}) %all-to-all-start) | async-done | bytes 262176 | tf_op jit(solution)/shard_map/all_to_all | solution.py:355
  (74 shorter events, 6.8 us)
Async XLA Ops:
  0.6 10.7 %copy-start = (bf16[24,8,512]{2,1,0:T(8,128)(2,1)S(1)}, bf16[24,8,512]{2,1,0:T(8,128)(2,1)}, u32[]{:S(2)}) copy-start(bf16[24,8,512]{2,1,0:T(8,128)(2,1)} %param.8) | copy-start | bytes 589828
  0.6 15.9 %copy-start.5 = (bf16[24,8,512]{2,1,0:T(8,128)(2,1)S(1)}, bf16[24,8,512]{2,1,0:T(8,128)(2,1)}, u32[]{:S(2)}) copy-start(bf16[24,8,512]{2,1,0:T(8,128)(2,1)} %param.9) | copy-start | bytes 589828
  0.7 15.9 %copy-start.1 = (bf16[2048,512]{1,0:T(8,128)(2,1)S(1)}, bf16[2048,512]{1,0:T(8,128)(2,1)}, u32[]{:S(2)}) copy-start(bf16[2048,512]{1,0:T(8,128)(2,1)} %w_down.1) | copy-start | bytes 6291460
  2.0 9.4 %collective-permute-start = (bf16[24,3,512]{2,1,0:T(4,128)(2,1)S(1)}, bf16[24,3,512]{2,1,0:T(4,128)(2,1)S(1)}, u32[]{:S(2)}, u32[]{:S(2)}) collective-permute-start(bf16[24,3,512]{2,1,0:T(4,128)(2,1)S(1)} %get-tuple-element.143), channel_id=1, source_target_pairs={{1,2},{2,1},{3,4},{4,3},{5,6},{6,5},{7,8},{8,7},{9,10},{10,9},{11,... | collective-permute-start | bytes 221192 | tf_op jit(solution)/shard_map/ppermute | solution.py:347
  7.8 3.5 %collective-permute-start.1 = (bf16[24,3,512]{2,1,0:T(4,128)(2,1)S(1)}, bf16[24,3,512]{2,1,0:T(4,128)(2,1)S(1)}, u32[]{:S(2)}, u32[]{:S(2)}) collective-permute-start(bf16[24,3,512]{2,1,0:T(4,128)(2,1)S(1)} %get-tuple-element.142), channel_id=1, source_target_pairs={{0,1},{1,0},{2,3},{3,2},{4,5},{5,4},{6,7},{7,6},{8,9},{9,8},{10,11... | collective-permute-start | bytes 221192 | tf_op jit(solution)/shard_map/ppermute | solution.py:347
  11.6 7.5 %collective-permute-start.2 = (bf16[3,16,512]{2,1,0:T(8,128)(2,1)S(1)}, bf16[3,16,512]{2,1,0:T(8,128)(2,1)S(1)}, u32[]{:S(2)}, u32[]{:S(2)}) collective-permute-start(bf16[3,16,512]{2,1,0:T(8,128)(2,1)S(1)} %get-tuple-element.139), channel_id=1, source_target_pairs={{32,64},{33,65},{34,66},{35,67},{36,68},{37,69},{38,70},{39,71},{4... | collective-permute-start | bytes 147464 | tf_op jit(solution)/shard_map/ppermute | solution.py:347
  12.2 5.2 %copy-start.2 = (bf16[512,1536]{1,0:T(8,128)(2,1)S(1)}, bf16[512,1536]{1,0:T(8,128)(2,1)}, u32[]{:S(2)}) copy-start(bf16[512,1536]{1,0:T(8,128)(2,1)} %w_qkv.5) | copy-start | bytes 4718596
  12.2 5.2 %copy-start.6 = (f32[2,512]{1,0:T(2,128)S(1)}, f32[2,512]{1,0:T(2,128)}, u32[]{:S(2)}) copy-start(f32[2,512]{1,0:T(2,128)} %gains.3) | copy-start | bytes 12292
  12.3 6.8 %collective-permute-start.3 = (bf16[3,16,512]{2,1,0:T(8,128)(2,1)S(1)}, bf16[3,16,512]{2,1,0:T(8,128)(2,1)S(1)}, u32[]{:S(2)}, u32[]{:S(2)}) collective-permute-start(bf16[3,16,512]{2,1,0:T(8,128)(2,1)S(1)} %get-tuple-element.138), channel_id=1, source_target_pairs={{0,32},{1,33},{2,34},{3,35},{4,36},{5,37},{6,38},{7,39},{8,40},{9,... | collective-permute-start | bytes 147464 | tf_op jit(solution)/shard_map/ppermute | solution.py:347
  16.6 2.5 %copy-start.8 = (bf16[512,512]{1,0:T(8,128)(2,1)S(1)}, bf16[512,512]{1,0:T(8,128)(2,1)}, u32[]{:S(2)}) copy-start(bf16[512,512]{1,0:T(8,128)(2,1)} %w_out.3) | copy-start | bytes 1572868
  26.1 5.9 %copy-start.3 = (bf16[192,512]{1,0:T(8,128)(2,1)}, bf16[192,512]{1,0:T(8,128)(2,1)S(1)}, u32[]{:S(2)}) copy-start(bf16[192,512]{1,0:T(8,128)(2,1)S(1)} %get-tuple-element.82.gm) | copy-start | bytes 589828
  26.1 5.9 %collective-permute-start.5 = (bf16[16,5,16,512]{3,2,1,0:T(8,128)(2,1)S(1)}, bf16[16,5,16,512]{3,2,1,0:T(8,128)(2,1)S(1)}, u32[]{:S(2)}, u32[]{:S(2)}) collective-permute-start(bf16[16,5,16,512]{3,2,1,0:T(8,128)(2,1)S(1)} %get-tuple-element.91), channel_id=1, source_target_pairs={{0,1},{1,0},{2,3},{3,2},{4,5},{5,4},{6,7},{7,6},{8,9},{9,8},{10,11... | collective-permute-start | bytes 3932168 | tf_op jit(solution)/shard_map/ppermute | solution.py:347
  26.2 5.8 %collective-permute-start.6 = (bf16[4,4,2,32,512]{4,3,2,1,0:T(8,128)(2,1)S(1)}, bf16[4,4,2,32,512]{4,3,2,1,0:T(8,128)(2,1)S(1)}, u32[]{:S(2)}, u32[]{:S(2)}) collective-permute-start(bf16[4,4,2,32,512]{4,3,2,1,0:T(8,128)(2,1)S(1)} %get-tuple-element.92), channel_id=1, source_target_pairs={{0,1},{1,0},{2,3},{3,2},{4,5},{5,4},{6,7},{7,6},{8,9},{9,8},{10,11... | collective-permute-start | bytes 3145736 | tf_op jit(solution)/shard_map/ppermute | solution.py:347
  32.0 5.6 %collective-permute-start.7 = (bf16[64,16,512]{2,1,0:T(8,128)(2,1)S(1)}, bf16[64,16,512]{2,1,0:T(8,128)(2,1)S(1)}, u32[]{:S(2)}, u32[]{:S(2)}) collective-permute-start(bf16[64,16,512]{2,1,0:T(8,128)(2,1)S(1)} %get-tuple-element.94), channel_id=1, source_target_pairs={{0,1},{1,0},{2,3},{3,2},{4,5},{5,4},{6,7},{7,6},{8,9},{9,8},{10,11... | collective-permute-start | bytes 3145736 | tf_op jit(solution)/shard_map/ppermute | solution.py:347
  33.0 14.3 %collective-permute-start.4 = (bf16[30,3,512]{2,1,0:T(4,128)(2,1)}, bf16[30,3,512]{2,1,0:T(4,128)(2,1)S(1)}, u32[]{:S(2)}, u32[]{:S(2)}) collective-permute-start(bf16[30,3,512]{2,1,0:T(4,128)(2,1)} %slice.101), channel_id=1, source_target_pairs={{1,2},{2,1},{3,4},{4,3},{5,6},{6,5},{7,8},{8,7},{9,10},{10,9},{11,... | collective-permute-start | bytes 276488 | tf_op jit(solution)/shard_map/ppermute | solution.py:347
  38.0 2.7 %copy-start.10 = (bf16[29,16,512]{2,1,0:T(8,128)(2,1)}, bf16[29,16,512]{2,1,0:T(8,128)(2,1)S(1)}, u32[]{:S(2)}) copy-start(bf16[29,16,512]{2,1,0:T(8,128)(2,1)S(1)} %get-tuple-element.111) | copy-start | bytes 1425412
  38.0 2.7 %copy-start.11 = (bf16[29,16,512]{2,1,0:T(8,128)(2,1)}, bf16[29,16,512]{2,1,0:T(8,128)(2,1)S(1)}, u32[]{:S(2)}) copy-start(bf16[29,16,512]{2,1,0:T(8,128)(2,1)S(1)} %get-tuple-element.110) | copy-start | bytes 1425412
  40.7 20.5 %collective-permute-start.10 = (bf16[20,16,512]{2,1,0:T(8,128)(2,1)}, bf16[20,16,512]{2,1,0:T(8,128)(2,1)}, u32[]{:S(2)}, u32[]{:S(2)}) collective-permute-start(bf16[20,16,512]{2,1,0:T(8,128)(2,1)} %get-tuple-element.107), channel_id=1, source_target_pairs={{0,96},{1,97},{2,98},{3,99},{4,100},{5,101},{6,102},{7,103},{8,104... | collective-permute-start | bytes 983048 | tf_op jit(solution)/shard_map/ppermute | solution.py:347
  47.4 16.3 %collective-permute-start.11 = (bf16[20,16,512]{2,1,0:T(8,128)(2,1)}, bf16[20,16,512]{2,1,0:T(8,128)(2,1)S(1)}, u32[]{:S(2)}, u32[]{:S(2)}) collective-permute-start(bf16[20,16,512]{2,1,0:T(8,128)(2,1)} %copy-done.13), channel_id=1, source_target_pairs={{0,64},{1,65},{2,66},{3,67},{4,68},{5,69},{6,70},{7,71},{8,72},{9,... | collective-permute-start | bytes 983048 | tf_op jit(solution)/shard_map/ppermute | solution.py:347
  49.8 14.6 %collective-permute-start.9 = (bf16[20,16,512]{2,1,0:T(8,128)(2,1)}, bf16[20,16,512]{2,1,0:T(8,128)(2,1)S(1)}, u32[]{:S(2)}, u32[]{:S(2)}) collective-permute-start(bf16[20,16,512]{2,1,0:T(8,128)(2,1)} %copy-done.12), channel_id=1, source_target_pairs={{0,32},{1,33},{2,34},{3,35},{4,36},{5,37},{6,38},{7,39},{8,40},{9,... | collective-permute-start | bytes 983048 | tf_op jit(solution)/shard_map/ppermute | solution.py:347
  50.7 13.7 %collective-permute-start.12 = (bf16[29,16,512]{2,1,0:T(8,128)(2,1)}, bf16[29,16,512]{2,1,0:T(8,128)(2,1)S(1)}, u32[]{:S(2)}, u32[]{:S(2)}) collective-permute-start(bf16[29,16,512]{2,1,0:T(8,128)(2,1)} %copy-done.11), channel_id=1, source_target_pairs={{0,8},{1,9},{2,10},{3,11},{4,12},{5,13},{6,14},{7,15},{8,0},{9,1},... | collective-permute-start | bytes 1425416 | tf_op jit(solution)/shard_map/ppermute | solution.py:347
  50.7 13.7 %collective-permute-start.13 = (bf16[29,16,512]{2,1,0:T(8,128)(2,1)}, bf16[29,16,512]{2,1,0:T(8,128)(2,1)S(1)}, u32[]{:S(2)}, u32[]{:S(2)}) collective-permute-start(bf16[29,16,512]{2,1,0:T(8,128)(2,1)} %copy-done.10), channel_id=1, source_target_pairs={{0,24},{1,25},{2,26},{3,27},{4,28},{5,29},{6,30},{7,31},{8,16},{9,... | collective-permute-start | bytes 1425416 | tf_op jit(solution)/shard_map/ppermute | solution.py:347
  61.2 11.6 %collective-permute-start.14 = (bf16[29,16,512]{2,1,0:T(8,128)(2,1)}, bf16[29,16,512]{2,1,0:T(8,128)(2,1)S(1)}, u32[]{:S(2)}, u32[]{:S(2)}) collective-permute-start(bf16[29,16,512]{2,1,0:T(8,128)(2,1)} %copy-done.9), channel_id=1, source_target_pairs={{0,16},{1,17},{2,18},{3,19},{4,20},{5,21},{6,22},{7,23},{8,24},{9,... | collective-permute-start | bytes 1425416 | tf_op jit(solution)/shard_map/ppermute | solution.py:347
  63.7 16.3 %collective-permute-start.8 = (bf16[3,8,512]{2,1,0:T(8,128)(2,1)S(1)}, bf16[3,8,512]{2,1,0:T(8,128)(2,1)S(1)}, u32[]{:S(2)}, u32[]{:S(2)}) collective-permute-start(bf16[3,8,512]{2,1,0:T(8,128)(2,1)S(1)} %get-tuple-element.140), channel_id=1, source_target_pairs={{32,64},{33,65},{34,66},{35,67},{36,68},{37,69},{38,70},{39,71},{4... | collective-permute-start | bytes 73736 | tf_op jit(solution)/shard_map/ppermute | solution.py:347
  74.0 8.8 %collective-permute-start.16 = (bf16[5,16,512]{2,1,0:T(8,128)(2,1)S(1)}, bf16[5,16,512]{2,1,0:T(8,128)(2,1)S(1)}, u32[]{:S(2)}, u32[]{:S(2)}) collective-permute-start(bf16[5,16,512]{2,1,0:T(8,128)(2,1)S(1)} %get-tuple-element.125), channel_id=1, source_target_pairs={{0,8},{1,9},{2,10},{3,11},{4,12},{5,13},{6,14},{7,15},{8,0},{9,1},... | collective-permute-start | bytes 245768 | tf_op jit(solution)/shard_map/ppermute | solution.py:347
  75.2 9.1 %collective-permute-start.17 = (bf16[5,16,512]{2,1,0:T(8,128)(2,1)S(1)}, bf16[5,16,512]{2,1,0:T(8,128)(2,1)S(1)}, u32[]{:S(2)}, u32[]{:S(2)}) collective-permute-start(bf16[5,16,512]{2,1,0:T(8,128)(2,1)S(1)} %get-tuple-element.126), channel_id=1, source_target_pairs={{0,24},{1,25},{2,26},{3,27},{4,28},{5,29},{6,30},{7,31},{8,16},{9,... | collective-permute-start | bytes 245768 | tf_op jit(solution)/shard_map/ppermute | solution.py:347
  76.9 7.4 %collective-permute-start.18 = (bf16[5,16,512]{2,1,0:T(8,128)(2,1)S(1)}, bf16[5,16,512]{2,1,0:T(8,128)(2,1)S(1)}, u32[]{:S(2)}, u32[]{:S(2)}) collective-permute-start(bf16[5,16,512]{2,1,0:T(8,128)(2,1)S(1)} %get-tuple-element.127), channel_id=1, source_target_pairs={{0,16},{1,17},{2,18},{3,19},{4,20},{5,21},{6,22},{7,23},{8,24},{9,... | collective-permute-start | bytes 245768 | tf_op jit(solution)/shard_map/ppermute | solution.py:347
  78.6 18.4 %copy-start.4 = (bf16[192,512]{1,0:T(8,128)(2,1)S(1)}, bf16[192,512]{1,0:T(8,128)(2,1)}, u32[]{:S(2)}) copy-start(bf16[192,512]{1,0:T(8,128)(2,1)} %copy-done.3) | copy-start | bytes 589828
  78.6 10.7 %collective-permute-start.15 = (bf16[10,16,512]{2,1,0:T(8,128)(2,1)S(1)}, bf16[10,16,512]{2,1,0:T(8,128)(2,1)S(1)}, u32[]{:S(2)}, u32[]{:S(2)}) collective-permute-start(bf16[10,16,512]{2,1,0:T(8,128)(2,1)S(1)} %get-tuple-element.118), channel_id=1, source_target_pairs={{0,32},{1,33},{2,34},{3,35},{4,36},{5,37},{6,38},{7,39},{8,40},{9,... | collective-permute-start | bytes 491528 | tf_op jit(solution)/shard_map/ppermute | solution.py:347
  80.1 6.7 %collective-permute-start.19 = (bf16[8,16,512]{2,1,0:T(8,128)(2,1)S(1)}, bf16[8,16,512]{2,1,0:T(8,128)(2,1)S(1)}, u32[]{:S(2)}, u32[]{:S(2)}) collective-permute-start(bf16[8,16,512]{2,1,0:T(8,128)(2,1)S(1)} %get-tuple-element.129), channel_id=1, source_target_pairs={{0,96},{1,97},{2,98},{3,99},{4,100},{5,101},{6,102},{7,103},{8,104... | collective-permute-start | bytes 393224 | tf_op jit(solution)/shard_map/ppermute | solution.py:347
  82.8 6.5 %collective-permute-start.20 = (bf16[8,16,512]{2,1,0:T(8,128)(2,1)S(1)}, bf16[8,16,512]{2,1,0:T(8,128)(2,1)S(1)}, u32[]{:S(2)}, u32[]{:S(2)}) collective-permute-start(bf16[8,16,512]{2,1,0:T(8,128)(2,1)S(1)} %get-tuple-element.130), channel_id=1, source_target_pairs={{0,64},{1,65},{2,66},{3,67},{4,68},{5,69},{6,70},{7,71},{8,72},{9,... | collective-permute-start | bytes 393224 | tf_op jit(solution)/shard_map/ppermute | solution.py:347
  90.3 17.6 %all-to-all-start = ((bf16[8,32,512]{2,1,0:T(8,128)(2,1)}), bf16[8,32,512]{2,1,0:T(8,128)(2,1)S(1)}, u32[]{:S(2)}, u32[]{:S(2)}) async-start(bf16[8,32,512]{2,1,0:T(8,128)(2,1)} %shard_map.136), calls=%async_computation | async-start | bytes 524288 | tf_op jit(solution)/shard_map/all_to_all | solution.py:355
  (4 other events, 4.4 us)

commit v7 on v6

--- a/solution.py
+++ b/solution.py
@@ -1,3 +1,4 @@
+import functools
 import math
 
 import jax
@@ -72,7 +73,7 @@
         gact[:, c * 512 : (c + 1) * 512] = nt(cot[...], w_down[c * 512 : (c + 1) * 512, :])
 
 
-def prep_mask_kernel(coord, mask, bias, pt_u, pt_k, pt_d):
+def prep_mask_kernel(coord, mask, bias):
     q = lax.broadcasted_iota(jnp.int32, (QT, KT), 0)
     k = lax.broadcasted_iota(jnp.int32, (QT, KT), 1)
     ki = k // EC
@@ -88,12 +89,15 @@
     for s in range(WINDOW * WINDOW):
         here = slot == s
         for t in range(TILES):
-            allowed[t] = jnp.where(here, mask[t, s], allowed[t])
+            allowed[t] = jnp.where(here, mask[t, 0, s], allowed[t])
     gc = coord[1] * COLS + kj - RIM
     for t in range(TILES):
         gr = coord[0] * ROWS + t * TILE + ki - RIM
         ok = (allowed[t] == 1) & (gr >= 0) & (gr < GRID_ROWS) & (gc >= 0) & (gc < GRID_COLS)
         bias[t] = jnp.where(ok, 0.0, -1e30)
+
+
+def prep_order_kernel(coord, pt_u, pt_k, pt_d):
     me = coord[2]
     lane = lax.broadcasted_iota(jnp.int32, (512, 512), 1)
     p = lax.broadcasted_iota(jnp.int32, (512, 512), 0)
@@ -195,8 +199,8 @@
 
 
 def backward_kernel(
-    coord, gm, w_out, w_qkv, q, kv, p_mid, p_out, ne, no, mid, rim_a, rim_b, tok, gain_mid, pt,
-    k_keep, k_send, gne_o, gnq_o, dq_s, dkv_s,
+    gm, w_out, q, kv, p_mid, p_out, ne, no, pt_u, pt_k,
+    k_keep, k_send, dq_s, dkv_o, dkv_s,
 ):
     ga = nt(gm[...], w_out[...]).astype(BF16)
     dkv_s[...] = jnp.zeros_like(dkv_s)
@@ -215,18 +219,22 @@
             dkv_s[rows, cols] += tn(ds, qs)
             dkv_s[rows, vcols] += tn(prob.astype(BF16), gas)
     dkv = dkv_s[...].astype(BF16)
-    dq = dq_s[...]
-    gk = nn(nt(pt[...], ne[...]).astype(BF16), dkv).astype(BF16)
-    gq = nn(nt(pt[...], no[...]).astype(BF16), dq).astype(BF16)
-    for i, part in enumerate([gq, gk[:, :D], gk[:, D:]]):
-        for j in range(16):
-            k_keep[j * 3 + i] = part[j * 16 : j * 16 + 16]
-            k_send[j * 3 + i] = part[256 + j * 16 : 256 + j * 16 + 16]
-    gne = nt(dkv, w_qkv[:, D:])
-    gnq = nt(dq, w_qkv[:, :D])
+    dkv_o[...] = dkv
+    gk = nn(nt(pt_k[...], ne[...]).astype(BF16), dkv).astype(BF16)
+    gq = nn(nt(pt_u[...], no[...]).astype(BF16), dq_s[...]).astype(BF16)
+    for at, out in ((0, k_keep), (256, k_send)):
+        out[:16] = gq[at : at + 256].reshape(16, 16, D)
+        for i in range(2):
+            for j in range(16):
+                out[16 + j * 2 + i] = gk[at + j * 16 : at + j * 16 + 16, i * D : (i + 1) * D]
+
+
+def inputs_kernel(coord, dq, dkv, w_qkv, mid, rim_a, rim_b, tok, gain_mid, gne_o, gnq_o, gain_o, send_o):
+    gne = nt(dkv[...], w_qkv[:, D:])
+    gnq = nt(dq[...], w_qkv[:, :D])
     gne_o[...] = gne[: (ROWS + 2 * RIM) * EC]
     sides = gne.reshape(ER, EC, D)[: ROWS + 2 * RIM, COLS:]
-    k_send[49:] = sides.reshape((ROWS + 2 * RIM) * COLS, D).astype(BF16).reshape(15, 16, D)
+    send_o[:15] = sides.reshape((ROWS + 2 * RIM) * COLS, D).astype(BF16).reshape(15, 16, D)
     gnq_o[...] = gnq
     gain_in = jnp.sum(gnq * unit_of(tok[...].astype(F32))[0], axis=0, keepdims=True)
     odd = coord[0] & 1
@@ -236,8 +244,8 @@
         part = gne_o[pl.ds(pl.multiple_of(at * EC, EC), size), :]
         gain_in = gain_in + jnp.sum(part * unit, axis=0, keepdims=True)
     spread = jnp.concatenate([gain_in, gain_mid[...], jnp.zeros((14, D), F32)], axis=0).astype(BF16)
-    k_keep[48] = spread
-    k_send[48] = spread
+    gain_o[...] = spread
+    send_o[15] = spread
 
 
 def add2(a, b):
@@ -249,38 +257,40 @@
     return ((a + b) + (c + d)).astype(BF16)
 
 
-def join_down_qkv_kernel(dk, dg, kk, kg, *outs):
-    gain = add2(kk[48], kg[48])
+def join_down_kv_kernel(dk, dg, kk, kg, gk, gg, *outs):
+    gain = add2(gk[...], gg[15])
     for d in range(4):
         outs[d][:16] = add2(dk[d * 16 : (d + 1) * 16], dg[d * 16 : (d + 1) * 16])
-        outs[d][16:28] = add2(kk[d * 12 : (d + 1) * 12], kg[d * 12 : (d + 1) * 12])
-        outs[d][28] = gain
-
-
-def join_up_kernel(keep, got, *outs):
-    for d in range(4):
-        outs[d][...] = add2(keep[d * 20 : (d + 1) * 20], got[d * 20 : (d + 1) * 20])
-
-
-def sum_up_kernel(*refs):
+        outs[d][16:24] = add2(kk[16 + d * 8 : 24 + d * 8], kg[16 + d * 8 : 24 + d * 8])
+        outs[d][24] = gain
+
+
+def join_up_q_kernel(which, uk, ug, kk, kg, *outs):
+    for out, d in zip(outs, which):
+        out[:20] = add2(uk[d * 20 : (d + 1) * 20], ug[d * 20 : (d + 1) * 20])
+        out[20:] = add2(kk[d * 4 : (d + 1) * 4], kg[d * 4 : (d + 1) * 4])
+
+
+def sum_up_q_kernel(*refs):
     parts, outs = refs[:4], refs[4:]
     for d in range(4):
-        outs[d][...] = add4([r[d * 5 : (d + 1) * 5] for r in parts])
-
-
-def sum_down_qkv_kernel(*refs):
+        outs[d][:5] = add4([r[d * 5 : (d + 1) * 5] for r in parts])
+        outs[d][5] = add4([r[20 + d] for r in parts])
+
+
+def sum_down_kv_kernel(*refs):
     parts, ride, outs = refs[:4], refs[4], refs[5:]
-    gain = add4([r[28] for r in parts])
+    gain = add4([r[24] for r in parts])
     for d in range(4):
         outs[d][:4] = add4([r[d * 4 : (d + 1) * 4] for r in parts])
-        outs[d][4:7] = add4([r[16 + d * 3 : 16 + (d + 1) * 3] for r in parts])
-        outs[d][7] = gain
-    outs[1][8:10] = ride[...]
+        outs[d][4:6] = add4([r[16 + d * 2 : 18 + d * 2] for r in parts])
+        outs[d][6] = gain
+    outs[1][7:9] = ride[...]
 
 
 def reduce_xy_kernel(*refs):
     out = refs[8]
-    sums = [add4([r[...] for r in refs[:4]]).reshape(-1, D), add4([r[:8] for r in refs[4:8]]).reshape(-1, D)]
+    sums = [add4([r[...] for r in refs[:4]]).reshape(-1, D), add4([r[:7] for r in refs[4:8]]).reshape(-1, D)]
     acc = jnp.concatenate(sums, axis=0)
     rows = acc.shape[0]
     i = lax.broadcasted_iota(jnp.int32, (256, rows), 0)
@@ -288,9 +298,10 @@
     z = i // 32
     r = i % 32
     up = (r % 4) * 16 + z * 2 + r // 4
-    down = 80 + z * 8 + (r - 8)
+    down = 96 + z * 8 + (r - 8)
     o = 64 + z * 2 + (r - 16)
-    qkv = 144 + ((r - 18) % 3) * 16 + z * 2 + (r - 18) // 3
+    part = (r - 18) % 3
+    qkv = jnp.where(part == 0, 80, 144 + part * 16) + z * 2 + (r - 18) // 3
     gain = 192 + (r - 24)
     src = jnp.where(r < 8, up, jnp.where(r < 16, down, jnp.where(r < 18, o, jnp.where(r < 24, qkv, gain))))
     pick = jnp.where((lane == src) & (r < 26), 1.0, 0.0).astype(BF16)
@@ -347,8 +358,12 @@
     return lax.ppermute(x, AXES, perm)
 
 
+def by(bits):
+    return [(k, k ^ bits) for k in range(256)]
+
+
 def to_three(chunks, bit):
-    return [chunks[0]] + [send(chunks[d], [(k, k ^ (bit * d)) for k in range(256)]) for d in (1, 3, 2)]
+    return [chunks[0]] + [send(chunks[d], by(bit * d)) for d in (1, 3, 2)]
 
 
 def exchange(x, groups):
@@ -361,21 +376,22 @@
     coord = jnp.stack([row, col, row * N_COL + col]).astype(jnp.int32)
     tok = tokens.reshape(TOK, D)
     cot = cotangent.reshape(TOK, D)
-    mask = tile_mask.reshape(TILES, WINDOW * WINDOW)
 
     row_odd = (row & 1) == 1
     col_odd = (col & 1) == 1
     first, last = tokens[:, :RIM], tokens[:, COLS - RIM :]
     side_b = send(jnp.where(col_odd, first, last), COL_B)
     side_a = send(jnp.where(col_odd, last, first), COL_A)
-    bias, pt_u, pt_k, pt_d = call(
-        prep_mask_kernel, [((TILES, QT, KT), F32), ((D, D), BF16), ((D, D), BF16), ((D, D), BF16)],
-        [], 2, 0, 2 * TOK * D * FF, 4_000_000, 8,
-    )(coord, mask)
-    side_a, side_b, cot, bias = lax.optimization_barrier((side_a, side_b, cot, bias))
+    (bias,) = call(
+        prep_mask_kernel, [((TILES, QT, KT), F32)], [], 2, 0, 2 * TOK * D * FF, 4_000_000, 8,
+    )(coord, tile_mask)
+    side_a, side_b, cot, bias, coord = lax.optimization_barrier((side_a, side_b, cot, bias, coord))
     mid = jnp.concatenate([tokens, side_a, side_b, jnp.zeros((ROWS, EC - COLS - 2 * RIM, D), BF16)], axis=1)
     rim_b = send(jnp.where(row_odd, mid[:RIM], mid[ROWS - RIM :]), ROW_B)
     rim_a = send(jnp.where(row_odd, mid[ROWS - RIM :], mid[:RIM]), ROW_A)
+    pt_u, pt_k, pt_d = call(
+        prep_order_kernel, [((D, D), BF16)] * 3, [], 1, 0, 2 * TOK * D * FF, 4_000_000, 8,
+    )(coord)
     (gact,) = call(
         prep_front_kernel, [((TOK, FF), F32)], [], 0, 2, 2 * TOK * D * FF, 4_000_000, 8,
     )(cot, w_down)
@@ -386,61 +402,76 @@
             ((TOK, D), BF16), ((TOK, D), BF16), ((ROWS * EC, D), BF16), ((ROWS * EC, 2 * D), BF16),
             ((2, 256, KT), F32), ((QT, D), BF16),
         ],
-        [], 0, 5, 600_000_000, 5_000_000, 16,
+        [], 0, 5, 600_000_000, 5_000_000, 10,
     )(mid, tok, gains, w_qkv, bias)
 
-    half_u, half_d, half_k = ((16, 5, 16, D), BF16), ((4, 4, 2, 32, D), BF16), ((49, 16, D), BF16)
+    half_u, half_d = ((16, 5, 16, D), BF16), ((4, 4, 2, 32, D), BF16)
+    half_q, half_k = ((16, 16, D), BF16), ((48, 16, D), BF16)
     u_keep, u_send, d_keep, d_send, gm, kv, p_out, ne, gain_mid = call(
         forward_kernel,
         [
             half_u, half_u, half_d, half_d, ((TOK, D), BF16), ((EXT, 2 * D), BF16), ((4, 256, KT), F32),
             ((EXT, D), BF16), ((1, D), F32),
         ],
-        [pltpu.VMEM((TOK, D), BF16)], 1, 16, 4_000_000_000, 20_000_000, 24,
+        [pltpu.VMEM((TOK, D), BF16)], 1, 16, 4_000_000_000, 20_000_000, 16,
     )(coord, rim_a, rim_b, tok, cot, gains, w_qkv, w_out, w_up, gact, bias, pt_u, pt_d, q, ne_mid, kv_mid, attn_mid)
 
     u_got = send(u_send, CORE_SWAP)
     d_got = send(d_send, CORE_SWAP)
-    k_keep, k_send, gne, gnq = call(
+    k_keep, k_send, dq, dkv = call(
         backward_kernel,
-        [half_k, ((64, 16, D), BF16), (((ROWS + 2 * RIM) * EC, D), F32), ((TOK, D), F32)],
-        [pltpu.VMEM((TOK, D), BF16), pltpu.VMEM((EXT, 2 * D), F32)], 1, 15, 3_000_000_000, 12_000_000, 20,
-    )(coord, gm, w_out, w_qkv, q, kv, p_mid, p_out, ne, no, mid, rim_a, rim_b, tok, gain_mid, pt_k)
+        [half_k, half_k, ((TOK, D), BF16), ((EXT, 2 * D), BF16)],
+        [pltpu.VMEM((EXT, 2 * D), F32)], 0, 10, 2_500_000_000, 10_000_000, 12,
+    )(gm, w_out, q, kv, p_mid, p_out, ne, no, pt_u, pt_k)
     u_got, d_got, k_send = lax.optimization_barrier((u_got, d_got, k_send))
-
-    def place(x, axis, at_end, size):
+    k_got = send(k_send, CORE_SWAP)
+    gne, gnq, g_keep, g_send = call(
+        inputs_kernel,
+        [(((ROWS + 2 * RIM) * EC, D), F32), ((TOK, D), F32), ((16, D), BF16), half_q],
+        [], 1, 8, 600_000_000, 4_000_000, 6,
+    )(coord, dq, dkv, w_qkv, mid, rim_a, rim_b, tok, gain_mid)
+    g_got = send(g_send, CORE_SWAP)
+
+    def place(x, axis, odd, end_if_odd, size):
         gap = size - RIM
         after = [(0, 0)] * 3
         before = [(0, 0)] * 3
         after[axis], before[axis] = (0, gap), (gap, 0)
         x = x.astype(F32)
-        return jnp.where(at_end, jnp.pad(x, before), jnp.pad(x, after))
+        x_odd, x_even = (before, after) if end_if_odd else (after, before)
+        return jnp.where(odd, jnp.pad(x, x_odd), jnp.pad(x, x_even))
 
     def join(body, ins, outs):
-        return list(call(body, [(o, BF16) for o in outs], [], 0, len(ins), 1_000_000, 4_000_000, 12)(*ins))
-
-    k_got = send(k_send, CORE_SWAP)
+        return list(call(body, [(o, BF16) for o in outs], [], 0, len(ins), 1_000_000, 4_000_000, 6)(*ins))
+
+    def join_up(which, got):
+        ins = [u_keep.reshape(80, 16, D), got.reshape(80, 16, D), k_keep, k_got]
+        return join(functools.partial(join_up_q_kernel, which), ins, [(24, 16, D)] * len(which))
+
+    u0, u1, u2, u3 = join_up((0, 1, 2, 3), u_got)
+    d_got, u0, u1, u2, u3 = lax.optimization_barrier((d_got, u0, u1, u2, u3))
+    b = join(
+        join_down_kv_kernel, [d_keep.reshape(64, 16, D), d_got.reshape(64, 16, D), k_keep, k_got, g_keep, g_got],
+        [(25, 16, D)] * 4,
+    )
     gne3 = gne.reshape(ROWS + 2 * RIM, EC, D)
     back_a = send(gne3[:, COLS : COLS + RIM].astype(BF16), COL_A)
-    b = join(
-        join_down_qkv_kernel, [d_keep.reshape(64, 16, D), d_got.reshape(64, 16, D), k_keep, k_got], [(29, 16, D)] * 4,
-    )
-    u_got, *b = lax.optimization_barrier((u_got, *b))
+    u1, u3 = send(u1, by(X_BIT)), send(u3, by(3 * X_BIT))
     b = to_three(b, Y_BIT)
-    u = join(join_up_kernel, [u_keep.reshape(80, 16, D), u_got.reshape(80, 16, D)], [(20, 16, D)] * 4)
-    u = to_three(u, X_BIT)
-    back_b = k_got[49:].reshape(ROWS + 2 * RIM, COLS, D)[:, RIM : 2 * RIM]
-    own = gne3[:, :COLS] + place(back_a, 1, col_odd, COLS) + place(back_b, 1, ~col_odd, COLS)
+    u1, u2, back_a, g_got = lax.optimization_barrier((u1, u2, back_a, g_got))
+    u = [u0, u1, u3, send(u2, by(2 * X_BIT))]
+    back_b = g_got[:15].reshape(ROWS + 2 * RIM, COLS, D)[:, RIM : 2 * RIM]
+    own = gne3[:, :COLS] + place(back_a, 1, col_odd, True, COLS) + place(back_b, 1, col_odd, False, COLS)
     head, tail = own[:RIM].astype(BF16), own[RIM + ROWS :].astype(BF16)
     ride = jnp.pad(jnp.where(row_odd, head, tail), ((0, 1), (0, 0), (0, 0))).reshape(2, 16, D)
     u, b, ride = lax.optimization_barrier((u, b, ride))
-    b = join(sum_down_qkv_kernel, [*b, ride], [(8, 16, D), (10, 16, D), (8, 16, D), (8, 16, D)])
+    b = join(sum_down_kv_kernel, [*b, ride], [(7, 16, D), (9, 16, D), (7, 16, D), (7, 16, D)])
     b = to_three(b, X_BIT)
-    u = join(sum_up_kernel, u, [(5, 16, D)] * 4)
+    u = join(sum_up_q_kernel, u, [(6, 16, D)] * 4)
     u = to_three(u, Y_BIT)
-    up_b = b[1][8:].reshape(4, COLS, D)[:RIM]
+    up_b = b[1][7:].reshape(4, COLS, D)[:RIM]
     (spread,) = call(
-        reduce_xy_kernel, [((8, 32, D), BF16)], [], 0, 8, 60_000_000, 4_000_000, 12,
+        reduce_xy_kernel, [((8, 32, D), BF16)], [], 0, 8, 60_000_000, 4_000_000, 5,
     )(*u, *b)
     got_z = exchange(spread, Z_GROUPS)
     g_up, g_down, g_out, g_qkv, g_gains = call(
@@ -450,7 +481,7 @@
     )(got_z)
 
     up_a = send(jnp.where(row_odd, tail, head), ROW_A)
-    gn = own[RIM : RIM + ROWS] + place(up_a, 0, row_odd, ROWS) + place(up_b, 0, ~row_odd, ROWS)
+    gn = own[RIM : RIM + ROWS] + place(up_a, 0, row_odd, True, ROWS) + place(up_b, 0, row_odd, False, ROWS)
     gn = gn + gnq.reshape(ROWS, COLS, D)
     unit, inv = unit_of(tokens.astype(F32))
     g1 = gn * gains[0]

time: 109 us -> 107 us (0.982)
  waiting for transfers between devices: 31.6 us -> 33.8 us
  starting transfers between devices: 48.5 us -> 46.8 us
  local copies, waits for them, and re-layouts: 2.97 us -> 1.39 us
  Pallas kernels: 21.4 us -> 20.3 us
    ppermute x21 -> x22, waiting for transfers between devices: 21.5 us -> 24.5 us  [send(): return lax.ppermute(x, AXES, perm)]
    all_to_all x1, starting transfers between devices: 6.39 us -> 3.41 us  [exchange(): return lax.all_to_all(x, AXES, 0, 0, axis_index_groups=groups, tiled=True)]
    ppermute x21 -> x22, starting transfers between devices: 42.1 us -> 43.4 us  [send(): return lax.ppermute(x, AXES, perm)]
    pallas_call x7 -> x9, Pallas kernels: 11.3 us -> 10.2 us  [the longest x1 4.02 us: per_device(): call(backward_kernel, [half_k, half_k, ((TOK, D), BF16), ((EXT, 2 * D), B...]
    unnamed x29 -> x16, local copies, waits for them, and re-layouts: 2.19 us -> 1.25 us
  transfers between devices with their start and end apart: 22 -> 23, of which waited for: 6 -> 6; matrix products, arithmetic and copies ran while one was open for 3% -> 2% of each run, Pallas kernels for 12% -> 11%
where the time goes in v7:
time: 107 us; the launch traced here: 106 us
  starting transfers between devices  46.8 us (44%)
  waiting for transfers between devices  33.8 us (32%)
  Pallas kernels  20.3 us (19%)
  other arithmetic  2.93 us (3%)
  local copies, waits for them, and re-layouts  1.39 us (1%)
    ppermute x22, starting transfers between devices, send(): return lax.ppermute(x, AXES, perm)  43.4 us
    ppermute x22, waiting for transfers between devices, send(): return lax.ppermute(x, AXES, perm)  24.5 us
    all_to_all x1, waiting for transfers between devices, exchange(): return lax.all_to_all(x, AXES, 0, 0, axis_index_groups=groups, tiled=True)  9.27 us
    pallas_call x1, Pallas kernels, per_device(): call(forward_kernel, [half_u, half_u, half_d, half_d, ((TOK, D), BF16), (...  6.99 us
    pallas_call x1, Pallas kernels, per_device(): call(backward_kernel, [half_k, half_k, ((TOK, D), BF16), ((EXT, 2 * D), B...  4.02 us
    all_to_all x1, starting transfers between devices, exchange(): return lax.all_to_all(x, AXES, 0, 0, axis_index_groups=groups, tiled=True)  3.41 us
  transfers between devices with their start and end apart: 23, of which 6 were waited for; matrix products, arithmetic and copies ran while one was open for 2% of the time, Pallas kernels for 11%

profile of v7, /device:TPU:8, one launch (start us, length us, event | category | flops | bytes accessed | tf_op | source)
XLA Modules:
  0.0 106.2 jit_solution(7907308255375523204)
XLA Ops:
  0.6 1.2 %broadcast_select_fusion = (bf16[24,3,512]{2,1,0:T(4,128)(2,1)S(1)}, bf16[24,3,512]{2,1,0:T(4,128)(2,1)S(1)}) fusion(pred[]{:T(512)S(6)} %eq.6, bf16[24,8,512]{2,1,0:T(8,128)(2,1)} %param.8), kind=kLoop, calls=%fused_computation.19 | loop fusion | flops 73728 | bytes 294913 | tf_op jit(solution)/shard_map/jit(_where)/select_n | solution.py:383
  1.8 5.9 %collective-permute-start = (bf16[24,3,512]{2,1,0:T(4,128)(2,1)S(1)}, bf16[24,3,512]{2,1,0:T(4,128)(2,1)S(1)}, u32[]{:S(2)}, u32[]{:S(2)}) collective-permute-start(bf16[24,3,512]{2,1,0:T(4,128)(2,1)S(1)} %get-tuple-element.159), channel_id=1, source_target_pairs={{1,2},{2,1},{3,4},{4,3},{5,6},{6,5},{7,8},{8,7},{9,10},{10,9},{11,... | collective-permute-start | bytes 221192 | tf_op jit(solution)/shard_map/ppermute | solution.py:358
  8.0 0.7 copy-done.7
  8.6 1.2 %shard_map.127.bias = f32[3,64,256]{2,1,0:T(8,128)S(1)} custom-call(s32[3]{0:T(128)S(1)} %pad_add_fusion.coord, s32[3,1,49]{2,1,0:T(1,128)S(1)} %copy-done.7), custom_call_target="tpu_custom_call" | custom-call | flops 402653184 | bytes 4000000 | tf_op jit(solution)/shard_map/pallas_call | solution.py:385
  9.9 1.3 %collective-permute-done = bf16[24,3,512]{2,1,0:T(4,128)(2,1)S(1)} collective-permute-done((bf16[24,3,512]{2,1,0:T(4,128)(2,1)S(1)}, bf16[24,3,512]{2,1,0:T(4,128)(2,1)S(1)}, u32[]{:S(2)}, u32[]{:S(2)}) %collective-permute-start) | collective-permute-done | bytes 73760 | tf_op jit(solution)/shard_map/ppermute | solution.py:358
  11.4 0.7 collective-permute-start.2
  12.1 4.3 %collective-permute-start.3 = (bf16[3,16,512]{2,1,0:T(8,128)(2,1)S(1)}, bf16[3,16,512]{2,1,0:T(8,128)(2,1)S(1)}, u32[]{:S(2)}, u32[]{:S(2)}) collective-permute-start(bf16[3,16,512]{2,1,0:T(8,128)(2,1)S(1)} %get-tuple-element.154), channel_id=1, source_target_pairs={{0,32},{1,33},{2,34},{3,35},{4,36},{5,37},{6,38},{7,39},{8,40},{9,... | collective-permute-start | bytes 147464 | tf_op jit(solution)/shard_map/ppermute | solution.py:358
  16.4 1.3 %shard_map.129 = (bf16[512,512]{1,0:T(8,128)(2,1)S(1)}, bf16[512,512]{1,0:T(8,128)(2,1)S(1)}, bf16[512,512]{1,0:T(8,128)(2,1)S(1)}) custom-call(s32[3]{0:T(128)S(1)} %pad_add_fusion.coord), custom_call_target="tpu_custom_call" | custom-call | flops 402653184 | bytes 4000000 | tf_op jit(solution)/shard_map/pallas_call | solution.py:392
  17.8 0.8 shard_map.128.gact
  18.6 0.5 copy-done.1
  19.1 1.6 %shard_map.130 = (bf16[192,512]{1,0:T(8,128)(2,1)S(1)}, bf16[192,512]{1,0:T(8,128)(2,1)S(1)}, bf16[384,512]{1,0:T(8,128)(2,1)S(1)}, bf16[384,1024]{1,0:T(8,128)(...) custom-call(bf16[24,16,512]{2,1,0:T(8,128)(2,1)S(1)} %maximum_maximum_fusion.mid, ...), custom_call_target="tpu_custom_call" | custom-call | flops 600000000 | bytes 5000000 | tf_op jit(solution)/shard_map/pallas_call | solution.py:399
  20.8 7.0 %shard_map.131 = (bf16[16,5,16,512]{3,2,1,0:T(8,128)(2,1)S(1)}, bf16[16,5,16,512]{3,2,1,0:T(8,128)(2,1)S(1)}, bf16[4,4,2,32,512]{4,3,2,1,0:T(8,128)(2,1)S(1)}, b...) custom-call(s32[3]{0:T(128)S(1)} %pad_add_fusion.coord, ...), custom_call_target="tpu_custom_call" | custom-call | flops 4000000000 | bytes 20000000 | tf_op jit(solution)/shard_map/pallas_call | solution.py:410
  28.4 4.0 %shard_map.132 = (bf16[48,16,512]{2,1,0:T(8,128)(2,1)S(1)}, bf16[48,16,512]{2,1,0:T(8,128)(2,1)S(1)}, bf16[192,512]{1,0:T(8,128)(2,1)S(1)}, bf16[512,1024]{1,0:T(8,128)(2,1)S(1)}) custom-call(bf16[192,512]{1,0:T(8,128)(2,1)S(1)} %get-tuple-element.90.gm, bf16[512,512]{1,0:T(8,128)(2,1)S(1)} %copy-done.6, bf16[192,512]{1,0:T(8,128)(2,1)S(1)} %get-tuple-element.86.q_i.q, ...), custom_call_target="tpu_custom_call" | custom-call | flops 2500000000 | bytes 10000000 | tf_op jit(solution)/shard_map/pallas_call | solution.py:421
  32.8 2.0 %collective-permute-done.6.kg = bf16[48,16,512]{2,1,0:T(8,128)(2,1)S(1)} collective-permute-done((bf16[48,16,512]{2,1,0:T(8,128)(2,1)S(1)}, bf16[48,16,512]{2,1,0:T(8,128)(2,1)S(1)}, u32[]{:S(2)}, u32[]{:S(2)}) %collective-permute-start.6) | collective-permute-done | bytes 786464 | tf_op jit(solution)/shard_map/ppermute | solution.py:358
  35.3 1.5 %shard_map.133 = (f32[480,512]{1,0:T(8,128)S(1)}, f32[192,512]{1,0:T(8,128)S(1)}, bf16[16,512]{1,0:T(8,128)(2,1)S(1)}, bf16[16,16,512]{2,1,0:T(8,128)(2,1)S(1)}) custom-call(s32[3]{0:T(128)S(1)} %pad_add_fusion.coord, bf16[192,512]{1,0:T(8,128)(2,1)S(1)} %get-tuple-element.97.dq, bf16[512,1024]{1,0:T(8,128)(2,1)S(1)} %get-tuple-element.98.dkv, ...), custom_call_target="tpu_custom_call" | custom-call | flops 600000000 | bytes 4000000 | tf_op jit(solution)/shard_map/pallas_call | solution.py:428
  37.2 4.8 %collective-permute-start.8 = (bf16[30,3,512]{2,1,0:T(4,128)(2,1)S(1)}, bf16[30,3,512]{2,1,0:T(4,128)(2,1)S(1)}, u32[]{:S(2)}, u32[]{:S(2)}) collective-permute-start(bf16[30,3,512]{2,1,0:T(4,128)(2,1)S(1)} %slice.100), channel_id=1, source_target_pairs={{1,2},{2,1},{3,4},{4,3},{5,6},{6,5},{7,8},{8,7},{9,10},{10,9},{11,... | collective-permute-start | bytes 276488 | tf_op jit(solution)/shard_map/ppermute | solution.py:358
  42.5 3.1 %collective-permute-start.14 = (bf16[25,16,512]{2,1,0:T(8,128)(2,1)S(1)}, bf16[25,16,512]{2,1,0:T(8,128)(2,1)S(1)}, u32[]{:S(2)}, u32[]{:S(2)}) collective-permute-start(bf16[25,16,512]{2,1,0:T(8,128)(2,1)S(1)} %get-tuple-element.127), channel_id=1, source_target_pairs={{0,24},{1,25},{2,26},{3,27},{4,28},{5,29},{6,30},{7,31},{8,16},{9,... | collective-permute-start | bytes 1228808 | tf_op jit(solution)/shard_map/ppermute | solution.py:358
  45.6 0.9 collective-permute-start.15
  46.6 7.5 %collective-permute-start.11 = (bf16[24,16,512]{2,1,0:T(8,128)(2,1)S(1)}, bf16[24,16,512]{2,1,0:T(8,128)(2,1)S(1)}, u32[]{:S(2)}, u32[]{:S(2)}) collective-permute-start(bf16[24,16,512]{2,1,0:T(8,128)(2,1)S(1)} %get-tuple-element.120), channel_id=1, source_target_pairs={{0,96},{1,97},{2,98},{3,99},{4,100},{5,101},{6,102},{7,103},{8,104... | collective-permute-start | bytes 1179656 | tf_op jit(solution)/shard_map/ppermute | solution.py:358
  54.6 15.2 %collective-permute-done.11.refs_2_ = bf16[24,16,512]{2,1,0:T(8,128)(2,1)S(1)} collective-permute-done((bf16[24,16,512]{2,1,0:T(8,128)(2,1)S(1)}, bf16[24,16,512]{2,1,0:T(8,128)(2,1)S(1)}, u32[]{:S(2)}, u32[]{:S(2)}) %collective-permute-start.11) | collective-permute-done | bytes 393248 | tf_op jit(solution)/shard_map/ppermute | solution.py:358
  69.7 0.7 collective-permute-start.10
  71.1 2.7 %collective-permute-start.18 = (bf16[6,16,512]{2,1,0:T(8,128)(2,1)S(1)}, bf16[6,16,512]{2,1,0:T(8,128)(2,1)S(1)}, u32[]{:S(2)}, u32[]{:S(2)}) collective-permute-start(bf16[6,16,512]{2,1,0:T(8,128)(2,1)S(1)} %get-tuple-element.142), channel_id=1, source_target_pairs={{0,24},{1,25},{2,26},{3,27},{4,28},{5,29},{6,30},{7,31},{8,16},{9,... | collective-permute-start | bytes 294920 | tf_op jit(solution)/shard_map/ppermute | solution.py:358
  73.8 1.2 %collective-permute-start.19 = (bf16[6,16,512]{2,1,0:T(8,128)(2,1)S(1)}, bf16[6,16,512]{2,1,0:T(8,128)(2,1)S(1)}, u32[]{:S(2)}, u32[]{:S(2)}) collective-permute-start(bf16[6,16,512]{2,1,0:T(8,128)(2,1)S(1)} %get-tuple-element.143), channel_id=1, source_target_pairs={{0,16},{1,17},{2,18},{3,19},{4,20},{5,21},{6,22},{7,23},{8,24},{9,... | collective-permute-start | bytes 294920 | tf_op jit(solution)/shard_map/ppermute | solution.py:358
  75.2 2.5 %collective-permute-start.16 = (bf16[9,16,512]{2,1,0:T(8,128)(2,1)S(1)}, bf16[9,16,512]{2,1,0:T(8,128)(2,1)S(1)}, u32[]{:S(2)}, u32[]{:S(2)}) collective-permute-start(bf16[9,16,512]{2,1,0:T(8,128)(2,1)S(1)} %get-tuple-element.134), channel_id=1, source_target_pairs={{0,32},{1,33},{2,34},{3,35},{4,36},{5,37},{6,38},{7,39},{8,40},{9,... | collective-permute-start | bytes 442376 | tf_op jit(solution)/shard_map/ppermute | solution.py:358
  77.7 6.7 %collective-permute-start.20 = (bf16[7,16,512]{2,1,0:T(8,128)(2,1)S(1)}, bf16[7,16,512]{2,1,0:T(8,128)(2,1)S(1)}, u32[]{:S(2)}, u32[]{:S(2)}) collective-permute-start(bf16[7,16,512]{2,1,0:T(8,128)(2,1)S(1)} %get-tuple-element.145), channel_id=1, source_target_pairs={{0,96},{1,97},{2,98},{3,99},{4,100},{5,101},{6,102},{7,103},{8,104... | collective-permute-start | bytes 344072 | tf_op jit(solution)/shard_map/ppermute | solution.py:358
  84.7 3.6 %collective-permute-done.20.refs_6_ = bf16[7,16,512]{2,1,0:T(8,128)(2,1)S(1)} collective-permute-done((bf16[7,16,512]{2,1,0:T(8,128)(2,1)S(1)}, bf16[7,16,512]{2,1,0:T(8,128)(2,1)S(1)}, u32[]{:S(2)}, u32[]{:S(2)}) %collective-permute-start.20) | collective-permute-done | bytes 114720 | tf_op jit(solution)/shard_map/ppermute | solution.py:358
  88.3 2.4 %collective-permute-done.21.refs_7_ = bf16[7,16,512]{2,1,0:T(8,128)(2,1)S(1)} collective-permute-done((bf16[7,16,512]{2,1,0:T(8,128)(2,1)S(1)}, bf16[7,16,512]{2,1,0:T(8,128)(2,1)S(1)}, u32[]{:S(2)}, u32[]{:S(2)}) %collective-permute-start.21) | collective-permute-done | bytes 114720 | tf_op jit(solution)/shard_map/ppermute | solution.py:358
  90.7 1.0 shard_map.138
  91.8 3.4 %all-to-all-start = ((bf16[8,32,512]{2,1,0:T(8,128)(2,1)}), bf16[8,32,512]{2,1,0:T(8,128)(2,1)S(1)}, u32[]{:S(2)}, u32[]{:S(2)}) async-start(bf16[8,32,512]{2,1,0:T(8,128)(2,1)} %shard_map.138), calls=%async_computation | async-start | bytes 524288 | tf_op jit(solution)/shard_map/all_to_all | solution.py:370
  95.4 0.9 fusion.7
  96.3 9.3 %all-to-all-done.got = bf16[8,32,512]{2,1,0:T(8,128)(2,1)S(1)} async-done(((bf16[8,32,512]{2,1,0:T(8,128)(2,1)}), bf16[8,32,512]{2,1,0:T(8,128)(2,1)S(1)}, u32[]{:S(2)}, u32[]{:S(2)}) %all-to-all-start) | async-done | bytes 262176 | tf_op jit(solution)/shard_map/all_to_all | solution.py:370
  105.6 0.7 shard_map.139
  (65 shorter events, 4.6 us)
Async XLA Ops:
  0.6 10.6 %copy-start = (bf16[24,8,512]{2,1,0:T(8,128)(2,1)S(1)}, bf16[24,8,512]{2,1,0:T(8,128)(2,1)}, u32[]{:S(2)}) copy-start(bf16[24,8,512]{2,1,0:T(8,128)(2,1)} %param.8) | copy-start | bytes 589828
  1.8 9.4 %collective-permute-start = (bf16[24,3,512]{2,1,0:T(4,128)(2,1)S(1)}, bf16[24,3,512]{2,1,0:T(4,128)(2,1)S(1)}, u32[]{:S(2)}, u32[]{:S(2)}) collective-permute-start(bf16[24,3,512]{2,1,0:T(4,128)(2,1)S(1)} %get-tuple-element.159), channel_id=1, source_target_pairs={{1,2},{2,1},{3,4},{4,3},{5,6},{6,5},{7,8},{8,7},{9,10},{10,9},{11,... | collective-permute-start | bytes 221192 | tf_op jit(solution)/shard_map/ppermute | solution.py:358
  7.7 3.5 %collective-permute-start.1 = (bf16[24,3,512]{2,1,0:T(4,128)(2,1)S(1)}, bf16[24,3,512]{2,1,0:T(4,128)(2,1)S(1)}, u32[]{:S(2)}, u32[]{:S(2)}) collective-permute-start(bf16[24,3,512]{2,1,0:T(4,128)(2,1)S(1)} %get-tuple-element.158), channel_id=1, source_target_pairs={{0,1},{1,0},{2,3},{3,2},{4,5},{5,4},{6,7},{7,6},{8,9},{9,8},{10,11... | collective-permute-start | bytes 221192 | tf_op jit(solution)/shard_map/ppermute | solution.py:358
  8.0 0.7 copy-start.7
  9.9 7.8 %copy-start.2 = (bf16[2048,512]{1,0:T(8,128)(2,1)S(1)}, bf16[2048,512]{1,0:T(8,128)(2,1)}, u32[]{:S(2)}) copy-start(bf16[2048,512]{1,0:T(8,128)(2,1)} %w_down.1) | copy-start | bytes 6291460
  9.9 7.8 %copy-start.3 = (bf16[24,8,512]{2,1,0:T(8,128)(2,1)S(1)}, bf16[24,8,512]{2,1,0:T(8,128)(2,1)}, u32[]{:S(2)}) copy-start(bf16[24,8,512]{2,1,0:T(8,128)(2,1)} %param.9) | copy-start | bytes 589828
  11.4 9.4 %collective-permute-start.2 = (bf16[3,16,512]{2,1,0:T(8,128)(2,1)S(1)}, bf16[3,16,512]{2,1,0:T(8,128)(2,1)S(1)}, u32[]{:S(2)}, u32[]{:S(2)}) collective-permute-start(bf16[3,16,512]{2,1,0:T(8,128)(2,1)S(1)} %get-tuple-element.155), channel_id=1, source_target_pairs={{32,64},{33,65},{34,66},{35,67},{36,68},{37,69},{38,70},{39,71},{4... | collective-permute-start | bytes 147464 | tf_op jit(solution)/shard_map/ppermute | solution.py:358
  12.1 8.7 %collective-permute-start.3 = (bf16[3,16,512]{2,1,0:T(8,128)(2,1)S(1)}, bf16[3,16,512]{2,1,0:T(8,128)(2,1)S(1)}, u32[]{:S(2)}, u32[]{:S(2)}) collective-permute-start(bf16[3,16,512]{2,1,0:T(8,128)(2,1)S(1)} %get-tuple-element.154), channel_id=1, source_target_pairs={{0,32},{1,33},{2,34},{3,35},{4,36},{5,37},{6,38},{7,39},{8,40},{9,... | collective-permute-start | bytes 147464 | tf_op jit(solution)/shard_map/ppermute | solution.py:358
  17.7 1.4 %copy-start.1 = (bf16[512,1536]{1,0:T(8,128)(2,1)S(1)}, bf16[512,1536]{1,0:T(8,128)(2,1)}, u32[]{:S(2)}) copy-start(bf16[512,1536]{1,0:T(8,128)(2,1)} %w_qkv.5) | copy-start | bytes 4718596
  17.7 1.4 %copy-start.4 = (f32[2,512]{1,0:T(2,128)S(1)}, f32[2,512]{1,0:T(2,128)}, u32[]{:S(2)}) copy-start(f32[2,512]{1,0:T(2,128)} %gains.3) | copy-start | bytes 12292
  17.8 3.1 %copy-start.6 = (bf16[512,512]{1,0:T(8,128)(2,1)S(1)}, bf16[512,512]{1,0:T(8,128)(2,1)}, u32[]{:S(2)}) copy-start(bf16[512,512]{1,0:T(8,128)(2,1)} %w_out.3) | copy-start | bytes 1572868
  18.6 2.2 %copy-start.5 = (bf16[512,2048]{1,0:T(8,128)(2,1)S(1)}, bf16[512,2048]{1,0:T(8,128)(2,1)}, u32[]{:S(2)}) copy-start(bf16[512,2048]{1,0:T(8,128)(2,1)} %w_up.1) | copy-start | bytes 6291460
  27.8 4.6 %collective-permute-start.4 = (bf16[16,5,16,512]{3,2,1,0:T(8,128)(2,1)S(1)}, bf16[16,5,16,512]{3,2,1,0:T(8,128)(2,1)S(1)}, u32[]{:S(2)}, u32[]{:S(2)}) collective-permute-start(bf16[16,5,16,512]{3,2,1,0:T(8,128)(2,1)S(1)} %get-tuple-element.101), channel_id=1, source_target_pairs={{0,1},{1,0},{2,3},{3,2},{4,5},{5,4},{6,7},{7,6},{8,9},{9,8},{10,11... | collective-permute-start | bytes 3932168 | tf_op jit(solution)/shard_map/ppermute | solution.py:358
  27.9 4.5 %collective-permute-start.5 = (bf16[4,4,2,32,512]{4,3,2,1,0:T(8,128)(2,1)S(1)}, bf16[4,4,2,32,512]{4,3,2,1,0:T(8,128)(2,1)S(1)}, u32[]{:S(2)}, u32[]{:S(2)}) collective-permute-start(bf16[4,4,2,32,512]{4,3,2,1,0:T(8,128)(2,1)S(1)} %get-tuple-element.102), channel_id=1, source_target_pairs={{0,1},{1,0},{2,3},{3,2},{4,5},{5,4},{6,7},{7,6},{8,9},{9,8},{10,11... | collective-permute-start | bytes 3145736 | tf_op jit(solution)/shard_map/ppermute | solution.py:358
  32.5 2.4 %collective-permute-start.6 = (bf16[48,16,512]{2,1,0:T(8,128)(2,1)S(1)}, bf16[48,16,512]{2,1,0:T(8,128)(2,1)S(1)}, u32[]{:S(2)}, u32[]{:S(2)}) collective-permute-start(bf16[48,16,512]{2,1,0:T(8,128)(2,1)S(1)} %get-tuple-element.108), channel_id=1, source_target_pairs={{0,1},{1,0},{2,3},{3,2},{4,5},{5,4},{6,7},{7,6},{8,9},{9,8},{10,11... | collective-permute-start | bytes 2359304 | tf_op jit(solution)/shard_map/ppermute | solution.py:358
  35.2 18.9 %collective-permute-start.7 = (bf16[24,16,512]{2,1,0:T(8,128)(2,1)S(1)}, bf16[24,16,512]{2,1,0:T(8,128)(2,1)S(1)}, u32[]{:S(2)}, u32[]{:S(2)}) collective-permute-start(bf16[24,16,512]{2,1,0:T(8,128)(2,1)S(1)} %get-tuple-element.113), channel_id=1, source_target_pairs={{0,32},{1,33},{2,34},{3,35},{4,36},{5,37},{6,38},{7,39},{8,40},{9,... | collective-permute-start | bytes 1179656 | tf_op jit(solution)/shard_map/ppermute | solution.py:358
  36.8 5.2 %collective-permute-start.9 = (bf16[16,16,512]{2,1,0:T(8,128)(2,1)S(1)}, bf16[16,16,512]{2,1,0:T(8,128)(2,1)S(1)}, u32[]{:S(2)}, u32[]{:S(2)}) collective-permute-start(bf16[16,16,512]{2,1,0:T(8,128)(2,1)S(1)} %get-tuple-element.115), channel_id=1, source_target_pairs={{0,1},{1,0},{2,3},{3,2},{4,5},{5,4},{6,7},{7,6},{8,9},{9,8},{10,11... | collective-permute-start | bytes 786440 | tf_op jit(solution)/shard_map/ppermute | solution.py:358
  37.2 9.4 %collective-permute-start.8 = (bf16[30,3,512]{2,1,0:T(4,128)(2,1)S(1)}, bf16[30,3,512]{2,1,0:T(4,128)(2,1)S(1)}, u32[]{:S(2)}, u32[]{:S(2)}) collective-permute-start(bf16[30,3,512]{2,1,0:T(4,128)(2,1)S(1)} %slice.100), channel_id=1, source_target_pairs={{1,2},{2,1},{3,4},{4,3},{5,6},{6,5},{7,8},{8,7},{9,10},{10,9},{11,... | collective-permute-start | bytes 276488 | tf_op jit(solution)/shard_map/ppermute | solution.py:358
  42.4 28.0 %collective-permute-start.13 = (bf16[25,16,512]{2,1,0:T(8,128)(2,1)S(1)}, bf16[25,16,512]{2,1,0:T(8,128)(2,1)S(1)}, u32[]{:S(2)}, u32[]{:S(2)}) collective-permute-start(bf16[25,16,512]{2,1,0:T(8,128)(2,1)S(1)} %get-tuple-element.126), channel_id=1, source_target_pairs={{0,8},{1,9},{2,10},{3,11},{4,12},{5,13},{6,14},{7,15},{8,0},{9,1},... | collective-permute-start | bytes 1228808 | tf_op jit(solution)/shard_map/ppermute | solution.py:358
  42.5 27.9 %collective-permute-start.14 = (bf16[25,16,512]{2,1,0:T(8,128)(2,1)S(1)}, bf16[25,16,512]{2,1,0:T(8,128)(2,1)S(1)}, u32[]{:S(2)}, u32[]{:S(2)}) collective-permute-start(bf16[25,16,512]{2,1,0:T(8,128)(2,1)S(1)} %get-tuple-element.127), channel_id=1, source_target_pairs={{0,24},{1,25},{2,26},{3,27},{4,28},{5,29},{6,30},{7,31},{8,16},{9,... | collective-permute-start | bytes 1228808 | tf_op jit(solution)/shard_map/ppermute | solution.py:358
  45.6 24.8 %collective-permute-start.15 = (bf16[25,16,512]{2,1,0:T(8,128)(2,1)S(1)}, bf16[25,16,512]{2,1,0:T(8,128)(2,1)S(1)}, u32[]{:S(2)}, u32[]{:S(2)}) collective-permute-start(bf16[25,16,512]{2,1,0:T(8,128)(2,1)S(1)} %get-tuple-element.128), channel_id=1, source_target_pairs={{0,16},{1,17},{2,18},{3,19},{4,20},{5,21},{6,22},{7,23},{8,24},{9,... | collective-permute-start | bytes 1228808 | tf_op jit(solution)/shard_map/ppermute | solution.py:358
  46.6 23.2 %collective-permute-start.11 = (bf16[24,16,512]{2,1,0:T(8,128)(2,1)S(1)}, bf16[24,16,512]{2,1,0:T(8,128)(2,1)S(1)}, u32[]{:S(2)}, u32[]{:S(2)}) collective-permute-start(bf16[24,16,512]{2,1,0:T(8,128)(2,1)S(1)} %get-tuple-element.120), channel_id=1, source_target_pairs={{0,96},{1,97},{2,98},{3,99},{4,100},{5,101},{6,102},{7,103},{8,104... | collective-permute-start | bytes 1179656 | tf_op jit(solution)/shard_map/ppermute | solution.py:358
  54.2 16.3 %collective-permute-start.12 = (bf16[24,16,512]{2,1,0:T(8,128)(2,1)S(1)}, bf16[24,16,512]{2,1,0:T(8,128)(2,1)S(1)}, u32[]{:S(2)}, u32[]{:S(2)}) collective-permute-start(bf16[24,16,512]{2,1,0:T(8,128)(2,1)S(1)} %get-tuple-element.121), channel_id=1, source_target_pairs={{0,64},{1,65},{2,66},{3,67},{4,68},{5,69},{6,70},{7,71},{8,72},{9,... | collective-permute-start | bytes 1179656 | tf_op jit(solution)/shard_map/ppermute | solution.py:358
  69.7 8.0 %collective-permute-start.10 = (bf16[3,8,512]{2,1,0:T(8,128)(2,1)S(1)}, bf16[3,8,512]{2,1,0:T(8,128)(2,1)S(1)}, u32[]{:S(2)}, u32[]{:S(2)}) collective-permute-start(bf16[3,8,512]{2,1,0:T(8,128)(2,1)S(1)} %get-tuple-element.156), channel_id=1, source_target_pairs={{32,64},{33,65},{34,66},{35,67},{36,68},{37,69},{38,70},{39,71},{4... | collective-permute-start | bytes 73736 | tf_op jit(solution)/shard_map/ppermute | solution.py:358
  70.6 13.8 %collective-permute-start.17 = (bf16[6,16,512]{2,1,0:T(8,128)(2,1)S(1)}, bf16[6,16,512]{2,1,0:T(8,128)(2,1)S(1)}, u32[]{:S(2)}, u32[]{:S(2)}) collective-permute-start(bf16[6,16,512]{2,1,0:T(8,128)(2,1)S(1)} %get-tuple-element.141), channel_id=1, source_target_pairs={{0,8},{1,9},{2,10},{3,11},{4,12},{5,13},{6,14},{7,15},{8,0},{9,1},... | collective-permute-start | bytes 294920 | tf_op jit(solution)/shard_map/ppermute | solution.py:358
  71.1 13.6 %collective-permute-start.18 = (bf16[6,16,512]{2,1,0:T(8,128)(2,1)S(1)}, bf16[6,16,512]{2,1,0:T(8,128)(2,1)S(1)}, u32[]{:S(2)}, u32[]{:S(2)}) collective-permute-start(bf16[6,16,512]{2,1,0:T(8,128)(2,1)S(1)} %get-tuple-element.142), channel_id=1, source_target_pairs={{0,24},{1,25},{2,26},{3,27},{4,28},{5,29},{6,30},{7,31},{8,16},{9,... | collective-permute-start | bytes 294920 | tf_op jit(solution)/shard_map/ppermute | solution.py:358
  73.8 10.9 %collective-permute-start.19 = (bf16[6,16,512]{2,1,0:T(8,128)(2,1)S(1)}, bf16[6,16,512]{2,1,0:T(8,128)(2,1)S(1)}, u32[]{:S(2)}, u32[]{:S(2)}) collective-permute-start(bf16[6,16,512]{2,1,0:T(8,128)(2,1)S(1)} %get-tuple-element.143), channel_id=1, source_target_pairs={{0,16},{1,17},{2,18},{3,19},{4,20},{5,21},{6,22},{7,23},{8,24},{9,... | collective-permute-start | bytes 294920 | tf_op jit(solution)/shard_map/ppermute | solution.py:358
  75.2 15.5 %collective-permute-start.16 = (bf16[9,16,512]{2,1,0:T(8,128)(2,1)S(1)}, bf16[9,16,512]{2,1,0:T(8,128)(2,1)S(1)}, u32[]{:S(2)}, u32[]{:S(2)}) collective-permute-start(bf16[9,16,512]{2,1,0:T(8,128)(2,1)S(1)} %get-tuple-element.134), channel_id=1, source_target_pairs={{0,32},{1,33},{2,34},{3,35},{4,36},{5,37},{6,38},{7,39},{8,40},{9,... | collective-permute-start | bytes 442376 | tf_op jit(solution)/shard_map/ppermute | solution.py:358
  77.7 10.6 %collective-permute-start.20 = (bf16[7,16,512]{2,1,0:T(8,128)(2,1)S(1)}, bf16[7,16,512]{2,1,0:T(8,128)(2,1)S(1)}, u32[]{:S(2)}, u32[]{:S(2)}) collective-permute-start(bf16[7,16,512]{2,1,0:T(8,128)(2,1)S(1)} %get-tuple-element.145), channel_id=1, source_target_pairs={{0,96},{1,97},{2,98},{3,99},{4,100},{5,101},{6,102},{7,103},{8,104... | collective-permute-start | bytes 344072 | tf_op jit(solution)/shard_map/ppermute | solution.py:358
  84.4 6.3 %collective-permute-start.21 = (bf16[7,16,512]{2,1,0:T(8,128)(2,1)S(1)}, bf16[7,16,512]{2,1,0:T(8,128)(2,1)S(1)}, u32[]{:S(2)}, u32[]{:S(2)}) collective-permute-start(bf16[7,16,512]{2,1,0:T(8,128)(2,1)S(1)} %get-tuple-element.146), channel_id=1, source_target_pairs={{0,64},{1,65},{2,66},{3,67},{4,68},{5,69},{6,70},{7,71},{8,72},{9,... | collective-permute-start | bytes 344072 | tf_op jit(solution)/shard_map/ppermute | solution.py:358
  91.8 13.8 %all-to-all-start = ((bf16[8,32,512]{2,1,0:T(8,128)(2,1)}), bf16[8,32,512]{2,1,0:T(8,128)(2,1)S(1)}, u32[]{:S(2)}, u32[]{:S(2)}) async-start(bf16[8,32,512]{2,1,0:T(8,128)(2,1)} %shard_map.138), calls=%async_computation | async-start | bytes 524288 | tf_op jit(solution)/shard_map/all_to_all | solution.py:370

commit v8 on v7

--- a/solution.py
+++ b/solution.py
@@ -1,4 +1,3 @@
-import functools
 import math
 
 import jax
@@ -27,6 +26,7 @@
 EC = 16
 EXT = ER * EC
 QT = TILE * TILE
+ZROWS = 112
 KT = 256
 F32 = jnp.float32
 BF16 = jnp.bfloat16
@@ -257,34 +257,59 @@
     return ((a + b) + (c + d)).astype(BF16)
 
 
+def halves():
+    return ((0, (1, 2), (0, 3)), (1, (3, 2), (0, 1)))
+
+
 def join_down_kv_kernel(dk, dg, kk, kg, gk, gg, *outs):
     gain = add2(gk[...], gg[15])
-    for d in range(4):
-        outs[d][:16] = add2(dk[d * 16 : (d + 1) * 16], dg[d * 16 : (d + 1) * 16])
-        outs[d][16:24] = add2(kk[16 + d * 8 : 24 + d * 8], kg[16 + d * 8 : 24 + d * 8])
-        outs[d][24] = gain
-
-
-def join_up_q_kernel(which, uk, ug, kk, kg, *outs):
-    for out, d in zip(outs, which):
-        out[:20] = add2(uk[d * 20 : (d + 1) * 20], ug[d * 20 : (d + 1) * 20])
-        out[20:] = add2(kk[d * 4 : (d + 1) * 4], kg[d * 4 : (d + 1) * 4])
-
-
-def sum_up_q_kernel(*refs):
-    parts, outs = refs[:4], refs[4:]
-    for d in range(4):
-        outs[d][:5] = add4([r[d * 5 : (d + 1) * 5] for r in parts])
-        outs[d][5] = add4([r[20 + d] for r in parts])
-
-
-def sum_down_kv_kernel(*refs):
-    parts, ride, outs = refs[:4], refs[4], refs[5:]
-    gain = add4([r[24] for r in parts])
-    for d in range(4):
-        outs[d][:4] = add4([r[d * 4 : (d + 1) * 4] for r in parts])
-        outs[d][4:6] = add4([r[16 + d * 2 : 18 + d * 2] for r in parts])
-        outs[d][6] = gain
+    for h, away, stay in halves():
+        for out, chunks in ((outs[h], away), (outs[2 + h], stay)):
+            for i, d in enumerate(chunks):
+                lo, at = d * 16 + h * 8, i * 12
+                out[at : at + 8] = add2(dk[lo : lo + 8], dg[lo : lo + 8])
+                lo = 16 + d * 8 + h * 4
+                out[at + 8 : at + 12] = add2(kk[lo : lo + 4], kg[lo : lo + 4])
+    outs[0][24] = gain
+    outs[2][24] = gain
+
+
+def join_up_q_kernel(uk, ug, kk, kg, *outs):
+    for h, away, stay in halves():
+        for out, chunks in ((outs[h], away), (outs[2 + h], stay)):
+            for i, d in enumerate(chunks):
+                lo, at = d * 20 + h * 10, i * 12
+                out[at : at + 10] = add2(uk[lo : lo + 10], ug[lo : lo + 10])
+                lo = d * 4 + h * 2
+                out[at + 10 : at + 12] = add2(kk[lo : lo + 2], kg[lo : lo + 2])
+
+
+def second_kernel(p_got, q_got, p_keep, q_keep, p_send, q_send, p_own, q_own):
+    p_own[:12] = add2(p_keep[:12], p_got[:12])
+    p_send[:12] = add2(p_keep[12:24], p_got[12:24])
+    q_own[...] = add2(q_keep[:12], q_got[:12])
+    q_send[...] = add2(q_keep[12:], q_got[12:])
+    if p_keep.shape[0] == 25:
+        gain = add2(p_keep[24], p_got[24])
+        p_own[12] = gain
+        p_send[12] = gain
+
+
+def sum_up_q_kernel(p_got, q_got, p_own, q_own, *outs):
+    for h, got, own in ((0, p_got, p_own), (1, q_got, q_own)):
+        for i in range(2):
+            outs[2 * h + i][:5] = add2(got[i * 5 : i * 5 + 5], own[i * 5 : i * 5 + 5])
+            outs[2 * h + i][5] = add2(got[10 + i], own[10 + i])
+
+
+def sum_down_kv_kernel(p_got, q_got, p_own, q_own, ride, *outs):
+    gain = add2(p_got[12], p_own[12])
+    for h, got, own in ((0, p_got, p_own), (1, q_got, q_own)):
+        for i in range(2):
+            out = outs[2 * h + i]
+            out[:4] = add2(got[i * 4 : i * 4 + 4], own[i * 4 : i * 4 + 4])
+            out[4:6] = add2(got[8 + i * 2 : 10 + i * 2], own[8 + i * 2 : 10 + i * 2])
+            out[6] = gain
     outs[1][7:9] = ride[...]
 
 
@@ -293,10 +318,10 @@
     sums = [add4([r[...] for r in refs[:4]]).reshape(-1, D), add4([r[:7] for r in refs[4:8]]).reshape(-1, D)]
     acc = jnp.concatenate(sums, axis=0)
     rows = acc.shape[0]
-    i = lax.broadcasted_iota(jnp.int32, (256, rows), 0)
-    lane = lax.broadcasted_iota(jnp.int32, (256, rows), 1)
-    z = i // 32
-    r = i % 32
+    i = lax.broadcasted_iota(jnp.int32, (8 * ZROWS, rows), 0)
+    lane = lax.broadcasted_iota(jnp.int32, (8 * ZROWS, rows), 1)
+    z = i // ZROWS
+    r = (i % ZROWS) // 4
     up = (r % 4) * 16 + z * 2 + r // 4
     down = 96 + z * 8 + (r - 8)
     o = 64 + z * 2 + (r - 16)
@@ -304,22 +329,26 @@
     qkv = jnp.where(part == 0, 80, 144 + part * 16) + z * 2 + (r - 18) // 3
     gain = 192 + (r - 24)
     src = jnp.where(r < 8, up, jnp.where(r < 16, down, jnp.where(r < 18, o, jnp.where(r < 24, qkv, gain))))
-    pick = jnp.where((lane == src) & (r < 26), 1.0, 0.0).astype(BF16)
-    out[...] = nn(pick, acc).astype(BF16).reshape(8, 32, D)
-
-
-def reduce_z_kernel(got, up, down, o, qkv, gain, acc_s):
+    hit = (lane == src) & (r < 26)
+    picked = jnp.zeros((8 * ZROWS, 128), F32)
+    for j in range(4):
+        pick = jnp.where(hit & (i % 4 == j), 1.0, 0.0).astype(BF16)
+        picked = picked + nn(pick, acc[:, j * 128 : (j + 1) * 128])
+    out[...] = picked.astype(BF16).reshape(8, ZROWS, 128)
+
+
+def reduce_z_kernel(got, up, down, o, qkv, gain):
     acc = got[0].astype(F32)
     for j in range(1, 8):
         acc = acc + got[j].astype(F32)
-    acc_s[...] = acc * (1.0 / math.sqrt(GRID_ROWS * GRID_COLS))
+    acc = acc * (1.0 / math.sqrt(GRID_ROWS * GRID_COLS))
     at = 0
-    for ref, rows in ((up, 8), (down, 8), (o, 2), (qkv, 6)):
-        for r in range(rows):
-            for j in range(4):
-                ref[4 * r + j : 4 * r + j + 1, :] = acc_s[at + r : at + r + 1, j * 128 : (j + 1) * 128]
-        at += rows
-    gain[...] = acc_s[at : at + 2, :]
+    for ref in (up, down, o, qkv):
+        ref[...] = acc[at : at + ref.shape[0]]
+        at += ref.shape[0]
+    for r in range(2):
+        for j in range(4):
+            gain[r : r + 1, j * 128 : (j + 1) * 128] = acc[at + 4 * r + j : at + 4 * r + j + 1]
 
 
 def call(body, outs, scratch, n_smem, n_in, flops, nbytes, mib):
@@ -444,43 +473,50 @@
     def join(body, ins, outs):
         return list(call(body, [(o, BF16) for o in outs], [], 0, len(ins), 1_000_000, 4_000_000, 6)(*ins))
 
-    def join_up(which, got):
-        ins = [u_keep.reshape(80, 16, D), got.reshape(80, 16, D), k_keep, k_got]
-        return join(functools.partial(join_up_q_kernel, which), ins, [(24, 16, D)] * len(which))
-
-    u0, u1, u2, u3 = join_up((0, 1, 2, 3), u_got)
-    d_got, u0, u1, u2, u3 = lax.optimization_barrier((d_got, u0, u1, u2, u3))
-    b = join(
+    def first(sent, bit):
+        return send(sent[0], by(bit)), send(sent[1], by(3 * bit))
+
+    def second(sent, bit):
+        return send(sent[0], by(3 * bit)), send(sent[1], by(bit))
+
+    k_got, gnq = lax.optimization_barrier((k_got, gnq))
+    u_p, u_q, *u_stay = join(
+        join_up_q_kernel, [u_keep.reshape(80, 16, D), u_got.reshape(80, 16, D), k_keep, k_got], [(24, 16, D)] * 4,
+    )
+    u_first = first((u_p, u_q), X_BIT)
+    b_p, b_q, *b_stay = join(
         join_down_kv_kernel, [d_keep.reshape(64, 16, D), d_got.reshape(64, 16, D), k_keep, k_got, g_keep, g_got],
-        [(25, 16, D)] * 4,
+        [(25, 16, D), (24, 16, D)] * 2,
     )
     gne3 = gne.reshape(ROWS + 2 * RIM, EC, D)
-    back_a = send(gne3[:, COLS : COLS + RIM].astype(BF16), COL_A)
-    u1, u3 = send(u1, by(X_BIT)), send(u3, by(3 * X_BIT))
-    b = to_three(b, Y_BIT)
-    u1, u2, back_a, g_got = lax.optimization_barrier((u1, u2, back_a, g_got))
-    u = [u0, u1, u3, send(u2, by(2 * X_BIT))]
+    side = gne3[:, COLS : COLS + RIM].astype(BF16)
+    b_first = first((b_p, b_q), Y_BIT)
+    u_first, side = lax.optimization_barrier((u_first, side))
+    back_a = send(side, COL_A)
+    u_p, u_q, *u_own = join(second_kernel, [*u_first, *u_stay], [(12, 16, D)] * 4)
+    u_second = second((u_p, u_q), X_BIT)
+    b_p, b_q, *b_own = join(second_kernel, [*b_first, *b_stay], [(13, 16, D), (12, 16, D)] * 2)
+    b_second = second((b_p, b_q), Y_BIT)
     back_b = g_got[:15].reshape(ROWS + 2 * RIM, COLS, D)[:, RIM : 2 * RIM]
     own = gne3[:, :COLS] + place(back_a, 1, col_odd, True, COLS) + place(back_b, 1, col_odd, False, COLS)
     head, tail = own[:RIM].astype(BF16), own[RIM + ROWS :].astype(BF16)
     ride = jnp.pad(jnp.where(row_odd, head, tail), ((0, 1), (0, 0), (0, 0))).reshape(2, 16, D)
-    u, b, ride = lax.optimization_barrier((u, b, ride))
-    b = join(sum_down_kv_kernel, [*b, ride], [(7, 16, D), (9, 16, D), (7, 16, D), (7, 16, D)])
+    u = join(sum_up_q_kernel, [*u_second, *u_own], [(6, 16, D)] * 4)
+    u = to_three(u, Y_BIT)
+    b = join(sum_down_kv_kernel, [*b_second, *b_own, ride], [(7, 16, D), (9, 16, D), (7, 16, D), (7, 16, D)])
     b = to_three(b, X_BIT)
-    u = join(sum_up_q_kernel, u, [(6, 16, D)] * 4)
-    u = to_three(u, Y_BIT)
     up_b = b[1][7:].reshape(4, COLS, D)[:RIM]
     (spread,) = call(
-        reduce_xy_kernel, [((8, 32, D), BF16)], [], 0, 8, 60_000_000, 4_000_000, 5,
+        reduce_xy_kernel, [((8, ZROWS, 128), BF16)], [], 0, 8, 60_000_000, 4_000_000, 5,
     )(*u, *b)
+    up_a = send(jnp.where(row_odd, tail, head), ROW_A)
     got_z = exchange(spread, Z_GROUPS)
     g_up, g_down, g_out, g_qkv, g_gains = call(
         reduce_z_kernel,
         [((32, 128), F32), ((32, 128), F32), ((8, 128), F32), ((24, 128), F32), ((2, D), F32)],
-        [pltpu.VMEM((32, D), F32)], 0, 1, 1_000_000, 400_000, 8,
+        [], 0, 1, 100_000_000_000, 400_000, 4,
     )(got_z)
 
-    up_a = send(jnp.where(row_odd, tail, head), ROW_A)
     gn = own[RIM : RIM + ROWS] + place(up_a, 0, row_odd, True, ROWS) + place(up_b, 0, row_odd, False, ROWS)
     gn = gn + gnq.reshape(ROWS, COLS, D)
     unit, inv = unit_of(tokens.astype(F32))

time: 107 us -> 101 us (0.944)
  waiting for transfers between devices: 33.8 us -> 23.3 us
  starting transfers between devices: 46.8 us -> 49.4 us
  Pallas kernels: 20.3 us -> 22.5 us
    ppermute x22 -> x24, waiting for transfers between devices: 24.5 us -> 14.2 us  [send(): return lax.ppermute(x, AXES, perm)]
    ppermute x22 -> x24, starting transfers between devices: 43.4 us -> 45.8 us  [send(): return lax.ppermute(x, AXES, perm)]
    pallas_call x1, Pallas kernels: 1.04 us -> 3.04 us  [per_device(): call(reduce_xy_kernel, [((8, ZROWS, 128), BF16)], [], 0, 8, 60000000, 400...]
  transfers between devices with their start and end apart: 23 -> 25, of which waited for: 6 -> 7; matrix products, arithmetic and copies ran while one was open for 2% -> 2% of each run, Pallas kernels for 11% -> 12%
where the time goes in v8:
time: 101 us; the launch traced here: 100 us
  starting transfers between devices  49.4 us (49%)
  waiting for transfers between devices  23.3 us (23%)
  Pallas kernels  22.5 us (22%)
  other arithmetic  2.92 us (3%)
  local copies, waits for them, and re-layouts  1.39 us (1%)
  between operations  1.03 us (1%)
    ppermute x24, starting transfers between devices, send(): return lax.ppermute(x, AXES, perm)  45.8 us
    ppermute x24, waiting for transfers between devices, send(): return lax.ppermute(x, AXES, perm)  14.2 us
    all_to_all x1, waiting for transfers between devices, exchange(): return lax.all_to_all(x, AXES, 0, 0, axis_index_groups=groups, tiled=True)  9.01 us
    pallas_call x1, Pallas kernels, per_device(): call(forward_kernel, [half_u, half_u, half_d, half_d, ((TOK, D), BF16), (...  6.99 us
    pallas_call x1, Pallas kernels, per_device(): call(backward_kernel, [half_k, half_k, ((TOK, D), BF16), ((EXT, 2 * D), B...  4.03 us
    all_to_all x1, starting transfers between devices, exchange(): return lax.all_to_all(x, AXES, 0, 0, axis_index_groups=groups, tiled=True)  3.57 us
    pallas_call x1, Pallas kernels, per_device(): call(reduce_xy_kernel, [((8, ZROWS, 128), BF16)], [], 0, 8, 60000000, 400...  3.04 us
  transfers between devices with their start and end apart: 25, of which 7 were waited for; matrix products, arithmetic and copies ran while one was open for 2% of the time, Pallas kernels for 12%

profile of v8, /device:TPU:8, one launch (start us, length us, event | category | flops | bytes accessed | tf_op | source)
XLA Modules:
  0.0 100.4 jit_solution(18402370953466412729)
XLA Ops:
  0.6 1.2 %broadcast_select_fusion = (bf16[24,3,512]{2,1,0:T(4,128)(2,1)S(1)}, bf16[24,3,512]{2,1,0:T(4,128)(2,1)S(1)}) fusion(pred[]{:T(512)S(6)} %eq.6, bf16[24,8,512]{2,1,0:T(8,128)(2,1)} %param.8), kind=kLoop, calls=%fused_computation.19 | loop fusion | flops 73728 | bytes 294913 | tf_op jit(solution)/shard_map/jit(_where)/select_n | solution.py:412
  1.8 5.9 %collective-permute-start = (bf16[24,3,512]{2,1,0:T(4,128)(2,1)S(1)}, bf16[24,3,512]{2,1,0:T(4,128)(2,1)S(1)}, u32[]{:S(2)}, u32[]{:S(2)}) collective-permute-start(bf16[24,3,512]{2,1,0:T(4,128)(2,1)S(1)} %get-tuple-element.149), channel_id=1, source_target_pairs={{1,2},{2,1},{3,4},{4,3},{5,6},{6,5},{7,8},{8,7},{9,10},{10,9},{11,... | collective-permute-start | bytes 221192 | tf_op jit(solution)/shard_map/ppermute | solution.py:387
  8.0 0.7 copy-done.7
  8.6 1.2 %shard_map.127.bias = f32[3,64,256]{2,1,0:T(8,128)S(1)} custom-call(s32[3]{0:T(128)S(1)} %pad_add_fusion.coord, s32[3,1,49]{2,1,0:T(1,128)S(1)} %copy-done.7), custom_call_target="tpu_custom_call" | custom-call | flops 402653184 | bytes 4000000 | tf_op jit(solution)/shard_map/pallas_call | solution.py:414
  9.9 1.3 %collective-permute-done = bf16[24,3,512]{2,1,0:T(4,128)(2,1)S(1)} collective-permute-done((bf16[24,3,512]{2,1,0:T(4,128)(2,1)S(1)}, bf16[24,3,512]{2,1,0:T(4,128)(2,1)S(1)}, u32[]{:S(2)}, u32[]{:S(2)}) %collective-permute-start) | collective-permute-done | bytes 73760 | tf_op jit(solution)/shard_map/ppermute | solution.py:387
  11.4 0.7 collective-permute-start.2
  12.1 4.3 %collective-permute-start.3 = (bf16[3,16,512]{2,1,0:T(8,128)(2,1)S(1)}, bf16[3,16,512]{2,1,0:T(8,128)(2,1)S(1)}, u32[]{:S(2)}, u32[]{:S(2)}) collective-permute-start(bf16[3,16,512]{2,1,0:T(8,128)(2,1)S(1)} %get-tuple-element.144), channel_id=1, source_target_pairs={{0,32},{1,33},{2,34},{3,35},{4,36},{5,37},{6,38},{7,39},{8,40},{9,... | collective-permute-start | bytes 147464 | tf_op jit(solution)/shard_map/ppermute | solution.py:387
  16.4 1.3 %shard_map.129 = (bf16[512,512]{1,0:T(8,128)(2,1)S(1)}, bf16[512,512]{1,0:T(8,128)(2,1)S(1)}, bf16[512,512]{1,0:T(8,128)(2,1)S(1)}) custom-call(s32[3]{0:T(128)S(1)} %pad_add_fusion.coord), custom_call_target="tpu_custom_call" | custom-call | flops 402653184 | bytes 4000000 | tf_op jit(solution)/shard_map/pallas_call | solution.py:421
  17.8 0.8 shard_map.128.gact
  19.1 1.6 %shard_map.130 = (bf16[192,512]{1,0:T(8,128)(2,1)S(1)}, bf16[192,512]{1,0:T(8,128)(2,1)S(1)}, bf16[384,512]{1,0:T(8,128)(2,1)S(1)}, bf16[384,1024]{1,0:T(8,128)(...) custom-call(bf16[24,16,512]{2,1,0:T(8,128)(2,1)S(1)} %maximum_maximum_fusion.mid, ...), custom_call_target="tpu_custom_call" | custom-call | flops 600000000 | bytes 5000000 | tf_op jit(solution)/shard_map/pallas_call | solution.py:428
  20.8 7.0 %shard_map.131 = (bf16[16,5,16,512]{3,2,1,0:T(8,128)(2,1)S(1)}, bf16[16,5,16,512]{3,2,1,0:T(8,128)(2,1)S(1)}, bf16[4,4,2,32,512]{4,3,2,1,0:T(8,128)(2,1)S(1)}, b...) custom-call(s32[3]{0:T(128)S(1)} %pad_add_fusion.coord, ...), custom_call_target="tpu_custom_call" | custom-call | flops 4000000000 | bytes 20000000 | tf_op jit(solution)/shard_map/pallas_call | solution.py:439
  28.4 4.0 %shard_map.132 = (bf16[48,16,512]{2,1,0:T(8,128)(2,1)S(1)}, bf16[48,16,512]{2,1,0:T(8,128)(2,1)S(1)}, bf16[192,512]{1,0:T(8,128)(2,1)S(1)}, bf16[512,1024]{1,0:T(8,128)(2,1)S(1)}) custom-call(bf16[192,512]{1,0:T(8,128)(2,1)S(1)} %get-tuple-element.85.gm, bf16[512,512]{1,0:T(8,128)(2,1)S(1)} %copy-done.6, bf16[192,512]{1,0:T(8,128)(2,1)S(1)} %get-tuple-element.81.q_i.q, ...), custom_call_target="tpu_custom_call" | custom-call | flops 2500000000 | bytes 10000000 | tf_op jit(solution)/shard_map/pallas_call | solution.py:450
  32.8 1.5 %shard_map.133 = (f32[480,512]{1,0:T(8,128)S(1)}, f32[192,512]{1,0:T(8,128)S(1)}, bf16[16,512]{1,0:T(8,128)(2,1)S(1)}, bf16[16,16,512]{2,1,0:T(8,128)(2,1)S(1)}) custom-call(s32[3]{0:T(128)S(1)} %pad_add_fusion.coord, bf16[192,512]{1,0:T(8,128)(2,1)S(1)} %get-tuple-element.92.dq, bf16[512,1024]{1,0:T(8,128)(2,1)S(1)} %get-tuple-element.93.dkv, ...), custom_call_target="tpu_custom_call" | custom-call | flops 600000000 | bytes 4000000 | tf_op jit(solution)/shard_map/pallas_call | solution.py:457
  35.3 8.1 %collective-permute-start.8 = (bf16[24,16,512]{2,1,0:T(8,128)(2,1)S(1)}, bf16[24,16,512]{2,1,0:T(8,128)(2,1)S(1)}, u32[]{:S(2)}, u32[]{:S(2)}) collective-permute-start(bf16[24,16,512]{2,1,0:T(8,128)(2,1)S(1)} %get-tuple-element.106), channel_id=1, source_target_pairs={{0,96},{1,97},{2,98},{3,99},{4,100},{5,101},{6,102},{7,103},{8,104... | collective-permute-start | bytes 1179656 | tf_op jit(solution)/shard_map/ppermute | solution.py:387
  43.9 2.8 %collective-permute-start.13 = (bf16[24,16,512]{2,1,0:T(8,128)(2,1)S(1)}, bf16[24,16,512]{2,1,0:T(8,128)(2,1)S(1)}, u32[]{:S(2)}, u32[]{:S(2)}) collective-permute-start(bf16[24,16,512]{2,1,0:T(8,128)(2,1)S(1)} %get-tuple-element.113), channel_id=1, source_target_pairs={{0,24},{1,25},{2,26},{3,27},{4,28},{5,29},{6,30},{7,31},{8,16},{9,... | collective-permute-start | bytes 1179656 | tf_op jit(solution)/shard_map/ppermute | solution.py:387
  46.8 5.9 %collective-permute-done.8.q_got = bf16[24,16,512]{2,1,0:T(8,128)(2,1)S(1)} collective-permute-done((bf16[24,16,512]{2,1,0:T(8,128)(2,1)S(1)}, bf16[24,16,512]{2,1,0:T(8,128)(2,1)S(1)}, u32[]{:S(2)}, u32[]{:S(2)}) %collective-permute-start.8) | collective-permute-done | bytes 393248 | tf_op jit(solution)/shard_map/ppermute | solution.py:387
  52.7 2.0 %collective-permute-start.9 = (bf16[30,3,512]{2,1,0:T(4,128)(2,1)S(1)}, bf16[30,3,512]{2,1,0:T(4,128)(2,1)S(1)}, u32[]{:S(2)}, u32[]{:S(2)}) collective-permute-start(bf16[30,3,512]{2,1,0:T(4,128)(2,1)S(1)} %slice.101), channel_id=1, source_target_pairs={{1,2},{2,1},{3,4},{4,3},{5,6},{6,5},{7,8},{8,7},{9,10},{10,9},{11,... | collective-permute-start | bytes 276488 | tf_op jit(solution)/shard_map/ppermute | solution.py:387
  55.0 3.0 %collective-permute-start.17 = (bf16[12,16,512]{2,1,0:T(8,128)(2,1)S(1)}, bf16[12,16,512]{2,1,0:T(8,128)(2,1)S(1)}, u32[]{:S(2)}, u32[]{:S(2)}) collective-permute-start(bf16[12,16,512]{2,1,0:T(8,128)(2,1)S(1)} %get-tuple-element.126), channel_id=1, source_target_pairs={{0,96},{1,97},{2,98},{3,99},{4,100},{5,101},{6,102},{7,103},{8,104... | collective-permute-start | bytes 589832 | tf_op jit(solution)/shard_map/ppermute | solution.py:387
  58.1 1.7 %collective-permute-start.14 = (bf16[13,16,512]{2,1,0:T(8,128)(2,1)S(1)}, bf16[13,16,512]{2,1,0:T(8,128)(2,1)S(1)}, u32[]{:S(2)}, u32[]{:S(2)}) collective-permute-start(bf16[13,16,512]{2,1,0:T(8,128)(2,1)S(1)} %get-tuple-element.116), channel_id=1, source_target_pairs={{0,24},{1,25},{2,26},{3,27},{4,28},{5,29},{6,30},{7,31},{8,16},{9,... | collective-permute-start | bytes 638984 | tf_op jit(solution)/shard_map/ppermute | solution.py:387
  59.8 1.9 %collective-permute-start.15 = (bf16[12,16,512]{2,1,0:T(8,128)(2,1)S(1)}, bf16[12,16,512]{2,1,0:T(8,128)(2,1)S(1)}, u32[]{:S(2)}, u32[]{:S(2)}) collective-permute-start(bf16[12,16,512]{2,1,0:T(8,128)(2,1)S(1)} %get-tuple-element.117), channel_id=1, source_target_pairs={{0,8},{1,9},{2,10},{3,11},{4,12},{5,13},{6,14},{7,15},{8,0},{9,1},... | collective-permute-start | bytes 589832 | tf_op jit(solution)/shard_map/ppermute | solution.py:387
  61.9 0.7 collective-permute-start.11
  62.6 1.0 %collective-permute-done.18.q_got = bf16[12,16,512]{2,1,0:T(8,128)(2,1)S(1)} collective-permute-done((bf16[12,16,512]{2,1,0:T(8,128)(2,1)S(1)}, bf16[12,16,512]{2,1,0:T(8,128)(2,1)S(1)}, u32[]{:S(2)}, u32[]{:S(2)}) %collective-permute-start.18) | collective-permute-done | bytes 196640 | tf_op jit(solution)/shard_map/ppermute | solution.py:387
  63.9 3.2 %collective-permute-start.20 = (bf16[6,16,512]{2,1,0:T(8,128)(2,1)S(1)}, bf16[6,16,512]{2,1,0:T(8,128)(2,1)S(1)}, u32[]{:S(2)}, u32[]{:S(2)}) collective-permute-start(bf16[6,16,512]{2,1,0:T(8,128)(2,1)S(1)} %get-tuple-element.132), channel_id=1, source_target_pairs={{0,24},{1,25},{2,26},{3,27},{4,28},{5,29},{6,30},{7,31},{8,16},{9,... | collective-permute-start | bytes 294920 | tf_op jit(solution)/shard_map/ppermute | solution.py:387
  67.1 1.4 %collective-permute-start.21 = (bf16[6,16,512]{2,1,0:T(8,128)(2,1)S(1)}, bf16[6,16,512]{2,1,0:T(8,128)(2,1)S(1)}, u32[]{:S(2)}, u32[]{:S(2)}) collective-permute-start(bf16[6,16,512]{2,1,0:T(8,128)(2,1)S(1)} %get-tuple-element.133), channel_id=1, source_target_pairs={{0,16},{1,17},{2,18},{3,19},{4,20},{5,21},{6,22},{7,23},{8,24},{9,... | collective-permute-start | bytes 294920 | tf_op jit(solution)/shard_map/ppermute | solution.py:387
  68.6 2.2 %collective-permute-start.16 = (bf16[9,16,512]{2,1,0:T(8,128)(2,1)S(1)}, bf16[9,16,512]{2,1,0:T(8,128)(2,1)S(1)}, u32[]{:S(2)}, u32[]{:S(2)}) collective-permute-start(bf16[9,16,512]{2,1,0:T(8,128)(2,1)S(1)} %get-tuple-element.120), channel_id=1, source_target_pairs={{0,32},{1,33},{2,34},{3,35},{4,36},{5,37},{6,38},{7,39},{8,40},{9,... | collective-permute-start | bytes 442376 | tf_op jit(solution)/shard_map/ppermute | solution.py:387
  70.8 6.0 %collective-permute-start.22 = (bf16[7,16,512]{2,1,0:T(8,128)(2,1)S(1)}, bf16[7,16,512]{2,1,0:T(8,128)(2,1)S(1)}, u32[]{:S(2)}, u32[]{:S(2)}) collective-permute-start(bf16[7,16,512]{2,1,0:T(8,128)(2,1)S(1)} %get-tuple-element.135), channel_id=1, source_target_pairs={{0,96},{1,97},{2,98},{3,99},{4,100},{5,101},{6,102},{7,103},{8,104... | collective-permute-start | bytes 344072 | tf_op jit(solution)/shard_map/ppermute | solution.py:387
  77.3 3.0 %collective-permute-done.22.refs_6_ = bf16[7,16,512]{2,1,0:T(8,128)(2,1)S(1)} collective-permute-done((bf16[7,16,512]{2,1,0:T(8,128)(2,1)S(1)}, bf16[7,16,512]{2,1,0:T(8,128)(2,1)S(1)}, u32[]{:S(2)}, u32[]{:S(2)}) %collective-permute-start.22) | collective-permute-done | bytes 114720 | tf_op jit(solution)/shard_map/ppermute | solution.py:387
  80.3 2.7 %collective-permute-done.23.refs_7_ = bf16[7,16,512]{2,1,0:T(8,128)(2,1)S(1)} collective-permute-done((bf16[7,16,512]{2,1,0:T(8,128)(2,1)S(1)}, bf16[7,16,512]{2,1,0:T(8,128)(2,1)S(1)}, u32[]{:S(2)}, u32[]{:S(2)}) %collective-permute-start.23) | collective-permute-done | bytes 114720 | tf_op jit(solution)/shard_map/ppermute | solution.py:387
  83.1 3.0 %shard_map.140 = bf16[8,112,128]{2,1,0:T(8,128)(2,1)} custom-call(bf16[6,16,512]{2,1,0:T(8,128)(2,1)S(1)} %get-tuple-element.130.refs_0_, bf16[6,16,512]{2,1,0:T(8,128)(2,1)S(1)} %collective-permute-done.19.refs_1_, bf16[6,16,512]{2,1,0:T(8,128)(2,1)S(1)} %collective-permute-done.20.refs_2_, bf16[6,16,512]{2,1,0:T(8,128)(2,1)S(1)} %collective-permute-done.21.refs_3_, ...), custom_call_target="tpu_custom_call" | custom-call | flops 60000000 | bytes 4000000 | tf_op jit(solution)/shard_map/pallas_call | solution.py:509
  86.1 3.6 %all-to-all-start = ((bf16[8,112,128]{2,1,0:T(8,128)(2,1)}), bf16[8,112,128]{2,1,0:T(8,128)(2,1)S(1)}, u32[]{:S(2)}, u32[]{:S(2)}) async-start(bf16[8,112,128]{2,1,0:T(8,128)(2,1)} %shard_map.140), calls=%async_computation | async-start | bytes 458752 | tf_op jit(solution)/shard_map/all_to_all | solution.py:399
  89.9 0.9 fusion.7
  90.8 9.0 %all-to-all-done.got = bf16[8,112,128]{2,1,0:T(8,128)(2,1)S(1)} async-done(((bf16[8,112,128]{2,1,0:T(8,128)(2,1)}), bf16[8,112,128]{2,1,0:T(8,128)(2,1)S(1)}, u32[]{:S(2)}, u32[]{:S(2)}) %all-to-all-start) | async-done | bytes 229408 | tf_op jit(solution)/shard_map/all_to_all | solution.py:399
  (71 shorter events, 5.9 us)
Async XLA Ops:
  0.6 10.6 %copy-start = (bf16[24,8,512]{2,1,0:T(8,128)(2,1)S(1)}, bf16[24,8,512]{2,1,0:T(8,128)(2,1)}, u32[]{:S(2)}) copy-start(bf16[24,8,512]{2,1,0:T(8,128)(2,1)} %param.8) | copy-start | bytes 589828
  1.8 9.4 %collective-permute-start = (bf16[24,3,512]{2,1,0:T(4,128)(2,1)S(1)}, bf16[24,3,512]{2,1,0:T(4,128)(2,1)S(1)}, u32[]{:S(2)}, u32[]{:S(2)}) collective-permute-start(bf16[24,3,512]{2,1,0:T(4,128)(2,1)S(1)} %get-tuple-element.149), channel_id=1, source_target_pairs={{1,2},{2,1},{3,4},{4,3},{5,6},{6,5},{7,8},{8,7},{9,10},{10,9},{11,... | collective-permute-start | bytes 221192 | tf_op jit(solution)/shard_map/ppermute | solution.py:387
  7.7 3.5 %collective-permute-start.1 = (bf16[24,3,512]{2,1,0:T(4,128)(2,1)S(1)}, bf16[24,3,512]{2,1,0:T(4,128)(2,1)S(1)}, u32[]{:S(2)}, u32[]{:S(2)}) collective-permute-start(bf16[24,3,512]{2,1,0:T(4,128)(2,1)S(1)} %get-tuple-element.148), channel_id=1, source_target_pairs={{0,1},{1,0},{2,3},{3,2},{4,5},{5,4},{6,7},{7,6},{8,9},{9,8},{10,11... | collective-permute-start | bytes 221192 | tf_op jit(solution)/shard_map/ppermute | solution.py:387
  9.9 7.8 %copy-start.2 = (bf16[2048,512]{1,0:T(8,128)(2,1)S(1)}, bf16[2048,512]{1,0:T(8,128)(2,1)}, u32[]{:S(2)}) copy-start(bf16[2048,512]{1,0:T(8,128)(2,1)} %w_down.1) | copy-start | bytes 6291460
  9.9 7.8 %copy-start.3 = (bf16[24,8,512]{2,1,0:T(8,128)(2,1)S(1)}, bf16[24,8,512]{2,1,0:T(8,128)(2,1)}, u32[]{:S(2)}) copy-start(bf16[24,8,512]{2,1,0:T(8,128)(2,1)} %param.9) | copy-start | bytes 589828
  11.4 9.4 %collective-permute-start.2 = (bf16[3,16,512]{2,1,0:T(8,128)(2,1)S(1)}, bf16[3,16,512]{2,1,0:T(8,128)(2,1)S(1)}, u32[]{:S(2)}, u32[]{:S(2)}) collective-permute-start(bf16[3,16,512]{2,1,0:T(8,128)(2,1)S(1)} %get-tuple-element.145), channel_id=1, source_target_pairs={{32,64},{33,65},{34,66},{35,67},{36,68},{37,69},{38,70},{39,71},{4... | collective-permute-start | bytes 147464 | tf_op jit(solution)/shard_map/ppermute | solution.py:387
  12.1 8.7 %collective-permute-start.3 = (bf16[3,16,512]{2,1,0:T(8,128)(2,1)S(1)}, bf16[3,16,512]{2,1,0:T(8,128)(2,1)S(1)}, u32[]{:S(2)}, u32[]{:S(2)}) collective-permute-start(bf16[3,16,512]{2,1,0:T(8,128)(2,1)S(1)} %get-tuple-element.144), channel_id=1, source_target_pairs={{0,32},{1,33},{2,34},{3,35},{4,36},{5,37},{6,38},{7,39},{8,40},{9,... | collective-permute-start | bytes 147464 | tf_op jit(solution)/shard_map/ppermute | solution.py:387
  17.7 1.4 %copy-start.1 = (bf16[512,1536]{1,0:T(8,128)(2,1)S(1)}, bf16[512,1536]{1,0:T(8,128)(2,1)}, u32[]{:S(2)}) copy-start(bf16[512,1536]{1,0:T(8,128)(2,1)} %w_qkv.5) | copy-start | bytes 4718596
  17.7 1.4 %copy-start.4 = (f32[2,512]{1,0:T(2,128)S(1)}, f32[2,512]{1,0:T(2,128)}, u32[]{:S(2)}) copy-start(f32[2,512]{1,0:T(2,128)} %gains.3) | copy-start | bytes 12292
  17.8 3.1 %copy-start.6 = (bf16[512,512]{1,0:T(8,128)(2,1)S(1)}, bf16[512,512]{1,0:T(8,128)(2,1)}, u32[]{:S(2)}) copy-start(bf16[512,512]{1,0:T(8,128)(2,1)} %w_out.3) | copy-start | bytes 1572868
  18.6 2.2 %copy-start.5 = (bf16[512,2048]{1,0:T(8,128)(2,1)S(1)}, bf16[512,2048]{1,0:T(8,128)(2,1)}, u32[]{:S(2)}) copy-start(bf16[512,2048]{1,0:T(8,128)(2,1)} %w_up.1) | copy-start | bytes 6291460
  27.8 4.6 %collective-permute-start.4 = (bf16[16,5,16,512]{3,2,1,0:T(8,128)(2,1)S(1)}, bf16[16,5,16,512]{3,2,1,0:T(8,128)(2,1)S(1)}, u32[]{:S(2)}, u32[]{:S(2)}) collective-permute-start(bf16[16,5,16,512]{3,2,1,0:T(8,128)(2,1)S(1)} %get-tuple-element.97), channel_id=1, source_target_pairs={{0,1},{1,0},{2,3},{3,2},{4,5},{5,4},{6,7},{7,6},{8,9},{9,8},{10,11... | collective-permute-start | bytes 3932168 | tf_op jit(solution)/shard_map/ppermute | solution.py:387
  27.9 4.5 %collective-permute-start.5 = (bf16[4,4,2,32,512]{4,3,2,1,0:T(8,128)(2,1)S(1)}, bf16[4,4,2,32,512]{4,3,2,1,0:T(8,128)(2,1)S(1)}, u32[]{:S(2)}, u32[]{:S(2)}) collective-permute-start(bf16[4,4,2,32,512]{4,3,2,1,0:T(8,128)(2,1)S(1)} %get-tuple-element.98), channel_id=1, source_target_pairs={{0,1},{1,0},{2,3},{3,2},{4,5},{5,4},{6,7},{7,6},{8,9},{9,8},{10,11... | collective-permute-start | bytes 3145736 | tf_op jit(solution)/shard_map/ppermute | solution.py:387
  32.5 2.4 %collective-permute-start.6 = (bf16[48,16,512]{2,1,0:T(8,128)(2,1)S(1)}, bf16[48,16,512]{2,1,0:T(8,128)(2,1)S(1)}, u32[]{:S(2)}, u32[]{:S(2)}) collective-permute-start(bf16[48,16,512]{2,1,0:T(8,128)(2,1)S(1)} %get-tuple-element.102), channel_id=1, source_target_pairs={{0,1},{1,0},{2,3},{3,2},{4,5},{5,4},{6,7},{7,6},{8,9},{9,8},{10,11... | collective-permute-start | bytes 2359304 | tf_op jit(solution)/shard_map/ppermute | solution.py:387
  34.3 9.1 %collective-permute-start.10 = (bf16[16,16,512]{2,1,0:T(8,128)(2,1)S(1)}, bf16[16,16,512]{2,1,0:T(8,128)(2,1)S(1)}, u32[]{:S(2)}, u32[]{:S(2)}) collective-permute-start(bf16[16,16,512]{2,1,0:T(8,128)(2,1)S(1)} %get-tuple-element.108), channel_id=1, source_target_pairs={{0,1},{1,0},{2,3},{3,2},{4,5},{5,4},{6,7},{7,6},{8,9},{9,8},{10,11... | collective-permute-start | bytes 786440 | tf_op jit(solution)/shard_map/ppermute | solution.py:387
  35.2 11.6 %collective-permute-start.7 = (bf16[24,16,512]{2,1,0:T(8,128)(2,1)S(1)}, bf16[24,16,512]{2,1,0:T(8,128)(2,1)S(1)}, u32[]{:S(2)}, u32[]{:S(2)}) collective-permute-start(bf16[24,16,512]{2,1,0:T(8,128)(2,1)S(1)} %get-tuple-element.105), channel_id=1, source_target_pairs={{0,32},{1,33},{2,34},{3,35},{4,36},{5,37},{6,38},{7,39},{8,40},{9,... | collective-permute-start | bytes 1179656 | tf_op jit(solution)/shard_map/ppermute | solution.py:387
  35.3 17.4 %collective-permute-start.8 = (bf16[24,16,512]{2,1,0:T(8,128)(2,1)S(1)}, bf16[24,16,512]{2,1,0:T(8,128)(2,1)S(1)}, u32[]{:S(2)}, u32[]{:S(2)}) collective-permute-start(bf16[24,16,512]{2,1,0:T(8,128)(2,1)S(1)} %get-tuple-element.106), channel_id=1, source_target_pairs={{0,96},{1,97},{2,98},{3,99},{4,100},{5,101},{6,102},{7,103},{8,104... | collective-permute-start | bytes 1179656 | tf_op jit(solution)/shard_map/ppermute | solution.py:387
  43.8 14.1 %collective-permute-start.12 = (bf16[25,16,512]{2,1,0:T(8,128)(2,1)S(1)}, bf16[25,16,512]{2,1,0:T(8,128)(2,1)S(1)}, u32[]{:S(2)}, u32[]{:S(2)}) collective-permute-start(bf16[25,16,512]{2,1,0:T(8,128)(2,1)S(1)} %get-tuple-element.112), channel_id=1, source_target_pairs={{0,8},{1,9},{2,10},{3,11},{4,12},{5,13},{6,14},{7,15},{8,0},{9,1},... | collective-permute-start | bytes 1228808 | tf_op jit(solution)/shard_map/ppermute | solution.py:387
  43.9 14.0 %collective-permute-start.13 = (bf16[24,16,512]{2,1,0:T(8,128)(2,1)S(1)}, bf16[24,16,512]{2,1,0:T(8,128)(2,1)S(1)}, u32[]{:S(2)}, u32[]{:S(2)}) collective-permute-start(bf16[24,16,512]{2,1,0:T(8,128)(2,1)S(1)} %get-tuple-element.113), channel_id=1, source_target_pairs={{0,24},{1,25},{2,26},{3,27},{4,28},{5,29},{6,30},{7,31},{8,16},{9,... | collective-permute-start | bytes 1179656 | tf_op jit(solution)/shard_map/ppermute | solution.py:387
  52.7 9.0 %collective-permute-start.9 = (bf16[30,3,512]{2,1,0:T(4,128)(2,1)S(1)}, bf16[30,3,512]{2,1,0:T(4,128)(2,1)S(1)}, u32[]{:S(2)}, u32[]{:S(2)}) collective-permute-start(bf16[30,3,512]{2,1,0:T(4,128)(2,1)S(1)} %slice.101), channel_id=1, source_target_pairs={{1,2},{2,1},{3,4},{4,3},{5,6},{6,5},{7,8},{8,7},{9,10},{10,9},{11,... | collective-permute-start | bytes 276488 | tf_op jit(solution)/shard_map/ppermute | solution.py:387
  55.0 7.6 %collective-permute-start.17 = (bf16[12,16,512]{2,1,0:T(8,128)(2,1)S(1)}, bf16[12,16,512]{2,1,0:T(8,128)(2,1)S(1)}, u32[]{:S(2)}, u32[]{:S(2)}) collective-permute-start(bf16[12,16,512]{2,1,0:T(8,128)(2,1)S(1)} %get-tuple-element.126), channel_id=1, source_target_pairs={{0,96},{1,97},{2,98},{3,99},{4,100},{5,101},{6,102},{7,103},{8,104... | collective-permute-start | bytes 589832 | tf_op jit(solution)/shard_map/ppermute | solution.py:387
  57.9 5.7 %collective-permute-start.18 = (bf16[12,16,512]{2,1,0:T(8,128)(2,1)S(1)}, bf16[12,16,512]{2,1,0:T(8,128)(2,1)S(1)}, u32[]{:S(2)}, u32[]{:S(2)}) collective-permute-start(bf16[12,16,512]{2,1,0:T(8,128)(2,1)S(1)} %get-tuple-element.127), channel_id=1, source_target_pairs={{0,32},{1,33},{2,34},{3,35},{4,36},{5,37},{6,38},{7,39},{8,40},{9,... | collective-permute-start | bytes 589832 | tf_op jit(solution)/shard_map/ppermute | solution.py:387
  58.1 10.3 %collective-permute-start.14 = (bf16[13,16,512]{2,1,0:T(8,128)(2,1)S(1)}, bf16[13,16,512]{2,1,0:T(8,128)(2,1)S(1)}, u32[]{:S(2)}, u32[]{:S(2)}) collective-permute-start(bf16[13,16,512]{2,1,0:T(8,128)(2,1)S(1)} %get-tuple-element.116), channel_id=1, source_target_pairs={{0,24},{1,25},{2,26},{3,27},{4,28},{5,29},{6,30},{7,31},{8,16},{9,... | collective-permute-start | bytes 638984 | tf_op jit(solution)/shard_map/ppermute | solution.py:387
  59.8 7.3 %collective-permute-start.15 = (bf16[12,16,512]{2,1,0:T(8,128)(2,1)S(1)}, bf16[12,16,512]{2,1,0:T(8,128)(2,1)S(1)}, u32[]{:S(2)}, u32[]{:S(2)}) collective-permute-start(bf16[12,16,512]{2,1,0:T(8,128)(2,1)S(1)} %get-tuple-element.117), channel_id=1, source_target_pairs={{0,8},{1,9},{2,10},{3,11},{4,12},{5,13},{6,14},{7,15},{8,0},{9,1},... | collective-permute-start | bytes 589832 | tf_op jit(solution)/shard_map/ppermute | solution.py:387
  61.9 8.9 %collective-permute-start.11 = (bf16[3,8,512]{2,1,0:T(8,128)(2,1)S(1)}, bf16[3,8,512]{2,1,0:T(8,128)(2,1)S(1)}, u32[]{:S(2)}, u32[]{:S(2)}) collective-permute-start(bf16[3,8,512]{2,1,0:T(8,128)(2,1)S(1)} %get-tuple-element.146), channel_id=1, source_target_pairs={{32,64},{33,65},{34,66},{35,67},{36,68},{37,69},{38,70},{39,71},{4... | collective-permute-start | bytes 73736 | tf_op jit(solution)/shard_map/ppermute | solution.py:387
  63.7 13.1 %collective-permute-start.19 = (bf16[6,16,512]{2,1,0:T(8,128)(2,1)S(1)}, bf16[6,16,512]{2,1,0:T(8,128)(2,1)S(1)}, u32[]{:S(2)}, u32[]{:S(2)}) collective-permute-start(bf16[6,16,512]{2,1,0:T(8,128)(2,1)S(1)} %get-tuple-element.131), channel_id=1, source_target_pairs={{0,8},{1,9},{2,10},{3,11},{4,12},{5,13},{6,14},{7,15},{8,0},{9,1},... | collective-permute-start | bytes 294920 | tf_op jit(solution)/shard_map/ppermute | solution.py:387
  63.9 13.3 %collective-permute-start.20 = (bf16[6,16,512]{2,1,0:T(8,128)(2,1)S(1)}, bf16[6,16,512]{2,1,0:T(8,128)(2,1)S(1)}, u32[]{:S(2)}, u32[]{:S(2)}) collective-permute-start(bf16[6,16,512]{2,1,0:T(8,128)(2,1)S(1)} %get-tuple-element.132), channel_id=1, source_target_pairs={{0,24},{1,25},{2,26},{3,27},{4,28},{5,29},{6,30},{7,31},{8,16},{9,... | collective-permute-start | bytes 294920 | tf_op jit(solution)/shard_map/ppermute | solution.py:387
  67.1 10.2 %collective-permute-start.21 = (bf16[6,16,512]{2,1,0:T(8,128)(2,1)S(1)}, bf16[6,16,512]{2,1,0:T(8,128)(2,1)S(1)}, u32[]{:S(2)}, u32[]{:S(2)}) collective-permute-start(bf16[6,16,512]{2,1,0:T(8,128)(2,1)S(1)} %get-tuple-element.133), channel_id=1, source_target_pairs={{0,16},{1,17},{2,18},{3,19},{4,20},{5,21},{6,22},{7,23},{8,24},{9,... | collective-permute-start | bytes 294920 | tf_op jit(solution)/shard_map/ppermute | solution.py:387
  68.6 14.5 %collective-permute-start.16 = (bf16[9,16,512]{2,1,0:T(8,128)(2,1)S(1)}, bf16[9,16,512]{2,1,0:T(8,128)(2,1)S(1)}, u32[]{:S(2)}, u32[]{:S(2)}) collective-permute-start(bf16[9,16,512]{2,1,0:T(8,128)(2,1)S(1)} %get-tuple-element.120), channel_id=1, source_target_pairs={{0,32},{1,33},{2,34},{3,35},{4,36},{5,37},{6,38},{7,39},{8,40},{9,... | collective-permute-start | bytes 442376 | tf_op jit(solution)/shard_map/ppermute | solution.py:387
  70.8 9.5 %collective-permute-start.22 = (bf16[7,16,512]{2,1,0:T(8,128)(2,1)S(1)}, bf16[7,16,512]{2,1,0:T(8,128)(2,1)S(1)}, u32[]{:S(2)}, u32[]{:S(2)}) collective-permute-start(bf16[7,16,512]{2,1,0:T(8,128)(2,1)S(1)} %get-tuple-element.135), channel_id=1, source_target_pairs={{0,96},{1,97},{2,98},{3,99},{4,100},{5,101},{6,102},{7,103},{8,104... | collective-permute-start | bytes 344072 | tf_op jit(solution)/shard_map/ppermute | solution.py:387
  76.8 6.3 %collective-permute-start.23 = (bf16[7,16,512]{2,1,0:T(8,128)(2,1)S(1)}, bf16[7,16,512]{2,1,0:T(8,128)(2,1)S(1)}, u32[]{:S(2)}, u32[]{:S(2)}) collective-permute-start(bf16[7,16,512]{2,1,0:T(8,128)(2,1)S(1)} %get-tuple-element.136), channel_id=1, source_target_pairs={{0,64},{1,65},{2,66},{3,67},{4,68},{5,69},{6,70},{7,71},{8,72},{9,... | collective-permute-start | bytes 344072 | tf_op jit(solution)/shard_map/ppermute | solution.py:387
  86.1 13.7 %all-to-all-start = ((bf16[8,112,128]{2,1,0:T(8,128)(2,1)}), bf16[8,112,128]{2,1,0:T(8,128)(2,1)S(1)}, u32[]{:S(2)}, u32[]{:S(2)}) async-start(bf16[8,112,128]{2,1,0:T(8,128)(2,1)} %shard_map.140), calls=%async_computation | async-start | bytes 458752 | tf_op jit(solution)/shard_map/all_to_all | solution.py:399
  (1 other events, 0.7 us)

commit v9 on v8

--- a/solution.py
+++ b/solution.py
@@ -314,14 +314,15 @@
 
 
 def reduce_xy_kernel(*refs):
-    out = refs[8]
+    out, flat_s = refs[8:]
     sums = [add4([r[...] for r in refs[:4]]).reshape(-1, D), add4([r[:7] for r in refs[4:8]]).reshape(-1, D)]
     acc = jnp.concatenate(sums, axis=0)
     rows = acc.shape[0]
-    i = lax.broadcasted_iota(jnp.int32, (8 * ZROWS, rows), 0)
-    lane = lax.broadcasted_iota(jnp.int32, (8 * ZROWS, rows), 1)
-    z = i // ZROWS
-    r = (i % ZROWS) // 4
+    per = ZROWS // 4
+    i = lax.broadcasted_iota(jnp.int32, (8 * per, rows), 0)
+    lane = lax.broadcasted_iota(jnp.int32, (8 * per, rows), 1)
+    z = i // per
+    r = i % per
     up = (r % 4) * 16 + z * 2 + r // 4
     down = 96 + z * 8 + (r - 8)
     o = 64 + z * 2 + (r - 16)
@@ -329,12 +330,10 @@
     qkv = jnp.where(part == 0, 80, 144 + part * 16) + z * 2 + (r - 18) // 3
     gain = 192 + (r - 24)
     src = jnp.where(r < 8, up, jnp.where(r < 16, down, jnp.where(r < 18, o, jnp.where(r < 24, qkv, gain))))
-    hit = (lane == src) & (r < 26)
-    picked = jnp.zeros((8 * ZROWS, 128), F32)
+    picked = nn(jnp.where((lane == src) & (r < 26), 1.0, 0.0).astype(BF16), acc)
     for j in range(4):
-        pick = jnp.where(hit & (i % 4 == j), 1.0, 0.0).astype(BF16)
-        picked = picked + nn(pick, acc[:, j * 128 : (j + 1) * 128])
-    out[...] = picked.astype(BF16).reshape(8, ZROWS, 128)
+        flat_s[pl.ds(j, 8 * per, stride=4), :] = picked[:, j * 128 : (j + 1) * 128]
+    out[...] = flat_s[...].astype(BF16).reshape(8, ZROWS, 128)
 
 
 def reduce_z_kernel(got, up, down, o, qkv, gain):
@@ -491,8 +490,8 @@
     gne3 = gne.reshape(ROWS + 2 * RIM, EC, D)
     side = gne3[:, COLS : COLS + RIM].astype(BF16)
     b_first = first((b_p, b_q), Y_BIT)
-    u_first, side = lax.optimization_barrier((u_first, side))
     back_a = send(side, COL_A)
+    b_first, back_a, g_got = lax.optimization_barrier((b_first, back_a, g_got))
     u_p, u_q, *u_own = join(second_kernel, [*u_first, *u_stay], [(12, 16, D)] * 4)
     u_second = second((u_p, u_q), X_BIT)
     b_p, b_q, *b_own = join(second_kernel, [*b_first, *b_stay], [(13, 16, D), (12, 16, D)] * 2)
@@ -507,10 +506,11 @@
     b = to_three(b, X_BIT)
     up_b = b[1][7:].reshape(4, COLS, D)[:RIM]
     (spread,) = call(
-        reduce_xy_kernel, [((8, ZROWS, 128), BF16)], [], 0, 8, 60_000_000, 4_000_000, 5,
+        reduce_xy_kernel, [((8, ZROWS, 128), BF16)], [pltpu.VMEM((8 * ZROWS, 128), F32)], 0, 8, 60_000_000, 4_000_000, 5,
     )(*u, *b)
     up_a = send(jnp.where(row_odd, tail, head), ROW_A)
     got_z = exchange(spread, Z_GROUPS)
+    got_z, up_a = lax.optimization_barrier((got_z, up_a))
     g_up, g_down, g_out, g_qkv, g_gains = call(
         reduce_z_kernel,
         [((32, 128), F32), ((32, 128), F32), ((8, 128), F32), ((24, 128), F32), ((2, D), F32)],

time: 101 us -> 98.6 us (0.976)
  Pallas kernels: 22.5 us -> 20.7 us
  starting transfers between devices: 49.4 us -> 48.3 us
    ppermute x24, starting transfers between devices: 45.8 us -> 43.1 us  [send(): return lax.ppermute(x, AXES, perm)]
    pallas_call x1, Pallas kernels: 3.04 us -> 1.28 us  [per_device(): call(reduce_xy_kernel, [((8, ZROWS, 128), BF16)], [pltpu.VMEM((8 * ZROWS,...]
    all_to_all x1, starting transfers between devices: 3.57 us -> 5.2 us  [exchange(): return lax.all_to_all(x, AXES, 0, 0, axis_index_groups=groups, tiled=True)]
  transfers between devices with their start and end apart: 25 -> 25, of which waited for: 7 -> 9; matrix products, arithmetic and copies ran while one was open for 2% -> 1% of each run, Pallas kernels for 12% -> 12%
where the time goes in v9:
time: 98.6 us; the launch traced here: 97.7 us
  starting transfers between devices  48.3 us (49%)
  waiting for transfers between devices  23.3 us (24%)
  Pallas kernels  20.7 us (21%)
  other arithmetic  2.92 us (3%)
  local copies, waits for them, and re-layouts  1.4 us (1%)
  between operations  1.02 us (1%)
    ppermute x24, starting transfers between devices, send(): return lax.ppermute(x, AXES, perm)  43.1 us
    ppermute x24, waiting for transfers between devices, send(): return lax.ppermute(x, AXES, perm)  13.9 us
    all_to_all x1, waiting for transfers between devices, exchange(): return lax.all_to_all(x, AXES, 0, 0, axis_index_groups=groups, tiled=True)  9.42 us
    pallas_call x1, Pallas kernels, per_device(): call(forward_kernel, [half_u, half_u, half_d, half_d, ((TOK, D), BF16), (...  6.99 us
    all_to_all x1, starting transfers between devices, exchange(): return lax.all_to_all(x, AXES, 0, 0, axis_index_groups=groups, tiled=True)  5.2 us
    pallas_call x1, Pallas kernels, per_device(): call(backward_kernel, [half_k, half_k, ((TOK, D), BF16), ((EXT, 2 * D), B...  4.03 us
  transfers between devices with their start and end apart: 25, of which 9 were waited for; matrix products, arithmetic and copies ran while one was open for 1% of the time, Pallas kernels for 12%

profile of v9, /device:TPU:8, one launch (start us, length us, event | category | flops | bytes accessed | tf_op | source)
XLA Modules:
  0.0 97.7 jit_solution(2744281448864045982)
XLA Ops:
  0.6 1.2 %broadcast_select_fusion = (bf16[24,3,512]{2,1,0:T(4,128)(2,1)S(1)}, bf16[24,3,512]{2,1,0:T(4,128)(2,1)S(1)}) fusion(pred[]{:T(512)S(6)} %eq.6, bf16[24,8,512]{2,1,0:T(8,128)(2,1)} %param.8), kind=kLoop, calls=%fused_computation.19 | loop fusion | flops 73728 | bytes 294913 | tf_op jit(solution)/shard_map/jit(_where)/select_n | solution.py:411
  1.8 5.9 %collective-permute-start = (bf16[24,3,512]{2,1,0:T(4,128)(2,1)S(1)}, bf16[24,3,512]{2,1,0:T(4,128)(2,1)S(1)}, u32[]{:S(2)}, u32[]{:S(2)}) collective-permute-start(bf16[24,3,512]{2,1,0:T(4,128)(2,1)S(1)} %get-tuple-element.155), channel_id=1, source_target_pairs={{1,2},{2,1},{3,4},{4,3},{5,6},{6,5},{7,8},{8,7},{9,10},{10,9},{11,... | collective-permute-start | bytes 221192 | tf_op jit(solution)/shard_map/ppermute | solution.py:386
  8.0 0.7 copy-done.7
  8.6 1.2 %shard_map.127.bias = f32[3,64,256]{2,1,0:T(8,128)S(1)} custom-call(s32[3]{0:T(128)S(1)} %pad_add_fusion.coord, s32[3,1,49]{2,1,0:T(1,128)S(1)} %copy-done.7), custom_call_target="tpu_custom_call" | custom-call | flops 402653184 | bytes 4000000 | tf_op jit(solution)/shard_map/pallas_call | solution.py:413
  9.9 1.3 %collective-permute-done = bf16[24,3,512]{2,1,0:T(4,128)(2,1)S(1)} collective-permute-done((bf16[24,3,512]{2,1,0:T(4,128)(2,1)S(1)}, bf16[24,3,512]{2,1,0:T(4,128)(2,1)S(1)}, u32[]{:S(2)}, u32[]{:S(2)}) %collective-permute-start) | collective-permute-done | bytes 73760 | tf_op jit(solution)/shard_map/ppermute | solution.py:386
  12.1 4.3 %collective-permute-start.3 = (bf16[3,16,512]{2,1,0:T(8,128)(2,1)S(1)}, bf16[3,16,512]{2,1,0:T(8,128)(2,1)S(1)}, u32[]{:S(2)}, u32[]{:S(2)}) collective-permute-start(bf16[3,16,512]{2,1,0:T(8,128)(2,1)S(1)} %get-tuple-element.150), channel_id=1, source_target_pairs={{0,32},{1,33},{2,34},{3,35},{4,36},{5,37},{6,38},{7,39},{8,40},{9,... | collective-permute-start | bytes 147464 | tf_op jit(solution)/shard_map/ppermute | solution.py:386
  16.4 1.3 %shard_map.129 = (bf16[512,512]{1,0:T(8,128)(2,1)S(1)}, bf16[512,512]{1,0:T(8,128)(2,1)S(1)}, bf16[512,512]{1,0:T(8,128)(2,1)S(1)}) custom-call(s32[3]{0:T(128)S(1)} %pad_add_fusion.coord), custom_call_target="tpu_custom_call" | custom-call | flops 402653184 | bytes 4000000 | tf_op jit(solution)/shard_map/pallas_call | solution.py:420
  17.8 0.8 shard_map.128.gact
  19.1 1.6 %shard_map.130 = (bf16[192,512]{1,0:T(8,128)(2,1)S(1)}, bf16[192,512]{1,0:T(8,128)(2,1)S(1)}, bf16[384,512]{1,0:T(8,128)(2,1)S(1)}, bf16[384,1024]{1,0:T(8,128)(...) custom-call(bf16[24,16,512]{2,1,0:T(8,128)(2,1)S(1)} %maximum_maximum_fusion.mid, ...), custom_call_target="tpu_custom_call" | custom-call | flops 600000000 | bytes 5000000 | tf_op jit(solution)/shard_map/pallas_call | solution.py:427
  20.8 7.0 %shard_map.131 = (bf16[16,5,16,512]{3,2,1,0:T(8,128)(2,1)S(1)}, bf16[16,5,16,512]{3,2,1,0:T(8,128)(2,1)S(1)}, bf16[4,4,2,32,512]{4,3,2,1,0:T(8,128)(2,1)S(1)}, b...) custom-call(s32[3]{0:T(128)S(1)} %pad_add_fusion.coord, ...), custom_call_target="tpu_custom_call" | custom-call | flops 4000000000 | bytes 20000000 | tf_op jit(solution)/shard_map/pallas_call | solution.py:438
  28.4 4.0 %shard_map.132 = (bf16[48,16,512]{2,1,0:T(8,128)(2,1)S(1)}, bf16[48,16,512]{2,1,0:T(8,128)(2,1)S(1)}, bf16[192,512]{1,0:T(8,128)(2,1)S(1)}, bf16[512,1024]{1,0:T(8,128)(2,1)S(1)}) custom-call(bf16[192,512]{1,0:T(8,128)(2,1)S(1)} %get-tuple-element.88.gm, bf16[512,512]{1,0:T(8,128)(2,1)S(1)} %copy-done.6, bf16[192,512]{1,0:T(8,128)(2,1)S(1)} %get-tuple-element.84.q_i.q, ...), custom_call_target="tpu_custom_call" | custom-call | flops 2500000000 | bytes 10000000 | tf_op jit(solution)/shard_map/pallas_call | solution.py:449
  32.8 1.5 %shard_map.133 = (f32[480,512]{1,0:T(8,128)S(1)}, f32[192,512]{1,0:T(8,128)S(1)}, bf16[16,512]{1,0:T(8,128)(2,1)S(1)}, bf16[16,16,512]{2,1,0:T(8,128)(2,1)S(1)}) custom-call(s32[3]{0:T(128)S(1)} %pad_add_fusion.coord, bf16[192,512]{1,0:T(8,128)(2,1)S(1)} %get-tuple-element.95.dq, bf16[512,1024]{1,0:T(8,128)(2,1)S(1)} %get-tuple-element.96.dkv, ...), custom_call_target="tpu_custom_call" | custom-call | flops 600000000 | bytes 4000000 | tf_op jit(solution)/shard_map/pallas_call | solution.py:456
  34.9 1.1 %collective-permute-done.7.gg = bf16[16,16,512]{2,1,0:T(8,128)(2,1)S(1)} collective-permute-done((bf16[16,16,512]{2,1,0:T(8,128)(2,1)S(1)}, bf16[16,16,512]{2,1,0:T(8,128)(2,1)S(1)}, u32[]{:S(2)}, u32[]{:S(2)}) %collective-permute-start.7) | collective-permute-done | bytes 262176 | tf_op jit(solution)/shard_map/ppermute | solution.py:386
  36.9 8.1 %collective-permute-start.12 = (bf16[24,16,512]{2,1,0:T(8,128)(2,1)S(1)}, bf16[24,16,512]{2,1,0:T(8,128)(2,1)S(1)}, u32[]{:S(2)}, u32[]{:S(2)}) collective-permute-start(bf16[24,16,512]{2,1,0:T(8,128)(2,1)S(1)} %get-tuple-element.117), channel_id=1, source_target_pairs={{0,96},{1,97},{2,98},{3,99},{4,100},{5,101},{6,102},{7,103},{8,104... | collective-permute-start | bytes 1179656 | tf_op jit(solution)/shard_map/ppermute | solution.py:386
  45.0 2.8 %collective-permute-start.9 = (bf16[24,16,512]{2,1,0:T(8,128)(2,1)S(1)}, bf16[24,16,512]{2,1,0:T(8,128)(2,1)S(1)}, u32[]{:S(2)}, u32[]{:S(2)}) collective-permute-start(bf16[24,16,512]{2,1,0:T(8,128)(2,1)S(1)} %get-tuple-element.111), channel_id=1, source_target_pairs={{0,24},{1,25},{2,26},{3,27},{4,28},{5,29},{6,30},{7,31},{8,16},{9,... | collective-permute-start | bytes 1179656 | tf_op jit(solution)/shard_map/ppermute | solution.py:386
  47.9 2.4 %collective-permute-start.10 = (bf16[30,3,512]{2,1,0:T(4,128)(2,1)S(1)}, bf16[30,3,512]{2,1,0:T(4,128)(2,1)S(1)}, u32[]{:S(2)}, u32[]{:S(2)}) collective-permute-start(bf16[30,3,512]{2,1,0:T(4,128)(2,1)S(1)} %slice.100), channel_id=1, source_target_pairs={{1,2},{2,1},{3,4},{4,3},{5,6},{6,5},{7,8},{8,7},{9,10},{10,9},{11,... | collective-permute-start | bytes 276488 | tf_op jit(solution)/shard_map/ppermute | solution.py:386
  50.3 4.0 %collective-permute-done.12.q_got = bf16[24,16,512]{2,1,0:T(8,128)(2,1)S(1)} collective-permute-done((bf16[24,16,512]{2,1,0:T(8,128)(2,1)S(1)}, bf16[24,16,512]{2,1,0:T(8,128)(2,1)S(1)}, u32[]{:S(2)}, u32[]{:S(2)}) %collective-permute-start.12) | collective-permute-done | bytes 393248 | tf_op jit(solution)/shard_map/ppermute | solution.py:386
  54.4 3.0 %collective-permute-start.13 = (bf16[12,16,512]{2,1,0:T(8,128)(2,1)S(1)}, bf16[12,16,512]{2,1,0:T(8,128)(2,1)S(1)}, u32[]{:S(2)}, u32[]{:S(2)}) collective-permute-start(bf16[12,16,512]{2,1,0:T(8,128)(2,1)S(1)} %get-tuple-element.120), channel_id=1, source_target_pairs={{0,96},{1,97},{2,98},{3,99},{4,100},{5,101},{6,102},{7,103},{8,104... | collective-permute-start | bytes 589832 | tf_op jit(solution)/shard_map/ppermute | solution.py:386
  57.8 2.6 %collective-permute-start.18 = (bf16[13,16,512]{2,1,0:T(8,128)(2,1)S(1)}, bf16[13,16,512]{2,1,0:T(8,128)(2,1)S(1)}, u32[]{:S(2)}, u32[]{:S(2)}) collective-permute-start(bf16[13,16,512]{2,1,0:T(8,128)(2,1)S(1)} %get-tuple-element.132), channel_id=1, source_target_pairs={{0,24},{1,25},{2,26},{3,27},{4,28},{5,29},{6,30},{7,31},{8,16},{9,... | collective-permute-start | bytes 638984 | tf_op jit(solution)/shard_map/ppermute | solution.py:386
  60.4 1.3 %collective-permute-start.19 = (bf16[12,16,512]{2,1,0:T(8,128)(2,1)S(1)}, bf16[12,16,512]{2,1,0:T(8,128)(2,1)S(1)}, u32[]{:S(2)}, u32[]{:S(2)}) collective-permute-start(bf16[12,16,512]{2,1,0:T(8,128)(2,1)S(1)} %get-tuple-element.133), channel_id=1, source_target_pairs={{0,8},{1,9},{2,10},{3,11},{4,12},{5,13},{6,14},{7,15},{8,0},{9,1},... | collective-permute-start | bytes 589832 | tf_op jit(solution)/shard_map/ppermute | solution.py:386
  62.0 1.2 %collective-permute-done.14.q_got = bf16[12,16,512]{2,1,0:T(8,128)(2,1)S(1)} collective-permute-done((bf16[12,16,512]{2,1,0:T(8,128)(2,1)S(1)}, bf16[12,16,512]{2,1,0:T(8,128)(2,1)S(1)}, u32[]{:S(2)}, u32[]{:S(2)}) %collective-permute-start.14) | collective-permute-done | bytes 196640 | tf_op jit(solution)/shard_map/ppermute | solution.py:386
  63.2 1.8 %collective-permute-start.15 = (bf16[6,16,512]{2,1,0:T(8,128)(2,1)S(1)}, bf16[6,16,512]{2,1,0:T(8,128)(2,1)S(1)}, u32[]{:S(2)}, u32[]{:S(2)}) collective-permute-start(bf16[6,16,512]{2,1,0:T(8,128)(2,1)S(1)} %get-tuple-element.125), channel_id=1, source_target_pairs={{0,8},{1,9},{2,10},{3,11},{4,12},{5,13},{6,14},{7,15},{8,0},{9,1},... | collective-permute-start | bytes 294920 | tf_op jit(solution)/shard_map/ppermute | solution.py:386
  65.0 2.0 %collective-permute-done.19.q_got = bf16[12,16,512]{2,1,0:T(8,128)(2,1)S(1)} collective-permute-done((bf16[12,16,512]{2,1,0:T(8,128)(2,1)S(1)}, bf16[12,16,512]{2,1,0:T(8,128)(2,1)S(1)}, u32[]{:S(2)}, u32[]{:S(2)}) %collective-permute-start.19) | collective-permute-done | bytes 196640 | tf_op jit(solution)/shard_map/ppermute | solution.py:386
  67.1 1.5 %collective-permute-start.20 = (bf16[9,16,512]{2,1,0:T(8,128)(2,1)S(1)}, bf16[9,16,512]{2,1,0:T(8,128)(2,1)S(1)}, u32[]{:S(2)}, u32[]{:S(2)}) collective-permute-start(bf16[9,16,512]{2,1,0:T(8,128)(2,1)S(1)} %get-tuple-element.137), channel_id=1, source_target_pairs={{0,32},{1,33},{2,34},{3,35},{4,36},{5,37},{6,38},{7,39},{8,40},{9,... | collective-permute-start | bytes 442376 | tf_op jit(solution)/shard_map/ppermute | solution.py:386
  68.6 1.0 %collective-permute-start.16 = (bf16[6,16,512]{2,1,0:T(8,128)(2,1)S(1)}, bf16[6,16,512]{2,1,0:T(8,128)(2,1)S(1)}, u32[]{:S(2)}, u32[]{:S(2)}) collective-permute-start(bf16[6,16,512]{2,1,0:T(8,128)(2,1)S(1)} %get-tuple-element.126), channel_id=1, source_target_pairs={{0,24},{1,25},{2,26},{3,27},{4,28},{5,29},{6,30},{7,31},{8,16},{9,... | collective-permute-start | bytes 294920 | tf_op jit(solution)/shard_map/ppermute | solution.py:386
  69.7 2.4 %collective-permute-start.17 = (bf16[6,16,512]{2,1,0:T(8,128)(2,1)S(1)}, bf16[6,16,512]{2,1,0:T(8,128)(2,1)S(1)}, u32[]{:S(2)}, u32[]{:S(2)}) collective-permute-start(bf16[6,16,512]{2,1,0:T(8,128)(2,1)S(1)} %get-tuple-element.127), channel_id=1, source_target_pairs={{0,16},{1,17},{2,18},{3,19},{4,20},{5,21},{6,22},{7,23},{8,24},{9,... | collective-permute-start | bytes 294920 | tf_op jit(solution)/shard_map/ppermute | solution.py:386
  72.7 2.3 %collective-permute-start.22 = (bf16[7,16,512]{2,1,0:T(8,128)(2,1)S(1)}, bf16[7,16,512]{2,1,0:T(8,128)(2,1)S(1)}, u32[]{:S(2)}, u32[]{:S(2)}) collective-permute-start(bf16[7,16,512]{2,1,0:T(8,128)(2,1)S(1)} %get-tuple-element.139), channel_id=1, source_target_pairs={{0,64},{1,65},{2,66},{3,67},{4,68},{5,69},{6,70},{7,71},{8,72},{9,... | collective-permute-start | bytes 344072 | tf_op jit(solution)/shard_map/ppermute | solution.py:386
  75.8 3.5 %collective-permute-done.21.refs_6_ = bf16[7,16,512]{2,1,0:T(8,128)(2,1)S(1)} collective-permute-done((bf16[7,16,512]{2,1,0:T(8,128)(2,1)S(1)}, bf16[7,16,512]{2,1,0:T(8,128)(2,1)S(1)}, u32[]{:S(2)}, u32[]{:S(2)}) %collective-permute-start.21) | collective-permute-done | bytes 114720 | tf_op jit(solution)/shard_map/ppermute | solution.py:386
  79.3 1.3 %shard_map.140 = bf16[8,112,128]{2,1,0:T(8,128)(2,1)} custom-call(bf16[6,16,512]{2,1,0:T(8,128)(2,1)S(1)} %get-tuple-element.124.refs_0_, bf16[6,16,512]{2,1,0:T(8,128)(2,1)S(1)} %collective-permute-done.15.refs_1_, bf16[6,16,512]{2,1,0:T(8,128)(2,1)S(1)} %collective-permute-done.16.refs_2_, bf16[6,16,512]{2,1,0:T(8,128)(2,1)S(1)} %collective-permute-done.17.refs_3_, ...), custom_call_target="tpu_custom_call" | custom-call | flops 60000000 | bytes 4000000 | tf_op jit(solution)/shard_map/pallas_call | solution.py:508
  80.6 5.2 %all-to-all-start = ((bf16[8,112,128]{2,1,0:T(8,128)(2,1)}), bf16[8,112,128]{2,1,0:T(8,128)(2,1)S(1)}, u32[]{:S(2)}, u32[]{:S(2)}) async-start(bf16[8,112,128]{2,1,0:T(8,128)(2,1)} %shard_map.140), calls=%async_computation | async-start | bytes 458752 | tf_op jit(solution)/shard_map/all_to_all | solution.py:398
  86.5 9.4 %all-to-all-done.got = bf16[8,112,128]{2,1,0:T(8,128)(2,1)S(1)} async-done(((bf16[8,112,128]{2,1,0:T(8,128)(2,1)}), bf16[8,112,128]{2,1,0:T(8,128)(2,1)S(1)}, u32[]{:S(2)}, u32[]{:S(2)}) %all-to-all-start) | async-done | bytes 229408 | tf_op jit(solution)/shard_map/all_to_all | solution.py:398
  96.1 0.9 fusion.7
  (71 shorter events, 7.9 us)
Async XLA Ops:
  0.6 10.6 %copy-start = (bf16[24,8,512]{2,1,0:T(8,128)(2,1)S(1)}, bf16[24,8,512]{2,1,0:T(8,128)(2,1)}, u32[]{:S(2)}) copy-start(bf16[24,8,512]{2,1,0:T(8,128)(2,1)} %param.8) | copy-start | bytes 589828
  1.8 9.4 %collective-permute-start = (bf16[24,3,512]{2,1,0:T(4,128)(2,1)S(1)}, bf16[24,3,512]{2,1,0:T(4,128)(2,1)S(1)}, u32[]{:S(2)}, u32[]{:S(2)}) collective-permute-start(bf16[24,3,512]{2,1,0:T(4,128)(2,1)S(1)} %get-tuple-element.155), channel_id=1, source_target_pairs={{1,2},{2,1},{3,4},{4,3},{5,6},{6,5},{7,8},{8,7},{9,10},{10,9},{11,... | collective-permute-start | bytes 221192 | tf_op jit(solution)/shard_map/ppermute | solution.py:386
  7.7 3.5 %collective-permute-start.1 = (bf16[24,3,512]{2,1,0:T(4,128)(2,1)S(1)}, bf16[24,3,512]{2,1,0:T(4,128)(2,1)S(1)}, u32[]{:S(2)}, u32[]{:S(2)}) collective-permute-start(bf16[24,3,512]{2,1,0:T(4,128)(2,1)S(1)} %get-tuple-element.154), channel_id=1, source_target_pairs={{0,1},{1,0},{2,3},{3,2},{4,5},{5,4},{6,7},{7,6},{8,9},{9,8},{10,11... | collective-permute-start | bytes 221192 | tf_op jit(solution)/shard_map/ppermute | solution.py:386
  9.9 7.8 %copy-start.2 = (bf16[2048,512]{1,0:T(8,128)(2,1)S(1)}, bf16[2048,512]{1,0:T(8,128)(2,1)}, u32[]{:S(2)}) copy-start(bf16[2048,512]{1,0:T(8,128)(2,1)} %w_down.1) | copy-start | bytes 6291460
  9.9 7.8 %copy-start.3 = (bf16[24,8,512]{2,1,0:T(8,128)(2,1)S(1)}, bf16[24,8,512]{2,1,0:T(8,128)(2,1)}, u32[]{:S(2)}) copy-start(bf16[24,8,512]{2,1,0:T(8,128)(2,1)} %param.9) | copy-start | bytes 589828
  11.4 9.4 %collective-permute-start.2 = (bf16[3,16,512]{2,1,0:T(8,128)(2,1)S(1)}, bf16[3,16,512]{2,1,0:T(8,128)(2,1)S(1)}, u32[]{:S(2)}, u32[]{:S(2)}) collective-permute-start(bf16[3,16,512]{2,1,0:T(8,128)(2,1)S(1)} %get-tuple-element.151), channel_id=1, source_target_pairs={{32,64},{33,65},{34,66},{35,67},{36,68},{37,69},{38,70},{39,71},{4... | collective-permute-start | bytes 147464 | tf_op jit(solution)/shard_map/ppermute | solution.py:386
  12.1 8.7 %collective-permute-start.3 = (bf16[3,16,512]{2,1,0:T(8,128)(2,1)S(1)}, bf16[3,16,512]{2,1,0:T(8,128)(2,1)S(1)}, u32[]{:S(2)}, u32[]{:S(2)}) collective-permute-start(bf16[3,16,512]{2,1,0:T(8,128)(2,1)S(1)} %get-tuple-element.150), channel_id=1, source_target_pairs={{0,32},{1,33},{2,34},{3,35},{4,36},{5,37},{6,38},{7,39},{8,40},{9,... | collective-permute-start | bytes 147464 | tf_op jit(solution)/shard_map/ppermute | solution.py:386
  17.7 1.4 %copy-start.1 = (bf16[512,1536]{1,0:T(8,128)(2,1)S(1)}, bf16[512,1536]{1,0:T(8,128)(2,1)}, u32[]{:S(2)}) copy-start(bf16[512,1536]{1,0:T(8,128)(2,1)} %w_qkv.5) | copy-start | bytes 4718596
  17.7 1.4 %copy-start.4 = (f32[2,512]{1,0:T(2,128)S(1)}, f32[2,512]{1,0:T(2,128)}, u32[]{:S(2)}) copy-start(f32[2,512]{1,0:T(2,128)} %gains.3) | copy-start | bytes 12292
  17.8 3.1 %copy-start.6 = (bf16[512,512]{1,0:T(8,128)(2,1)S(1)}, bf16[512,512]{1,0:T(8,128)(2,1)}, u32[]{:S(2)}) copy-start(bf16[512,512]{1,0:T(8,128)(2,1)} %w_out.3) | copy-start | bytes 1572868
  18.6 2.2 %copy-start.5 = (bf16[512,2048]{1,0:T(8,128)(2,1)S(1)}, bf16[512,2048]{1,0:T(8,128)(2,1)}, u32[]{:S(2)}) copy-start(bf16[512,2048]{1,0:T(8,128)(2,1)} %w_up.1) | copy-start | bytes 6291460
  27.8 4.7 %collective-permute-start.4 = (bf16[16,5,16,512]{3,2,1,0:T(8,128)(2,1)S(1)}, bf16[16,5,16,512]{3,2,1,0:T(8,128)(2,1)S(1)}, u32[]{:S(2)}, u32[]{:S(2)}) collective-permute-start(bf16[16,5,16,512]{3,2,1,0:T(8,128)(2,1)S(1)} %get-tuple-element.100), channel_id=1, source_target_pairs={{0,1},{1,0},{2,3},{3,2},{4,5},{5,4},{6,7},{7,6},{8,9},{9,8},{10,11... | collective-permute-start | bytes 3932168 | tf_op jit(solution)/shard_map/ppermute | solution.py:386
  27.9 4.5 %collective-permute-start.5 = (bf16[4,4,2,32,512]{4,3,2,1,0:T(8,128)(2,1)S(1)}, bf16[4,4,2,32,512]{4,3,2,1,0:T(8,128)(2,1)S(1)}, u32[]{:S(2)}, u32[]{:S(2)}) collective-permute-start(bf16[4,4,2,32,512]{4,3,2,1,0:T(8,128)(2,1)S(1)} %get-tuple-element.101), channel_id=1, source_target_pairs={{0,1},{1,0},{2,3},{3,2},{4,5},{5,4},{6,7},{7,6},{8,9},{9,8},{10,11... | collective-permute-start | bytes 3145736 | tf_op jit(solution)/shard_map/ppermute | solution.py:386
  32.5 2.4 %collective-permute-start.6 = (bf16[48,16,512]{2,1,0:T(8,128)(2,1)S(1)}, bf16[48,16,512]{2,1,0:T(8,128)(2,1)S(1)}, u32[]{:S(2)}, u32[]{:S(2)}) collective-permute-start(bf16[48,16,512]{2,1,0:T(8,128)(2,1)S(1)} %get-tuple-element.105), channel_id=1, source_target_pairs={{0,1},{1,0},{2,3},{3,2},{4,5},{5,4},{6,7},{7,6},{8,9},{9,8},{10,11... | collective-permute-start | bytes 2359304 | tf_op jit(solution)/shard_map/ppermute | solution.py:386
  34.3 1.6 %collective-permute-start.7 = (bf16[16,16,512]{2,1,0:T(8,128)(2,1)S(1)}, bf16[16,16,512]{2,1,0:T(8,128)(2,1)S(1)}, u32[]{:S(2)}, u32[]{:S(2)}) collective-permute-start(bf16[16,16,512]{2,1,0:T(8,128)(2,1)S(1)} %get-tuple-element.109), channel_id=1, source_target_pairs={{0,1},{1,0},{2,3},{3,2},{4,5},{5,4},{6,7},{7,6},{8,9},{9,8},{10,11... | collective-permute-start | bytes 786440 | tf_op jit(solution)/shard_map/ppermute | solution.py:386
  36.3 21.2 %collective-permute-start.8 = (bf16[25,16,512]{2,1,0:T(8,128)(2,1)S(1)}, bf16[25,16,512]{2,1,0:T(8,128)(2,1)S(1)}, u32[]{:S(2)}, u32[]{:S(2)}) collective-permute-start(bf16[25,16,512]{2,1,0:T(8,128)(2,1)S(1)} %get-tuple-element.110), channel_id=1, source_target_pairs={{0,8},{1,9},{2,10},{3,11},{4,12},{5,13},{6,14},{7,15},{8,0},{9,1},... | collective-permute-start | bytes 1228808 | tf_op jit(solution)/shard_map/ppermute | solution.py:386
  36.8 13.5 %collective-permute-start.11 = (bf16[24,16,512]{2,1,0:T(8,128)(2,1)S(1)}, bf16[24,16,512]{2,1,0:T(8,128)(2,1)S(1)}, u32[]{:S(2)}, u32[]{:S(2)}) collective-permute-start(bf16[24,16,512]{2,1,0:T(8,128)(2,1)S(1)} %get-tuple-element.116), channel_id=1, source_target_pairs={{0,32},{1,33},{2,34},{3,35},{4,36},{5,37},{6,38},{7,39},{8,40},{9,... | collective-permute-start | bytes 1179656 | tf_op jit(solution)/shard_map/ppermute | solution.py:386
  36.9 17.3 %collective-permute-start.12 = (bf16[24,16,512]{2,1,0:T(8,128)(2,1)S(1)}, bf16[24,16,512]{2,1,0:T(8,128)(2,1)S(1)}, u32[]{:S(2)}, u32[]{:S(2)}) collective-permute-start(bf16[24,16,512]{2,1,0:T(8,128)(2,1)S(1)} %get-tuple-element.117), channel_id=1, source_target_pairs={{0,96},{1,97},{2,98},{3,99},{4,100},{5,101},{6,102},{7,103},{8,104... | collective-permute-start | bytes 1179656 | tf_op jit(solution)/shard_map/ppermute | solution.py:386
  45.0 12.5 %collective-permute-start.9 = (bf16[24,16,512]{2,1,0:T(8,128)(2,1)S(1)}, bf16[24,16,512]{2,1,0:T(8,128)(2,1)S(1)}, u32[]{:S(2)}, u32[]{:S(2)}) collective-permute-start(bf16[24,16,512]{2,1,0:T(8,128)(2,1)S(1)} %get-tuple-element.111), channel_id=1, source_target_pairs={{0,24},{1,25},{2,26},{3,27},{4,28},{5,29},{6,30},{7,31},{8,16},{9,... | collective-permute-start | bytes 1179656 | tf_op jit(solution)/shard_map/ppermute | solution.py:386
  47.9 9.6 %collective-permute-start.10 = (bf16[30,3,512]{2,1,0:T(4,128)(2,1)S(1)}, bf16[30,3,512]{2,1,0:T(4,128)(2,1)S(1)}, u32[]{:S(2)}, u32[]{:S(2)}) collective-permute-start(bf16[30,3,512]{2,1,0:T(4,128)(2,1)S(1)} %slice.100), channel_id=1, source_target_pairs={{1,2},{2,1},{3,4},{4,3},{5,6},{6,5},{7,8},{8,7},{9,10},{10,9},{11,... | collective-permute-start | bytes 276488 | tf_op jit(solution)/shard_map/ppermute | solution.py:386
  54.4 7.5 %collective-permute-start.13 = (bf16[12,16,512]{2,1,0:T(8,128)(2,1)S(1)}, bf16[12,16,512]{2,1,0:T(8,128)(2,1)S(1)}, u32[]{:S(2)}, u32[]{:S(2)}) collective-permute-start(bf16[12,16,512]{2,1,0:T(8,128)(2,1)S(1)} %get-tuple-element.120), channel_id=1, source_target_pairs={{0,96},{1,97},{2,98},{3,99},{4,100},{5,101},{6,102},{7,103},{8,104... | collective-permute-start | bytes 589832 | tf_op jit(solution)/shard_map/ppermute | solution.py:386
  57.5 5.7 %collective-permute-start.14 = (bf16[12,16,512]{2,1,0:T(8,128)(2,1)S(1)}, bf16[12,16,512]{2,1,0:T(8,128)(2,1)S(1)}, u32[]{:S(2)}, u32[]{:S(2)}) collective-permute-start(bf16[12,16,512]{2,1,0:T(8,128)(2,1)S(1)} %get-tuple-element.121), channel_id=1, source_target_pairs={{0,32},{1,33},{2,34},{3,35},{4,36},{5,37},{6,38},{7,39},{8,40},{9,... | collective-permute-start | bytes 589832 | tf_op jit(solution)/shard_map/ppermute | solution.py:386
  57.8 9.3 %collective-permute-start.18 = (bf16[13,16,512]{2,1,0:T(8,128)(2,1)S(1)}, bf16[13,16,512]{2,1,0:T(8,128)(2,1)S(1)}, u32[]{:S(2)}, u32[]{:S(2)}) collective-permute-start(bf16[13,16,512]{2,1,0:T(8,128)(2,1)S(1)} %get-tuple-element.132), channel_id=1, source_target_pairs={{0,24},{1,25},{2,26},{3,27},{4,28},{5,29},{6,30},{7,31},{8,16},{9,... | collective-permute-start | bytes 638984 | tf_op jit(solution)/shard_map/ppermute | solution.py:386
  60.4 6.6 %collective-permute-start.19 = (bf16[12,16,512]{2,1,0:T(8,128)(2,1)S(1)}, bf16[12,16,512]{2,1,0:T(8,128)(2,1)S(1)}, u32[]{:S(2)}, u32[]{:S(2)}) collective-permute-start(bf16[12,16,512]{2,1,0:T(8,128)(2,1)S(1)} %get-tuple-element.133), channel_id=1, source_target_pairs={{0,8},{1,9},{2,10},{3,11},{4,12},{5,13},{6,14},{7,15},{8,0},{9,1},... | collective-permute-start | bytes 589832 | tf_op jit(solution)/shard_map/ppermute | solution.py:386
  63.2 9.4 %collective-permute-start.15 = (bf16[6,16,512]{2,1,0:T(8,128)(2,1)S(1)}, bf16[6,16,512]{2,1,0:T(8,128)(2,1)S(1)}, u32[]{:S(2)}, u32[]{:S(2)}) collective-permute-start(bf16[6,16,512]{2,1,0:T(8,128)(2,1)S(1)} %get-tuple-element.125), channel_id=1, source_target_pairs={{0,8},{1,9},{2,10},{3,11},{4,12},{5,13},{6,14},{7,15},{8,0},{9,1},... | collective-permute-start | bytes 294920 | tf_op jit(solution)/shard_map/ppermute | solution.py:386
  67.1 12.2 %collective-permute-start.20 = (bf16[9,16,512]{2,1,0:T(8,128)(2,1)S(1)}, bf16[9,16,512]{2,1,0:T(8,128)(2,1)S(1)}, u32[]{:S(2)}, u32[]{:S(2)}) collective-permute-start(bf16[9,16,512]{2,1,0:T(8,128)(2,1)S(1)} %get-tuple-element.137), channel_id=1, source_target_pairs={{0,32},{1,33},{2,34},{3,35},{4,36},{5,37},{6,38},{7,39},{8,40},{9,... | collective-permute-start | bytes 442376 | tf_op jit(solution)/shard_map/ppermute | solution.py:386
  68.6 6.5 %collective-permute-start.16 = (bf16[6,16,512]{2,1,0:T(8,128)(2,1)S(1)}, bf16[6,16,512]{2,1,0:T(8,128)(2,1)S(1)}, u32[]{:S(2)}, u32[]{:S(2)}) collective-permute-start(bf16[6,16,512]{2,1,0:T(8,128)(2,1)S(1)} %get-tuple-element.126), channel_id=1, source_target_pairs={{0,24},{1,25},{2,26},{3,27},{4,28},{5,29},{6,30},{7,31},{8,16},{9,... | collective-permute-start | bytes 294920 | tf_op jit(solution)/shard_map/ppermute | solution.py:386
  69.7 6.1 %collective-permute-start.17 = (bf16[6,16,512]{2,1,0:T(8,128)(2,1)S(1)}, bf16[6,16,512]{2,1,0:T(8,128)(2,1)S(1)}, u32[]{:S(2)}, u32[]{:S(2)}) collective-permute-start(bf16[6,16,512]{2,1,0:T(8,128)(2,1)S(1)} %get-tuple-element.127), channel_id=1, source_target_pairs={{0,16},{1,17},{2,18},{3,19},{4,20},{5,21},{6,22},{7,23},{8,24},{9,... | collective-permute-start | bytes 294920 | tf_op jit(solution)/shard_map/ppermute | solution.py:386
  72.1 7.2 %collective-permute-start.21 = (bf16[7,16,512]{2,1,0:T(8,128)(2,1)S(1)}, bf16[7,16,512]{2,1,0:T(8,128)(2,1)S(1)}, u32[]{:S(2)}, u32[]{:S(2)}) collective-permute-start(bf16[7,16,512]{2,1,0:T(8,128)(2,1)S(1)} %get-tuple-element.138), channel_id=1, source_target_pairs={{0,96},{1,97},{2,98},{3,99},{4,100},{5,101},{6,102},{7,103},{8,104... | collective-permute-start | bytes 344072 | tf_op jit(solution)/shard_map/ppermute | solution.py:386
  72.7 6.6 %collective-permute-start.22 = (bf16[7,16,512]{2,1,0:T(8,128)(2,1)S(1)}, bf16[7,16,512]{2,1,0:T(8,128)(2,1)S(1)}, u32[]{:S(2)}, u32[]{:S(2)}) collective-permute-start(bf16[7,16,512]{2,1,0:T(8,128)(2,1)S(1)} %get-tuple-element.139), channel_id=1, source_target_pairs={{0,64},{1,65},{2,66},{3,67},{4,68},{5,69},{6,70},{7,71},{8,72},{9,... | collective-permute-start | bytes 344072 | tf_op jit(solution)/shard_map/ppermute | solution.py:386
  80.6 15.3 %all-to-all-start = ((bf16[8,112,128]{2,1,0:T(8,128)(2,1)}), bf16[8,112,128]{2,1,0:T(8,128)(2,1)S(1)}, u32[]{:S(2)}, u32[]{:S(2)}) async-start(bf16[8,112,128]{2,1,0:T(8,128)(2,1)} %shard_map.140), calls=%async_computation | async-start | bytes 458752 | tf_op jit(solution)/shard_map/all_to_all | solution.py:398
  85.8 0.7 collective-permute-start.23
  (1 other events, 0.7 us)

commit v10 on v9

--- a/solution.py
+++ b/solution.py
@@ -229,12 +229,10 @@
                 out[16 + j * 2 + i] = gk[at + j * 16 : at + j * 16 + 16, i * D : (i + 1) * D]
 
 
-def inputs_kernel(coord, dq, dkv, w_qkv, mid, rim_a, rim_b, tok, gain_mid, gne_o, gnq_o, gain_o, send_o):
+def inputs_kernel(coord, dq, dkv, w_qkv, mid, rim_a, rim_b, tok, gain_mid, gne_o, gnq_o, gain_o, row_a, row_b):
     gne = nt(dkv[...], w_qkv[:, D:])
     gnq = nt(dq[...], w_qkv[:, :D])
     gne_o[...] = gne[: (ROWS + 2 * RIM) * EC]
-    sides = gne.reshape(ER, EC, D)[: ROWS + 2 * RIM, COLS:]
-    send_o[:15] = sides.reshape((ROWS + 2 * RIM) * COLS, D).astype(BF16).reshape(15, 16, D)
     gnq_o[...] = gnq
     gain_in = jnp.sum(gnq * unit_of(tok[...].astype(F32))[0], axis=0, keepdims=True)
     odd = coord[0] & 1
@@ -245,7 +243,9 @@
         gain_in = gain_in + jnp.sum(part * unit, axis=0, keepdims=True)
     spread = jnp.concatenate([gain_in, gain_mid[...], jnp.zeros((14, D), F32)], axis=0).astype(BF16)
     gain_o[...] = spread
-    send_o[15] = spread
+    for ref, at in ((row_a, odd * (RIM + ROWS)), (row_b, (1 - odd) * (RIM + ROWS))):
+        rim = gne_o[pl.ds(pl.multiple_of(at * EC, EC), RIM * EC), :]
+        ref[...] = rim.astype(BF16).reshape(RIM, EC, D)
 
 
 def add2(a, b):
@@ -262,7 +262,7 @@
 
 
 def join_down_kv_kernel(dk, dg, kk, kg, gk, gg, *outs):
-    gain = add2(gk[...], gg[15])
+    gain = add2(gk[...], gg[...])
     for h, away, stay in halves():
         for out, chunks in ((outs[h], away), (outs[2 + h], stay)):
             for i, d in enumerate(chunks):
@@ -274,7 +274,8 @@
     outs[2][24] = gain
 
 
-def join_up_q_kernel(uk, ug, kk, kg, *outs):
+def join_up_q_kernel(uk, ug, kk, kg, ride, *outs):
+    outs[0][24:] = ride[...]
     for h, away, stay in halves():
         for out, chunks in ((outs[h], away), (outs[2 + h], stay)):
             for i, d in enumerate(chunks):
@@ -302,7 +303,7 @@
             outs[2 * h + i][5] = add2(got[10 + i], own[10 + i])
 
 
-def sum_down_kv_kernel(p_got, q_got, p_own, q_own, ride, *outs):
+def sum_down_kv_kernel(p_got, q_got, p_own, q_own, *outs):
     gain = add2(p_got[12], p_own[12])
     for h, got, own in ((0, p_got, p_own), (1, q_got, q_own)):
         for i in range(2):
@@ -310,12 +311,11 @@
             out[:4] = add2(got[i * 4 : i * 4 + 4], own[i * 4 : i * 4 + 4])
             out[4:6] = add2(got[8 + i * 2 : 10 + i * 2], own[8 + i * 2 : 10 + i * 2])
             out[6] = gain
-    outs[1][7:9] = ride[...]
 
 
 def reduce_xy_kernel(*refs):
     out, flat_s = refs[8:]
-    sums = [add4([r[...] for r in refs[:4]]).reshape(-1, D), add4([r[:7] for r in refs[4:8]]).reshape(-1, D)]
+    sums = [add4([r[...] for r in refs[:4]]).reshape(-1, D), add4([r[...] for r in refs[4:8]]).reshape(-1, D)]
     acc = jnp.concatenate(sums, axis=0)
     rows = acc.shape[0]
     per = ZROWS // 4
@@ -453,12 +453,15 @@
     )(gm, w_out, q, kv, p_mid, p_out, ne, no, pt_u, pt_k)
     u_got, d_got, k_send = lax.optimization_barrier((u_got, d_got, k_send))
     k_got = send(k_send, CORE_SWAP)
-    gne, gnq, g_keep, g_send = call(
+    gne, gnq, gain, row_a, row_b = call(
         inputs_kernel,
-        [(((ROWS + 2 * RIM) * EC, D), F32), ((TOK, D), F32), ((16, D), BF16), half_q],
+        [
+            (((ROWS + 2 * RIM) * EC, D), F32), ((TOK, D), F32), ((16, D), BF16),
+            ((RIM, EC, D), BF16), ((RIM, EC, D), BF16),
+        ],
         [], 1, 8, 600_000_000, 4_000_000, 6,
     )(coord, dq, dkv, w_qkv, mid, rim_a, rim_b, tok, gain_mid)
-    g_got = send(g_send, CORE_SWAP)
+    gain_got = send(gain, CORE_SWAP)
 
     def place(x, axis, odd, end_if_odd, size):
         gap = size - RIM
@@ -480,44 +483,41 @@
 
     k_got, gnq = lax.optimization_barrier((k_got, gnq))
     u_p, u_q, *u_stay = join(
-        join_up_q_kernel, [u_keep.reshape(80, 16, D), u_got.reshape(80, 16, D), k_keep, k_got], [(24, 16, D)] * 4,
+        join_up_q_kernel, [u_keep.reshape(80, 16, D), u_got.reshape(80, 16, D), k_keep, k_got, row_b],
+        [(27, 16, D)] + [(24, 16, D)] * 3,
     )
     u_first = first((u_p, u_q), X_BIT)
     b_p, b_q, *b_stay = join(
-        join_down_kv_kernel, [d_keep.reshape(64, 16, D), d_got.reshape(64, 16, D), k_keep, k_got, g_keep, g_got],
+        join_down_kv_kernel, [d_keep.reshape(64, 16, D), d_got.reshape(64, 16, D), k_keep, k_got, gain, gain_got],
         [(25, 16, D), (24, 16, D)] * 2,
     )
-    gne3 = gne.reshape(ROWS + 2 * RIM, EC, D)
-    side = gne3[:, COLS : COLS + RIM].astype(BF16)
     b_first = first((b_p, b_q), Y_BIT)
-    back_a = send(side, COL_A)
-    b_first, back_a, g_got = lax.optimization_barrier((b_first, back_a, g_got))
+    row_a = send(row_a, ROW_A)
+    b_first, row_a = lax.optimization_barrier((b_first, row_a))
     u_p, u_q, *u_own = join(second_kernel, [*u_first, *u_stay], [(12, 16, D)] * 4)
     u_second = second((u_p, u_q), X_BIT)
     b_p, b_q, *b_own = join(second_kernel, [*b_first, *b_stay], [(13, 16, D), (12, 16, D)] * 2)
     b_second = second((b_p, b_q), Y_BIT)
-    back_b = g_got[:15].reshape(ROWS + 2 * RIM, COLS, D)[:, RIM : 2 * RIM]
-    own = gne3[:, :COLS] + place(back_a, 1, col_odd, True, COLS) + place(back_b, 1, col_odd, False, COLS)
-    head, tail = own[:RIM].astype(BF16), own[RIM + ROWS :].astype(BF16)
-    ride = jnp.pad(jnp.where(row_odd, head, tail), ((0, 1), (0, 0), (0, 0))).reshape(2, 16, D)
+    gne = gne.reshape(ROWS + 2 * RIM, EC, D)[RIM : RIM + ROWS]
+    gne = gne + place(row_a, 0, row_odd, True, ROWS) + place(u_first[0][24:], 0, row_odd, False, ROWS)
     u = join(sum_up_q_kernel, [*u_second, *u_own], [(6, 16, D)] * 4)
     u = to_three(u, Y_BIT)
-    b = join(sum_down_kv_kernel, [*b_second, *b_own, ride], [(7, 16, D), (9, 16, D), (7, 16, D), (7, 16, D)])
+    b = join(sum_down_kv_kernel, [*b_second, *b_own], [(7, 16, D)] * 4)
     b = to_three(b, X_BIT)
-    up_b = b[1][7:].reshape(4, COLS, D)[:RIM]
     (spread,) = call(
         reduce_xy_kernel, [((8, ZROWS, 128), BF16)], [pltpu.VMEM((8 * ZROWS, 128), F32)], 0, 8, 60_000_000, 4_000_000, 5,
     )(*u, *b)
-    up_a = send(jnp.where(row_odd, tail, head), ROW_A)
     got_z = exchange(spread, Z_GROUPS)
-    got_z, up_a = lax.optimization_barrier((got_z, up_a))
+    back_b = send(gne[:, COLS + RIM : COLS + 2 * RIM].astype(BF16), COL_B)
+    back_a = send(gne[:, COLS : COLS + RIM].astype(BF16), COL_A)
+    got_z, back_a, back_b = lax.optimization_barrier((got_z, back_a, back_b))
     g_up, g_down, g_out, g_qkv, g_gains = call(
         reduce_z_kernel,
         [((32, 128), F32), ((32, 128), F32), ((8, 128), F32), ((24, 128), F32), ((2, D), F32)],
         [], 0, 1, 100_000_000_000, 400_000, 4,
     )(got_z)
 
-    gn = own[RIM : RIM + ROWS] + place(up_a, 0, row_odd, True, ROWS) + place(up_b, 0, row_odd, False, ROWS)
+    gn = gne[:, :COLS] + place(back_a, 1, col_odd, True, COLS) + place(back_b, 1, col_odd, False, COLS)
     gn = gn + gnq.reshape(ROWS, COLS, D)
     unit, inv = unit_of(tokens.astype(F32))
     g1 = gn * gains[0]

time: 98.6 us -> 96.8 us (0.982)
  waiting for transfers between devices: 23.3 us -> 17.3 us
  starting transfers between devices: 48.3 us -> 52.4 us
    all_to_all x1, waiting for transfers between devices: 9.42 us -> 0.01 us  [exchange(): return lax.all_to_all(x, AXES, 0, 0, axis_index_groups=groups, tiled=True)]
    ppermute x24 -> x25, starting transfers between devices: 43.1 us -> 47.8 us  [send(): return lax.ppermute(x, AXES, perm)]
    ppermute x24 -> x25, waiting for transfers between devices: 13.9 us -> 17.3 us  [send(): return lax.ppermute(x, AXES, perm)]
  transfers between devices with their start and end apart: 25 -> 26, of which waited for: 9 -> 10; matrix products, arithmetic and copies ran while one was open for 1% -> 1% of each run, Pallas kernels for 12% -> 12%
where the time goes in v10:
time: 96.8 us; the launch traced here: 95.9 us
  starting transfers between devices  52.4 us (54%)
  Pallas kernels  20.7 us (21%)
  waiting for transfers between devices  17.3 us (18%)
  other arithmetic  2.93 us (3%)
  local copies, waits for them, and re-layouts  1.46 us (2%)
  between operations  1.02 us (1%)
    ppermute x25, starting transfers between devices, send(): return lax.ppermute(x, AXES, perm)  47.8 us
    ppermute x25, waiting for transfers between devices, send(): return lax.ppermute(x, AXES, perm)  17.3 us
    pallas_call x1, Pallas kernels, per_device(): call(forward_kernel, [half_u, half_u, half_d, half_d, ((TOK, D), BF16), (...  6.99 us
    all_to_all x1, starting transfers between devices, exchange(): return lax.all_to_all(x, AXES, 0, 0, axis_index_groups=groups, tiled=True)  4.62 us
    pallas_call x1, Pallas kernels, per_device(): call(backward_kernel, [half_k, half_k, ((TOK, D), BF16), ((EXT, 2 * D), B...  4.02 us
  transfers between devices with their start and end apart: 26, of which 10 were waited for; matrix products, arithmetic and copies ran while one was open for 1% of the time, Pallas kernels for 12%

profile of v10, /device:TPU:8, one launch (start us, length us, event | category | flops | bytes accessed | tf_op | source)
XLA Modules:
  0.0 95.9 jit_solution(111139296769606134)
XLA Ops:
  0.6 1.2 %broadcast_select_fusion = (bf16[24,3,512]{2,1,0:T(4,128)(2,1)S(1)}, bf16[24,3,512]{2,1,0:T(4,128)(2,1)S(1)}) fusion(pred[]{:T(512)S(6)} %eq.6, bf16[24,8,512]{2,1,0:T(8,128)(2,1)} %param.8), kind=kLoop, calls=%fused_computation.16 | loop fusion | flops 73728 | bytes 294913 | tf_op jit(solution)/shard_map/jit(_where)/select_n | solution.py:411
  1.8 5.9 %collective-permute-start = (bf16[24,3,512]{2,1,0:T(4,128)(2,1)S(1)}, bf16[24,3,512]{2,1,0:T(4,128)(2,1)S(1)}, u32[]{:S(2)}, u32[]{:S(2)}) collective-permute-start(bf16[24,3,512]{2,1,0:T(4,128)(2,1)S(1)} %get-tuple-element.159), channel_id=1, source_target_pairs={{1,2},{2,1},{3,4},{4,3},{5,6},{6,5},{7,8},{8,7},{9,10},{10,9},{11,... | collective-permute-start | bytes 221192 | tf_op jit(solution)/shard_map/ppermute | solution.py:386
  8.6 1.2 %shard_map.127.bias = f32[3,64,256]{2,1,0:T(8,128)S(1)} custom-call(s32[3]{0:T(128)S(1)} %pad_add_fusion.coord, s32[3,1,49]{2,1,0:T(1,128)S(1)} %copy-done.7), custom_call_target="tpu_custom_call" | custom-call | flops 402653184 | bytes 4000000 | tf_op jit(solution)/shard_map/pallas_call | solution.py:413
  9.9 1.3 %collective-permute-done = bf16[24,3,512]{2,1,0:T(4,128)(2,1)S(1)} collective-permute-done((bf16[24,3,512]{2,1,0:T(4,128)(2,1)S(1)}, bf16[24,3,512]{2,1,0:T(4,128)(2,1)S(1)}, u32[]{:S(2)}, u32[]{:S(2)}) %collective-permute-start) | collective-permute-done | bytes 73760 | tf_op jit(solution)/shard_map/ppermute | solution.py:386
  12.1 4.3 %collective-permute-start.3 = (bf16[3,16,512]{2,1,0:T(8,128)(2,1)S(1)}, bf16[3,16,512]{2,1,0:T(8,128)(2,1)S(1)}, u32[]{:S(2)}, u32[]{:S(2)}) collective-permute-start(bf16[3,16,512]{2,1,0:T(8,128)(2,1)S(1)} %get-tuple-element.156), channel_id=1, source_target_pairs={{0,32},{1,33},{2,34},{3,35},{4,36},{5,37},{6,38},{7,39},{8,40},{9,... | collective-permute-start | bytes 147464 | tf_op jit(solution)/shard_map/ppermute | solution.py:386
  16.4 1.3 %shard_map.129 = (bf16[512,512]{1,0:T(8,128)(2,1)S(1)}, bf16[512,512]{1,0:T(8,128)(2,1)S(1)}, bf16[512,512]{1,0:T(8,128)(2,1)S(1)}) custom-call(s32[3]{0:T(128)S(1)} %pad_add_fusion.coord), custom_call_target="tpu_custom_call" | custom-call | flops 402653184 | bytes 4000000 | tf_op jit(solution)/shard_map/pallas_call | solution.py:420
  17.8 0.8 shard_map.128.gact
  19.1 1.6 %shard_map.130 = (bf16[192,512]{1,0:T(8,128)(2,1)S(1)}, bf16[192,512]{1,0:T(8,128)(2,1)S(1)}, bf16[384,512]{1,0:T(8,128)(2,1)S(1)}, bf16[384,1024]{1,0:T(8,128)(...) custom-call(bf16[24,16,512]{2,1,0:T(8,128)(2,1)S(1)} %maximum_maximum_fusion.mid, ...), custom_call_target="tpu_custom_call" | custom-call | flops 600000000 | bytes 5000000 | tf_op jit(solution)/shard_map/pallas_call | solution.py:427
  20.8 7.0 %shard_map.131 = (bf16[16,5,16,512]{3,2,1,0:T(8,128)(2,1)S(1)}, bf16[16,5,16,512]{3,2,1,0:T(8,128)(2,1)S(1)}, bf16[4,4,2,32,512]{4,3,2,1,0:T(8,128)(2,1)S(1)}, b...) custom-call(s32[3]{0:T(128)S(1)} %pad_add_fusion.coord, ...), custom_call_target="tpu_custom_call" | custom-call | flops 4000000000 | bytes 20000000 | tf_op jit(solution)/shard_map/pallas_call | solution.py:438
  28.4 4.0 %shard_map.132 = (bf16[48,16,512]{2,1,0:T(8,128)(2,1)S(1)}, bf16[48,16,512]{2,1,0:T(8,128)(2,1)S(1)}, bf16[192,512]{1,0:T(8,128)(2,1)S(1)}, bf16[512,1024]{1,0:T(8,128)(2,1)S(1)}) custom-call(bf16[192,512]{1,0:T(8,128)(2,1)S(1)} %get-tuple-element.89.gm, bf16[512,512]{1,0:T(8,128)(2,1)S(1)} %copy-done.6, bf16[192,512]{1,0:T(8,128)(2,1)S(1)} %get-tuple-element.85.q_i.q, ...), custom_call_target="tpu_custom_call" | custom-call | flops 2500000000 | bytes 10000000 | tf_op jit(solution)/shard_map/pallas_call | solution.py:449
  32.8 1.5 %shard_map.133 = (f32[480,512]{1,0:T(8,128)S(1)}, f32[192,512]{1,0:T(8,128)S(1)}, bf16[16,512]{1,0:T(8,128)(2,1)S(1)}, bf16[3,16,512]{2,1,0:T(8,128)(2,1)S(1)}, bf16[3,16,512]{2,1,0:T(8,128)(2,1)S(1)}) custom-call(s32[3]{0:T(128)S(1)} %pad_add_fusion.coord, bf16[192,512]{1,0:T(8,128)(2,1)S(1)} %get-tuple-element.96.dq, ...), custom_call_target="tpu_custom_call" | custom-call | flops 600000000 | bytes 4000000 | tf_op jit(solution)/shard_map/pallas_call | solution.py:456
  34.8 0.8 collective-permute-done.7.gg
  36.0 2.5 %collective-permute-start.9 = (bf16[24,16,512]{2,1,0:T(8,128)(2,1)S(1)}, bf16[24,16,512]{2,1,0:T(8,128)(2,1)S(1)}, u32[]{:S(2)}, u32[]{:S(2)}) collective-permute-start(bf16[24,16,512]{2,1,0:T(8,128)(2,1)S(1)} %get-tuple-element.111), channel_id=1, source_target_pairs={{0,24},{1,25},{2,26},{3,27},{4,28},{5,29},{6,30},{7,31},{8,16},{9,... | collective-permute-start | bytes 1179656 | tf_op jit(solution)/shard_map/ppermute | solution.py:386
  39.0 8.5 %collective-permute-start.12 = (bf16[24,16,512]{2,1,0:T(8,128)(2,1)S(1)}, bf16[24,16,512]{2,1,0:T(8,128)(2,1)S(1)}, u32[]{:S(2)}, u32[]{:S(2)}) collective-permute-start(bf16[24,16,512]{2,1,0:T(8,128)(2,1)S(1)} %get-tuple-element.118), channel_id=1, source_target_pairs={{0,96},{1,97},{2,98},{3,99},{4,100},{5,101},{6,102},{7,103},{8,104... | collective-permute-start | bytes 1179656 | tf_op jit(solution)/shard_map/ppermute | solution.py:386
  48.4 1.4 %collective-permute-start.18 = (bf16[13,16,512]{2,1,0:T(8,128)(2,1)S(1)}, bf16[13,16,512]{2,1,0:T(8,128)(2,1)S(1)}, u32[]{:S(2)}, u32[]{:S(2)}) collective-permute-start(bf16[13,16,512]{2,1,0:T(8,128)(2,1)S(1)} %get-tuple-element.133), channel_id=1, source_target_pairs={{0,24},{1,25},{2,26},{3,27},{4,28},{5,29},{6,30},{7,31},{8,16},{9,... | collective-permute-start | bytes 638984 | tf_op jit(solution)/shard_map/ppermute | solution.py:386
  49.8 2.9 %collective-permute-start.19 = (bf16[12,16,512]{2,1,0:T(8,128)(2,1)S(1)}, bf16[12,16,512]{2,1,0:T(8,128)(2,1)S(1)}, u32[]{:S(2)}, u32[]{:S(2)}) collective-permute-start(bf16[12,16,512]{2,1,0:T(8,128)(2,1)S(1)} %get-tuple-element.134), channel_id=1, source_target_pairs={{0,8},{1,9},{2,10},{3,11},{4,12},{5,13},{6,14},{7,15},{8,0},{9,1},... | collective-permute-start | bytes 589832 | tf_op jit(solution)/shard_map/ppermute | solution.py:386
  52.9 3.6 %collective-permute-done.12.q_got = bf16[24,16,512]{2,1,0:T(8,128)(2,1)S(1)} collective-permute-done((bf16[24,16,512]{2,1,0:T(8,128)(2,1)S(1)}, bf16[24,16,512]{2,1,0:T(8,128)(2,1)S(1)}, u32[]{:S(2)}, u32[]{:S(2)}) %collective-permute-start.12) | collective-permute-done | bytes 393248 | tf_op jit(solution)/shard_map/ppermute | solution.py:386
  56.7 6.0 %collective-permute-start.13 = (bf16[12,16,512]{2,1,0:T(8,128)(2,1)S(1)}, bf16[12,16,512]{2,1,0:T(8,128)(2,1)S(1)}, u32[]{:S(2)}, u32[]{:S(2)}) collective-permute-start(bf16[12,16,512]{2,1,0:T(8,128)(2,1)S(1)} %get-tuple-element.121), channel_id=1, source_target_pairs={{0,96},{1,97},{2,98},{3,99},{4,100},{5,101},{6,102},{7,103},{8,104... | collective-permute-start | bytes 589832 | tf_op jit(solution)/shard_map/ppermute | solution.py:386
  62.8 2.1 %collective-permute-start.20 = (bf16[7,16,512]{2,1,0:T(8,128)(2,1)S(1)}, bf16[7,16,512]{2,1,0:T(8,128)(2,1)S(1)}, u32[]{:S(2)}, u32[]{:S(2)}) collective-permute-start(bf16[7,16,512]{2,1,0:T(8,128)(2,1)S(1)} %get-tuple-element.138), channel_id=1, source_target_pairs={{0,32},{1,33},{2,34},{3,35},{4,36},{5,37},{6,38},{7,39},{8,40},{9,... | collective-permute-start | bytes 344072 | tf_op jit(solution)/shard_map/ppermute | solution.py:386
  65.0 1.2 %collective-permute-start.21 = (bf16[7,16,512]{2,1,0:T(8,128)(2,1)S(1)}, bf16[7,16,512]{2,1,0:T(8,128)(2,1)S(1)}, u32[]{:S(2)}, u32[]{:S(2)}) collective-permute-start(bf16[7,16,512]{2,1,0:T(8,128)(2,1)S(1)} %get-tuple-element.139), channel_id=1, source_target_pairs={{0,96},{1,97},{2,98},{3,99},{4,100},{5,101},{6,102},{7,103},{8,104... | collective-permute-start | bytes 344072 | tf_op jit(solution)/shard_map/ppermute | solution.py:386
  66.2 1.8 %collective-permute-start.22 = (bf16[7,16,512]{2,1,0:T(8,128)(2,1)S(1)}, bf16[7,16,512]{2,1,0:T(8,128)(2,1)S(1)}, u32[]{:S(2)}, u32[]{:S(2)}) collective-permute-start(bf16[7,16,512]{2,1,0:T(8,128)(2,1)S(1)} %get-tuple-element.140), channel_id=1, source_target_pairs={{0,64},{1,65},{2,66},{3,67},{4,68},{5,69},{6,70},{7,71},{8,72},{9,... | collective-permute-start | bytes 344072 | tf_op jit(solution)/shard_map/ppermute | solution.py:386
  68.3 1.3 %collective-permute-done.14.q_got = bf16[12,16,512]{2,1,0:T(8,128)(2,1)S(1)} collective-permute-done((bf16[12,16,512]{2,1,0:T(8,128)(2,1)S(1)}, bf16[12,16,512]{2,1,0:T(8,128)(2,1)S(1)}, u32[]{:S(2)}, u32[]{:S(2)}) %collective-permute-start.14) | collective-permute-done | bytes 196640 | tf_op jit(solution)/shard_map/ppermute | solution.py:386
  69.7 0.8 collective-permute-start.15
  70.5 1.2 %collective-permute-start.16 = (bf16[6,16,512]{2,1,0:T(8,128)(2,1)S(1)}, bf16[6,16,512]{2,1,0:T(8,128)(2,1)S(1)}, u32[]{:S(2)}, u32[]{:S(2)}) collective-permute-start(bf16[6,16,512]{2,1,0:T(8,128)(2,1)S(1)} %get-tuple-element.127), channel_id=1, source_target_pairs={{0,24},{1,25},{2,26},{3,27},{4,28},{5,29},{6,30},{7,31},{8,16},{9,... | collective-permute-start | bytes 294920 | tf_op jit(solution)/shard_map/ppermute | solution.py:386
  71.7 2.2 %collective-permute-start.17 = (bf16[6,16,512]{2,1,0:T(8,128)(2,1)S(1)}, bf16[6,16,512]{2,1,0:T(8,128)(2,1)S(1)}, u32[]{:S(2)}, u32[]{:S(2)}) collective-permute-start(bf16[6,16,512]{2,1,0:T(8,128)(2,1)S(1)} %get-tuple-element.128), channel_id=1, source_target_pairs={{0,16},{1,17},{2,18},{3,19},{4,20},{5,21},{6,22},{7,23},{8,24},{9,... | collective-permute-start | bytes 294920 | tf_op jit(solution)/shard_map/ppermute | solution.py:386
  75.1 2.8 %collective-permute-done.17.refs_3_ = bf16[6,16,512]{2,1,0:T(8,128)(2,1)S(1)} collective-permute-done((bf16[6,16,512]{2,1,0:T(8,128)(2,1)S(1)}, bf16[6,16,512]{2,1,0:T(8,128)(2,1)S(1)}, u32[]{:S(2)}, u32[]{:S(2)}) %collective-permute-start.17) | collective-permute-done | bytes 98336 | tf_op jit(solution)/shard_map/ppermute | solution.py:386
  77.9 1.3 %shard_map.140 = bf16[8,112,128]{2,1,0:T(8,128)(2,1)} custom-call(bf16[6,16,512]{2,1,0:T(8,128)(2,1)S(1)} %get-tuple-element.125.refs_0_, bf16[6,16,512]{2,1,0:T(8,128)(2,1)S(1)} %collective-permute-done.15.refs_1_, bf16[6,16,512]{2,1,0:T(8,128)(2,1)S(1)} %collective-permute-done.16.refs_2_, bf16[6,16,512]{2,1,0:T(8,128)(2,1)S(1)} %collective-permute-done.17.refs_3_, ...), custom_call_target="tpu_custom_call" | custom-call | flops 60000000 | bytes 4000000 | tf_op jit(solution)/shard_map/pallas_call | solution.py:507
  79.2 4.6 %all-to-all-start = ((bf16[8,112,128]{2,1,0:T(8,128)(2,1)}), bf16[8,112,128]{2,1,0:T(8,128)(2,1)S(1)}, u32[]{:S(2)}, u32[]{:S(2)}) async-start(bf16[8,112,128]{2,1,0:T(8,128)(2,1)} %shard_map.140), calls=%async_computation | async-start | bytes 458752 | tf_op jit(solution)/shard_map/all_to_all | solution.py:398
  83.9 1.9 %collective-permute-start.23 = (bf16[24,3,512]{2,1,0:T(4,128)(2,1)S(1)}, bf16[24,3,512]{2,1,0:T(4,128)(2,1)S(1)}, u32[]{:S(2)}, u32[]{:S(2)}) collective-permute-start(bf16[24,3,512]{2,1,0:T(4,128)(2,1)S(1)} %get-tuple-element.155), channel_id=1, source_target_pairs={{1,2},{2,1},{3,4},{4,3},{5,6},{6,5},{7,8},{8,7},{9,10},{10,9},{11,... | collective-permute-start | bytes 221192 | tf_op jit(solution)/shard_map/ppermute | solution.py:386
  85.8 2.2 %collective-permute-start.24 = (bf16[24,3,512]{2,1,0:T(4,128)(2,1)S(1)}, bf16[24,3,512]{2,1,0:T(4,128)(2,1)S(1)}, u32[]{:S(2)}, u32[]{:S(2)}) collective-permute-start(bf16[24,3,512]{2,1,0:T(4,128)(2,1)S(1)} %get-tuple-element.154), channel_id=1, source_target_pairs={{0,1},{1,0},{2,3},{3,2},{4,5},{5,4},{6,7},{7,6},{8,9},{9,8},{10,11... | collective-permute-start | bytes 221192 | tf_op jit(solution)/shard_map/ppermute | solution.py:386
  88.0 6.0 %collective-permute-done.23 = bf16[24,3,512]{2,1,0:T(4,128)(2,1)S(1)} collective-permute-done((bf16[24,3,512]{2,1,0:T(4,128)(2,1)S(1)}, bf16[24,3,512]{2,1,0:T(4,128)(2,1)S(1)}, u32[]{:S(2)}, u32[]{:S(2)}) %collective-permute-start.23) | collective-permute-done | bytes 73760 | tf_op jit(solution)/shard_map/ppermute | solution.py:386
  95.0 0.9 fusion.6
  (71 shorter events, 8.8 us)
Async XLA Ops:
  0.6 10.6 %copy-start = (bf16[24,8,512]{2,1,0:T(8,128)(2,1)S(1)}, bf16[24,8,512]{2,1,0:T(8,128)(2,1)}, u32[]{:S(2)}) copy-start(bf16[24,8,512]{2,1,0:T(8,128)(2,1)} %param.8) | copy-start | bytes 589828
  1.8 9.4 %collective-permute-start = (bf16[24,3,512]{2,1,0:T(4,128)(2,1)S(1)}, bf16[24,3,512]{2,1,0:T(4,128)(2,1)S(1)}, u32[]{:S(2)}, u32[]{:S(2)}) collective-permute-start(bf16[24,3,512]{2,1,0:T(4,128)(2,1)S(1)} %get-tuple-element.159), channel_id=1, source_target_pairs={{1,2},{2,1},{3,4},{4,3},{5,6},{6,5},{7,8},{8,7},{9,10},{10,9},{11,... | collective-permute-start | bytes 221192 | tf_op jit(solution)/shard_map/ppermute | solution.py:386
  7.7 3.5 %collective-permute-start.1 = (bf16[24,3,512]{2,1,0:T(4,128)(2,1)S(1)}, bf16[24,3,512]{2,1,0:T(4,128)(2,1)S(1)}, u32[]{:S(2)}, u32[]{:S(2)}) collective-permute-start(bf16[24,3,512]{2,1,0:T(4,128)(2,1)S(1)} %get-tuple-element.158), channel_id=1, source_target_pairs={{0,1},{1,0},{2,3},{3,2},{4,5},{5,4},{6,7},{7,6},{8,9},{9,8},{10,11... | collective-permute-start | bytes 221192 | tf_op jit(solution)/shard_map/ppermute | solution.py:386
  9.9 7.8 %copy-start.2 = (bf16[2048,512]{1,0:T(8,128)(2,1)S(1)}, bf16[2048,512]{1,0:T(8,128)(2,1)}, u32[]{:S(2)}) copy-start(bf16[2048,512]{1,0:T(8,128)(2,1)} %w_down.1) | copy-start | bytes 6291460
  9.9 7.8 %copy-start.3 = (bf16[24,8,512]{2,1,0:T(8,128)(2,1)S(1)}, bf16[24,8,512]{2,1,0:T(8,128)(2,1)}, u32[]{:S(2)}) copy-start(bf16[24,8,512]{2,1,0:T(8,128)(2,1)} %param.9) | copy-start | bytes 589828
  11.4 9.3 %collective-permute-start.2 = (bf16[3,16,512]{2,1,0:T(8,128)(2,1)S(1)}, bf16[3,16,512]{2,1,0:T(8,128)(2,1)S(1)}, u32[]{:S(2)}, u32[]{:S(2)}) collective-permute-start(bf16[3,16,512]{2,1,0:T(8,128)(2,1)S(1)} %get-tuple-element.157), channel_id=1, source_target_pairs={{32,64},{33,65},{34,66},{35,67},{36,68},{37,69},{38,70},{39,71},{4... | collective-permute-start | bytes 147464 | tf_op jit(solution)/shard_map/ppermute | solution.py:386
  12.1 8.7 %collective-permute-start.3 = (bf16[3,16,512]{2,1,0:T(8,128)(2,1)S(1)}, bf16[3,16,512]{2,1,0:T(8,128)(2,1)S(1)}, u32[]{:S(2)}, u32[]{:S(2)}) collective-permute-start(bf16[3,16,512]{2,1,0:T(8,128)(2,1)S(1)} %get-tuple-element.156), channel_id=1, source_target_pairs={{0,32},{1,33},{2,34},{3,35},{4,36},{5,37},{6,38},{7,39},{8,40},{9,... | collective-permute-start | bytes 147464 | tf_op jit(solution)/shard_map/ppermute | solution.py:386
  17.8 3.0 %copy-start.6 = (bf16[512,512]{1,0:T(8,128)(2,1)S(1)}, bf16[512,512]{1,0:T(8,128)(2,1)}, u32[]{:S(2)}) copy-start(bf16[512,512]{1,0:T(8,128)(2,1)} %w_out.3) | copy-start | bytes 1572868
  18.6 2.2 %copy-start.5 = (bf16[512,2048]{1,0:T(8,128)(2,1)S(1)}, bf16[512,2048]{1,0:T(8,128)(2,1)}, u32[]{:S(2)}) copy-start(bf16[512,2048]{1,0:T(8,128)(2,1)} %w_up.1) | copy-start | bytes 6291460
  27.8 4.6 %collective-permute-start.4 = (bf16[16,5,16,512]{3,2,1,0:T(8,128)(2,1)S(1)}, bf16[16,5,16,512]{3,2,1,0:T(8,128)(2,1)S(1)}, u32[]{:S(2)}, u32[]{:S(2)}) collective-permute-start(bf16[16,5,16,512]{3,2,1,0:T(8,128)(2,1)S(1)} %get-tuple-element.101), channel_id=1, source_target_pairs={{0,1},{1,0},{2,3},{3,2},{4,5},{5,4},{6,7},{7,6},{8,9},{9,8},{10,11... | collective-permute-start | bytes 3932168 | tf_op jit(solution)/shard_map/ppermute | solution.py:386
  27.9 4.5 %collective-permute-start.5 = (bf16[4,4,2,32,512]{4,3,2,1,0:T(8,128)(2,1)S(1)}, bf16[4,4,2,32,512]{4,3,2,1,0:T(8,128)(2,1)S(1)}, u32[]{:S(2)}, u32[]{:S(2)}) collective-permute-start(bf16[4,4,2,32,512]{4,3,2,1,0:T(8,128)(2,1)S(1)} %get-tuple-element.102), channel_id=1, source_target_pairs={{0,1},{1,0},{2,3},{3,2},{4,5},{5,4},{6,7},{7,6},{8,9},{9,8},{10,11... | collective-permute-start | bytes 3145736 | tf_op jit(solution)/shard_map/ppermute | solution.py:386
  32.5 2.4 %collective-permute-start.6 = (bf16[48,16,512]{2,1,0:T(8,128)(2,1)S(1)}, bf16[48,16,512]{2,1,0:T(8,128)(2,1)S(1)}, u32[]{:S(2)}, u32[]{:S(2)}) collective-permute-start(bf16[48,16,512]{2,1,0:T(8,128)(2,1)S(1)} %get-tuple-element.106), channel_id=1, source_target_pairs={{0,1},{1,0},{2,3},{3,2},{4,5},{5,4},{6,7},{7,6},{8,9},{9,8},{10,11... | collective-permute-start | bytes 2359304 | tf_op jit(solution)/shard_map/ppermute | solution.py:386
  34.3 1.3 %collective-permute-start.7 = (bf16[16,512]{1,0:T(8,128)(2,1)S(1)}, bf16[16,512]{1,0:T(8,128)(2,1)S(1)}, u32[]{:S(2)}, u32[]{:S(2)}) collective-permute-start(bf16[16,512]{1,0:T(8,128)(2,1)S(1)} %get-tuple-element.109.gk), channel_id=1, source_target_pairs={{0,1},{1,0},{2,3},{3,2},{4,5},{5,4},{6,7},{7,6},{8,9},{9,8},{10,11... | collective-permute-start | bytes 49160 | tf_op jit(solution)/shard_map/ppermute | solution.py:386
  35.9 12.2 %collective-permute-start.8 = (bf16[25,16,512]{2,1,0:T(8,128)(2,1)S(1)}, bf16[25,16,512]{2,1,0:T(8,128)(2,1)S(1)}, u32[]{:S(2)}, u32[]{:S(2)}) collective-permute-start(bf16[25,16,512]{2,1,0:T(8,128)(2,1)S(1)} %get-tuple-element.110), channel_id=1, source_target_pairs={{0,8},{1,9},{2,10},{3,11},{4,12},{5,13},{6,14},{7,15},{8,0},{9,1},... | collective-permute-start | bytes 1228808 | tf_op jit(solution)/shard_map/ppermute | solution.py:386
  36.0 12.1 %collective-permute-start.9 = (bf16[24,16,512]{2,1,0:T(8,128)(2,1)S(1)}, bf16[24,16,512]{2,1,0:T(8,128)(2,1)S(1)}, u32[]{:S(2)}, u32[]{:S(2)}) collective-permute-start(bf16[24,16,512]{2,1,0:T(8,128)(2,1)S(1)} %get-tuple-element.111), channel_id=1, source_target_pairs={{0,24},{1,25},{2,26},{3,27},{4,28},{5,29},{6,30},{7,31},{8,16},{9,... | collective-permute-start | bytes 1179656 | tf_op jit(solution)/shard_map/ppermute | solution.py:386
  38.9 17.6 %collective-permute-start.11 = (bf16[27,16,512]{2,1,0:T(8,128)(2,1)S(1)}, bf16[27,16,512]{2,1,0:T(8,128)(2,1)S(1)}, u32[]{:S(2)}, u32[]{:S(2)}) collective-permute-start(bf16[27,16,512]{2,1,0:T(8,128)(2,1)S(1)} %get-tuple-element.117), channel_id=1, source_target_pairs={{0,32},{1,33},{2,34},{3,35},{4,36},{5,37},{6,38},{7,39},{8,40},{9,... | collective-permute-start | bytes 1327112 | tf_op jit(solution)/shard_map/ppermute | solution.py:386
  39.0 17.5 %collective-permute-start.12 = (bf16[24,16,512]{2,1,0:T(8,128)(2,1)S(1)}, bf16[24,16,512]{2,1,0:T(8,128)(2,1)S(1)}, u32[]{:S(2)}, u32[]{:S(2)}) collective-permute-start(bf16[24,16,512]{2,1,0:T(8,128)(2,1)S(1)} %get-tuple-element.118), channel_id=1, source_target_pairs={{0,96},{1,97},{2,98},{3,99},{4,100},{5,101},{6,102},{7,103},{8,104... | collective-permute-start | bytes 1179656 | tf_op jit(solution)/shard_map/ppermute | solution.py:386
  47.5 0.7 collective-permute-start.10
  48.4 14.4 %collective-permute-start.18 = (bf16[13,16,512]{2,1,0:T(8,128)(2,1)S(1)}, bf16[13,16,512]{2,1,0:T(8,128)(2,1)S(1)}, u32[]{:S(2)}, u32[]{:S(2)}) collective-permute-start(bf16[13,16,512]{2,1,0:T(8,128)(2,1)S(1)} %get-tuple-element.133), channel_id=1, source_target_pairs={{0,24},{1,25},{2,26},{3,27},{4,28},{5,29},{6,30},{7,31},{8,16},{9,... | collective-permute-start | bytes 638984 | tf_op jit(solution)/shard_map/ppermute | solution.py:386
  49.8 12.9 %collective-permute-start.19 = (bf16[12,16,512]{2,1,0:T(8,128)(2,1)S(1)}, bf16[12,16,512]{2,1,0:T(8,128)(2,1)S(1)}, u32[]{:S(2)}, u32[]{:S(2)}) collective-permute-start(bf16[12,16,512]{2,1,0:T(8,128)(2,1)S(1)} %get-tuple-element.134), channel_id=1, source_target_pairs={{0,8},{1,9},{2,10},{3,11},{4,12},{5,13},{6,14},{7,15},{8,0},{9,1},... | collective-permute-start | bytes 589832 | tf_op jit(solution)/shard_map/ppermute | solution.py:386
  56.7 11.6 %collective-permute-start.13 = (bf16[12,16,512]{2,1,0:T(8,128)(2,1)S(1)}, bf16[12,16,512]{2,1,0:T(8,128)(2,1)S(1)}, u32[]{:S(2)}, u32[]{:S(2)}) collective-permute-start(bf16[12,16,512]{2,1,0:T(8,128)(2,1)S(1)} %get-tuple-element.121), channel_id=1, source_target_pairs={{0,96},{1,97},{2,98},{3,99},{4,100},{5,101},{6,102},{7,103},{8,104... | collective-permute-start | bytes 589832 | tf_op jit(solution)/shard_map/ppermute | solution.py:386
  62.7 6.9 %collective-permute-start.14 = (bf16[12,16,512]{2,1,0:T(8,128)(2,1)S(1)}, bf16[12,16,512]{2,1,0:T(8,128)(2,1)S(1)}, u32[]{:S(2)}, u32[]{:S(2)}) collective-permute-start(bf16[12,16,512]{2,1,0:T(8,128)(2,1)S(1)} %get-tuple-element.122), channel_id=1, source_target_pairs={{0,32},{1,33},{2,34},{3,35},{4,36},{5,37},{6,38},{7,39},{8,40},{9,... | collective-permute-start | bytes 589832 | tf_op jit(solution)/shard_map/ppermute | solution.py:386
  62.8 8.9 %collective-permute-start.20 = (bf16[7,16,512]{2,1,0:T(8,128)(2,1)S(1)}, bf16[7,16,512]{2,1,0:T(8,128)(2,1)S(1)}, u32[]{:S(2)}, u32[]{:S(2)}) collective-permute-start(bf16[7,16,512]{2,1,0:T(8,128)(2,1)S(1)} %get-tuple-element.138), channel_id=1, source_target_pairs={{0,32},{1,33},{2,34},{3,35},{4,36},{5,37},{6,38},{7,39},{8,40},{9,... | collective-permute-start | bytes 344072 | tf_op jit(solution)/shard_map/ppermute | solution.py:386
  65.0 9.1 %collective-permute-start.21 = (bf16[7,16,512]{2,1,0:T(8,128)(2,1)S(1)}, bf16[7,16,512]{2,1,0:T(8,128)(2,1)S(1)}, u32[]{:S(2)}, u32[]{:S(2)}) collective-permute-start(bf16[7,16,512]{2,1,0:T(8,128)(2,1)S(1)} %get-tuple-element.139), channel_id=1, source_target_pairs={{0,96},{1,97},{2,98},{3,99},{4,100},{5,101},{6,102},{7,103},{8,104... | collective-permute-start | bytes 344072 | tf_op jit(solution)/shard_map/ppermute | solution.py:386
  66.2 7.9 %collective-permute-start.22 = (bf16[7,16,512]{2,1,0:T(8,128)(2,1)S(1)}, bf16[7,16,512]{2,1,0:T(8,128)(2,1)S(1)}, u32[]{:S(2)}, u32[]{:S(2)}) collective-permute-start(bf16[7,16,512]{2,1,0:T(8,128)(2,1)S(1)} %get-tuple-element.140), channel_id=1, source_target_pairs={{0,64},{1,65},{2,66},{3,67},{4,68},{5,69},{6,70},{7,71},{8,72},{9,... | collective-permute-start | bytes 344072 | tf_op jit(solution)/shard_map/ppermute | solution.py:386
  69.7 4.7 %collective-permute-start.15 = (bf16[6,16,512]{2,1,0:T(8,128)(2,1)S(1)}, bf16[6,16,512]{2,1,0:T(8,128)(2,1)S(1)}, u32[]{:S(2)}, u32[]{:S(2)}) collective-permute-start(bf16[6,16,512]{2,1,0:T(8,128)(2,1)S(1)} %get-tuple-element.126), channel_id=1, source_target_pairs={{0,8},{1,9},{2,10},{3,11},{4,12},{5,13},{6,14},{7,15},{8,0},{9,1},... | collective-permute-start | bytes 294920 | tf_op jit(solution)/shard_map/ppermute | solution.py:386
  70.5 4.6 %collective-permute-start.16 = (bf16[6,16,512]{2,1,0:T(8,128)(2,1)S(1)}, bf16[6,16,512]{2,1,0:T(8,128)(2,1)S(1)}, u32[]{:S(2)}, u32[]{:S(2)}) collective-permute-start(bf16[6,16,512]{2,1,0:T(8,128)(2,1)S(1)} %get-tuple-element.127), channel_id=1, source_target_pairs={{0,24},{1,25},{2,26},{3,27},{4,28},{5,29},{6,30},{7,31},{8,16},{9,... | collective-permute-start | bytes 294920 | tf_op jit(solution)/shard_map/ppermute | solution.py:386
  71.7 6.1 %collective-permute-start.17 = (bf16[6,16,512]{2,1,0:T(8,128)(2,1)S(1)}, bf16[6,16,512]{2,1,0:T(8,128)(2,1)S(1)}, u32[]{:S(2)}, u32[]{:S(2)}) collective-permute-start(bf16[6,16,512]{2,1,0:T(8,128)(2,1)S(1)} %get-tuple-element.128), channel_id=1, source_target_pairs={{0,16},{1,17},{2,18},{3,19},{4,20},{5,21},{6,22},{7,23},{8,24},{9,... | collective-permute-start | bytes 294920 | tf_op jit(solution)/shard_map/ppermute | solution.py:386
  74.0 20.0 %slice-start = ((f32[2,512]{1,0:T(2,128)}), f32[1,512]{1,0:T(1,128)S(1)}, s32[]{:S(2)}) async-start(f32[2,512]{1,0:T(2,128)} %gains.3), calls=%async_computation.1 | async-start | bytes 4096 | tf_op jit(solution)/shard_map/slice | solution.py:523
  79.2 14.8 %all-to-all-start = ((bf16[8,112,128]{2,1,0:T(8,128)(2,1)}), bf16[8,112,128]{2,1,0:T(8,128)(2,1)S(1)}, u32[]{:S(2)}, u32[]{:S(2)}) async-start(bf16[8,112,128]{2,1,0:T(8,128)(2,1)} %shard_map.140), calls=%async_computation | async-start | bytes 458752 | tf_op jit(solution)/shard_map/all_to_all | solution.py:398
  83.9 10.1 %collective-permute-start.23 = (bf16[24,3,512]{2,1,0:T(4,128)(2,1)S(1)}, bf16[24,3,512]{2,1,0:T(4,128)(2,1)S(1)}, u32[]{:S(2)}, u32[]{:S(2)}) collective-permute-start(bf16[24,3,512]{2,1,0:T(4,128)(2,1)S(1)} %get-tuple-element.155), channel_id=1, source_target_pairs={{1,2},{2,1},{3,4},{4,3},{5,6},{6,5},{7,8},{8,7},{9,10},{10,9},{11,... | collective-permute-start | bytes 221192 | tf_op jit(solution)/shard_map/ppermute | solution.py:386
  85.8 8.2 %collective-permute-start.24 = (bf16[24,3,512]{2,1,0:T(4,128)(2,1)S(1)}, bf16[24,3,512]{2,1,0:T(4,128)(2,1)S(1)}, u32[]{:S(2)}, u32[]{:S(2)}) collective-permute-start(bf16[24,3,512]{2,1,0:T(4,128)(2,1)S(1)} %get-tuple-element.154), channel_id=1, source_target_pairs={{0,1},{1,0},{2,3},{3,2},{4,5},{5,4},{6,7},{7,6},{8,9},{9,8},{10,11... | collective-permute-start | bytes 221192 | tf_op jit(solution)/shard_map/ppermute | solution.py:386
  (3 other events, 3.5 us)

commit v11 on v10

--- a/solution.py
+++ b/solution.py
@@ -97,7 +97,7 @@
         bias[t] = jnp.where(ok, 0.0, -1e30)
 
 
-def prep_order_kernel(coord, pt_u, pt_k, pt_d):
+def prep_order_kernel(coord, pt_u, pt_k):
     me = coord[2]
     lane = lax.broadcasted_iota(jnp.int32, (512, 512), 1)
     p = lax.broadcasted_iota(jnp.int32, (512, 512), 0)
@@ -106,8 +106,6 @@
     here = me & 121
     pt_u[...] = jnp.where(lane == ((core_z + hi * 32 + lo * 8) ^ here) * 2 + (p & 1), 1.0, 0.0).astype(BF16)
     pt_k[...] = jnp.where(lane == ((core_z + hi * 8 + lo * 32) ^ here) * 2 + (p & 1), 1.0, 0.0).astype(BF16)
-    k_d = (((p >> 5) & 1) * 32 + ((p >> 6) & 3) * 8 + ((p >> 3) & 3) * 2 + (p >> 8)) ^ (me & 57)
-    pt_d[...] = jnp.where(lane == k_d * 8 + (p & 7), 1.0, 0.0).astype(BF16)
 
 
 def attend(qt, keys, vals, bias_t):
@@ -136,8 +134,8 @@
 
 
 def forward_kernel(
-    coord, rim_a, rim_b, tok, cot, gains, w_qkv, w_out, w_up, gact, bias, pt_u, pt_d, q_i, ne_i, kv_i, attn_i,
-    u_keep, u_send, d_keep, d_send, gm_o, kv_o, p_o, ne_o, gain_o, attn_s,
+    coord, rim_a, rim_b, tok, cot, gains, w_qkv, w_out, w_up, gact, bias, pt_u, q_i, ne_i, kv_i, attn_i,
+    u_keep, u_send, d_keep, d_send, gm_o, kv_o, p_o, ne_o, gain_o, attn_s, rows_s,
 ):
     odd = coord[0] & 1
     edge = RIM * EC
@@ -181,14 +179,14 @@
         gu = nn(nmt, gp).astype(BF16)
         u_keep[:, c] = gu[:256].reshape(16, 16, D)
         u_send[:, c] = gu[256:].reshape(16, 16, D)
-        act_t = nt(pt_d[...], act).astype(BF16)
-        gd = nn(act_t, cot[...]).astype(BF16)
+        rows_s[c & 1] = tn(act, cot[...]).reshape(64, 8, D)
         xh = (c & 1) ^ ((coord[2] >> 6) & 1)
         for y in range(4):
             for xl in range(2):
-                at = (y * 2 + xl) * 32
-                d_keep[y, xh * 2 + xl, c >> 1] = gd[at : at + 32]
-                d_send[y, xh * 2 + xl, c >> 1] = gd[256 + at : 256 + at + 32]
+                for co, ref in ((0, d_keep), (1, d_send)):
+                    at = (xl * 32 + y * 8 + co) ^ (coord[2] & 57)
+                    part = jnp.concatenate([rows_s[c & 1, at + 2 * zl] for zl in range(4)], axis=0)
+                    ref[y, xh * 2 + xl, c >> 1] = part.astype(BF16)
     g = gn * gains[1:2, :]
     gm = (cot[...].astype(F32) + inv_m * (g - um * jnp.mean(g * um, axis=-1, keepdims=True))).astype(BF16)
     gm_o[...] = gm
@@ -200,14 +198,14 @@
 
 def backward_kernel(
     gm, w_out, q, kv, p_mid, p_out, ne, no, pt_u, pt_k,
-    k_keep, k_send, dq_s, dkv_o, dkv_s,
+    k_keep, k_send, dq_s, dkv_o,
 ):
     ga = nt(gm[...], w_out[...]).astype(BF16)
-    dkv_s[...] = jnp.zeros_like(dkv_s)
-    for t in range(TILES):
-        for g in range(2):
-            cols = slice(g * 256, (g + 1) * 256)
-            vcols = slice(D + g * 256, D + (g + 1) * 256)
+    for g in range(2):
+        cols = slice(g * 256, (g + 1) * 256)
+        vcols = slice(D + g * 256, D + (g + 1) * 256)
+        left_k = left_v = None
+        for t in range(TILES):
             rows = slice(t * 128, t * 128 + KT)
             prob = p_mid[g] if t == 1 else p_out[t + g]
             gas = stack_heads(ga[t * QT : (t + 1) * QT, cols])
@@ -216,10 +214,16 @@
             inner = jnp.sum(prob * gp, axis=-1, keepdims=True)
             ds = (prob * (gp - inner) * 0.125).astype(BF16)
             dq_s[t * QT : (t + 1) * QT, cols] = unstack_heads(nn(ds, kv[rows, cols])).astype(BF16)
-            dkv_s[rows, cols] += tn(ds, qs)
-            dkv_s[rows, vcols] += tn(prob.astype(BF16), gas)
-    dkv = dkv_s[...].astype(BF16)
-    dkv_o[...] = dkv
+            dk, dv = tn(ds, qs), tn(prob.astype(BF16), gas)
+            top_k, top_v = dk[:128], dv[:128]
+            if t:
+                top_k, top_v = top_k + left_k, top_v + left_v
+            left_k, left_v = dk[128:], dv[128:]
+            dkv_o[t * 128 : t * 128 + 128, cols] = top_k.astype(BF16)
+            dkv_o[t * 128 : t * 128 + 128, vcols] = top_v.astype(BF16)
+        dkv_o[TILES * 128 :, cols] = left_k.astype(BF16)
+        dkv_o[TILES * 128 :, vcols] = left_v.astype(BF16)
+    dkv = dkv_o[...]
     gk = nn(nt(pt_k[...], ne[...]).astype(BF16), dkv).astype(BF16)
     gq = nn(nt(pt_u[...], no[...]).astype(BF16), dq_s[...]).astype(BF16)
     for at, out in ((0, k_keep), (256, k_send)):
@@ -261,8 +265,7 @@
     return ((0, (1, 2), (0, 3)), (1, (3, 2), (0, 1)))
 
 
-def join_down_kv_kernel(dk, dg, kk, kg, gk, gg, *outs):
-    gain = add2(gk[...], gg[...])
+def join_down_kv_kernel(dk, dg, kk, kg, *outs):
     for h, away, stay in halves():
         for out, chunks in ((outs[h], away), (outs[2 + h], stay)):
             for i, d in enumerate(chunks):
@@ -270,12 +273,9 @@
                 out[at : at + 8] = add2(dk[lo : lo + 8], dg[lo : lo + 8])
                 lo = 16 + d * 8 + h * 4
                 out[at + 8 : at + 12] = add2(kk[lo : lo + 4], kg[lo : lo + 4])
-    outs[0][24] = gain
-    outs[2][24] = gain
-
-
-def join_up_q_kernel(uk, ug, kk, kg, ride, *outs):
-    outs[0][24:] = ride[...]
+
+
+def join_up_q_kernel(uk, ug, kk, kg, gk, gg, ride, *outs):
     for h, away, stay in halves():
         for out, chunks in ((outs[h], away), (outs[2 + h], stay)):
             for i, d in enumerate(chunks):
@@ -283,6 +283,10 @@
                 out[at : at + 10] = add2(uk[lo : lo + 10], ug[lo : lo + 10])
                 lo = d * 4 + h * 2
                 out[at + 10 : at + 12] = add2(kk[lo : lo + 2], kg[lo : lo + 2])
+    gain = add2(gk[...], gg[...])
+    outs[0][24] = gain
+    outs[2][24] = gain
+    outs[0][25:] = ride[...]
 
 
 def second_kernel(p_got, q_got, p_keep, q_keep, p_send, q_send, p_own, q_own):
@@ -297,20 +301,21 @@
 
 
 def sum_up_q_kernel(p_got, q_got, p_own, q_own, *outs):
-    for h, got, own in ((0, p_got, p_own), (1, q_got, q_own)):
-        for i in range(2):
-            outs[2 * h + i][:5] = add2(got[i * 5 : i * 5 + 5], own[i * 5 : i * 5 + 5])
-            outs[2 * h + i][5] = add2(got[10 + i], own[10 + i])
-
-
-def sum_down_kv_kernel(p_got, q_got, p_own, q_own, *outs):
     gain = add2(p_got[12], p_own[12])
     for h, got, own in ((0, p_got, p_own), (1, q_got, q_own)):
         for i in range(2):
             out = outs[2 * h + i]
+            out[:5] = add2(got[i * 5 : i * 5 + 5], own[i * 5 : i * 5 + 5])
+            out[5] = add2(got[10 + i], own[10 + i])
+            out[6] = gain
+
+
+def sum_down_kv_kernel(p_got, q_got, p_own, q_own, *outs):
+    for h, got, own in ((0, p_got, p_own), (1, q_got, q_own)):
+        for i in range(2):
+            out = outs[2 * h + i]
             out[:4] = add2(got[i * 4 : i * 4 + 4], own[i * 4 : i * 4 + 4])
-            out[4:6] = add2(got[8 + i * 2 : 10 + i * 2], own[8 + i * 2 : 10 + i * 2])
-            out[6] = gain
+            out[4:] = add2(got[8 + i * 2 : 10 + i * 2], own[8 + i * 2 : 10 + i * 2])
 
 
 def reduce_xy_kernel(*refs):
@@ -324,11 +329,11 @@
     z = i // per
     r = i % per
     up = (r % 4) * 16 + z * 2 + r // 4
-    down = 96 + z * 8 + (r - 8)
+    down = 112 + z * 8 + (r - 8)
     o = 64 + z * 2 + (r - 16)
     part = (r - 18) % 3
-    qkv = jnp.where(part == 0, 80, 144 + part * 16) + z * 2 + (r - 18) // 3
-    gain = 192 + (r - 24)
+    qkv = jnp.where(part == 0, 80, 160 + part * 16) + z * 2 + (r - 18) // 3
+    gain = 96 + (r - 24)
     src = jnp.where(r < 8, up, jnp.where(r < 16, down, jnp.where(r < 18, o, jnp.where(r < 24, qkv, gain))))
     picked = nn(jnp.where((lane == src) & (r < 26), 1.0, 0.0).astype(BF16), acc)
     for j in range(4):
@@ -417,8 +422,8 @@
     mid = jnp.concatenate([tokens, side_a, side_b, jnp.zeros((ROWS, EC - COLS - 2 * RIM, D), BF16)], axis=1)
     rim_b = send(jnp.where(row_odd, mid[:RIM], mid[ROWS - RIM :]), ROW_B)
     rim_a = send(jnp.where(row_odd, mid[ROWS - RIM :], mid[:RIM]), ROW_A)
-    pt_u, pt_k, pt_d = call(
-        prep_order_kernel, [((D, D), BF16)] * 3, [], 1, 0, 2 * TOK * D * FF, 4_000_000, 8,
+    pt_u, pt_k = call(
+        prep_order_kernel, [((D, D), BF16)] * 2, [], 1, 0, 2 * TOK * D * FF, 4_000_000, 8,
     )(coord)
     (gact,) = call(
         prep_front_kernel, [((TOK, FF), F32)], [], 0, 2, 2 * TOK * D * FF, 4_000_000, 8,
@@ -441,15 +446,15 @@
             half_u, half_u, half_d, half_d, ((TOK, D), BF16), ((EXT, 2 * D), BF16), ((4, 256, KT), F32),
             ((EXT, D), BF16), ((1, D), F32),
         ],
-        [pltpu.VMEM((TOK, D), BF16)], 1, 16, 4_000_000_000, 20_000_000, 16,
-    )(coord, rim_a, rim_b, tok, cot, gains, w_qkv, w_out, w_up, gact, bias, pt_u, pt_d, q, ne_mid, kv_mid, attn_mid)
+        [pltpu.VMEM((TOK, D), BF16), pltpu.VMEM((2, 64, 8, D), F32)], 1, 15, 4_000_000_000, 20_000_000, 16,
+    )(coord, rim_a, rim_b, tok, cot, gains, w_qkv, w_out, w_up, gact, bias, pt_u, q, ne_mid, kv_mid, attn_mid)
 
     u_got = send(u_send, CORE_SWAP)
     d_got = send(d_send, CORE_SWAP)
     k_keep, k_send, dq, dkv = call(
         backward_kernel,
         [half_k, half_k, ((TOK, D), BF16), ((EXT, 2 * D), BF16)],
-        [pltpu.VMEM((EXT, 2 * D), F32)], 0, 10, 2_500_000_000, 10_000_000, 12,
+        [], 0, 10, 2_500_000_000, 10_000_000, 12,
     )(gm, w_out, q, kv, p_mid, p_out, ne, no, pt_u, pt_k)
     u_got, d_got, k_send = lax.optimization_barrier((u_got, d_got, k_send))
     k_got = send(k_send, CORE_SWAP)
@@ -481,28 +486,27 @@
     def second(sent, bit):
         return send(sent[0], by(3 * bit)), send(sent[1], by(bit))
 
-    k_got, gnq = lax.optimization_barrier((k_got, gnq))
+    k_got, gnq, gain_got = lax.optimization_barrier((k_got, gnq, gain_got))
     u_p, u_q, *u_stay = join(
-        join_up_q_kernel, [u_keep.reshape(80, 16, D), u_got.reshape(80, 16, D), k_keep, k_got, row_b],
-        [(27, 16, D)] + [(24, 16, D)] * 3,
+        join_up_q_kernel, [u_keep.reshape(80, 16, D), u_got.reshape(80, 16, D), k_keep, k_got, gain, gain_got, row_b],
+        [(28, 16, D), (24, 16, D), (25, 16, D), (24, 16, D)],
     )
     u_first = first((u_p, u_q), X_BIT)
     b_p, b_q, *b_stay = join(
-        join_down_kv_kernel, [d_keep.reshape(64, 16, D), d_got.reshape(64, 16, D), k_keep, k_got, gain, gain_got],
-        [(25, 16, D), (24, 16, D)] * 2,
+        join_down_kv_kernel, [d_keep.reshape(64, 16, D), d_got.reshape(64, 16, D), k_keep, k_got], [(24, 16, D)] * 4,
     )
     b_first = first((b_p, b_q), Y_BIT)
     row_a = send(row_a, ROW_A)
     b_first, row_a = lax.optimization_barrier((b_first, row_a))
-    u_p, u_q, *u_own = join(second_kernel, [*u_first, *u_stay], [(12, 16, D)] * 4)
+    u_p, u_q, *u_own = join(second_kernel, [*u_first, *u_stay], [(13, 16, D), (12, 16, D)] * 2)
     u_second = second((u_p, u_q), X_BIT)
-    b_p, b_q, *b_own = join(second_kernel, [*b_first, *b_stay], [(13, 16, D), (12, 16, D)] * 2)
+    b_p, b_q, *b_own = join(second_kernel, [*b_first, *b_stay], [(12, 16, D)] * 4)
     b_second = second((b_p, b_q), Y_BIT)
     gne = gne.reshape(ROWS + 2 * RIM, EC, D)[RIM : RIM + ROWS]
-    gne = gne + place(row_a, 0, row_odd, True, ROWS) + place(u_first[0][24:], 0, row_odd, False, ROWS)
-    u = join(sum_up_q_kernel, [*u_second, *u_own], [(6, 16, D)] * 4)
+    gne = gne + place(row_a, 0, row_odd, True, ROWS) + place(u_first[0][25:], 0, row_odd, False, ROWS)
+    u = join(sum_up_q_kernel, [*u_second, *u_own], [(7, 16, D)] * 4)
     u = to_three(u, Y_BIT)
-    b = join(sum_down_kv_kernel, [*b_second, *b_own], [(7, 16, D)] * 4)
+    b = join(sum_down_kv_kernel, [*b_second, *b_own], [(6, 16, D)] * 4)
     b = to_three(b, X_BIT)
     (spread,) = call(
         reduce_xy_kernel, [((8, ZROWS, 128), BF16)], [pltpu.VMEM((8 * ZROWS, 128), F32)], 0, 8, 60_000_000, 4_000_000, 5,

time: 96.8 us -> 96.2 us (level)
  Pallas kernels: 20.7 us -> 19.5 us
  transfers between devices with their start and end apart: 26 -> 26, of which waited for: 10 -> 9; matrix products, arithmetic and copies ran while one was open for 1% -> 1% of each run, Pallas kernels for 12% -> 12%
where the time goes in v11:
time: 96.2 us; the launch traced here: 95 us
  starting transfers between devices  52.6 us (55%)
  Pallas kernels  19.5 us (20%)
  waiting for transfers between devices  17.5 us (18%)
  other arithmetic  2.93 us (3%)
  local copies, waits for them, and re-layouts  1.46 us (2%)
  between operations  1.02 us (1%)
    ppermute x25, starting transfers between devices, send(): return lax.ppermute(x, AXES, perm)  47.7 us
    ppermute x25, waiting for transfers between devices, send(): return lax.ppermute(x, AXES, perm)  17 us
    pallas_call x1, Pallas kernels, per_device(): call(forward_kernel, [half_u, half_u, half_d, half_d, ((TOK, D), BF16), (...  6.02 us
    all_to_all x1, starting transfers between devices, exchange(): return lax.all_to_all(x, AXES, 0, 0, axis_index_groups=groups, tiled=True)  4.88 us
    pallas_call x1, Pallas kernels, per_device(): call(backward_kernel, [half_k, half_k, ((TOK, D), BF16), ((EXT, 2 * D), B...  4.02 us
  transfers between devices with their start and end apart: 26, of which 9 were waited for; matrix products, arithmetic and copies ran while one was open for 1% of the time, Pallas kernels for 12%

profile of v11, /device:TPU:8, one launch (start us, length us, event | category | flops | bytes accessed | tf_op | source)
XLA Modules:
  0.0 95.0 jit_solution(15325434260406346109)
XLA Ops:
  0.6 1.2 %broadcast_select_fusion = (bf16[24,3,512]{2,1,0:T(4,128)(2,1)S(1)}, bf16[24,3,512]{2,1,0:T(4,128)(2,1)S(1)}) fusion(pred[]{:T(512)S(6)} %eq.6, bf16[24,8,512]{2,1,0:T(8,128)(2,1)} %param.8), kind=kLoop, calls=%fused_computation.16 | loop fusion | flops 73728 | bytes 294913 | tf_op jit(solution)/shard_map/jit(_where)/select_n | solution.py:416
  1.8 5.9 %collective-permute-start = (bf16[24,3,512]{2,1,0:T(4,128)(2,1)S(1)}, bf16[24,3,512]{2,1,0:T(4,128)(2,1)S(1)}, u32[]{:S(2)}, u32[]{:S(2)}) collective-permute-start(bf16[24,3,512]{2,1,0:T(4,128)(2,1)S(1)} %get-tuple-element.159), channel_id=1, source_target_pairs={{1,2},{2,1},{3,4},{4,3},{5,6},{6,5},{7,8},{8,7},{9,10},{10,9},{11,... | collective-permute-start | bytes 221192 | tf_op jit(solution)/shard_map/ppermute | solution.py:391
  8.6 1.2 %shard_map.127.bias = f32[3,64,256]{2,1,0:T(8,128)S(1)} custom-call(s32[3]{0:T(128)S(1)} %pad_add_fusion.coord, s32[3,1,49]{2,1,0:T(1,128)S(1)} %copy-done.7), custom_call_target="tpu_custom_call" | custom-call | flops 402653184 | bytes 4000000 | tf_op jit(solution)/shard_map/pallas_call | solution.py:418
  9.9 1.3 %collective-permute-done = bf16[24,3,512]{2,1,0:T(4,128)(2,1)S(1)} collective-permute-done((bf16[24,3,512]{2,1,0:T(4,128)(2,1)S(1)}, bf16[24,3,512]{2,1,0:T(4,128)(2,1)S(1)}, u32[]{:S(2)}, u32[]{:S(2)}) %collective-permute-start) | collective-permute-done | bytes 73760 | tf_op jit(solution)/shard_map/ppermute | solution.py:391
  12.1 4.3 %collective-permute-start.3 = (bf16[3,16,512]{2,1,0:T(8,128)(2,1)S(1)}, bf16[3,16,512]{2,1,0:T(8,128)(2,1)S(1)}, u32[]{:S(2)}, u32[]{:S(2)}) collective-permute-start(bf16[3,16,512]{2,1,0:T(8,128)(2,1)S(1)} %get-tuple-element.156), channel_id=1, source_target_pairs={{0,32},{1,33},{2,34},{3,35},{4,36},{5,37},{6,38},{7,39},{8,40},{9,... | collective-permute-start | bytes 147464 | tf_op jit(solution)/shard_map/ppermute | solution.py:391
  16.4 1.0 %shard_map.129 = (bf16[512,512]{1,0:T(8,128)(2,1)S(1)}, bf16[512,512]{1,0:T(8,128)(2,1)S(1)}) custom-call(s32[3]{0:T(128)S(1)} %pad_add_fusion.coord), custom_call_target="tpu_custom_call" | custom-call | flops 402653184 | bytes 4000000 | tf_op jit(solution)/shard_map/pallas_call | solution.py:425
  17.5 0.8 shard_map.128.gact
  18.9 1.6 %shard_map.130 = (bf16[192,512]{1,0:T(8,128)(2,1)S(1)}, bf16[192,512]{1,0:T(8,128)(2,1)S(1)}, bf16[384,512]{1,0:T(8,128)(2,1)S(1)}, bf16[384,1024]{1,0:T(8,128)(...) custom-call(bf16[24,16,512]{2,1,0:T(8,128)(2,1)S(1)} %maximum_maximum_fusion.mid, ...), custom_call_target="tpu_custom_call" | custom-call | flops 600000000 | bytes 5000000 | tf_op jit(solution)/shard_map/pallas_call | solution.py:432
  20.6 6.0 %shard_map.131 = (bf16[16,5,16,512]{3,2,1,0:T(8,128)(2,1)S(1)}, bf16[16,5,16,512]{3,2,1,0:T(8,128)(2,1)S(1)}, bf16[4,4,2,32,512]{4,3,2,1,0:T(8,128)(2,1)S(1)}, b...) custom-call(s32[3]{0:T(128)S(1)} %pad_add_fusion.coord, ...), custom_call_target="tpu_custom_call" | custom-call | flops 4000000000 | bytes 20000000 | tf_op jit(solution)/shard_map/pallas_call | solution.py:443
  27.2 4.0 %shard_map.132 = (bf16[48,16,512]{2,1,0:T(8,128)(2,1)S(1)}, bf16[48,16,512]{2,1,0:T(8,128)(2,1)S(1)}, bf16[192,512]{1,0:T(8,128)(2,1)S(1)}, bf16[512,1024]{1,0:T(8,128)(2,1)S(1)}) custom-call(bf16[192,512]{1,0:T(8,128)(2,1)S(1)} %get-tuple-element.88.gm, bf16[512,512]{1,0:T(8,128)(2,1)S(1)} %copy-done.6, bf16[192,512]{1,0:T(8,128)(2,1)S(1)} %get-tuple-element.84.q_i.q, ...), custom_call_target="tpu_custom_call" | custom-call | flops 2500000000 | bytes 10000000 | tf_op jit(solution)/shard_map/pallas_call | solution.py:454
  31.6 1.5 %shard_map.133 = (f32[480,512]{1,0:T(8,128)S(1)}, f32[192,512]{1,0:T(8,128)S(1)}, bf16[16,512]{1,0:T(8,128)(2,1)S(1)}, bf16[3,16,512]{2,1,0:T(8,128)(2,1)S(1)}, bf16[3,16,512]{2,1,0:T(8,128)(2,1)S(1)}) custom-call(s32[3]{0:T(128)S(1)} %pad_add_fusion.coord, bf16[192,512]{1,0:T(8,128)(2,1)S(1)} %get-tuple-element.95.dq, ...), custom_call_target="tpu_custom_call" | custom-call | flops 600000000 | bytes 4000000 | tf_op jit(solution)/shard_map/pallas_call | solution.py:461
  33.4 1.0 %collective-permute-done.7.gg = bf16[16,512]{1,0:T(8,128)(2,1)S(1)} collective-permute-done((bf16[16,512]{1,0:T(8,128)(2,1)S(1)}, bf16[16,512]{1,0:T(8,128)(2,1)S(1)}, u32[]{:S(2)}, u32[]{:S(2)}) %collective-permute-start.7) | collective-permute-done | bytes 16416 | tf_op jit(solution)/shard_map/ppermute | solution.py:391
  34.8 2.5 %collective-permute-start.9 = (bf16[24,16,512]{2,1,0:T(8,128)(2,1)S(1)}, bf16[24,16,512]{2,1,0:T(8,128)(2,1)S(1)}, u32[]{:S(2)}, u32[]{:S(2)}) collective-permute-start(bf16[24,16,512]{2,1,0:T(8,128)(2,1)S(1)} %get-tuple-element.110), channel_id=1, source_target_pairs={{0,24},{1,25},{2,26},{3,27},{4,28},{5,29},{6,30},{7,31},{8,16},{9,... | collective-permute-start | bytes 1179656 | tf_op jit(solution)/shard_map/ppermute | solution.py:391
  37.8 8.5 %collective-permute-start.12 = (bf16[24,16,512]{2,1,0:T(8,128)(2,1)S(1)}, bf16[24,16,512]{2,1,0:T(8,128)(2,1)S(1)}, u32[]{:S(2)}, u32[]{:S(2)}) collective-permute-start(bf16[24,16,512]{2,1,0:T(8,128)(2,1)S(1)} %get-tuple-element.118), channel_id=1, source_target_pairs={{0,96},{1,97},{2,98},{3,99},{4,100},{5,101},{6,102},{7,103},{8,104... | collective-permute-start | bytes 1179656 | tf_op jit(solution)/shard_map/ppermute | solution.py:391
  47.1 1.4 %collective-permute-start.18 = (bf16[12,16,512]{2,1,0:T(8,128)(2,1)S(1)}, bf16[12,16,512]{2,1,0:T(8,128)(2,1)S(1)}, u32[]{:S(2)}, u32[]{:S(2)}) collective-permute-start(bf16[12,16,512]{2,1,0:T(8,128)(2,1)S(1)} %get-tuple-element.133), channel_id=1, source_target_pairs={{0,24},{1,25},{2,26},{3,27},{4,28},{5,29},{6,30},{7,31},{8,16},{9,... | collective-permute-start | bytes 589832 | tf_op jit(solution)/shard_map/ppermute | solution.py:391
  48.6 2.9 %collective-permute-start.19 = (bf16[12,16,512]{2,1,0:T(8,128)(2,1)S(1)}, bf16[12,16,512]{2,1,0:T(8,128)(2,1)S(1)}, u32[]{:S(2)}, u32[]{:S(2)}) collective-permute-start(bf16[12,16,512]{2,1,0:T(8,128)(2,1)S(1)} %get-tuple-element.134), channel_id=1, source_target_pairs={{0,8},{1,9},{2,10},{3,11},{4,12},{5,13},{6,14},{7,15},{8,0},{9,1},... | collective-permute-start | bytes 589832 | tf_op jit(solution)/shard_map/ppermute | solution.py:391
  51.7 3.6 %collective-permute-done.12.q_got = bf16[24,16,512]{2,1,0:T(8,128)(2,1)S(1)} collective-permute-done((bf16[24,16,512]{2,1,0:T(8,128)(2,1)S(1)}, bf16[24,16,512]{2,1,0:T(8,128)(2,1)S(1)}, u32[]{:S(2)}, u32[]{:S(2)}) %collective-permute-start.12) | collective-permute-done | bytes 393248 | tf_op jit(solution)/shard_map/ppermute | solution.py:391
  55.5 6.0 %collective-permute-start.13 = (bf16[13,16,512]{2,1,0:T(8,128)(2,1)S(1)}, bf16[13,16,512]{2,1,0:T(8,128)(2,1)S(1)}, u32[]{:S(2)}, u32[]{:S(2)}) collective-permute-start(bf16[13,16,512]{2,1,0:T(8,128)(2,1)S(1)} %get-tuple-element.121), channel_id=1, source_target_pairs={{0,96},{1,97},{2,98},{3,99},{4,100},{5,101},{6,102},{7,103},{8,104... | collective-permute-start | bytes 638984 | tf_op jit(solution)/shard_map/ppermute | solution.py:391
  61.6 2.1 %collective-permute-start.20 = (bf16[6,16,512]{2,1,0:T(8,128)(2,1)S(1)}, bf16[6,16,512]{2,1,0:T(8,128)(2,1)S(1)}, u32[]{:S(2)}, u32[]{:S(2)}) collective-permute-start(bf16[6,16,512]{2,1,0:T(8,128)(2,1)S(1)} %get-tuple-element.138), channel_id=1, source_target_pairs={{0,32},{1,33},{2,34},{3,35},{4,36},{5,37},{6,38},{7,39},{8,40},{9,... | collective-permute-start | bytes 294920 | tf_op jit(solution)/shard_map/ppermute | solution.py:391
  63.7 1.2 %collective-permute-start.21 = (bf16[6,16,512]{2,1,0:T(8,128)(2,1)S(1)}, bf16[6,16,512]{2,1,0:T(8,128)(2,1)S(1)}, u32[]{:S(2)}, u32[]{:S(2)}) collective-permute-start(bf16[6,16,512]{2,1,0:T(8,128)(2,1)S(1)} %get-tuple-element.139), channel_id=1, source_target_pairs={{0,96},{1,97},{2,98},{3,99},{4,100},{5,101},{6,102},{7,103},{8,104... | collective-permute-start | bytes 294920 | tf_op jit(solution)/shard_map/ppermute | solution.py:391
  64.9 1.8 %collective-permute-start.22 = (bf16[6,16,512]{2,1,0:T(8,128)(2,1)S(1)}, bf16[6,16,512]{2,1,0:T(8,128)(2,1)S(1)}, u32[]{:S(2)}, u32[]{:S(2)}) collective-permute-start(bf16[6,16,512]{2,1,0:T(8,128)(2,1)S(1)} %get-tuple-element.140), channel_id=1, source_target_pairs={{0,64},{1,65},{2,66},{3,67},{4,68},{5,69},{6,70},{7,71},{8,72},{9,... | collective-permute-start | bytes 294920 | tf_op jit(solution)/shard_map/ppermute | solution.py:391
  66.7 1.5 %collective-permute-done.14.q_got = bf16[12,16,512]{2,1,0:T(8,128)(2,1)S(1)} collective-permute-done((bf16[12,16,512]{2,1,0:T(8,128)(2,1)S(1)}, bf16[12,16,512]{2,1,0:T(8,128)(2,1)S(1)}, u32[]{:S(2)}, u32[]{:S(2)}) %collective-permute-start.14) | collective-permute-done | bytes 196640 | tf_op jit(solution)/shard_map/ppermute | solution.py:391
  68.3 0.7 collective-permute-start.15
  69.1 1.4 %collective-permute-start.16 = (bf16[7,16,512]{2,1,0:T(8,128)(2,1)S(1)}, bf16[7,16,512]{2,1,0:T(8,128)(2,1)S(1)}, u32[]{:S(2)}, u32[]{:S(2)}) collective-permute-start(bf16[7,16,512]{2,1,0:T(8,128)(2,1)S(1)} %get-tuple-element.127), channel_id=1, source_target_pairs={{0,24},{1,25},{2,26},{3,27},{4,28},{5,29},{6,30},{7,31},{8,16},{9,... | collective-permute-start | bytes 344072 | tf_op jit(solution)/shard_map/ppermute | solution.py:391
  70.5 2.0 %collective-permute-start.17 = (bf16[7,16,512]{2,1,0:T(8,128)(2,1)S(1)}, bf16[7,16,512]{2,1,0:T(8,128)(2,1)S(1)}, u32[]{:S(2)}, u32[]{:S(2)}) collective-permute-start(bf16[7,16,512]{2,1,0:T(8,128)(2,1)S(1)} %get-tuple-element.128), channel_id=1, source_target_pairs={{0,16},{1,17},{2,18},{3,19},{4,20},{5,21},{6,22},{7,23},{8,24},{9,... | collective-permute-start | bytes 344072 | tf_op jit(solution)/shard_map/ppermute | solution.py:391
  73.9 2.9 %collective-permute-done.17.refs_3_ = bf16[7,16,512]{2,1,0:T(8,128)(2,1)S(1)} collective-permute-done((bf16[7,16,512]{2,1,0:T(8,128)(2,1)S(1)}, bf16[7,16,512]{2,1,0:T(8,128)(2,1)S(1)}, u32[]{:S(2)}, u32[]{:S(2)}) %collective-permute-start.17) | collective-permute-done | bytes 114720 | tf_op jit(solution)/shard_map/ppermute | solution.py:391
  76.8 1.3 %shard_map.140 = bf16[8,112,128]{2,1,0:T(8,128)(2,1)} custom-call(bf16[7,16,512]{2,1,0:T(8,128)(2,1)S(1)} %get-tuple-element.125.refs_0_, bf16[7,16,512]{2,1,0:T(8,128)(2,1)S(1)} %collective-permute-done.15.refs_1_, bf16[7,16,512]{2,1,0:T(8,128)(2,1)S(1)} %collective-permute-done.16.refs_2_, bf16[7,16,512]{2,1,0:T(8,128)(2,1)S(1)} %collective-permute-done.17.refs_3_, ...), custom_call_target="tpu_custom_call" | custom-call | flops 60000000 | bytes 4000000 | tf_op jit(solution)/shard_map/pallas_call | solution.py:511
  78.1 4.9 %all-to-all-start = ((bf16[8,112,128]{2,1,0:T(8,128)(2,1)}), bf16[8,112,128]{2,1,0:T(8,128)(2,1)S(1)}, u32[]{:S(2)}, u32[]{:S(2)}) async-start(bf16[8,112,128]{2,1,0:T(8,128)(2,1)} %shard_map.140), calls=%async_computation | async-start | bytes 458752 | tf_op jit(solution)/shard_map/all_to_all | solution.py:403
  83.1 1.9 %collective-permute-start.23 = (bf16[24,3,512]{2,1,0:T(4,128)(2,1)S(1)}, bf16[24,3,512]{2,1,0:T(4,128)(2,1)S(1)}, u32[]{:S(2)}, u32[]{:S(2)}) collective-permute-start(bf16[24,3,512]{2,1,0:T(4,128)(2,1)S(1)} %get-tuple-element.155), channel_id=1, source_target_pairs={{1,2},{2,1},{3,4},{4,3},{5,6},{6,5},{7,8},{8,7},{9,10},{10,9},{11,... | collective-permute-start | bytes 221192 | tf_op jit(solution)/shard_map/ppermute | solution.py:391
  85.0 2.2 %collective-permute-start.24 = (bf16[24,3,512]{2,1,0:T(4,128)(2,1)S(1)}, bf16[24,3,512]{2,1,0:T(4,128)(2,1)S(1)}, u32[]{:S(2)}, u32[]{:S(2)}) collective-permute-start(bf16[24,3,512]{2,1,0:T(4,128)(2,1)S(1)} %get-tuple-element.154), channel_id=1, source_target_pairs={{0,1},{1,0},{2,3},{3,2},{4,5},{5,4},{6,7},{7,6},{8,9},{9,8},{10,11... | collective-permute-start | bytes 221192 | tf_op jit(solution)/shard_map/ppermute | solution.py:391
  87.2 5.5 %collective-permute-done.23 = bf16[24,3,512]{2,1,0:T(4,128)(2,1)S(1)} collective-permute-done((bf16[24,3,512]{2,1,0:T(4,128)(2,1)S(1)}, bf16[24,3,512]{2,1,0:T(4,128)(2,1)S(1)}, u32[]{:S(2)}, u32[]{:S(2)}) %collective-permute-start.23) | collective-permute-done | bytes 73760 | tf_op jit(solution)/shard_map/ppermute | solution.py:391
  94.2 0.9 fusion.6
  (71 shorter events, 8.9 us)
Async XLA Ops:
  0.6 10.6 %copy-start = (bf16[24,8,512]{2,1,0:T(8,128)(2,1)S(1)}, bf16[24,8,512]{2,1,0:T(8,128)(2,1)}, u32[]{:S(2)}) copy-start(bf16[24,8,512]{2,1,0:T(8,128)(2,1)} %param.8) | copy-start | bytes 589828
  1.8 9.4 %collective-permute-start = (bf16[24,3,512]{2,1,0:T(4,128)(2,1)S(1)}, bf16[24,3,512]{2,1,0:T(4,128)(2,1)S(1)}, u32[]{:S(2)}, u32[]{:S(2)}) collective-permute-start(bf16[24,3,512]{2,1,0:T(4,128)(2,1)S(1)} %get-tuple-element.159), channel_id=1, source_target_pairs={{1,2},{2,1},{3,4},{4,3},{5,6},{6,5},{7,8},{8,7},{9,10},{10,9},{11,... | collective-permute-start | bytes 221192 | tf_op jit(solution)/shard_map/ppermute | solution.py:391
  7.7 3.5 %collective-permute-start.1 = (bf16[24,3,512]{2,1,0:T(4,128)(2,1)S(1)}, bf16[24,3,512]{2,1,0:T(4,128)(2,1)S(1)}, u32[]{:S(2)}, u32[]{:S(2)}) collective-permute-start(bf16[24,3,512]{2,1,0:T(4,128)(2,1)S(1)} %get-tuple-element.158), channel_id=1, source_target_pairs={{0,1},{1,0},{2,3},{3,2},{4,5},{5,4},{6,7},{7,6},{8,9},{9,8},{10,11... | collective-permute-start | bytes 221192 | tf_op jit(solution)/shard_map/ppermute | solution.py:391
  9.9 7.6 %copy-start.2 = (bf16[2048,512]{1,0:T(8,128)(2,1)S(1)}, bf16[2048,512]{1,0:T(8,128)(2,1)}, u32[]{:S(2)}) copy-start(bf16[2048,512]{1,0:T(8,128)(2,1)} %w_down.1) | copy-start | bytes 6291460
  9.9 7.6 %copy-start.3 = (bf16[24,8,512]{2,1,0:T(8,128)(2,1)S(1)}, bf16[24,8,512]{2,1,0:T(8,128)(2,1)}, u32[]{:S(2)}) copy-start(bf16[24,8,512]{2,1,0:T(8,128)(2,1)} %param.9) | copy-start | bytes 589828
  11.4 9.1 %collective-permute-start.2 = (bf16[3,16,512]{2,1,0:T(8,128)(2,1)S(1)}, bf16[3,16,512]{2,1,0:T(8,128)(2,1)S(1)}, u32[]{:S(2)}, u32[]{:S(2)}) collective-permute-start(bf16[3,16,512]{2,1,0:T(8,128)(2,1)S(1)} %get-tuple-element.157), channel_id=1, source_target_pairs={{32,64},{33,65},{34,66},{35,67},{36,68},{37,69},{38,70},{39,71},{4... | collective-permute-start | bytes 147464 | tf_op jit(solution)/shard_map/ppermute | solution.py:391
  12.1 8.4 %collective-permute-start.3 = (bf16[3,16,512]{2,1,0:T(8,128)(2,1)S(1)}, bf16[3,16,512]{2,1,0:T(8,128)(2,1)S(1)}, u32[]{:S(2)}, u32[]{:S(2)}) collective-permute-start(bf16[3,16,512]{2,1,0:T(8,128)(2,1)S(1)} %get-tuple-element.156), channel_id=1, source_target_pairs={{0,32},{1,33},{2,34},{3,35},{4,36},{5,37},{6,38},{7,39},{8,40},{9,... | collective-permute-start | bytes 147464 | tf_op jit(solution)/shard_map/ppermute | solution.py:391
  17.5 3.0 %copy-start.6 = (bf16[512,512]{1,0:T(8,128)(2,1)S(1)}, bf16[512,512]{1,0:T(8,128)(2,1)}, u32[]{:S(2)}) copy-start(bf16[512,512]{1,0:T(8,128)(2,1)} %w_out.3) | copy-start | bytes 1572868
  18.4 2.2 %copy-start.5 = (bf16[512,2048]{1,0:T(8,128)(2,1)S(1)}, bf16[512,2048]{1,0:T(8,128)(2,1)}, u32[]{:S(2)}) copy-start(bf16[512,2048]{1,0:T(8,128)(2,1)} %w_up.1) | copy-start | bytes 6291460
  26.6 4.6 %collective-permute-start.4 = (bf16[16,5,16,512]{3,2,1,0:T(8,128)(2,1)S(1)}, bf16[16,5,16,512]{3,2,1,0:T(8,128)(2,1)S(1)}, u32[]{:S(2)}, u32[]{:S(2)}) collective-permute-start(bf16[16,5,16,512]{3,2,1,0:T(8,128)(2,1)S(1)} %get-tuple-element.100), channel_id=1, source_target_pairs={{0,1},{1,0},{2,3},{3,2},{4,5},{5,4},{6,7},{7,6},{8,9},{9,8},{10,11... | collective-permute-start | bytes 3932168 | tf_op jit(solution)/shard_map/ppermute | solution.py:391
  26.7 4.5 %collective-permute-start.5 = (bf16[4,4,2,32,512]{4,3,2,1,0:T(8,128)(2,1)S(1)}, bf16[4,4,2,32,512]{4,3,2,1,0:T(8,128)(2,1)S(1)}, u32[]{:S(2)}, u32[]{:S(2)}) collective-permute-start(bf16[4,4,2,32,512]{4,3,2,1,0:T(8,128)(2,1)S(1)} %get-tuple-element.101), channel_id=1, source_target_pairs={{0,1},{1,0},{2,3},{3,2},{4,5},{5,4},{6,7},{7,6},{8,9},{9,8},{10,11... | collective-permute-start | bytes 3145736 | tf_op jit(solution)/shard_map/ppermute | solution.py:391
  31.2 3.1 %collective-permute-start.6 = (bf16[48,16,512]{2,1,0:T(8,128)(2,1)S(1)}, bf16[48,16,512]{2,1,0:T(8,128)(2,1)S(1)}, u32[]{:S(2)}, u32[]{:S(2)}) collective-permute-start(bf16[48,16,512]{2,1,0:T(8,128)(2,1)S(1)} %get-tuple-element.105), channel_id=1, source_target_pairs={{0,1},{1,0},{2,3},{3,2},{4,5},{5,4},{6,7},{7,6},{8,9},{9,8},{10,11... | collective-permute-start | bytes 2359304 | tf_op jit(solution)/shard_map/ppermute | solution.py:391
  33.1 1.3 %collective-permute-start.7 = (bf16[16,512]{1,0:T(8,128)(2,1)S(1)}, bf16[16,512]{1,0:T(8,128)(2,1)S(1)}, u32[]{:S(2)}, u32[]{:S(2)}) collective-permute-start(bf16[16,512]{1,0:T(8,128)(2,1)S(1)} %get-tuple-element.107.gk), channel_id=1, source_target_pairs={{0,1},{1,0},{2,3},{3,2},{4,5},{5,4},{6,7},{7,6},{8,9},{9,8},{10,11... | collective-permute-start | bytes 49160 | tf_op jit(solution)/shard_map/ppermute | solution.py:391
  34.7 12.2 %collective-permute-start.8 = (bf16[24,16,512]{2,1,0:T(8,128)(2,1)S(1)}, bf16[24,16,512]{2,1,0:T(8,128)(2,1)S(1)}, u32[]{:S(2)}, u32[]{:S(2)}) collective-permute-start(bf16[24,16,512]{2,1,0:T(8,128)(2,1)S(1)} %get-tuple-element.109), channel_id=1, source_target_pairs={{0,8},{1,9},{2,10},{3,11},{4,12},{5,13},{6,14},{7,15},{8,0},{9,1},... | collective-permute-start | bytes 1179656 | tf_op jit(solution)/shard_map/ppermute | solution.py:391
  34.8 12.1 %collective-permute-start.9 = (bf16[24,16,512]{2,1,0:T(8,128)(2,1)S(1)}, bf16[24,16,512]{2,1,0:T(8,128)(2,1)S(1)}, u32[]{:S(2)}, u32[]{:S(2)}) collective-permute-start(bf16[24,16,512]{2,1,0:T(8,128)(2,1)S(1)} %get-tuple-element.110), channel_id=1, source_target_pairs={{0,24},{1,25},{2,26},{3,27},{4,28},{5,29},{6,30},{7,31},{8,16},{9,... | collective-permute-start | bytes 1179656 | tf_op jit(solution)/shard_map/ppermute | solution.py:391
  37.7 17.6 %collective-permute-start.11 = (bf16[28,16,512]{2,1,0:T(8,128)(2,1)S(1)}, bf16[28,16,512]{2,1,0:T(8,128)(2,1)S(1)}, u32[]{:S(2)}, u32[]{:S(2)}) collective-permute-start(bf16[28,16,512]{2,1,0:T(8,128)(2,1)S(1)} %get-tuple-element.117), channel_id=1, source_target_pairs={{0,32},{1,33},{2,34},{3,35},{4,36},{5,37},{6,38},{7,39},{8,40},{9,... | collective-permute-start | bytes 1376264 | tf_op jit(solution)/shard_map/ppermute | solution.py:391
  37.8 17.5 %collective-permute-start.12 = (bf16[24,16,512]{2,1,0:T(8,128)(2,1)S(1)}, bf16[24,16,512]{2,1,0:T(8,128)(2,1)S(1)}, u32[]{:S(2)}, u32[]{:S(2)}) collective-permute-start(bf16[24,16,512]{2,1,0:T(8,128)(2,1)S(1)} %get-tuple-element.118), channel_id=1, source_target_pairs={{0,96},{1,97},{2,98},{3,99},{4,100},{5,101},{6,102},{7,103},{8,104... | collective-permute-start | bytes 1179656 | tf_op jit(solution)/shard_map/ppermute | solution.py:391
  46.3 0.7 collective-permute-start.10
  47.1 14.4 %collective-permute-start.18 = (bf16[12,16,512]{2,1,0:T(8,128)(2,1)S(1)}, bf16[12,16,512]{2,1,0:T(8,128)(2,1)S(1)}, u32[]{:S(2)}, u32[]{:S(2)}) collective-permute-start(bf16[12,16,512]{2,1,0:T(8,128)(2,1)S(1)} %get-tuple-element.133), channel_id=1, source_target_pairs={{0,24},{1,25},{2,26},{3,27},{4,28},{5,29},{6,30},{7,31},{8,16},{9,... | collective-permute-start | bytes 589832 | tf_op jit(solution)/shard_map/ppermute | solution.py:391
  48.6 12.9 %collective-permute-start.19 = (bf16[12,16,512]{2,1,0:T(8,128)(2,1)S(1)}, bf16[12,16,512]{2,1,0:T(8,128)(2,1)S(1)}, u32[]{:S(2)}, u32[]{:S(2)}) collective-permute-start(bf16[12,16,512]{2,1,0:T(8,128)(2,1)S(1)} %get-tuple-element.134), channel_id=1, source_target_pairs={{0,8},{1,9},{2,10},{3,11},{4,12},{5,13},{6,14},{7,15},{8,0},{9,1},... | collective-permute-start | bytes 589832 | tf_op jit(solution)/shard_map/ppermute | solution.py:391
  55.5 12.7 %collective-permute-start.13 = (bf16[13,16,512]{2,1,0:T(8,128)(2,1)S(1)}, bf16[13,16,512]{2,1,0:T(8,128)(2,1)S(1)}, u32[]{:S(2)}, u32[]{:S(2)}) collective-permute-start(bf16[13,16,512]{2,1,0:T(8,128)(2,1)S(1)} %get-tuple-element.121), channel_id=1, source_target_pairs={{0,96},{1,97},{2,98},{3,99},{4,100},{5,101},{6,102},{7,103},{8,104... | collective-permute-start | bytes 638984 | tf_op jit(solution)/shard_map/ppermute | solution.py:391
  61.5 6.7 %collective-permute-start.14 = (bf16[12,16,512]{2,1,0:T(8,128)(2,1)S(1)}, bf16[12,16,512]{2,1,0:T(8,128)(2,1)S(1)}, u32[]{:S(2)}, u32[]{:S(2)}) collective-permute-start(bf16[12,16,512]{2,1,0:T(8,128)(2,1)S(1)} %get-tuple-element.122), channel_id=1, source_target_pairs={{0,32},{1,33},{2,34},{3,35},{4,36},{5,37},{6,38},{7,39},{8,40},{9,... | collective-permute-start | bytes 589832 | tf_op jit(solution)/shard_map/ppermute | solution.py:391
  61.6 8.9 %collective-permute-start.20 = (bf16[6,16,512]{2,1,0:T(8,128)(2,1)S(1)}, bf16[6,16,512]{2,1,0:T(8,128)(2,1)S(1)}, u32[]{:S(2)}, u32[]{:S(2)}) collective-permute-start(bf16[6,16,512]{2,1,0:T(8,128)(2,1)S(1)} %get-tuple-element.138), channel_id=1, source_target_pairs={{0,32},{1,33},{2,34},{3,35},{4,36},{5,37},{6,38},{7,39},{8,40},{9,... | collective-permute-start | bytes 294920 | tf_op jit(solution)/shard_map/ppermute | solution.py:391
  63.7 8.9 %collective-permute-start.21 = (bf16[6,16,512]{2,1,0:T(8,128)(2,1)S(1)}, bf16[6,16,512]{2,1,0:T(8,128)(2,1)S(1)}, u32[]{:S(2)}, u32[]{:S(2)}) collective-permute-start(bf16[6,16,512]{2,1,0:T(8,128)(2,1)S(1)} %get-tuple-element.139), channel_id=1, source_target_pairs={{0,96},{1,97},{2,98},{3,99},{4,100},{5,101},{6,102},{7,103},{8,104... | collective-permute-start | bytes 294920 | tf_op jit(solution)/shard_map/ppermute | solution.py:391
  64.9 7.7 %collective-permute-start.22 = (bf16[6,16,512]{2,1,0:T(8,128)(2,1)S(1)}, bf16[6,16,512]{2,1,0:T(8,128)(2,1)S(1)}, u32[]{:S(2)}, u32[]{:S(2)}) collective-permute-start(bf16[6,16,512]{2,1,0:T(8,128)(2,1)S(1)} %get-tuple-element.140), channel_id=1, source_target_pairs={{0,64},{1,65},{2,66},{3,67},{4,68},{5,69},{6,70},{7,71},{8,72},{9,... | collective-permute-start | bytes 294920 | tf_op jit(solution)/shard_map/ppermute | solution.py:391
  68.3 4.9 %collective-permute-start.15 = (bf16[7,16,512]{2,1,0:T(8,128)(2,1)S(1)}, bf16[7,16,512]{2,1,0:T(8,128)(2,1)S(1)}, u32[]{:S(2)}, u32[]{:S(2)}) collective-permute-start(bf16[7,16,512]{2,1,0:T(8,128)(2,1)S(1)} %get-tuple-element.126), channel_id=1, source_target_pairs={{0,8},{1,9},{2,10},{3,11},{4,12},{5,13},{6,14},{7,15},{8,0},{9,1},... | collective-permute-start | bytes 344072 | tf_op jit(solution)/shard_map/ppermute | solution.py:391
  69.1 4.8 %collective-permute-start.16 = (bf16[7,16,512]{2,1,0:T(8,128)(2,1)S(1)}, bf16[7,16,512]{2,1,0:T(8,128)(2,1)S(1)}, u32[]{:S(2)}, u32[]{:S(2)}) collective-permute-start(bf16[7,16,512]{2,1,0:T(8,128)(2,1)S(1)} %get-tuple-element.127), channel_id=1, source_target_pairs={{0,24},{1,25},{2,26},{3,27},{4,28},{5,29},{6,30},{7,31},{8,16},{9,... | collective-permute-start | bytes 344072 | tf_op jit(solution)/shard_map/ppermute | solution.py:391
  70.5 6.3 %collective-permute-start.17 = (bf16[7,16,512]{2,1,0:T(8,128)(2,1)S(1)}, bf16[7,16,512]{2,1,0:T(8,128)(2,1)S(1)}, u32[]{:S(2)}, u32[]{:S(2)}) collective-permute-start(bf16[7,16,512]{2,1,0:T(8,128)(2,1)S(1)} %get-tuple-element.128), channel_id=1, source_target_pairs={{0,16},{1,17},{2,18},{3,19},{4,20},{5,21},{6,22},{7,23},{8,24},{9,... | collective-permute-start | bytes 344072 | tf_op jit(solution)/shard_map/ppermute | solution.py:391
  72.7 20.5 %slice-start = ((f32[2,512]{1,0:T(2,128)}), f32[1,512]{1,0:T(1,128)S(1)}, s32[]{:S(2)}) async-start(f32[2,512]{1,0:T(2,128)} %gains.3), calls=%async_computation.1 | async-start | bytes 4096 | tf_op jit(solution)/shard_map/slice | solution.py:527
  78.1 15.0 %all-to-all-start = ((bf16[8,112,128]{2,1,0:T(8,128)(2,1)}), bf16[8,112,128]{2,1,0:T(8,128)(2,1)S(1)}, u32[]{:S(2)}, u32[]{:S(2)}) async-start(bf16[8,112,128]{2,1,0:T(8,128)(2,1)} %shard_map.140), calls=%async_computation | async-start | bytes 458752 | tf_op jit(solution)/shard_map/all_to_all | solution.py:403
  83.1 9.6 %collective-permute-start.23 = (bf16[24,3,512]{2,1,0:T(4,128)(2,1)S(1)}, bf16[24,3,512]{2,1,0:T(4,128)(2,1)S(1)}, u32[]{:S(2)}, u32[]{:S(2)}) collective-permute-start(bf16[24,3,512]{2,1,0:T(4,128)(2,1)S(1)} %get-tuple-element.155), channel_id=1, source_target_pairs={{1,2},{2,1},{3,4},{4,3},{5,6},{6,5},{7,8},{8,7},{9,10},{10,9},{11,... | collective-permute-start | bytes 221192 | tf_op jit(solution)/shard_map/ppermute | solution.py:391
  85.0 7.7 %collective-permute-start.24 = (bf16[24,3,512]{2,1,0:T(4,128)(2,1)S(1)}, bf16[24,3,512]{2,1,0:T(4,128)(2,1)S(1)}, u32[]{:S(2)}, u32[]{:S(2)}) collective-permute-start(bf16[24,3,512]{2,1,0:T(4,128)(2,1)S(1)} %get-tuple-element.154), channel_id=1, source_target_pairs={{0,1},{1,0},{2,3},{3,2},{4,5},{5,4},{6,7},{7,6},{8,9},{9,8},{10,11... | collective-permute-start | bytes 221192 | tf_op jit(solution)/shard_map/ppermute | solution.py:391
  (3 other events, 3.5 us)

commit v12 on v11

--- a/solution.py
+++ b/solution.py
@@ -233,22 +233,23 @@
                 out[16 + j * 2 + i] = gk[at + j * 16 : at + j * 16 + 16, i * D : (i + 1) * D]
 
 
-def inputs_kernel(coord, dq, dkv, w_qkv, mid, rim_a, rim_b, tok, gain_mid, gne_o, gnq_o, gain_o, row_a, row_b):
+def inputs_kernel(coord, dq, dkv, w_qkv, mid, rim_a, rim_b, tok, gain_mid, gne_o, gnq_o, gain_o, row_a, row_b, gne_s):
     gne = nt(dkv[...], w_qkv[:, D:])
     gnq = nt(dq[...], w_qkv[:, :D])
-    gne_o[...] = gne[: (ROWS + 2 * RIM) * EC]
+    gne_s[...] = gne[: (ROWS + 2 * RIM) * EC]
+    gne_o[...] = gne[RIM * EC : (RIM + ROWS) * EC]
     gnq_o[...] = gnq
     gain_in = jnp.sum(gnq * unit_of(tok[...].astype(F32))[0], axis=0, keepdims=True)
     odd = coord[0] & 1
     for ref, at in ((rim_a, odd * (RIM + ROWS)), (mid, RIM), (rim_b, (1 - odd) * (RIM + ROWS))):
         size = ref.shape[0] * EC
         unit, _ = unit_of(ref[...].reshape(size, D).astype(F32))
-        part = gne_o[pl.ds(pl.multiple_of(at * EC, EC), size), :]
+        part = gne_s[pl.ds(pl.multiple_of(at * EC, EC), size), :]
         gain_in = gain_in + jnp.sum(part * unit, axis=0, keepdims=True)
     spread = jnp.concatenate([gain_in, gain_mid[...], jnp.zeros((14, D), F32)], axis=0).astype(BF16)
     gain_o[...] = spread
     for ref, at in ((row_a, odd * (RIM + ROWS)), (row_b, (1 - odd) * (RIM + ROWS))):
-        rim = gne_o[pl.ds(pl.multiple_of(at * EC, EC), RIM * EC), :]
+        rim = gne_s[pl.ds(pl.multiple_of(at * EC, EC), RIM * EC), :]
         ref[...] = rim.astype(BF16).reshape(RIM, EC, D)
 
 
@@ -461,10 +462,10 @@
     gne, gnq, gain, row_a, row_b = call(
         inputs_kernel,
         [
-            (((ROWS + 2 * RIM) * EC, D), F32), ((TOK, D), F32), ((16, D), BF16),
+            ((ROWS * EC, D), F32), ((TOK, D), F32), ((16, D), BF16),
             ((RIM, EC, D), BF16), ((RIM, EC, D), BF16),
         ],
-        [], 1, 8, 600_000_000, 4_000_000, 6,
+        [pltpu.VMEM(((ROWS + 2 * RIM) * EC, D), F32)], 1, 8, 600_000_000, 4_000_000, 6,
     )(coord, dq, dkv, w_qkv, mid, rim_a, rim_b, tok, gain_mid)
     gain_got = send(gain, CORE_SWAP)
 
@@ -502,25 +503,27 @@
     u_second = second((u_p, u_q), X_BIT)
     b_p, b_q, *b_own = join(second_kernel, [*b_first, *b_stay], [(12, 16, D)] * 4)
     b_second = second((b_p, b_q), Y_BIT)
-    gne = gne.reshape(ROWS + 2 * RIM, EC, D)[RIM : RIM + ROWS]
+    gne = gne.reshape(ROWS, EC, D)
     gne = gne + place(row_a, 0, row_odd, True, ROWS) + place(u_first[0][25:], 0, row_odd, False, ROWS)
     u = join(sum_up_q_kernel, [*u_second, *u_own], [(7, 16, D)] * 4)
     u = to_three(u, Y_BIT)
     b = join(sum_down_kv_kernel, [*b_second, *b_own], [(6, 16, D)] * 4)
     b = to_three(b, X_BIT)
+    to_a = gne[:, COLS : COLS + RIM].astype(BF16)
+    to_b = gne[:, COLS + RIM : COLS + 2 * RIM].astype(BF16)
+    u, b, gne, to_a, to_b = lax.optimization_barrier((u, b, gne, to_a, to_b))
     (spread,) = call(
         reduce_xy_kernel, [((8, ZROWS, 128), BF16)], [pltpu.VMEM((8 * ZROWS, 128), F32)], 0, 8, 60_000_000, 4_000_000, 5,
     )(*u, *b)
     got_z = exchange(spread, Z_GROUPS)
-    back_b = send(gne[:, COLS + RIM : COLS + 2 * RIM].astype(BF16), COL_B)
-    back_a = send(gne[:, COLS : COLS + RIM].astype(BF16), COL_A)
-    got_z, back_a, back_b = lax.optimization_barrier((got_z, back_a, back_b))
+    back_b, back_a = send(to_b, COL_B), send(to_a, COL_A)
     g_up, g_down, g_out, g_qkv, g_gains = call(
         reduce_z_kernel,
         [((32, 128), F32), ((32, 128), F32), ((8, 128), F32), ((24, 128), F32), ((2, D), F32)],
         [], 0, 1, 100_000_000_000, 400_000, 4,
     )(got_z)
 
+    g_gains, back_a, back_b = lax.optimization_barrier((g_gains, back_a, back_b))
     gn = gne[:, :COLS] + place(back_a, 1, col_odd, True, COLS) + place(back_b, 1, col_odd, False, COLS)
     gn = gn + gnq.reshape(ROWS, COLS, D)
     unit, inv = unit_of(tokens.astype(F32))

time: 96.2 us -> 95.9 us (level)
    ppermute x25, waiting for transfers between devices: 17 us -> 11.6 us  [send(): return lax.ppermute(x, AXES, perm)]
    all_to_all x1, waiting for transfers between devices: 0.47 us -> 5.8 us  [exchange(): return lax.all_to_all(x, AXES, 0, 0, axis_index_groups=groups, tiled=True)]
  transfers between devices with their start and end apart: 26 -> 26, of which waited for: 9 -> 10; matrix products, arithmetic and copies ran while one was open for 1% -> 1% of each run, Pallas kernels for 12% -> 12%
where the time goes in v12:
time: 95.9 us; the launch traced here: 95.2 us
  starting transfers between devices  52.9 us (55%)
  Pallas kernels  19.5 us (20%)
  waiting for transfers between devices  17.4 us (18%)
  other arithmetic  2.94 us (3%)
  local copies, waits for them, and re-layouts  1.41 us (1%)
  between operations  1.02 us (1%)
    ppermute x25, starting transfers between devices, send(): return lax.ppermute(x, AXES, perm)  48.2 us
    ppermute x25, waiting for transfers between devices, send(): return lax.ppermute(x, AXES, perm)  11.6 us
    pallas_call x1, Pallas kernels, per_device(): call(forward_kernel, [half_u, half_u, half_d, half_d, ((TOK, D), BF16), (...  6.02 us
    all_to_all x1, waiting for transfers between devices, exchange(): return lax.all_to_all(x, AXES, 0, 0, axis_index_groups=groups, tiled=True)  5.8 us
    all_to_all x1, starting transfers between devices, exchange(): return lax.all_to_all(x, AXES, 0, 0, axis_index_groups=groups, tiled=True)  4.78 us
    pallas_call x1, Pallas kernels, per_device(): call(backward_kernel, [half_k, half_k, ((TOK, D), BF16), ((EXT, 2 * D), B...  4.01 us
  transfers between devices with their start and end apart: 26, of which 10 were waited for; matrix products, arithmetic and copies ran while one was open for 1% of the time, Pallas kernels for 12%

profile of v12, /device:TPU:8, one launch (start us, length us, event | category | flops | bytes accessed | tf_op | source)
XLA Modules:
  0.0 95.2 jit_solution(16859670364981989597)
XLA Ops:
  0.6 1.2 %broadcast_select_fusion = (bf16[24,3,512]{2,1,0:T(4,128)(2,1)S(1)}, bf16[24,3,512]{2,1,0:T(4,128)(2,1)S(1)}) fusion(pred[]{:T(512)S(6)} %eq.6, bf16[24,8,512]{2,1,0:T(8,128)(2,1)} %param.8), kind=kLoop, calls=%fused_computation.14 | loop fusion | flops 73728 | bytes 294913 | tf_op jit(solution)/shard_map/jit(_where)/select_n | solution.py:417
  1.8 5.9 %collective-permute-start = (bf16[24,3,512]{2,1,0:T(4,128)(2,1)S(1)}, bf16[24,3,512]{2,1,0:T(4,128)(2,1)S(1)}, u32[]{:S(2)}, u32[]{:S(2)}) collective-permute-start(bf16[24,3,512]{2,1,0:T(4,128)(2,1)S(1)} %get-tuple-element.181), channel_id=1, source_target_pairs={{1,2},{2,1},{3,4},{4,3},{5,6},{6,5},{7,8},{8,7},{9,10},{10,9},{11,... | collective-permute-start | bytes 221192 | tf_op jit(solution)/shard_map/ppermute | solution.py:392
  8.6 1.2 %shard_map.127.bias = f32[3,64,256]{2,1,0:T(8,128)S(1)} custom-call(s32[3]{0:T(128)S(1)} %pad_add_fusion.coord, s32[3,1,49]{2,1,0:T(1,128)S(1)} %copy-done.7), custom_call_target="tpu_custom_call" | custom-call | flops 402653184 | bytes 4000000 | tf_op jit(solution)/shard_map/pallas_call | solution.py:419
  9.9 1.3 %collective-permute-done = bf16[24,3,512]{2,1,0:T(4,128)(2,1)S(1)} collective-permute-done((bf16[24,3,512]{2,1,0:T(4,128)(2,1)S(1)}, bf16[24,3,512]{2,1,0:T(4,128)(2,1)S(1)}, u32[]{:S(2)}, u32[]{:S(2)}) %collective-permute-start) | collective-permute-done | bytes 73760 | tf_op jit(solution)/shard_map/ppermute | solution.py:392
  12.1 4.3 %collective-permute-start.3 = (bf16[3,16,512]{2,1,0:T(8,128)(2,1)S(1)}, bf16[3,16,512]{2,1,0:T(8,128)(2,1)S(1)}, u32[]{:S(2)}, u32[]{:S(2)}) collective-permute-start(bf16[3,16,512]{2,1,0:T(8,128)(2,1)S(1)} %get-tuple-element.178), channel_id=1, source_target_pairs={{0,32},{1,33},{2,34},{3,35},{4,36},{5,37},{6,38},{7,39},{8,40},{9,... | collective-permute-start | bytes 147464 | tf_op jit(solution)/shard_map/ppermute | solution.py:392
  16.4 1.0 %shard_map.129 = (bf16[512,512]{1,0:T(8,128)(2,1)S(1)}, bf16[512,512]{1,0:T(8,128)(2,1)S(1)}) custom-call(s32[3]{0:T(128)S(1)} %pad_add_fusion.coord), custom_call_target="tpu_custom_call" | custom-call | flops 402653184 | bytes 4000000 | tf_op jit(solution)/shard_map/pallas_call | solution.py:426
  18.9 1.6 %shard_map.130 = (bf16[192,512]{1,0:T(8,128)(2,1)S(1)}, bf16[192,512]{1,0:T(8,128)(2,1)S(1)}, bf16[384,512]{1,0:T(8,128)(2,1)S(1)}, bf16[384,1024]{1,0:T(8,128)(...) custom-call(bf16[24,16,512]{2,1,0:T(8,128)(2,1)S(1)} %maximum_maximum_fusion.mid, ...), custom_call_target="tpu_custom_call" | custom-call | flops 600000000 | bytes 5000000 | tf_op jit(solution)/shard_map/pallas_call | solution.py:433
  20.6 6.0 %shard_map.131 = (bf16[16,5,16,512]{3,2,1,0:T(8,128)(2,1)S(1)}, bf16[16,5,16,512]{3,2,1,0:T(8,128)(2,1)S(1)}, bf16[4,4,2,32,512]{4,3,2,1,0:T(8,128)(2,1)S(1)}, b...) custom-call(s32[3]{0:T(128)S(1)} %pad_add_fusion.coord, ...), custom_call_target="tpu_custom_call" | custom-call | flops 4000000000 | bytes 20000000 | tf_op jit(solution)/shard_map/pallas_call | solution.py:444
  27.2 4.0 %shard_map.132 = (bf16[48,16,512]{2,1,0:T(8,128)(2,1)S(1)}, bf16[48,16,512]{2,1,0:T(8,128)(2,1)S(1)}, bf16[192,512]{1,0:T(8,128)(2,1)S(1)}, bf16[512,1024]{1,0:T(8,128)(2,1)S(1)}) custom-call(bf16[192,512]{1,0:T(8,128)(2,1)S(1)} %get-tuple-element.99.gm, bf16[512,512]{1,0:T(8,128)(2,1)S(1)} %copy-done.6, bf16[192,512]{1,0:T(8,128)(2,1)S(1)} %get-tuple-element.95.q_i.q, ...), custom_call_target="tpu_custom_call" | custom-call | flops 2500000000 | bytes 10000000 | tf_op jit(solution)/shard_map/pallas_call | solution.py:455
  31.6 1.5 %shard_map.133 = (f32[384,512]{1,0:T(8,128)S(1)}, f32[192,512]{1,0:T(8,128)S(1)}, bf16[16,512]{1,0:T(8,128)(2,1)S(1)}, bf16[3,16,512]{2,1,0:T(8,128)(2,1)S(1)}, bf16[3,16,512]{2,1,0:T(8,128)(2,1)S(1)}) custom-call(s32[3]{0:T(128)S(1)} %pad_add_fusion.coord, bf16[192,512]{1,0:T(8,128)(2,1)S(1)} %get-tuple-element.113.dq, ...), custom_call_target="tpu_custom_call" | custom-call | flops 600000000 | bytes 4000000 | tf_op jit(solution)/shard_map/pallas_call | solution.py:462
  33.4 1.0 collective-permute-done.7.gg
  35.3 2.5 %collective-permute-start.16 = (bf16[24,16,512]{2,1,0:T(8,128)(2,1)S(1)}, bf16[24,16,512]{2,1,0:T(8,128)(2,1)S(1)}, u32[]{:S(2)}, u32[]{:S(2)}) collective-permute-start(bf16[24,16,512]{2,1,0:T(8,128)(2,1)S(1)} %get-tuple-element.136), channel_id=1, source_target_pairs={{0,24},{1,25},{2,26},{3,27},{4,28},{5,29},{6,30},{7,31},{8,16},{9,... | collective-permute-start | bytes 1179656 | tf_op jit(solution)/shard_map/ppermute | solution.py:392
  37.8 8.5 %collective-permute-start.9 = (bf16[24,16,512]{2,1,0:T(8,128)(2,1)S(1)}, bf16[24,16,512]{2,1,0:T(8,128)(2,1)S(1)}, u32[]{:S(2)}, u32[]{:S(2)}) collective-permute-start(bf16[24,16,512]{2,1,0:T(8,128)(2,1)S(1)} %get-tuple-element.122), channel_id=1, source_target_pairs={{0,96},{1,97},{2,98},{3,99},{4,100},{5,101},{6,102},{7,103},{8,104... | collective-permute-start | bytes 1179656 | tf_op jit(solution)/shard_map/ppermute | solution.py:392
  47.2 1.8 %collective-permute-start.18 = (bf16[12,16,512]{2,1,0:T(8,128)(2,1)S(1)}, bf16[12,16,512]{2,1,0:T(8,128)(2,1)S(1)}, u32[]{:S(2)}, u32[]{:S(2)}) collective-permute-start(bf16[12,16,512]{2,1,0:T(8,128)(2,1)S(1)} %get-tuple-element.142), channel_id=1, source_target_pairs={{0,24},{1,25},{2,26},{3,27},{4,28},{5,29},{6,30},{7,31},{8,16},{9,... | collective-permute-start | bytes 589832 | tf_op jit(solution)/shard_map/ppermute | solution.py:392
  49.1 2.9 %collective-permute-start.19 = (bf16[12,16,512]{2,1,0:T(8,128)(2,1)S(1)}, bf16[12,16,512]{2,1,0:T(8,128)(2,1)S(1)}, u32[]{:S(2)}, u32[]{:S(2)}) collective-permute-start(bf16[12,16,512]{2,1,0:T(8,128)(2,1)S(1)} %get-tuple-element.143), channel_id=1, source_target_pairs={{0,8},{1,9},{2,10},{3,11},{4,12},{5,13},{6,14},{7,15},{8,0},{9,1},... | collective-permute-start | bytes 589832 | tf_op jit(solution)/shard_map/ppermute | solution.py:392
  52.0 3.3 %collective-permute-done.9.q_got = bf16[24,16,512]{2,1,0:T(8,128)(2,1)S(1)} collective-permute-done((bf16[24,16,512]{2,1,0:T(8,128)(2,1)S(1)}, bf16[24,16,512]{2,1,0:T(8,128)(2,1)S(1)}, u32[]{:S(2)}, u32[]{:S(2)}) %collective-permute-start.9) | collective-permute-done | bytes 393248 | tf_op jit(solution)/shard_map/ppermute | solution.py:392
  55.5 5.8 %collective-permute-start.10 = (bf16[13,16,512]{2,1,0:T(8,128)(2,1)S(1)}, bf16[13,16,512]{2,1,0:T(8,128)(2,1)S(1)}, u32[]{:S(2)}, u32[]{:S(2)}) collective-permute-start(bf16[13,16,512]{2,1,0:T(8,128)(2,1)S(1)} %get-tuple-element.125), channel_id=1, source_target_pairs={{0,96},{1,97},{2,98},{3,99},{4,100},{5,101},{6,102},{7,103},{8,104... | collective-permute-start | bytes 638984 | tf_op jit(solution)/shard_map/ppermute | solution.py:392
  61.5 2.1 %collective-permute-start.20 = (bf16[6,16,512]{2,1,0:T(8,128)(2,1)S(1)}, bf16[6,16,512]{2,1,0:T(8,128)(2,1)S(1)}, u32[]{:S(2)}, u32[]{:S(2)}) collective-permute-start(bf16[6,16,512]{2,1,0:T(8,128)(2,1)S(1)} %get-tuple-element.147), channel_id=1, source_target_pairs={{0,32},{1,33},{2,34},{3,35},{4,36},{5,37},{6,38},{7,39},{8,40},{9,... | collective-permute-start | bytes 294920 | tf_op jit(solution)/shard_map/ppermute | solution.py:392
  63.7 1.4 %collective-permute-start.21 = (bf16[6,16,512]{2,1,0:T(8,128)(2,1)S(1)}, bf16[6,16,512]{2,1,0:T(8,128)(2,1)S(1)}, u32[]{:S(2)}, u32[]{:S(2)}) collective-permute-start(bf16[6,16,512]{2,1,0:T(8,128)(2,1)S(1)} %get-tuple-element.148), channel_id=1, source_target_pairs={{0,96},{1,97},{2,98},{3,99},{4,100},{5,101},{6,102},{7,103},{8,104... | collective-permute-start | bytes 294920 | tf_op jit(solution)/shard_map/ppermute | solution.py:392
  65.1 1.8 %collective-permute-start.22 = (bf16[6,16,512]{2,1,0:T(8,128)(2,1)S(1)}, bf16[6,16,512]{2,1,0:T(8,128)(2,1)S(1)}, u32[]{:S(2)}, u32[]{:S(2)}) collective-permute-start(bf16[6,16,512]{2,1,0:T(8,128)(2,1)S(1)} %get-tuple-element.149), channel_id=1, source_target_pairs={{0,64},{1,65},{2,66},{3,67},{4,68},{5,69},{6,70},{7,71},{8,72},{9,... | collective-permute-start | bytes 294920 | tf_op jit(solution)/shard_map/ppermute | solution.py:392
  66.9 1.2 %collective-permute-done.11.q_got = bf16[12,16,512]{2,1,0:T(8,128)(2,1)S(1)} collective-permute-done((bf16[12,16,512]{2,1,0:T(8,128)(2,1)S(1)}, bf16[12,16,512]{2,1,0:T(8,128)(2,1)S(1)}, u32[]{:S(2)}, u32[]{:S(2)}) %collective-permute-start.11) | collective-permute-done | bytes 196640 | tf_op jit(solution)/shard_map/ppermute | solution.py:392
  68.1 1.1 %collective-permute-start.12 = (bf16[7,16,512]{2,1,0:T(8,128)(2,1)S(1)}, bf16[7,16,512]{2,1,0:T(8,128)(2,1)S(1)}, u32[]{:S(2)}, u32[]{:S(2)}) collective-permute-start(bf16[7,16,512]{2,1,0:T(8,128)(2,1)S(1)} %get-tuple-element.130), channel_id=1, source_target_pairs={{0,8},{1,9},{2,10},{3,11},{4,12},{5,13},{6,14},{7,15},{8,0},{9,1},... | collective-permute-start | bytes 344072 | tf_op jit(solution)/shard_map/ppermute | solution.py:392
  69.2 1.4 %collective-permute-start.13 = (bf16[7,16,512]{2,1,0:T(8,128)(2,1)S(1)}, bf16[7,16,512]{2,1,0:T(8,128)(2,1)S(1)}, u32[]{:S(2)}, u32[]{:S(2)}) collective-permute-start(bf16[7,16,512]{2,1,0:T(8,128)(2,1)S(1)} %get-tuple-element.131), channel_id=1, source_target_pairs={{0,24},{1,25},{2,26},{3,27},{4,28},{5,29},{6,30},{7,31},{8,16},{9,... | collective-permute-start | bytes 344072 | tf_op jit(solution)/shard_map/ppermute | solution.py:392
  70.7 1.7 %collective-permute-start.14 = (bf16[7,16,512]{2,1,0:T(8,128)(2,1)S(1)}, bf16[7,16,512]{2,1,0:T(8,128)(2,1)S(1)}, u32[]{:S(2)}, u32[]{:S(2)}) collective-permute-start(bf16[7,16,512]{2,1,0:T(8,128)(2,1)S(1)} %get-tuple-element.132), channel_id=1, source_target_pairs={{0,16},{1,17},{2,18},{3,19},{4,20},{5,21},{6,22},{7,23},{8,24},{9,... | collective-permute-start | bytes 344072 | tf_op jit(solution)/shard_map/ppermute | solution.py:392
  73.0 1.0 %collective-permute-done.13.refs_2_ = bf16[7,16,512]{2,1,0:T(8,128)(2,1)S(1)} collective-permute-done((bf16[7,16,512]{2,1,0:T(8,128)(2,1)S(1)}, bf16[7,16,512]{2,1,0:T(8,128)(2,1)S(1)}, u32[]{:S(2)}, u32[]{:S(2)}) %collective-permute-start.13) | collective-permute-done | bytes 114720 | tf_op jit(solution)/shard_map/ppermute | solution.py:392
  74.0 2.9 %collective-permute-done.14.refs_3_ = bf16[7,16,512]{2,1,0:T(8,128)(2,1)S(1)} collective-permute-done((bf16[7,16,512]{2,1,0:T(8,128)(2,1)S(1)}, bf16[7,16,512]{2,1,0:T(8,128)(2,1)S(1)}, u32[]{:S(2)}, u32[]{:S(2)}) %collective-permute-start.14) | collective-permute-done | bytes 114720 | tf_op jit(solution)/shard_map/ppermute | solution.py:392
  77.0 1.3 %shard_map.140 = bf16[8,112,128]{2,1,0:T(8,128)(2,1)} custom-call(bf16[7,16,512]{2,1,0:T(8,128)(2,1)S(1)} %get-tuple-element.153.refs_0_, bf16[7,16,512]{2,1,0:T(8,128)(2,1)S(1)} %collective-permute-done.12.refs_1_, bf16[7,16,512]{2,1,0:T(8,128)(2,1)S(1)} %collective-permute-done.13.refs_2_, bf16[7,16,512]{2,1,0:T(8,128)(2,1)S(1)} %collective-permute-done.14.refs_3_, ...), custom_call_target="tpu_custom_call" | custom-call | flops 60000000 | bytes 4000000 | tf_op jit(solution)/shard_map/pallas_call | solution.py:515
  78.3 4.8 %all-to-all-start = ((bf16[8,112,128]{2,1,0:T(8,128)(2,1)}), bf16[8,112,128]{2,1,0:T(8,128)(2,1)S(1)}, u32[]{:S(2)}, u32[]{:S(2)}) async-start(bf16[8,112,128]{2,1,0:T(8,128)(2,1)} %shard_map.140), calls=%async_computation | async-start | bytes 458752 | tf_op jit(solution)/shard_map/all_to_all | solution.py:404
  83.2 1.9 %collective-permute-start.23 = (bf16[24,3,512]{2,1,0:T(4,128)(2,1)S(1)}, bf16[24,3,512]{2,1,0:T(4,128)(2,1)S(1)}, u32[]{:S(2)}, u32[]{:S(2)}) collective-permute-start(bf16[24,3,512]{2,1,0:T(4,128)(2,1)S(1)} %get-tuple-element.162), channel_id=1, source_target_pairs={{1,2},{2,1},{3,4},{4,3},{5,6},{6,5},{7,8},{8,7},{9,10},{10,9},{11,... | collective-permute-start | bytes 221192 | tf_op jit(solution)/shard_map/ppermute | solution.py:392
  85.1 2.2 %collective-permute-start.24 = (bf16[24,3,512]{2,1,0:T(4,128)(2,1)S(1)}, bf16[24,3,512]{2,1,0:T(4,128)(2,1)S(1)}, u32[]{:S(2)}, u32[]{:S(2)}) collective-permute-start(bf16[24,3,512]{2,1,0:T(4,128)(2,1)S(1)} %get-tuple-element.163), channel_id=1, source_target_pairs={{0,1},{1,0},{2,3},{3,2},{4,5},{5,4},{6,7},{7,6},{8,9},{9,8},{10,11... | collective-permute-start | bytes 221192 | tf_op jit(solution)/shard_map/ppermute | solution.py:392
  87.3 5.8 %all-to-all-done.got = bf16[8,112,128]{2,1,0:T(8,128)(2,1)S(1)} async-done(((bf16[8,112,128]{2,1,0:T(8,128)(2,1)}), bf16[8,112,128]{2,1,0:T(8,128)(2,1)S(1)}, u32[]{:S(2)}, u32[]{:S(2)}) %all-to-all-start) | async-done | bytes 229408 | tf_op jit(solution)/shard_map/all_to_all | solution.py:404
  94.3 0.9 fusion.6
  (70 shorter events, 8.9 us)
Async XLA Ops:
  0.6 10.6 %copy-start = (bf16[24,8,512]{2,1,0:T(8,128)(2,1)S(1)}, bf16[24,8,512]{2,1,0:T(8,128)(2,1)}, u32[]{:S(2)}) copy-start(bf16[24,8,512]{2,1,0:T(8,128)(2,1)} %param.8) | copy-start | bytes 589828
  1.8 9.4 %collective-permute-start = (bf16[24,3,512]{2,1,0:T(4,128)(2,1)S(1)}, bf16[24,3,512]{2,1,0:T(4,128)(2,1)S(1)}, u32[]{:S(2)}, u32[]{:S(2)}) collective-permute-start(bf16[24,3,512]{2,1,0:T(4,128)(2,1)S(1)} %get-tuple-element.181), channel_id=1, source_target_pairs={{1,2},{2,1},{3,4},{4,3},{5,6},{6,5},{7,8},{8,7},{9,10},{10,9},{11,... | collective-permute-start | bytes 221192 | tf_op jit(solution)/shard_map/ppermute | solution.py:392
  7.7 3.5 %collective-permute-start.1 = (bf16[24,3,512]{2,1,0:T(4,128)(2,1)S(1)}, bf16[24,3,512]{2,1,0:T(4,128)(2,1)S(1)}, u32[]{:S(2)}, u32[]{:S(2)}) collective-permute-start(bf16[24,3,512]{2,1,0:T(4,128)(2,1)S(1)} %get-tuple-element.180), channel_id=1, source_target_pairs={{0,1},{1,0},{2,3},{3,2},{4,5},{5,4},{6,7},{7,6},{8,9},{9,8},{10,11... | collective-permute-start | bytes 221192 | tf_op jit(solution)/shard_map/ppermute | solution.py:392
  9.9 7.6 %copy-start.2 = (bf16[2048,512]{1,0:T(8,128)(2,1)S(1)}, bf16[2048,512]{1,0:T(8,128)(2,1)}, u32[]{:S(2)}) copy-start(bf16[2048,512]{1,0:T(8,128)(2,1)} %w_down.1) | copy-start | bytes 6291460
  9.9 7.6 %copy-start.3 = (bf16[24,8,512]{2,1,0:T(8,128)(2,1)S(1)}, bf16[24,8,512]{2,1,0:T(8,128)(2,1)}, u32[]{:S(2)}) copy-start(bf16[24,8,512]{2,1,0:T(8,128)(2,1)} %param.9) | copy-start | bytes 589828
  11.4 9.1 %collective-permute-start.2 = (bf16[3,16,512]{2,1,0:T(8,128)(2,1)S(1)}, bf16[3,16,512]{2,1,0:T(8,128)(2,1)S(1)}, u32[]{:S(2)}, u32[]{:S(2)}) collective-permute-start(bf16[3,16,512]{2,1,0:T(8,128)(2,1)S(1)} %get-tuple-element.179), channel_id=1, source_target_pairs={{32,64},{33,65},{34,66},{35,67},{36,68},{37,69},{38,70},{39,71},{4... | collective-permute-start | bytes 147464 | tf_op jit(solution)/shard_map/ppermute | solution.py:392
  12.1 8.4 %collective-permute-start.3 = (bf16[3,16,512]{2,1,0:T(8,128)(2,1)S(1)}, bf16[3,16,512]{2,1,0:T(8,128)(2,1)S(1)}, u32[]{:S(2)}, u32[]{:S(2)}) collective-permute-start(bf16[3,16,512]{2,1,0:T(8,128)(2,1)S(1)} %get-tuple-element.178), channel_id=1, source_target_pairs={{0,32},{1,33},{2,34},{3,35},{4,36},{5,37},{6,38},{7,39},{8,40},{9,... | collective-permute-start | bytes 147464 | tf_op jit(solution)/shard_map/ppermute | solution.py:392
  17.5 3.0 %copy-start.6 = (bf16[512,512]{1,0:T(8,128)(2,1)S(1)}, bf16[512,512]{1,0:T(8,128)(2,1)}, u32[]{:S(2)}) copy-start(bf16[512,512]{1,0:T(8,128)(2,1)} %w_out.3) | copy-start | bytes 1572868
  18.4 2.2 %copy-start.5 = (bf16[512,2048]{1,0:T(8,128)(2,1)S(1)}, bf16[512,2048]{1,0:T(8,128)(2,1)}, u32[]{:S(2)}) copy-start(bf16[512,2048]{1,0:T(8,128)(2,1)} %w_up.1) | copy-start | bytes 6291460
  26.6 4.6 %collective-permute-start.4 = (bf16[16,5,16,512]{3,2,1,0:T(8,128)(2,1)S(1)}, bf16[16,5,16,512]{3,2,1,0:T(8,128)(2,1)S(1)}, u32[]{:S(2)}, u32[]{:S(2)}) collective-permute-start(bf16[16,5,16,512]{3,2,1,0:T(8,128)(2,1)S(1)} %get-tuple-element.101), channel_id=1, source_target_pairs={{0,1},{1,0},{2,3},{3,2},{4,5},{5,4},{6,7},{7,6},{8,9},{9,8},{10,11... | collective-permute-start | bytes 3932168 | tf_op jit(solution)/shard_map/ppermute | solution.py:392
  26.7 4.5 %collective-permute-start.5 = (bf16[4,4,2,32,512]{4,3,2,1,0:T(8,128)(2,1)S(1)}, bf16[4,4,2,32,512]{4,3,2,1,0:T(8,128)(2,1)S(1)}, u32[]{:S(2)}, u32[]{:S(2)}) collective-permute-start(bf16[4,4,2,32,512]{4,3,2,1,0:T(8,128)(2,1)S(1)} %get-tuple-element.102), channel_id=1, source_target_pairs={{0,1},{1,0},{2,3},{3,2},{4,5},{5,4},{6,7},{7,6},{8,9},{9,8},{10,11... | collective-permute-start | bytes 3145736 | tf_op jit(solution)/shard_map/ppermute | solution.py:392
  31.2 3.1 %collective-permute-start.6 = (bf16[48,16,512]{2,1,0:T(8,128)(2,1)S(1)}, bf16[48,16,512]{2,1,0:T(8,128)(2,1)S(1)}, u32[]{:S(2)}, u32[]{:S(2)}) collective-permute-start(bf16[48,16,512]{2,1,0:T(8,128)(2,1)S(1)} %get-tuple-element.112), channel_id=1, source_target_pairs={{0,1},{1,0},{2,3},{3,2},{4,5},{5,4},{6,7},{7,6},{8,9},{9,8},{10,11... | collective-permute-start | bytes 2359304 | tf_op jit(solution)/shard_map/ppermute | solution.py:392
  33.1 1.3 %collective-permute-start.7 = (bf16[16,512]{1,0:T(8,128)(2,1)S(1)}, bf16[16,512]{1,0:T(8,128)(2,1)S(1)}, u32[]{:S(2)}, u32[]{:S(2)}) collective-permute-start(bf16[16,512]{1,0:T(8,128)(2,1)S(1)} %get-tuple-element.117.gk), channel_id=1, source_target_pairs={{0,1},{1,0},{2,3},{3,2},{4,5},{5,4},{6,7},{7,6},{8,9},{9,8},{10,11... | collective-permute-start | bytes 49160 | tf_op jit(solution)/shard_map/ppermute | solution.py:392
  34.7 20.6 %collective-permute-start.8 = (bf16[28,16,512]{2,1,0:T(8,128)(2,1)S(1)}, bf16[28,16,512]{2,1,0:T(8,128)(2,1)S(1)}, u32[]{:S(2)}, u32[]{:S(2)}) collective-permute-start(bf16[28,16,512]{2,1,0:T(8,128)(2,1)S(1)} %get-tuple-element.121), channel_id=1, source_target_pairs={{0,32},{1,33},{2,34},{3,35},{4,36},{5,37},{6,38},{7,39},{8,40},{9,... | collective-permute-start | bytes 1376264 | tf_op jit(solution)/shard_map/ppermute | solution.py:392
  35.2 11.7 %collective-permute-start.15 = (bf16[24,16,512]{2,1,0:T(8,128)(2,1)S(1)}, bf16[24,16,512]{2,1,0:T(8,128)(2,1)S(1)}, u32[]{:S(2)}, u32[]{:S(2)}) collective-permute-start(bf16[24,16,512]{2,1,0:T(8,128)(2,1)S(1)} %get-tuple-element.135), channel_id=1, source_target_pairs={{0,8},{1,9},{2,10},{3,11},{4,12},{5,13},{6,14},{7,15},{8,0},{9,1},... | collective-permute-start | bytes 1179656 | tf_op jit(solution)/shard_map/ppermute | solution.py:392
  35.3 11.7 %collective-permute-start.16 = (bf16[24,16,512]{2,1,0:T(8,128)(2,1)S(1)}, bf16[24,16,512]{2,1,0:T(8,128)(2,1)S(1)}, u32[]{:S(2)}, u32[]{:S(2)}) collective-permute-start(bf16[24,16,512]{2,1,0:T(8,128)(2,1)S(1)} %get-tuple-element.136), channel_id=1, source_target_pairs={{0,24},{1,25},{2,26},{3,27},{4,28},{5,29},{6,30},{7,31},{8,16},{9,... | collective-permute-start | bytes 1179656 | tf_op jit(solution)/shard_map/ppermute | solution.py:392
  37.8 17.5 %collective-permute-start.9 = (bf16[24,16,512]{2,1,0:T(8,128)(2,1)S(1)}, bf16[24,16,512]{2,1,0:T(8,128)(2,1)S(1)}, u32[]{:S(2)}, u32[]{:S(2)}) collective-permute-start(bf16[24,16,512]{2,1,0:T(8,128)(2,1)S(1)} %get-tuple-element.122), channel_id=1, source_target_pairs={{0,96},{1,97},{2,98},{3,99},{4,100},{5,101},{6,102},{7,103},{8,104... | collective-permute-start | bytes 1179656 | tf_op jit(solution)/shard_map/ppermute | solution.py:392
  46.3 0.7 collective-permute-start.17
  47.2 14.1 %collective-permute-start.18 = (bf16[12,16,512]{2,1,0:T(8,128)(2,1)S(1)}, bf16[12,16,512]{2,1,0:T(8,128)(2,1)S(1)}, u32[]{:S(2)}, u32[]{:S(2)}) collective-permute-start(bf16[12,16,512]{2,1,0:T(8,128)(2,1)S(1)} %get-tuple-element.142), channel_id=1, source_target_pairs={{0,24},{1,25},{2,26},{3,27},{4,28},{5,29},{6,30},{7,31},{8,16},{9,... | collective-permute-start | bytes 589832 | tf_op jit(solution)/shard_map/ppermute | solution.py:392
  49.1 12.3 %collective-permute-start.19 = (bf16[12,16,512]{2,1,0:T(8,128)(2,1)S(1)}, bf16[12,16,512]{2,1,0:T(8,128)(2,1)S(1)}, u32[]{:S(2)}, u32[]{:S(2)}) collective-permute-start(bf16[12,16,512]{2,1,0:T(8,128)(2,1)S(1)} %get-tuple-element.143), channel_id=1, source_target_pairs={{0,8},{1,9},{2,10},{3,11},{4,12},{5,13},{6,14},{7,15},{8,0},{9,1},... | collective-permute-start | bytes 589832 | tf_op jit(solution)/shard_map/ppermute | solution.py:392
  55.5 12.6 %collective-permute-start.10 = (bf16[13,16,512]{2,1,0:T(8,128)(2,1)S(1)}, bf16[13,16,512]{2,1,0:T(8,128)(2,1)S(1)}, u32[]{:S(2)}, u32[]{:S(2)}) collective-permute-start(bf16[13,16,512]{2,1,0:T(8,128)(2,1)S(1)} %get-tuple-element.125), channel_id=1, source_target_pairs={{0,96},{1,97},{2,98},{3,99},{4,100},{5,101},{6,102},{7,103},{8,104... | collective-permute-start | bytes 638984 | tf_op jit(solution)/shard_map/ppermute | solution.py:392
  61.3 6.7 %collective-permute-start.11 = (bf16[12,16,512]{2,1,0:T(8,128)(2,1)S(1)}, bf16[12,16,512]{2,1,0:T(8,128)(2,1)S(1)}, u32[]{:S(2)}, u32[]{:S(2)}) collective-permute-start(bf16[12,16,512]{2,1,0:T(8,128)(2,1)S(1)} %get-tuple-element.126), channel_id=1, source_target_pairs={{0,32},{1,33},{2,34},{3,35},{4,36},{5,37},{6,38},{7,39},{8,40},{9,... | collective-permute-start | bytes 589832 | tf_op jit(solution)/shard_map/ppermute | solution.py:392
  61.5 9.2 %collective-permute-start.20 = (bf16[6,16,512]{2,1,0:T(8,128)(2,1)S(1)}, bf16[6,16,512]{2,1,0:T(8,128)(2,1)S(1)}, u32[]{:S(2)}, u32[]{:S(2)}) collective-permute-start(bf16[6,16,512]{2,1,0:T(8,128)(2,1)S(1)} %get-tuple-element.147), channel_id=1, source_target_pairs={{0,32},{1,33},{2,34},{3,35},{4,36},{5,37},{6,38},{7,39},{8,40},{9,... | collective-permute-start | bytes 294920 | tf_op jit(solution)/shard_map/ppermute | solution.py:392
  63.7 8.7 %collective-permute-start.21 = (bf16[6,16,512]{2,1,0:T(8,128)(2,1)S(1)}, bf16[6,16,512]{2,1,0:T(8,128)(2,1)S(1)}, u32[]{:S(2)}, u32[]{:S(2)}) collective-permute-start(bf16[6,16,512]{2,1,0:T(8,128)(2,1)S(1)} %get-tuple-element.148), channel_id=1, source_target_pairs={{0,96},{1,97},{2,98},{3,99},{4,100},{5,101},{6,102},{7,103},{8,104... | collective-permute-start | bytes 294920 | tf_op jit(solution)/shard_map/ppermute | solution.py:392
  65.1 7.3 %collective-permute-start.22 = (bf16[6,16,512]{2,1,0:T(8,128)(2,1)S(1)}, bf16[6,16,512]{2,1,0:T(8,128)(2,1)S(1)}, u32[]{:S(2)}, u32[]{:S(2)}) collective-permute-start(bf16[6,16,512]{2,1,0:T(8,128)(2,1)S(1)} %get-tuple-element.149), channel_id=1, source_target_pairs={{0,64},{1,65},{2,66},{3,67},{4,68},{5,69},{6,70},{7,71},{8,72},{9,... | collective-permute-start | bytes 294920 | tf_op jit(solution)/shard_map/ppermute | solution.py:392
  68.1 4.9 %collective-permute-start.12 = (bf16[7,16,512]{2,1,0:T(8,128)(2,1)S(1)}, bf16[7,16,512]{2,1,0:T(8,128)(2,1)S(1)}, u32[]{:S(2)}, u32[]{:S(2)}) collective-permute-start(bf16[7,16,512]{2,1,0:T(8,128)(2,1)S(1)} %get-tuple-element.130), channel_id=1, source_target_pairs={{0,8},{1,9},{2,10},{3,11},{4,12},{5,13},{6,14},{7,15},{8,0},{9,1},... | collective-permute-start | bytes 344072 | tf_op jit(solution)/shard_map/ppermute | solution.py:392
  69.2 4.8 %collective-permute-start.13 = (bf16[7,16,512]{2,1,0:T(8,128)(2,1)S(1)}, bf16[7,16,512]{2,1,0:T(8,128)(2,1)S(1)}, u32[]{:S(2)}, u32[]{:S(2)}) collective-permute-start(bf16[7,16,512]{2,1,0:T(8,128)(2,1)S(1)} %get-tuple-element.131), channel_id=1, source_target_pairs={{0,24},{1,25},{2,26},{3,27},{4,28},{5,29},{6,30},{7,31},{8,16},{9,... | collective-permute-start | bytes 344072 | tf_op jit(solution)/shard_map/ppermute | solution.py:392
  70.7 6.3 %collective-permute-start.14 = (bf16[7,16,512]{2,1,0:T(8,128)(2,1)S(1)}, bf16[7,16,512]{2,1,0:T(8,128)(2,1)S(1)}, u32[]{:S(2)}, u32[]{:S(2)}) collective-permute-start(bf16[7,16,512]{2,1,0:T(8,128)(2,1)S(1)} %get-tuple-element.132), channel_id=1, source_target_pairs={{0,16},{1,17},{2,18},{3,19},{4,20},{5,21},{6,22},{7,23},{8,24},{9,... | collective-permute-start | bytes 344072 | tf_op jit(solution)/shard_map/ppermute | solution.py:392
  78.3 14.9 %all-to-all-start = ((bf16[8,112,128]{2,1,0:T(8,128)(2,1)}), bf16[8,112,128]{2,1,0:T(8,128)(2,1)S(1)}, u32[]{:S(2)}, u32[]{:S(2)}) async-start(bf16[8,112,128]{2,1,0:T(8,128)(2,1)} %shard_map.140), calls=%async_computation | async-start | bytes 458752 | tf_op jit(solution)/shard_map/all_to_all | solution.py:404
  83.2 10.8 %slice-start = ((f32[2,512]{1,0:T(2,128)}), f32[1,512]{1,0:T(1,128)S(1)}, s32[]{:S(2)}) async-start(f32[2,512]{1,0:T(2,128)} %gains.3), calls=%async_computation.1 | async-start | bytes 4096 | tf_op jit(solution)/shard_map/slice | solution.py:530
  83.2 10.7 %collective-permute-start.23 = (bf16[24,3,512]{2,1,0:T(4,128)(2,1)S(1)}, bf16[24,3,512]{2,1,0:T(4,128)(2,1)S(1)}, u32[]{:S(2)}, u32[]{:S(2)}) collective-permute-start(bf16[24,3,512]{2,1,0:T(4,128)(2,1)S(1)} %get-tuple-element.162), channel_id=1, source_target_pairs={{1,2},{2,1},{3,4},{4,3},{5,6},{6,5},{7,8},{8,7},{9,10},{10,9},{11,... | collective-permute-start | bytes 221192 | tf_op jit(solution)/shard_map/ppermute | solution.py:392
  85.1 8.8 %collective-permute-start.24 = (bf16[24,3,512]{2,1,0:T(4,128)(2,1)S(1)}, bf16[24,3,512]{2,1,0:T(4,128)(2,1)S(1)}, u32[]{:S(2)}, u32[]{:S(2)}) collective-permute-start(bf16[24,3,512]{2,1,0:T(4,128)(2,1)S(1)} %get-tuple-element.163), channel_id=1, source_target_pairs={{0,1},{1,0},{2,3},{3,2},{4,5},{5,4},{6,7},{7,6},{8,9},{9,8},{10,11... | collective-permute-start | bytes 221192 | tf_op jit(solution)/shard_map/ppermute | solution.py:392
  (3 other events, 3.5 us)

commit v13 on v12

--- a/solution.py
+++ b/solution.py
@@ -397,7 +397,8 @@
 
 
 def to_three(chunks, bit):
-    return [chunks[0]] + [send(chunks[d], by(bit * d)) for d in (1, 3, 2)]
+    got = {d: send(chunks[d], by(bit * d)) for d in (2, 1, 3)}
+    return [chunks[0], got[2], got[1], got[3]]
 
 
 def exchange(x, groups):
@@ -487,16 +488,17 @@
     def second(sent, bit):
         return send(sent[0], by(3 * bit)), send(sent[1], by(bit))
 
-    k_got, gnq, gain_got = lax.optimization_barrier((k_got, gnq, gain_got))
+    k_got, gnq = lax.optimization_barrier((k_got, gnq))
+    b_p, b_q, *b_stay = join(
+        join_down_kv_kernel, [d_keep.reshape(64, 16, D), d_got.reshape(64, 16, D), k_keep, k_got], [(24, 16, D)] * 4,
+    )
+    b_p, b_q, gain_got = lax.optimization_barrier((b_p, b_q, gain_got))
+    b_first = first((b_p, b_q), Y_BIT)
     u_p, u_q, *u_stay = join(
         join_up_q_kernel, [u_keep.reshape(80, 16, D), u_got.reshape(80, 16, D), k_keep, k_got, gain, gain_got, row_b],
         [(28, 16, D), (24, 16, D), (25, 16, D), (24, 16, D)],
     )
     u_first = first((u_p, u_q), X_BIT)
-    b_p, b_q, *b_stay = join(
-        join_down_kv_kernel, [d_keep.reshape(64, 16, D), d_got.reshape(64, 16, D), k_keep, k_got], [(24, 16, D)] * 4,
-    )
-    b_first = first((b_p, b_q), Y_BIT)
     row_a = send(row_a, ROW_A)
     b_first, row_a = lax.optimization_barrier((b_first, row_a))
     u_p, u_q, *u_own = join(second_kernel, [*u_first, *u_stay], [(13, 16, D), (12, 16, D)] * 2)

time: 95.9 us -> 95.9 us (level)
  transfers between devices with their start and end apart: 26 -> 26, of which waited for: 10 -> 10; matrix products, arithmetic and copies ran while one was open for 1% -> 1% of each run, Pallas kernels for 12% -> 13%
where the time goes in v13:
time: 95.9 us; the launch traced here: 94.3 us
  starting transfers between devices  52.9 us (55%)
  Pallas kernels  19.5 us (20%)
  waiting for transfers between devices  16.6 us (17%)
  other arithmetic  2.94 us (3%)
  local copies, waits for them, and re-layouts  1.41 us (1%)
  between operations  1.02 us (1%)
    ppermute x25, starting transfers between devices, send(): return lax.ppermute(x, AXES, perm)  48 us
    ppermute x25, waiting for transfers between devices, send(): return lax.ppermute(x, AXES, perm)  10.8 us
    pallas_call x1, Pallas kernels, per_device(): call(forward_kernel, [half_u, half_u, half_d, half_d, ((TOK, D), BF16), (...  6.02 us
    all_to_all x1, waiting for transfers between devices, exchange(): return lax.all_to_all(x, AXES, 0, 0, axis_index_groups=groups, tiled=True)  5.8 us
    all_to_all x1, starting transfers between devices, exchange(): return lax.all_to_all(x, AXES, 0, 0, axis_index_groups=groups, tiled=True)  4.88 us
    pallas_call x1, Pallas kernels, per_device(): call(backward_kernel, [half_k, half_k, ((TOK, D), BF16), ((EXT, 2 * D), B...  4.01 us
  transfers between devices with their start and end apart: 26, of which 10 were waited for; matrix products, arithmetic and copies ran while one was open for 1% of the time, Pallas kernels for 13%

profile of v13, /device:TPU:8, one launch (start us, length us, event | category | flops | bytes accessed | tf_op | source)
XLA Modules:
  0.0 94.3 jit_solution(10215283522559741224)
XLA Ops:
  0.6 1.2 %broadcast_select_fusion = (bf16[24,3,512]{2,1,0:T(4,128)(2,1)S(1)}, bf16[24,3,512]{2,1,0:T(4,128)(2,1)S(1)}) fusion(pred[]{:T(512)S(6)} %eq.6, bf16[24,8,512]{2,1,0:T(8,128)(2,1)} %param.8), kind=kLoop, calls=%fused_computation.14 | loop fusion | flops 73728 | bytes 294913 | tf_op jit(solution)/shard_map/jit(_where)/select_n | solution.py:418
  1.8 5.9 %collective-permute-start = (bf16[24,3,512]{2,1,0:T(4,128)(2,1)S(1)}, bf16[24,3,512]{2,1,0:T(4,128)(2,1)S(1)}, u32[]{:S(2)}, u32[]{:S(2)}) collective-permute-start(bf16[24,3,512]{2,1,0:T(4,128)(2,1)S(1)} %get-tuple-element.185), channel_id=1, source_target_pairs={{1,2},{2,1},{3,4},{4,3},{5,6},{6,5},{7,8},{8,7},{9,10},{10,9},{11,... | collective-permute-start | bytes 221192 | tf_op jit(solution)/shard_map/ppermute | solution.py:392
  8.6 1.2 %shard_map.127.bias = f32[3,64,256]{2,1,0:T(8,128)S(1)} custom-call(s32[3]{0:T(128)S(1)} %pad_add_fusion.coord, s32[3,1,49]{2,1,0:T(1,128)S(1)} %copy-done.7), custom_call_target="tpu_custom_call" | custom-call | flops 402653184 | bytes 4000000 | tf_op jit(solution)/shard_map/pallas_call | solution.py:420
  9.9 1.3 %collective-permute-done = bf16[24,3,512]{2,1,0:T(4,128)(2,1)S(1)} collective-permute-done((bf16[24,3,512]{2,1,0:T(4,128)(2,1)S(1)}, bf16[24,3,512]{2,1,0:T(4,128)(2,1)S(1)}, u32[]{:S(2)}, u32[]{:S(2)}) %collective-permute-start) | collective-permute-done | bytes 73760 | tf_op jit(solution)/shard_map/ppermute | solution.py:392
  12.1 4.3 %collective-permute-start.3 = (bf16[3,16,512]{2,1,0:T(8,128)(2,1)S(1)}, bf16[3,16,512]{2,1,0:T(8,128)(2,1)S(1)}, u32[]{:S(2)}, u32[]{:S(2)}) collective-permute-start(bf16[3,16,512]{2,1,0:T(8,128)(2,1)S(1)} %get-tuple-element.182), channel_id=1, source_target_pairs={{0,32},{1,33},{2,34},{3,35},{4,36},{5,37},{6,38},{7,39},{8,40},{9,... | collective-permute-start | bytes 147464 | tf_op jit(solution)/shard_map/ppermute | solution.py:392
  16.4 1.0 %shard_map.129 = (bf16[512,512]{1,0:T(8,128)(2,1)S(1)}, bf16[512,512]{1,0:T(8,128)(2,1)S(1)}) custom-call(s32[3]{0:T(128)S(1)} %pad_add_fusion.coord), custom_call_target="tpu_custom_call" | custom-call | flops 402653184 | bytes 4000000 | tf_op jit(solution)/shard_map/pallas_call | solution.py:427
  17.5 0.8 shard_map.128.gact
  18.9 1.6 %shard_map.130 = (bf16[192,512]{1,0:T(8,128)(2,1)S(1)}, bf16[192,512]{1,0:T(8,128)(2,1)S(1)}, bf16[384,512]{1,0:T(8,128)(2,1)S(1)}, bf16[384,1024]{1,0:T(8,128)(...) custom-call(bf16[24,16,512]{2,1,0:T(8,128)(2,1)S(1)} %maximum_maximum_fusion.mid, ...), custom_call_target="tpu_custom_call" | custom-call | flops 600000000 | bytes 5000000 | tf_op jit(solution)/shard_map/pallas_call | solution.py:434
  20.6 6.0 %shard_map.131 = (bf16[16,5,16,512]{3,2,1,0:T(8,128)(2,1)S(1)}, bf16[16,5,16,512]{3,2,1,0:T(8,128)(2,1)S(1)}, bf16[4,4,2,32,512]{4,3,2,1,0:T(8,128)(2,1)S(1)}, b...) custom-call(s32[3]{0:T(128)S(1)} %pad_add_fusion.coord, ...), custom_call_target="tpu_custom_call" | custom-call | flops 4000000000 | bytes 20000000 | tf_op jit(solution)/shard_map/pallas_call | solution.py:445
  27.2 4.0 %shard_map.132 = (bf16[48,16,512]{2,1,0:T(8,128)(2,1)S(1)}, bf16[48,16,512]{2,1,0:T(8,128)(2,1)S(1)}, bf16[192,512]{1,0:T(8,128)(2,1)S(1)}, bf16[512,1024]{1,0:T(8,128)(2,1)S(1)}) custom-call(bf16[192,512]{1,0:T(8,128)(2,1)S(1)} %get-tuple-element.101.gm, bf16[512,512]{1,0:T(8,128)(2,1)S(1)} %copy-done.6, bf16[192,512]{1,0:T(8,128)(2,1)S(1)} %get-tuple-element.97.q_i.q, ...), custom_call_target="tpu_custom_call" | custom-call | flops 2500000000 | bytes 10000000 | tf_op jit(solution)/shard_map/pallas_call | solution.py:456
  31.6 1.5 %shard_map.133 = (f32[384,512]{1,0:T(8,128)S(1)}, f32[192,512]{1,0:T(8,128)S(1)}, bf16[16,512]{1,0:T(8,128)(2,1)S(1)}, bf16[3,16,512]{2,1,0:T(8,128)(2,1)S(1)}, bf16[3,16,512]{2,1,0:T(8,128)(2,1)S(1)}) custom-call(s32[3]{0:T(128)S(1)} %pad_add_fusion.coord, bf16[192,512]{1,0:T(8,128)(2,1)S(1)} %get-tuple-element.115.dq, ...), custom_call_target="tpu_custom_call" | custom-call | flops 600000000 | bytes 4000000 | tf_op jit(solution)/shard_map/pallas_call | solution.py:463
  34.9 2.5 %collective-permute-start.16 = (bf16[24,16,512]{2,1,0:T(8,128)(2,1)S(1)}, bf16[24,16,512]{2,1,0:T(8,128)(2,1)S(1)}, u32[]{:S(2)}, u32[]{:S(2)}) collective-permute-start(bf16[24,16,512]{2,1,0:T(8,128)(2,1)S(1)} %get-tuple-element.140), channel_id=1, source_target_pairs={{0,24},{1,25},{2,26},{3,27},{4,28},{5,29},{6,30},{7,31},{8,16},{9,... | collective-permute-start | bytes 1179656 | tf_op jit(solution)/shard_map/ppermute | solution.py:392
  37.4 8.4 %collective-permute-start.9 = (bf16[24,16,512]{2,1,0:T(8,128)(2,1)S(1)}, bf16[24,16,512]{2,1,0:T(8,128)(2,1)S(1)}, u32[]{:S(2)}, u32[]{:S(2)}) collective-permute-start(bf16[24,16,512]{2,1,0:T(8,128)(2,1)S(1)} %get-tuple-element.128), channel_id=1, source_target_pairs={{0,96},{1,97},{2,98},{3,99},{4,100},{5,101},{6,102},{7,103},{8,104... | collective-permute-start | bytes 1179656 | tf_op jit(solution)/shard_map/ppermute | solution.py:392
  46.9 1.8 %collective-permute-start.18 = (bf16[12,16,512]{2,1,0:T(8,128)(2,1)S(1)}, bf16[12,16,512]{2,1,0:T(8,128)(2,1)S(1)}, u32[]{:S(2)}, u32[]{:S(2)}) collective-permute-start(bf16[12,16,512]{2,1,0:T(8,128)(2,1)S(1)} %get-tuple-element.146), channel_id=1, source_target_pairs={{0,24},{1,25},{2,26},{3,27},{4,28},{5,29},{6,30},{7,31},{8,16},{9,... | collective-permute-start | bytes 589832 | tf_op jit(solution)/shard_map/ppermute | solution.py:392
  48.7 2.9 %collective-permute-start.19 = (bf16[12,16,512]{2,1,0:T(8,128)(2,1)S(1)}, bf16[12,16,512]{2,1,0:T(8,128)(2,1)S(1)}, u32[]{:S(2)}, u32[]{:S(2)}) collective-permute-start(bf16[12,16,512]{2,1,0:T(8,128)(2,1)S(1)} %get-tuple-element.147), channel_id=1, source_target_pairs={{0,8},{1,9},{2,10},{3,11},{4,12},{5,13},{6,14},{7,15},{8,0},{9,1},... | collective-permute-start | bytes 589832 | tf_op jit(solution)/shard_map/ppermute | solution.py:392
  51.6 3.2 %collective-permute-done.9.q_got = bf16[24,16,512]{2,1,0:T(8,128)(2,1)S(1)} collective-permute-done((bf16[24,16,512]{2,1,0:T(8,128)(2,1)S(1)}, bf16[24,16,512]{2,1,0:T(8,128)(2,1)S(1)}, u32[]{:S(2)}, u32[]{:S(2)}) %collective-permute-start.9) | collective-permute-done | bytes 393248 | tf_op jit(solution)/shard_map/ppermute | solution.py:392
  55.0 5.8 %collective-permute-start.10 = (bf16[13,16,512]{2,1,0:T(8,128)(2,1)S(1)}, bf16[13,16,512]{2,1,0:T(8,128)(2,1)S(1)}, u32[]{:S(2)}, u32[]{:S(2)}) collective-permute-start(bf16[13,16,512]{2,1,0:T(8,128)(2,1)S(1)} %get-tuple-element.131), channel_id=1, source_target_pairs={{0,96},{1,97},{2,98},{3,99},{4,100},{5,101},{6,102},{7,103},{8,104... | collective-permute-start | bytes 638984 | tf_op jit(solution)/shard_map/ppermute | solution.py:392
  61.0 2.6 %collective-permute-start.20 = (bf16[6,16,512]{2,1,0:T(8,128)(2,1)S(1)}, bf16[6,16,512]{2,1,0:T(8,128)(2,1)S(1)}, u32[]{:S(2)}, u32[]{:S(2)}) collective-permute-start(bf16[6,16,512]{2,1,0:T(8,128)(2,1)S(1)} %get-tuple-element.151), channel_id=1, source_target_pairs={{0,64},{1,65},{2,66},{3,67},{4,68},{5,69},{6,70},{7,71},{8,72},{9,... | collective-permute-start | bytes 294920 | tf_op jit(solution)/shard_map/ppermute | solution.py:392
  63.8 1.7 %collective-permute-start.21 = (bf16[6,16,512]{2,1,0:T(8,128)(2,1)S(1)}, bf16[6,16,512]{2,1,0:T(8,128)(2,1)S(1)}, u32[]{:S(2)}, u32[]{:S(2)}) collective-permute-start(bf16[6,16,512]{2,1,0:T(8,128)(2,1)S(1)} %get-tuple-element.152), channel_id=1, source_target_pairs={{0,32},{1,33},{2,34},{3,35},{4,36},{5,37},{6,38},{7,39},{8,40},{9,... | collective-permute-start | bytes 294920 | tf_op jit(solution)/shard_map/ppermute | solution.py:392
  65.5 0.8 collective-permute-start.22
  66.4 0.9 collective-permute-done.11.q_got
  67.4 2.1 %collective-permute-start.12 = (bf16[7,16,512]{2,1,0:T(8,128)(2,1)S(1)}, bf16[7,16,512]{2,1,0:T(8,128)(2,1)S(1)}, u32[]{:S(2)}, u32[]{:S(2)}) collective-permute-start(bf16[7,16,512]{2,1,0:T(8,128)(2,1)S(1)} %get-tuple-element.136), channel_id=1, source_target_pairs={{0,16},{1,17},{2,18},{3,19},{4,20},{5,21},{6,22},{7,23},{8,24},{9,... | collective-permute-start | bytes 344072 | tf_op jit(solution)/shard_map/ppermute | solution.py:392
  69.5 1.9 %collective-permute-start.13 = (bf16[7,16,512]{2,1,0:T(8,128)(2,1)S(1)}, bf16[7,16,512]{2,1,0:T(8,128)(2,1)S(1)}, u32[]{:S(2)}, u32[]{:S(2)}) collective-permute-start(bf16[7,16,512]{2,1,0:T(8,128)(2,1)S(1)} %get-tuple-element.137), channel_id=1, source_target_pairs={{0,8},{1,9},{2,10},{3,11},{4,12},{5,13},{6,14},{7,15},{8,0},{9,1},... | collective-permute-start | bytes 344072 | tf_op jit(solution)/shard_map/ppermute | solution.py:392
  71.7 2.1 %collective-permute-done.12.refs_1_ = bf16[7,16,512]{2,1,0:T(8,128)(2,1)S(1)} collective-permute-done((bf16[7,16,512]{2,1,0:T(8,128)(2,1)S(1)}, bf16[7,16,512]{2,1,0:T(8,128)(2,1)S(1)}, u32[]{:S(2)}, u32[]{:S(2)}) %collective-permute-start.12) | collective-permute-done | bytes 114720 | tf_op jit(solution)/shard_map/ppermute | solution.py:392
  73.8 1.6 %collective-permute-done.13.refs_2_ = bf16[7,16,512]{2,1,0:T(8,128)(2,1)S(1)} collective-permute-done((bf16[7,16,512]{2,1,0:T(8,128)(2,1)S(1)}, bf16[7,16,512]{2,1,0:T(8,128)(2,1)S(1)}, u32[]{:S(2)}, u32[]{:S(2)}) %collective-permute-start.13) | collective-permute-done | bytes 114720 | tf_op jit(solution)/shard_map/ppermute | solution.py:392
  75.4 0.8 collective-permute-done.14.refs_3_
  76.2 1.3 %shard_map.140 = bf16[8,112,128]{2,1,0:T(8,128)(2,1)} custom-call(bf16[7,16,512]{2,1,0:T(8,128)(2,1)S(1)} %get-tuple-element.157.refs_0_, bf16[7,16,512]{2,1,0:T(8,128)(2,1)S(1)} %collective-permute-done.12.refs_1_, bf16[7,16,512]{2,1,0:T(8,128)(2,1)S(1)} %collective-permute-done.13.refs_2_, bf16[7,16,512]{2,1,0:T(8,128)(2,1)S(1)} %collective-permute-done.14.refs_3_, ...), custom_call_target="tpu_custom_call" | custom-call | flops 60000000 | bytes 4000000 | tf_op jit(solution)/shard_map/pallas_call | solution.py:517
  77.5 4.9 %all-to-all-start = ((bf16[8,112,128]{2,1,0:T(8,128)(2,1)}), bf16[8,112,128]{2,1,0:T(8,128)(2,1)S(1)}, u32[]{:S(2)}, u32[]{:S(2)}) async-start(bf16[8,112,128]{2,1,0:T(8,128)(2,1)} %shard_map.140), calls=%async_computation | async-start | bytes 458752 | tf_op jit(solution)/shard_map/all_to_all | solution.py:405
  82.5 1.9 %collective-permute-start.23 = (bf16[24,3,512]{2,1,0:T(4,128)(2,1)S(1)}, bf16[24,3,512]{2,1,0:T(4,128)(2,1)S(1)}, u32[]{:S(2)}, u32[]{:S(2)}) collective-permute-start(bf16[24,3,512]{2,1,0:T(4,128)(2,1)S(1)} %get-tuple-element.166), channel_id=1, source_target_pairs={{1,2},{2,1},{3,4},{4,3},{5,6},{6,5},{7,8},{8,7},{9,10},{10,9},{11,... | collective-permute-start | bytes 221192 | tf_op jit(solution)/shard_map/ppermute | solution.py:392
  84.4 2.2 %collective-permute-start.24 = (bf16[24,3,512]{2,1,0:T(4,128)(2,1)S(1)}, bf16[24,3,512]{2,1,0:T(4,128)(2,1)S(1)}, u32[]{:S(2)}, u32[]{:S(2)}) collective-permute-start(bf16[24,3,512]{2,1,0:T(4,128)(2,1)S(1)} %get-tuple-element.167), channel_id=1, source_target_pairs={{0,1},{1,0},{2,3},{3,2},{4,5},{5,4},{6,7},{7,6},{8,9},{9,8},{10,11... | collective-permute-start | bytes 221192 | tf_op jit(solution)/shard_map/ppermute | solution.py:392
  86.6 5.8 %all-to-all-done.got = bf16[8,112,128]{2,1,0:T(8,128)(2,1)S(1)} async-done(((bf16[8,112,128]{2,1,0:T(8,128)(2,1)}), bf16[8,112,128]{2,1,0:T(8,128)(2,1)S(1)}, u32[]{:S(2)}, u32[]{:S(2)}) %all-to-all-start) | async-done | bytes 229408 | tf_op jit(solution)/shard_map/all_to_all | solution.py:405
  93.5 0.9 fusion.6
  (70 shorter events, 8.2 us)
Async XLA Ops:
  0.6 10.6 %copy-start = (bf16[24,8,512]{2,1,0:T(8,128)(2,1)S(1)}, bf16[24,8,512]{2,1,0:T(8,128)(2,1)}, u32[]{:S(2)}) copy-start(bf16[24,8,512]{2,1,0:T(8,128)(2,1)} %param.8) | copy-start | bytes 589828
  1.8 9.4 %collective-permute-start = (bf16[24,3,512]{2,1,0:T(4,128)(2,1)S(1)}, bf16[24,3,512]{2,1,0:T(4,128)(2,1)S(1)}, u32[]{:S(2)}, u32[]{:S(2)}) collective-permute-start(bf16[24,3,512]{2,1,0:T(4,128)(2,1)S(1)} %get-tuple-element.185), channel_id=1, source_target_pairs={{1,2},{2,1},{3,4},{4,3},{5,6},{6,5},{7,8},{8,7},{9,10},{10,9},{11,... | collective-permute-start | bytes 221192 | tf_op jit(solution)/shard_map/ppermute | solution.py:392
  7.7 3.5 %collective-permute-start.1 = (bf16[24,3,512]{2,1,0:T(4,128)(2,1)S(1)}, bf16[24,3,512]{2,1,0:T(4,128)(2,1)S(1)}, u32[]{:S(2)}, u32[]{:S(2)}) collective-permute-start(bf16[24,3,512]{2,1,0:T(4,128)(2,1)S(1)} %get-tuple-element.184), channel_id=1, source_target_pairs={{0,1},{1,0},{2,3},{3,2},{4,5},{5,4},{6,7},{7,6},{8,9},{9,8},{10,11... | collective-permute-start | bytes 221192 | tf_op jit(solution)/shard_map/ppermute | solution.py:392
  9.9 7.6 %copy-start.2 = (bf16[2048,512]{1,0:T(8,128)(2,1)S(1)}, bf16[2048,512]{1,0:T(8,128)(2,1)}, u32[]{:S(2)}) copy-start(bf16[2048,512]{1,0:T(8,128)(2,1)} %w_down.1) | copy-start | bytes 6291460
  9.9 7.6 %copy-start.3 = (bf16[24,8,512]{2,1,0:T(8,128)(2,1)S(1)}, bf16[24,8,512]{2,1,0:T(8,128)(2,1)}, u32[]{:S(2)}) copy-start(bf16[24,8,512]{2,1,0:T(8,128)(2,1)} %param.9) | copy-start | bytes 589828
  11.4 9.1 %collective-permute-start.2 = (bf16[3,16,512]{2,1,0:T(8,128)(2,1)S(1)}, bf16[3,16,512]{2,1,0:T(8,128)(2,1)S(1)}, u32[]{:S(2)}, u32[]{:S(2)}) collective-permute-start(bf16[3,16,512]{2,1,0:T(8,128)(2,1)S(1)} %get-tuple-element.183), channel_id=1, source_target_pairs={{32,64},{33,65},{34,66},{35,67},{36,68},{37,69},{38,70},{39,71},{4... | collective-permute-start | bytes 147464 | tf_op jit(solution)/shard_map/ppermute | solution.py:392
  12.1 8.4 %collective-permute-start.3 = (bf16[3,16,512]{2,1,0:T(8,128)(2,1)S(1)}, bf16[3,16,512]{2,1,0:T(8,128)(2,1)S(1)}, u32[]{:S(2)}, u32[]{:S(2)}) collective-permute-start(bf16[3,16,512]{2,1,0:T(8,128)(2,1)S(1)} %get-tuple-element.182), channel_id=1, source_target_pairs={{0,32},{1,33},{2,34},{3,35},{4,36},{5,37},{6,38},{7,39},{8,40},{9,... | collective-permute-start | bytes 147464 | tf_op jit(solution)/shard_map/ppermute | solution.py:392
  17.5 3.0 %copy-start.6 = (bf16[512,512]{1,0:T(8,128)(2,1)S(1)}, bf16[512,512]{1,0:T(8,128)(2,1)}, u32[]{:S(2)}) copy-start(bf16[512,512]{1,0:T(8,128)(2,1)} %w_out.3) | copy-start | bytes 1572868
  18.4 2.2 %copy-start.5 = (bf16[512,2048]{1,0:T(8,128)(2,1)S(1)}, bf16[512,2048]{1,0:T(8,128)(2,1)}, u32[]{:S(2)}) copy-start(bf16[512,2048]{1,0:T(8,128)(2,1)} %w_up.1) | copy-start | bytes 6291460
  26.6 4.6 %collective-permute-start.4 = (bf16[16,5,16,512]{3,2,1,0:T(8,128)(2,1)S(1)}, bf16[16,5,16,512]{3,2,1,0:T(8,128)(2,1)S(1)}, u32[]{:S(2)}, u32[]{:S(2)}) collective-permute-start(bf16[16,5,16,512]{3,2,1,0:T(8,128)(2,1)S(1)} %get-tuple-element.103), channel_id=1, source_target_pairs={{0,1},{1,0},{2,3},{3,2},{4,5},{5,4},{6,7},{7,6},{8,9},{9,8},{10,11... | collective-permute-start | bytes 3932168 | tf_op jit(solution)/shard_map/ppermute | solution.py:392
  26.7 4.5 %collective-permute-start.5 = (bf16[4,4,2,32,512]{4,3,2,1,0:T(8,128)(2,1)S(1)}, bf16[4,4,2,32,512]{4,3,2,1,0:T(8,128)(2,1)S(1)}, u32[]{:S(2)}, u32[]{:S(2)}) collective-permute-start(bf16[4,4,2,32,512]{4,3,2,1,0:T(8,128)(2,1)S(1)} %get-tuple-element.104), channel_id=1, source_target_pairs={{0,1},{1,0},{2,3},{3,2},{4,5},{5,4},{6,7},{7,6},{8,9},{9,8},{10,11... | collective-permute-start | bytes 3145736 | tf_op jit(solution)/shard_map/ppermute | solution.py:392
  31.2 2.4 %collective-permute-start.6 = (bf16[48,16,512]{2,1,0:T(8,128)(2,1)S(1)}, bf16[48,16,512]{2,1,0:T(8,128)(2,1)S(1)}, u32[]{:S(2)}, u32[]{:S(2)}) collective-permute-start(bf16[48,16,512]{2,1,0:T(8,128)(2,1)S(1)} %get-tuple-element.114), channel_id=1, source_target_pairs={{0,1},{1,0},{2,3},{3,2},{4,5},{5,4},{6,7},{7,6},{8,9},{9,8},{10,11... | collective-permute-start | bytes 2359304 | tf_op jit(solution)/shard_map/ppermute | solution.py:392
  33.1 1.3 %collective-permute-start.7 = (bf16[16,512]{1,0:T(8,128)(2,1)S(1)}, bf16[16,512]{1,0:T(8,128)(2,1)S(1)}, u32[]{:S(2)}, u32[]{:S(2)}) collective-permute-start(bf16[16,512]{1,0:T(8,128)(2,1)S(1)} %get-tuple-element.120.gk), channel_id=1, source_target_pairs={{0,1},{1,0},{2,3},{3,2},{4,5},{5,4},{6,7},{7,6},{8,9},{9,8},{10,11... | collective-permute-start | bytes 49160 | tf_op jit(solution)/shard_map/ppermute | solution.py:392
  34.7 20.1 %collective-permute-start.8 = (bf16[28,16,512]{2,1,0:T(8,128)(2,1)S(1)}, bf16[28,16,512]{2,1,0:T(8,128)(2,1)S(1)}, u32[]{:S(2)}, u32[]{:S(2)}) collective-permute-start(bf16[28,16,512]{2,1,0:T(8,128)(2,1)S(1)} %get-tuple-element.127), channel_id=1, source_target_pairs={{0,32},{1,33},{2,34},{3,35},{4,36},{5,37},{6,38},{7,39},{8,40},{9,... | collective-permute-start | bytes 1376264 | tf_op jit(solution)/shard_map/ppermute | solution.py:392
  34.8 11.7 %collective-permute-start.15 = (bf16[24,16,512]{2,1,0:T(8,128)(2,1)S(1)}, bf16[24,16,512]{2,1,0:T(8,128)(2,1)S(1)}, u32[]{:S(2)}, u32[]{:S(2)}) collective-permute-start(bf16[24,16,512]{2,1,0:T(8,128)(2,1)S(1)} %get-tuple-element.139), channel_id=1, source_target_pairs={{0,8},{1,9},{2,10},{3,11},{4,12},{5,13},{6,14},{7,15},{8,0},{9,1},... | collective-permute-start | bytes 1179656 | tf_op jit(solution)/shard_map/ppermute | solution.py:392
  34.9 11.7 %collective-permute-start.16 = (bf16[24,16,512]{2,1,0:T(8,128)(2,1)S(1)}, bf16[24,16,512]{2,1,0:T(8,128)(2,1)S(1)}, u32[]{:S(2)}, u32[]{:S(2)}) collective-permute-start(bf16[24,16,512]{2,1,0:T(8,128)(2,1)S(1)} %get-tuple-element.140), channel_id=1, source_target_pairs={{0,24},{1,25},{2,26},{3,27},{4,28},{5,29},{6,30},{7,31},{8,16},{9,... | collective-permute-start | bytes 1179656 | tf_op jit(solution)/shard_map/ppermute | solution.py:392
  37.4 17.4 %collective-permute-start.9 = (bf16[24,16,512]{2,1,0:T(8,128)(2,1)S(1)}, bf16[24,16,512]{2,1,0:T(8,128)(2,1)S(1)}, u32[]{:S(2)}, u32[]{:S(2)}) collective-permute-start(bf16[24,16,512]{2,1,0:T(8,128)(2,1)S(1)} %get-tuple-element.128), channel_id=1, source_target_pairs={{0,96},{1,97},{2,98},{3,99},{4,100},{5,101},{6,102},{7,103},{8,104... | collective-permute-start | bytes 1179656 | tf_op jit(solution)/shard_map/ppermute | solution.py:392
  45.8 0.7 collective-permute-start.17
  46.9 14.0 %collective-permute-start.18 = (bf16[12,16,512]{2,1,0:T(8,128)(2,1)S(1)}, bf16[12,16,512]{2,1,0:T(8,128)(2,1)S(1)}, u32[]{:S(2)}, u32[]{:S(2)}) collective-permute-start(bf16[12,16,512]{2,1,0:T(8,128)(2,1)S(1)} %get-tuple-element.146), channel_id=1, source_target_pairs={{0,24},{1,25},{2,26},{3,27},{4,28},{5,29},{6,30},{7,31},{8,16},{9,... | collective-permute-start | bytes 589832 | tf_op jit(solution)/shard_map/ppermute | solution.py:392
  48.7 12.2 %collective-permute-start.19 = (bf16[12,16,512]{2,1,0:T(8,128)(2,1)S(1)}, bf16[12,16,512]{2,1,0:T(8,128)(2,1)S(1)}, u32[]{:S(2)}, u32[]{:S(2)}) collective-permute-start(bf16[12,16,512]{2,1,0:T(8,128)(2,1)S(1)} %get-tuple-element.147), channel_id=1, source_target_pairs={{0,8},{1,9},{2,10},{3,11},{4,12},{5,13},{6,14},{7,15},{8,0},{9,1},... | collective-permute-start | bytes 589832 | tf_op jit(solution)/shard_map/ppermute | solution.py:392
  55.0 12.3 %collective-permute-start.10 = (bf16[13,16,512]{2,1,0:T(8,128)(2,1)S(1)}, bf16[13,16,512]{2,1,0:T(8,128)(2,1)S(1)}, u32[]{:S(2)}, u32[]{:S(2)}) collective-permute-start(bf16[13,16,512]{2,1,0:T(8,128)(2,1)S(1)} %get-tuple-element.131), channel_id=1, source_target_pairs={{0,96},{1,97},{2,98},{3,99},{4,100},{5,101},{6,102},{7,103},{8,104... | collective-permute-start | bytes 638984 | tf_op jit(solution)/shard_map/ppermute | solution.py:392
  60.9 6.4 %collective-permute-start.11 = (bf16[12,16,512]{2,1,0:T(8,128)(2,1)S(1)}, bf16[12,16,512]{2,1,0:T(8,128)(2,1)S(1)}, u32[]{:S(2)}, u32[]{:S(2)}) collective-permute-start(bf16[12,16,512]{2,1,0:T(8,128)(2,1)S(1)} %get-tuple-element.132), channel_id=1, source_target_pairs={{0,32},{1,33},{2,34},{3,35},{4,36},{5,37},{6,38},{7,39},{8,40},{9,... | collective-permute-start | bytes 589832 | tf_op jit(solution)/shard_map/ppermute | solution.py:392
  61.0 10.3 %collective-permute-start.20 = (bf16[6,16,512]{2,1,0:T(8,128)(2,1)S(1)}, bf16[6,16,512]{2,1,0:T(8,128)(2,1)S(1)}, u32[]{:S(2)}, u32[]{:S(2)}) collective-permute-start(bf16[6,16,512]{2,1,0:T(8,128)(2,1)S(1)} %get-tuple-element.151), channel_id=1, source_target_pairs={{0,64},{1,65},{2,66},{3,67},{4,68},{5,69},{6,70},{7,71},{8,72},{9,... | collective-permute-start | bytes 294920 | tf_op jit(solution)/shard_map/ppermute | solution.py:392
  63.8 7.9 %collective-permute-start.21 = (bf16[6,16,512]{2,1,0:T(8,128)(2,1)S(1)}, bf16[6,16,512]{2,1,0:T(8,128)(2,1)S(1)}, u32[]{:S(2)}, u32[]{:S(2)}) collective-permute-start(bf16[6,16,512]{2,1,0:T(8,128)(2,1)S(1)} %get-tuple-element.152), channel_id=1, source_target_pairs={{0,32},{1,33},{2,34},{3,35},{4,36},{5,37},{6,38},{7,39},{8,40},{9,... | collective-permute-start | bytes 294920 | tf_op jit(solution)/shard_map/ppermute | solution.py:392
  65.5 6.2 %collective-permute-start.22 = (bf16[6,16,512]{2,1,0:T(8,128)(2,1)S(1)}, bf16[6,16,512]{2,1,0:T(8,128)(2,1)S(1)}, u32[]{:S(2)}, u32[]{:S(2)}) collective-permute-start(bf16[6,16,512]{2,1,0:T(8,128)(2,1)S(1)} %get-tuple-element.153), channel_id=1, source_target_pairs={{0,96},{1,97},{2,98},{3,99},{4,100},{5,101},{6,102},{7,103},{8,104... | collective-permute-start | bytes 294920 | tf_op jit(solution)/shard_map/ppermute | solution.py:392
  67.4 6.4 %collective-permute-start.12 = (bf16[7,16,512]{2,1,0:T(8,128)(2,1)S(1)}, bf16[7,16,512]{2,1,0:T(8,128)(2,1)S(1)}, u32[]{:S(2)}, u32[]{:S(2)}) collective-permute-start(bf16[7,16,512]{2,1,0:T(8,128)(2,1)S(1)} %get-tuple-element.136), channel_id=1, source_target_pairs={{0,16},{1,17},{2,18},{3,19},{4,20},{5,21},{6,22},{7,23},{8,24},{9,... | collective-permute-start | bytes 344072 | tf_op jit(solution)/shard_map/ppermute | solution.py:392
  69.5 5.9 %collective-permute-start.13 = (bf16[7,16,512]{2,1,0:T(8,128)(2,1)S(1)}, bf16[7,16,512]{2,1,0:T(8,128)(2,1)S(1)}, u32[]{:S(2)}, u32[]{:S(2)}) collective-permute-start(bf16[7,16,512]{2,1,0:T(8,128)(2,1)S(1)} %get-tuple-element.137), channel_id=1, source_target_pairs={{0,8},{1,9},{2,10},{3,11},{4,12},{5,13},{6,14},{7,15},{8,0},{9,1},... | collective-permute-start | bytes 344072 | tf_op jit(solution)/shard_map/ppermute | solution.py:392
  71.4 4.8 %collective-permute-start.14 = (bf16[7,16,512]{2,1,0:T(8,128)(2,1)S(1)}, bf16[7,16,512]{2,1,0:T(8,128)(2,1)S(1)}, u32[]{:S(2)}, u32[]{:S(2)}) collective-permute-start(bf16[7,16,512]{2,1,0:T(8,128)(2,1)S(1)} %get-tuple-element.138), channel_id=1, source_target_pairs={{0,24},{1,25},{2,26},{3,27},{4,28},{5,29},{6,30},{7,31},{8,16},{9,... | collective-permute-start | bytes 344072 | tf_op jit(solution)/shard_map/ppermute | solution.py:392
  77.5 15.0 %all-to-all-start = ((bf16[8,112,128]{2,1,0:T(8,128)(2,1)}), bf16[8,112,128]{2,1,0:T(8,128)(2,1)S(1)}, u32[]{:S(2)}, u32[]{:S(2)}) async-start(bf16[8,112,128]{2,1,0:T(8,128)(2,1)} %shard_map.140), calls=%async_computation | async-start | bytes 458752 | tf_op jit(solution)/shard_map/all_to_all | solution.py:405
  82.5 10.7 %slice-start = ((f32[2,512]{1,0:T(2,128)}), f32[1,512]{1,0:T(1,128)S(1)}, s32[]{:S(2)}) async-start(f32[2,512]{1,0:T(2,128)} %gains.3), calls=%async_computation.1 | async-start | bytes 4096 | tf_op jit(solution)/shard_map/slice | solution.py:532
  82.5 10.6 %collective-permute-start.23 = (bf16[24,3,512]{2,1,0:T(4,128)(2,1)S(1)}, bf16[24,3,512]{2,1,0:T(4,128)(2,1)S(1)}, u32[]{:S(2)}, u32[]{:S(2)}) collective-permute-start(bf16[24,3,512]{2,1,0:T(4,128)(2,1)S(1)} %get-tuple-element.166), channel_id=1, source_target_pairs={{1,2},{2,1},{3,4},{4,3},{5,6},{6,5},{7,8},{8,7},{9,10},{10,9},{11,... | collective-permute-start | bytes 221192 | tf_op jit(solution)/shard_map/ppermute | solution.py:392
  84.4 8.7 %collective-permute-start.24 = (bf16[24,3,512]{2,1,0:T(4,128)(2,1)S(1)}, bf16[24,3,512]{2,1,0:T(4,128)(2,1)S(1)}, u32[]{:S(2)}, u32[]{:S(2)}) collective-permute-start(bf16[24,3,512]{2,1,0:T(4,128)(2,1)S(1)} %get-tuple-element.167), channel_id=1, source_target_pairs={{0,1},{1,0},{2,3},{3,2},{4,5},{5,4},{6,7},{7,6},{8,9},{9,8},{10,11... | collective-permute-start | bytes 221192 | tf_op jit(solution)/shard_map/ppermute | solution.py:392
  (3 other events, 3.5 us)

commit v14 on v13

--- a/solution.py
+++ b/solution.py
@@ -109,9 +109,9 @@
 
 
 def attend(qt, keys, vals, bias_t):
-    s = nt(stack_heads(qt), keys) * 0.125 + jnp.concatenate([bias_t] * 4, axis=0)
+    s = nt(stack_heads(qt * 0.125), keys) + jnp.concatenate([bias_t] * 4, axis=0)
     e = jnp.exp(s - jnp.max(s, axis=-1, keepdims=True))
-    prob = e / jnp.sum(e, axis=-1, keepdims=True)
+    prob = e * (1.0 / jnp.sum(e, axis=-1, keepdims=True))
     return prob, unstack_heads(nn(prob.astype(BF16), vals)).astype(BF16)
 
 
@@ -210,9 +210,9 @@
             prob = p_mid[g] if t == 1 else p_out[t + g]
             gas = stack_heads(ga[t * QT : (t + 1) * QT, cols])
             qs = stack_heads(q[t * QT : (t + 1) * QT, cols])
-            gp = nt(gas, kv[rows, vcols])
+            gp = nt(gas * 0.125, kv[rows, vcols])
             inner = jnp.sum(prob * gp, axis=-1, keepdims=True)
-            ds = (prob * (gp - inner) * 0.125).astype(BF16)
+            ds = (prob * (gp - inner)).astype(BF16)
             dq_s[t * QT : (t + 1) * QT, cols] = unstack_heads(nn(ds, kv[rows, cols])).astype(BF16)
             dk, dv = tn(ds, qs), tn(prob.astype(BF16), gas)
             top_k, top_v = dk[:128], dv[:128]

time: 95.9 us -> 95.9 us (level)
  no operation moved by 1% of the time
where the time goes in v14:
time: 95.9 us; the launch traced here: 94.3 us
  starting transfers between devices  52.8 us (55%)
  Pallas kernels  19.5 us (20%)
  waiting for transfers between devices  16.6 us (17%)
  other arithmetic  2.94 us (3%)
  local copies, waits for them, and re-layouts  1.41 us (1%)
  between operations  1.02 us (1%)
    ppermute x25, starting transfers between devices, send(): return lax.ppermute(x, AXES, perm)  48 us
    ppermute x25, waiting for transfers between devices, send(): return lax.ppermute(x, AXES, perm)  10.8 us
    pallas_call x1, Pallas kernels, per_device(): call(forward_kernel, [half_u, half_u, half_d, half_d, ((TOK, D), BF16), (...  6.03 us
    all_to_all x1, waiting for transfers between devices, exchange(): return lax.all_to_all(x, AXES, 0, 0, axis_index_groups=groups, tiled=True)  5.8 us
    all_to_all x1, starting transfers between devices, exchange(): return lax.all_to_all(x, AXES, 0, 0, axis_index_groups=groups, tiled=True)  4.81 us
    pallas_call x1, Pallas kernels, per_device(): call(backward_kernel, [half_k, half_k, ((TOK, D), BF16), ((EXT, 2 * D), B...  4.03 us
  transfers between devices with their start and end apart: 26, of which 10 were waited for; matrix products, arithmetic and copies ran while one was open for 1% of the time, Pallas kernels for 13%

profile of v14, /device:TPU:8, one launch (start us, length us, event | category | flops | bytes accessed | tf_op | source)
XLA Modules:
  0.0 94.3 jit_solution(16363871637062713913)
XLA Ops:
  0.6 1.2 %broadcast_select_fusion = (bf16[24,3,512]{2,1,0:T(4,128)(2,1)S(1)}, bf16[24,3,512]{2,1,0:T(4,128)(2,1)S(1)}) fusion(pred[]{:T(512)S(6)} %eq.6, bf16[24,8,512]{2,1,0:T(8,128)(2,1)} %param.8), kind=kLoop, calls=%fused_computation.14 | loop fusion | flops 73728 | bytes 294913 | tf_op jit(solution)/shard_map/jit(_where)/select_n | solution.py:418
  1.8 5.9 %collective-permute-start = (bf16[24,3,512]{2,1,0:T(4,128)(2,1)S(1)}, bf16[24,3,512]{2,1,0:T(4,128)(2,1)S(1)}, u32[]{:S(2)}, u32[]{:S(2)}) collective-permute-start(bf16[24,3,512]{2,1,0:T(4,128)(2,1)S(1)} %get-tuple-element.185), channel_id=1, source_target_pairs={{1,2},{2,1},{3,4},{4,3},{5,6},{6,5},{7,8},{8,7},{9,10},{10,9},{11,... | collective-permute-start | bytes 221192 | tf_op jit(solution)/shard_map/ppermute | solution.py:392
  8.6 1.2 %shard_map.127.bias = f32[3,64,256]{2,1,0:T(8,128)S(1)} custom-call(s32[3]{0:T(128)S(1)} %pad_add_fusion.coord, s32[3,1,49]{2,1,0:T(1,128)S(1)} %copy-done.7), custom_call_target="tpu_custom_call" | custom-call | flops 402653184 | bytes 4000000 | tf_op jit(solution)/shard_map/pallas_call | solution.py:420
  9.9 1.3 %collective-permute-done = bf16[24,3,512]{2,1,0:T(4,128)(2,1)S(1)} collective-permute-done((bf16[24,3,512]{2,1,0:T(4,128)(2,1)S(1)}, bf16[24,3,512]{2,1,0:T(4,128)(2,1)S(1)}, u32[]{:S(2)}, u32[]{:S(2)}) %collective-permute-start) | collective-permute-done | bytes 73760 | tf_op jit(solution)/shard_map/ppermute | solution.py:392
  12.1 4.3 %collective-permute-start.3 = (bf16[3,16,512]{2,1,0:T(8,128)(2,1)S(1)}, bf16[3,16,512]{2,1,0:T(8,128)(2,1)S(1)}, u32[]{:S(2)}, u32[]{:S(2)}) collective-permute-start(bf16[3,16,512]{2,1,0:T(8,128)(2,1)S(1)} %get-tuple-element.182), channel_id=1, source_target_pairs={{0,32},{1,33},{2,34},{3,35},{4,36},{5,37},{6,38},{7,39},{8,40},{9,... | collective-permute-start | bytes 147464 | tf_op jit(solution)/shard_map/ppermute | solution.py:392
  16.4 1.0 %shard_map.129 = (bf16[512,512]{1,0:T(8,128)(2,1)S(1)}, bf16[512,512]{1,0:T(8,128)(2,1)S(1)}) custom-call(s32[3]{0:T(128)S(1)} %pad_add_fusion.coord), custom_call_target="tpu_custom_call" | custom-call | flops 402653184 | bytes 4000000 | tf_op jit(solution)/shard_map/pallas_call | solution.py:427
  17.5 0.8 shard_map.128.gact
  18.9 1.6 %shard_map.130 = (bf16[192,512]{1,0:T(8,128)(2,1)S(1)}, bf16[192,512]{1,0:T(8,128)(2,1)S(1)}, bf16[384,512]{1,0:T(8,128)(2,1)S(1)}, bf16[384,1024]{1,0:T(8,128)(...) custom-call(bf16[24,16,512]{2,1,0:T(8,128)(2,1)S(1)} %maximum_maximum_fusion.mid, ...), custom_call_target="tpu_custom_call" | custom-call | flops 600000000 | bytes 5000000 | tf_op jit(solution)/shard_map/pallas_call | solution.py:434
  20.6 6.0 %shard_map.131 = (bf16[16,5,16,512]{3,2,1,0:T(8,128)(2,1)S(1)}, bf16[16,5,16,512]{3,2,1,0:T(8,128)(2,1)S(1)}, bf16[4,4,2,32,512]{4,3,2,1,0:T(8,128)(2,1)S(1)}, b...) custom-call(s32[3]{0:T(128)S(1)} %pad_add_fusion.coord, ...), custom_call_target="tpu_custom_call" | custom-call | flops 4000000000 | bytes 20000000 | tf_op jit(solution)/shard_map/pallas_call | solution.py:445
  27.2 4.0 %shard_map.132 = (bf16[48,16,512]{2,1,0:T(8,128)(2,1)S(1)}, bf16[48,16,512]{2,1,0:T(8,128)(2,1)S(1)}, bf16[192,512]{1,0:T(8,128)(2,1)S(1)}, bf16[512,1024]{1,0:T(8,128)(2,1)S(1)}) custom-call(bf16[192,512]{1,0:T(8,128)(2,1)S(1)} %get-tuple-element.101.gm, bf16[512,512]{1,0:T(8,128)(2,1)S(1)} %copy-done.6, bf16[192,512]{1,0:T(8,128)(2,1)S(1)} %get-tuple-element.97.q_i.q, ...), custom_call_target="tpu_custom_call" | custom-call | flops 2500000000 | bytes 10000000 | tf_op jit(solution)/shard_map/pallas_call | solution.py:456
  31.6 1.5 %shard_map.133 = (f32[384,512]{1,0:T(8,128)S(1)}, f32[192,512]{1,0:T(8,128)S(1)}, bf16[16,512]{1,0:T(8,128)(2,1)S(1)}, bf16[3,16,512]{2,1,0:T(8,128)(2,1)S(1)}, bf16[3,16,512]{2,1,0:T(8,128)(2,1)S(1)}) custom-call(s32[3]{0:T(128)S(1)} %pad_add_fusion.coord, bf16[192,512]{1,0:T(8,128)(2,1)S(1)} %get-tuple-element.115.dq, ...), custom_call_target="tpu_custom_call" | custom-call | flops 600000000 | bytes 4000000 | tf_op jit(solution)/shard_map/pallas_call | solution.py:463
  34.9 2.5 %collective-permute-start.16 = (bf16[24,16,512]{2,1,0:T(8,128)(2,1)S(1)}, bf16[24,16,512]{2,1,0:T(8,128)(2,1)S(1)}, u32[]{:S(2)}, u32[]{:S(2)}) collective-permute-start(bf16[24,16,512]{2,1,0:T(8,128)(2,1)S(1)} %get-tuple-element.140), channel_id=1, source_target_pairs={{0,24},{1,25},{2,26},{3,27},{4,28},{5,29},{6,30},{7,31},{8,16},{9,... | collective-permute-start | bytes 1179656 | tf_op jit(solution)/shard_map/ppermute | solution.py:392
  37.4 8.4 %collective-permute-start.9 = (bf16[24,16,512]{2,1,0:T(8,128)(2,1)S(1)}, bf16[24,16,512]{2,1,0:T(8,128)(2,1)S(1)}, u32[]{:S(2)}, u32[]{:S(2)}) collective-permute-start(bf16[24,16,512]{2,1,0:T(8,128)(2,1)S(1)} %get-tuple-element.128), channel_id=1, source_target_pairs={{0,96},{1,97},{2,98},{3,99},{4,100},{5,101},{6,102},{7,103},{8,104... | collective-permute-start | bytes 1179656 | tf_op jit(solution)/shard_map/ppermute | solution.py:392
  46.9 1.8 %collective-permute-start.18 = (bf16[12,16,512]{2,1,0:T(8,128)(2,1)S(1)}, bf16[12,16,512]{2,1,0:T(8,128)(2,1)S(1)}, u32[]{:S(2)}, u32[]{:S(2)}) collective-permute-start(bf16[12,16,512]{2,1,0:T(8,128)(2,1)S(1)} %get-tuple-element.146), channel_id=1, source_target_pairs={{0,24},{1,25},{2,26},{3,27},{4,28},{5,29},{6,30},{7,31},{8,16},{9,... | collective-permute-start | bytes 589832 | tf_op jit(solution)/shard_map/ppermute | solution.py:392
  48.7 2.9 %collective-permute-start.19 = (bf16[12,16,512]{2,1,0:T(8,128)(2,1)S(1)}, bf16[12,16,512]{2,1,0:T(8,128)(2,1)S(1)}, u32[]{:S(2)}, u32[]{:S(2)}) collective-permute-start(bf16[12,16,512]{2,1,0:T(8,128)(2,1)S(1)} %get-tuple-element.147), channel_id=1, source_target_pairs={{0,8},{1,9},{2,10},{3,11},{4,12},{5,13},{6,14},{7,15},{8,0},{9,1},... | collective-permute-start | bytes 589832 | tf_op jit(solution)/shard_map/ppermute | solution.py:392
  51.6 3.2 %collective-permute-done.9.q_got = bf16[24,16,512]{2,1,0:T(8,128)(2,1)S(1)} collective-permute-done((bf16[24,16,512]{2,1,0:T(8,128)(2,1)S(1)}, bf16[24,16,512]{2,1,0:T(8,128)(2,1)S(1)}, u32[]{:S(2)}, u32[]{:S(2)}) %collective-permute-start.9) | collective-permute-done | bytes 393248 | tf_op jit(solution)/shard_map/ppermute | solution.py:392
  55.0 5.8 %collective-permute-start.10 = (bf16[13,16,512]{2,1,0:T(8,128)(2,1)S(1)}, bf16[13,16,512]{2,1,0:T(8,128)(2,1)S(1)}, u32[]{:S(2)}, u32[]{:S(2)}) collective-permute-start(bf16[13,16,512]{2,1,0:T(8,128)(2,1)S(1)} %get-tuple-element.131), channel_id=1, source_target_pairs={{0,96},{1,97},{2,98},{3,99},{4,100},{5,101},{6,102},{7,103},{8,104... | collective-permute-start | bytes 638984 | tf_op jit(solution)/shard_map/ppermute | solution.py:392
  61.0 2.6 %collective-permute-start.20 = (bf16[6,16,512]{2,1,0:T(8,128)(2,1)S(1)}, bf16[6,16,512]{2,1,0:T(8,128)(2,1)S(1)}, u32[]{:S(2)}, u32[]{:S(2)}) collective-permute-start(bf16[6,16,512]{2,1,0:T(8,128)(2,1)S(1)} %get-tuple-element.151), channel_id=1, source_target_pairs={{0,64},{1,65},{2,66},{3,67},{4,68},{5,69},{6,70},{7,71},{8,72},{9,... | collective-permute-start | bytes 294920 | tf_op jit(solution)/shard_map/ppermute | solution.py:392
  63.8 1.7 %collective-permute-start.21 = (bf16[6,16,512]{2,1,0:T(8,128)(2,1)S(1)}, bf16[6,16,512]{2,1,0:T(8,128)(2,1)S(1)}, u32[]{:S(2)}, u32[]{:S(2)}) collective-permute-start(bf16[6,16,512]{2,1,0:T(8,128)(2,1)S(1)} %get-tuple-element.152), channel_id=1, source_target_pairs={{0,32},{1,33},{2,34},{3,35},{4,36},{5,37},{6,38},{7,39},{8,40},{9,... | collective-permute-start | bytes 294920 | tf_op jit(solution)/shard_map/ppermute | solution.py:392
  65.5 0.8 collective-permute-start.22
  66.3 0.9 collective-permute-done.11.q_got
  67.4 2.1 %collective-permute-start.12 = (bf16[7,16,512]{2,1,0:T(8,128)(2,1)S(1)}, bf16[7,16,512]{2,1,0:T(8,128)(2,1)S(1)}, u32[]{:S(2)}, u32[]{:S(2)}) collective-permute-start(bf16[7,16,512]{2,1,0:T(8,128)(2,1)S(1)} %get-tuple-element.136), channel_id=1, source_target_pairs={{0,16},{1,17},{2,18},{3,19},{4,20},{5,21},{6,22},{7,23},{8,24},{9,... | collective-permute-start | bytes 344072 | tf_op jit(solution)/shard_map/ppermute | solution.py:392
  69.5 1.9 %collective-permute-start.13 = (bf16[7,16,512]{2,1,0:T(8,128)(2,1)S(1)}, bf16[7,16,512]{2,1,0:T(8,128)(2,1)S(1)}, u32[]{:S(2)}, u32[]{:S(2)}) collective-permute-start(bf16[7,16,512]{2,1,0:T(8,128)(2,1)S(1)} %get-tuple-element.137), channel_id=1, source_target_pairs={{0,8},{1,9},{2,10},{3,11},{4,12},{5,13},{6,14},{7,15},{8,0},{9,1},... | collective-permute-start | bytes 344072 | tf_op jit(solution)/shard_map/ppermute | solution.py:392
  71.7 2.1 %collective-permute-done.12.refs_1_ = bf16[7,16,512]{2,1,0:T(8,128)(2,1)S(1)} collective-permute-done((bf16[7,16,512]{2,1,0:T(8,128)(2,1)S(1)}, bf16[7,16,512]{2,1,0:T(8,128)(2,1)S(1)}, u32[]{:S(2)}, u32[]{:S(2)}) %collective-permute-start.12) | collective-permute-done | bytes 114720 | tf_op jit(solution)/shard_map/ppermute | solution.py:392
  73.8 1.6 %collective-permute-done.13.refs_2_ = bf16[7,16,512]{2,1,0:T(8,128)(2,1)S(1)} collective-permute-done((bf16[7,16,512]{2,1,0:T(8,128)(2,1)S(1)}, bf16[7,16,512]{2,1,0:T(8,128)(2,1)S(1)}, u32[]{:S(2)}, u32[]{:S(2)}) %collective-permute-start.13) | collective-permute-done | bytes 114720 | tf_op jit(solution)/shard_map/ppermute | solution.py:392
  75.4 0.8 collective-permute-done.14.refs_3_
  76.2 1.3 %shard_map.140 = bf16[8,112,128]{2,1,0:T(8,128)(2,1)} custom-call(bf16[7,16,512]{2,1,0:T(8,128)(2,1)S(1)} %get-tuple-element.157.refs_0_, bf16[7,16,512]{2,1,0:T(8,128)(2,1)S(1)} %collective-permute-done.12.refs_1_, bf16[7,16,512]{2,1,0:T(8,128)(2,1)S(1)} %collective-permute-done.13.refs_2_, bf16[7,16,512]{2,1,0:T(8,128)(2,1)S(1)} %collective-permute-done.14.refs_3_, ...), custom_call_target="tpu_custom_call" | custom-call | flops 60000000 | bytes 4000000 | tf_op jit(solution)/shard_map/pallas_call | solution.py:517
  77.5 4.8 %all-to-all-start = ((bf16[8,112,128]{2,1,0:T(8,128)(2,1)}), bf16[8,112,128]{2,1,0:T(8,128)(2,1)S(1)}, u32[]{:S(2)}, u32[]{:S(2)}) async-start(bf16[8,112,128]{2,1,0:T(8,128)(2,1)} %shard_map.140), calls=%async_computation | async-start | bytes 458752 | tf_op jit(solution)/shard_map/all_to_all | solution.py:405
  82.4 1.9 %collective-permute-start.23 = (bf16[24,3,512]{2,1,0:T(4,128)(2,1)S(1)}, bf16[24,3,512]{2,1,0:T(4,128)(2,1)S(1)}, u32[]{:S(2)}, u32[]{:S(2)}) collective-permute-start(bf16[24,3,512]{2,1,0:T(4,128)(2,1)S(1)} %get-tuple-element.166), channel_id=1, source_target_pairs={{1,2},{2,1},{3,4},{4,3},{5,6},{6,5},{7,8},{8,7},{9,10},{10,9},{11,... | collective-permute-start | bytes 221192 | tf_op jit(solution)/shard_map/ppermute | solution.py:392
  84.4 2.2 %collective-permute-start.24 = (bf16[24,3,512]{2,1,0:T(4,128)(2,1)S(1)}, bf16[24,3,512]{2,1,0:T(4,128)(2,1)S(1)}, u32[]{:S(2)}, u32[]{:S(2)}) collective-permute-start(bf16[24,3,512]{2,1,0:T(4,128)(2,1)S(1)} %get-tuple-element.167), channel_id=1, source_target_pairs={{0,1},{1,0},{2,3},{3,2},{4,5},{5,4},{6,7},{7,6},{8,9},{9,8},{10,11... | collective-permute-start | bytes 221192 | tf_op jit(solution)/shard_map/ppermute | solution.py:392
  86.6 5.8 %all-to-all-done.got = bf16[8,112,128]{2,1,0:T(8,128)(2,1)S(1)} async-done(((bf16[8,112,128]{2,1,0:T(8,128)(2,1)}), bf16[8,112,128]{2,1,0:T(8,128)(2,1)S(1)}, u32[]{:S(2)}, u32[]{:S(2)}) %all-to-all-start) | async-done | bytes 229408 | tf_op jit(solution)/shard_map/all_to_all | solution.py:405
  93.4 0.9 fusion.6
  (70 shorter events, 8.2 us)
Async XLA Ops:
  0.6 10.6 %copy-start = (bf16[24,8,512]{2,1,0:T(8,128)(2,1)S(1)}, bf16[24,8,512]{2,1,0:T(8,128)(2,1)}, u32[]{:S(2)}) copy-start(bf16[24,8,512]{2,1,0:T(8,128)(2,1)} %param.8) | copy-start | bytes 589828
  1.8 9.4 %collective-permute-start = (bf16[24,3,512]{2,1,0:T(4,128)(2,1)S(1)}, bf16[24,3,512]{2,1,0:T(4,128)(2,1)S(1)}, u32[]{:S(2)}, u32[]{:S(2)}) collective-permute-start(bf16[24,3,512]{2,1,0:T(4,128)(2,1)S(1)} %get-tuple-element.185), channel_id=1, source_target_pairs={{1,2},{2,1},{3,4},{4,3},{5,6},{6,5},{7,8},{8,7},{9,10},{10,9},{11,... | collective-permute-start | bytes 221192 | tf_op jit(solution)/shard_map/ppermute | solution.py:392
  7.7 3.5 %collective-permute-start.1 = (bf16[24,3,512]{2,1,0:T(4,128)(2,1)S(1)}, bf16[24,3,512]{2,1,0:T(4,128)(2,1)S(1)}, u32[]{:S(2)}, u32[]{:S(2)}) collective-permute-start(bf16[24,3,512]{2,1,0:T(4,128)(2,1)S(1)} %get-tuple-element.184), channel_id=1, source_target_pairs={{0,1},{1,0},{2,3},{3,2},{4,5},{5,4},{6,7},{7,6},{8,9},{9,8},{10,11... | collective-permute-start | bytes 221192 | tf_op jit(solution)/shard_map/ppermute | solution.py:392
  9.9 7.6 %copy-start.2 = (bf16[2048,512]{1,0:T(8,128)(2,1)S(1)}, bf16[2048,512]{1,0:T(8,128)(2,1)}, u32[]{:S(2)}) copy-start(bf16[2048,512]{1,0:T(8,128)(2,1)} %w_down.1) | copy-start | bytes 6291460
  9.9 7.6 %copy-start.3 = (bf16[24,8,512]{2,1,0:T(8,128)(2,1)S(1)}, bf16[24,8,512]{2,1,0:T(8,128)(2,1)}, u32[]{:S(2)}) copy-start(bf16[24,8,512]{2,1,0:T(8,128)(2,1)} %param.9) | copy-start | bytes 589828
  11.4 9.1 %collective-permute-start.2 = (bf16[3,16,512]{2,1,0:T(8,128)(2,1)S(1)}, bf16[3,16,512]{2,1,0:T(8,128)(2,1)S(1)}, u32[]{:S(2)}, u32[]{:S(2)}) collective-permute-start(bf16[3,16,512]{2,1,0:T(8,128)(2,1)S(1)} %get-tuple-element.183), channel_id=1, source_target_pairs={{32,64},{33,65},{34,66},{35,67},{36,68},{37,69},{38,70},{39,71},{4... | collective-permute-start | bytes 147464 | tf_op jit(solution)/shard_map/ppermute | solution.py:392
  12.1 8.4 %collective-permute-start.3 = (bf16[3,16,512]{2,1,0:T(8,128)(2,1)S(1)}, bf16[3,16,512]{2,1,0:T(8,128)(2,1)S(1)}, u32[]{:S(2)}, u32[]{:S(2)}) collective-permute-start(bf16[3,16,512]{2,1,0:T(8,128)(2,1)S(1)} %get-tuple-element.182), channel_id=1, source_target_pairs={{0,32},{1,33},{2,34},{3,35},{4,36},{5,37},{6,38},{7,39},{8,40},{9,... | collective-permute-start | bytes 147464 | tf_op jit(solution)/shard_map/ppermute | solution.py:392
  17.5 3.0 %copy-start.6 = (bf16[512,512]{1,0:T(8,128)(2,1)S(1)}, bf16[512,512]{1,0:T(8,128)(2,1)}, u32[]{:S(2)}) copy-start(bf16[512,512]{1,0:T(8,128)(2,1)} %w_out.3) | copy-start | bytes 1572868
  18.4 2.2 %copy-start.5 = (bf16[512,2048]{1,0:T(8,128)(2,1)S(1)}, bf16[512,2048]{1,0:T(8,128)(2,1)}, u32[]{:S(2)}) copy-start(bf16[512,2048]{1,0:T(8,128)(2,1)} %w_up.1) | copy-start | bytes 6291460
  26.6 4.6 %collective-permute-start.4 = (bf16[16,5,16,512]{3,2,1,0:T(8,128)(2,1)S(1)}, bf16[16,5,16,512]{3,2,1,0:T(8,128)(2,1)S(1)}, u32[]{:S(2)}, u32[]{:S(2)}) collective-permute-start(bf16[16,5,16,512]{3,2,1,0:T(8,128)(2,1)S(1)} %get-tuple-element.103), channel_id=1, source_target_pairs={{0,1},{1,0},{2,3},{3,2},{4,5},{5,4},{6,7},{7,6},{8,9},{9,8},{10,11... | collective-permute-start | bytes 3932168 | tf_op jit(solution)/shard_map/ppermute | solution.py:392
  26.7 4.5 %collective-permute-start.5 = (bf16[4,4,2,32,512]{4,3,2,1,0:T(8,128)(2,1)S(1)}, bf16[4,4,2,32,512]{4,3,2,1,0:T(8,128)(2,1)S(1)}, u32[]{:S(2)}, u32[]{:S(2)}) collective-permute-start(bf16[4,4,2,32,512]{4,3,2,1,0:T(8,128)(2,1)S(1)} %get-tuple-element.104), channel_id=1, source_target_pairs={{0,1},{1,0},{2,3},{3,2},{4,5},{5,4},{6,7},{7,6},{8,9},{9,8},{10,11... | collective-permute-start | bytes 3145736 | tf_op jit(solution)/shard_map/ppermute | solution.py:392
  31.3 2.4 %collective-permute-start.6 = (bf16[48,16,512]{2,1,0:T(8,128)(2,1)S(1)}, bf16[48,16,512]{2,1,0:T(8,128)(2,1)S(1)}, u32[]{:S(2)}, u32[]{:S(2)}) collective-permute-start(bf16[48,16,512]{2,1,0:T(8,128)(2,1)S(1)} %get-tuple-element.114), channel_id=1, source_target_pairs={{0,1},{1,0},{2,3},{3,2},{4,5},{5,4},{6,7},{7,6},{8,9},{9,8},{10,11... | collective-permute-start | bytes 2359304 | tf_op jit(solution)/shard_map/ppermute | solution.py:392
  33.1 1.3 %collective-permute-start.7 = (bf16[16,512]{1,0:T(8,128)(2,1)S(1)}, bf16[16,512]{1,0:T(8,128)(2,1)S(1)}, u32[]{:S(2)}, u32[]{:S(2)}) collective-permute-start(bf16[16,512]{1,0:T(8,128)(2,1)S(1)} %get-tuple-element.120.gk), channel_id=1, source_target_pairs={{0,1},{1,0},{2,3},{3,2},{4,5},{5,4},{6,7},{7,6},{8,9},{9,8},{10,11... | collective-permute-start | bytes 49160 | tf_op jit(solution)/shard_map/ppermute | solution.py:392
  34.7 20.1 %collective-permute-start.8 = (bf16[28,16,512]{2,1,0:T(8,128)(2,1)S(1)}, bf16[28,16,512]{2,1,0:T(8,128)(2,1)S(1)}, u32[]{:S(2)}, u32[]{:S(2)}) collective-permute-start(bf16[28,16,512]{2,1,0:T(8,128)(2,1)S(1)} %get-tuple-element.127), channel_id=1, source_target_pairs={{0,32},{1,33},{2,34},{3,35},{4,36},{5,37},{6,38},{7,39},{8,40},{9,... | collective-permute-start | bytes 1376264 | tf_op jit(solution)/shard_map/ppermute | solution.py:392
  34.8 11.7 %collective-permute-start.15 = (bf16[24,16,512]{2,1,0:T(8,128)(2,1)S(1)}, bf16[24,16,512]{2,1,0:T(8,128)(2,1)S(1)}, u32[]{:S(2)}, u32[]{:S(2)}) collective-permute-start(bf16[24,16,512]{2,1,0:T(8,128)(2,1)S(1)} %get-tuple-element.139), channel_id=1, source_target_pairs={{0,8},{1,9},{2,10},{3,11},{4,12},{5,13},{6,14},{7,15},{8,0},{9,1},... | collective-permute-start | bytes 1179656 | tf_op jit(solution)/shard_map/ppermute | solution.py:392
  34.9 11.8 %collective-permute-start.16 = (bf16[24,16,512]{2,1,0:T(8,128)(2,1)S(1)}, bf16[24,16,512]{2,1,0:T(8,128)(2,1)S(1)}, u32[]{:S(2)}, u32[]{:S(2)}) collective-permute-start(bf16[24,16,512]{2,1,0:T(8,128)(2,1)S(1)} %get-tuple-element.140), channel_id=1, source_target_pairs={{0,24},{1,25},{2,26},{3,27},{4,28},{5,29},{6,30},{7,31},{8,16},{9,... | collective-permute-start | bytes 1179656 | tf_op jit(solution)/shard_map/ppermute | solution.py:392
  37.4 17.4 %collective-permute-start.9 = (bf16[24,16,512]{2,1,0:T(8,128)(2,1)S(1)}, bf16[24,16,512]{2,1,0:T(8,128)(2,1)S(1)}, u32[]{:S(2)}, u32[]{:S(2)}) collective-permute-start(bf16[24,16,512]{2,1,0:T(8,128)(2,1)S(1)} %get-tuple-element.128), channel_id=1, source_target_pairs={{0,96},{1,97},{2,98},{3,99},{4,100},{5,101},{6,102},{7,103},{8,104... | collective-permute-start | bytes 1179656 | tf_op jit(solution)/shard_map/ppermute | solution.py:392
  45.8 0.7 collective-permute-start.17
  46.9 14.0 %collective-permute-start.18 = (bf16[12,16,512]{2,1,0:T(8,128)(2,1)S(1)}, bf16[12,16,512]{2,1,0:T(8,128)(2,1)S(1)}, u32[]{:S(2)}, u32[]{:S(2)}) collective-permute-start(bf16[12,16,512]{2,1,0:T(8,128)(2,1)S(1)} %get-tuple-element.146), channel_id=1, source_target_pairs={{0,24},{1,25},{2,26},{3,27},{4,28},{5,29},{6,30},{7,31},{8,16},{9,... | collective-permute-start | bytes 589832 | tf_op jit(solution)/shard_map/ppermute | solution.py:392
  48.7 12.2 %collective-permute-start.19 = (bf16[12,16,512]{2,1,0:T(8,128)(2,1)S(1)}, bf16[12,16,512]{2,1,0:T(8,128)(2,1)S(1)}, u32[]{:S(2)}, u32[]{:S(2)}) collective-permute-start(bf16[12,16,512]{2,1,0:T(8,128)(2,1)S(1)} %get-tuple-element.147), channel_id=1, source_target_pairs={{0,8},{1,9},{2,10},{3,11},{4,12},{5,13},{6,14},{7,15},{8,0},{9,1},... | collective-permute-start | bytes 589832 | tf_op jit(solution)/shard_map/ppermute | solution.py:392
  55.0 12.3 %collective-permute-start.10 = (bf16[13,16,512]{2,1,0:T(8,128)(2,1)S(1)}, bf16[13,16,512]{2,1,0:T(8,128)(2,1)S(1)}, u32[]{:S(2)}, u32[]{:S(2)}) collective-permute-start(bf16[13,16,512]{2,1,0:T(8,128)(2,1)S(1)} %get-tuple-element.131), channel_id=1, source_target_pairs={{0,96},{1,97},{2,98},{3,99},{4,100},{5,101},{6,102},{7,103},{8,104... | collective-permute-start | bytes 638984 | tf_op jit(solution)/shard_map/ppermute | solution.py:392
  60.9 6.4 %collective-permute-start.11 = (bf16[12,16,512]{2,1,0:T(8,128)(2,1)S(1)}, bf16[12,16,512]{2,1,0:T(8,128)(2,1)S(1)}, u32[]{:S(2)}, u32[]{:S(2)}) collective-permute-start(bf16[12,16,512]{2,1,0:T(8,128)(2,1)S(1)} %get-tuple-element.132), channel_id=1, source_target_pairs={{0,32},{1,33},{2,34},{3,35},{4,36},{5,37},{6,38},{7,39},{8,40},{9,... | collective-permute-start | bytes 589832 | tf_op jit(solution)/shard_map/ppermute | solution.py:392
  61.0 10.4 %collective-permute-start.20 = (bf16[6,16,512]{2,1,0:T(8,128)(2,1)S(1)}, bf16[6,16,512]{2,1,0:T(8,128)(2,1)S(1)}, u32[]{:S(2)}, u32[]{:S(2)}) collective-permute-start(bf16[6,16,512]{2,1,0:T(8,128)(2,1)S(1)} %get-tuple-element.151), channel_id=1, source_target_pairs={{0,64},{1,65},{2,66},{3,67},{4,68},{5,69},{6,70},{7,71},{8,72},{9,... | collective-permute-start | bytes 294920 | tf_op jit(solution)/shard_map/ppermute | solution.py:392
  63.8 7.9 %collective-permute-start.21 = (bf16[6,16,512]{2,1,0:T(8,128)(2,1)S(1)}, bf16[6,16,512]{2,1,0:T(8,128)(2,1)S(1)}, u32[]{:S(2)}, u32[]{:S(2)}) collective-permute-start(bf16[6,16,512]{2,1,0:T(8,128)(2,1)S(1)} %get-tuple-element.152), channel_id=1, source_target_pairs={{0,32},{1,33},{2,34},{3,35},{4,36},{5,37},{6,38},{7,39},{8,40},{9,... | collective-permute-start | bytes 294920 | tf_op jit(solution)/shard_map/ppermute | solution.py:392
  65.5 6.2 %collective-permute-start.22 = (bf16[6,16,512]{2,1,0:T(8,128)(2,1)S(1)}, bf16[6,16,512]{2,1,0:T(8,128)(2,1)S(1)}, u32[]{:S(2)}, u32[]{:S(2)}) collective-permute-start(bf16[6,16,512]{2,1,0:T(8,128)(2,1)S(1)} %get-tuple-element.153), channel_id=1, source_target_pairs={{0,96},{1,97},{2,98},{3,99},{4,100},{5,101},{6,102},{7,103},{8,104... | collective-permute-start | bytes 294920 | tf_op jit(solution)/shard_map/ppermute | solution.py:392
  67.4 6.4 %collective-permute-start.12 = (bf16[7,16,512]{2,1,0:T(8,128)(2,1)S(1)}, bf16[7,16,512]{2,1,0:T(8,128)(2,1)S(1)}, u32[]{:S(2)}, u32[]{:S(2)}) collective-permute-start(bf16[7,16,512]{2,1,0:T(8,128)(2,1)S(1)} %get-tuple-element.136), channel_id=1, source_target_pairs={{0,16},{1,17},{2,18},{3,19},{4,20},{5,21},{6,22},{7,23},{8,24},{9,... | collective-permute-start | bytes 344072 | tf_op jit(solution)/shard_map/ppermute | solution.py:392
  69.5 5.9 %collective-permute-start.13 = (bf16[7,16,512]{2,1,0:T(8,128)(2,1)S(1)}, bf16[7,16,512]{2,1,0:T(8,128)(2,1)S(1)}, u32[]{:S(2)}, u32[]{:S(2)}) collective-permute-start(bf16[7,16,512]{2,1,0:T(8,128)(2,1)S(1)} %get-tuple-element.137), channel_id=1, source_target_pairs={{0,8},{1,9},{2,10},{3,11},{4,12},{5,13},{6,14},{7,15},{8,0},{9,1},... | collective-permute-start | bytes 344072 | tf_op jit(solution)/shard_map/ppermute | solution.py:392
  71.4 4.8 %collective-permute-start.14 = (bf16[7,16,512]{2,1,0:T(8,128)(2,1)S(1)}, bf16[7,16,512]{2,1,0:T(8,128)(2,1)S(1)}, u32[]{:S(2)}, u32[]{:S(2)}) collective-permute-start(bf16[7,16,512]{2,1,0:T(8,128)(2,1)S(1)} %get-tuple-element.138), channel_id=1, source_target_pairs={{0,24},{1,25},{2,26},{3,27},{4,28},{5,29},{6,30},{7,31},{8,16},{9,... | collective-permute-start | bytes 344072 | tf_op jit(solution)/shard_map/ppermute | solution.py:392
  77.5 14.9 %all-to-all-start = ((bf16[8,112,128]{2,1,0:T(8,128)(2,1)}), bf16[8,112,128]{2,1,0:T(8,128)(2,1)S(1)}, u32[]{:S(2)}, u32[]{:S(2)}) async-start(bf16[8,112,128]{2,1,0:T(8,128)(2,1)} %shard_map.140), calls=%async_computation | async-start | bytes 458752 | tf_op jit(solution)/shard_map/all_to_all | solution.py:405
  82.4 10.7 %slice-start = ((f32[2,512]{1,0:T(2,128)}), f32[1,512]{1,0:T(1,128)S(1)}, s32[]{:S(2)}) async-start(f32[2,512]{1,0:T(2,128)} %gains.3), calls=%async_computation.1 | async-start | bytes 4096 | tf_op jit(solution)/shard_map/slice | solution.py:532
  82.4 10.6 %collective-permute-start.23 = (bf16[24,3,512]{2,1,0:T(4,128)(2,1)S(1)}, bf16[24,3,512]{2,1,0:T(4,128)(2,1)S(1)}, u32[]{:S(2)}, u32[]{:S(2)}) collective-permute-start(bf16[24,3,512]{2,1,0:T(4,128)(2,1)S(1)} %get-tuple-element.166), channel_id=1, source_target_pairs={{1,2},{2,1},{3,4},{4,3},{5,6},{6,5},{7,8},{8,7},{9,10},{10,9},{11,... | collective-permute-start | bytes 221192 | tf_op jit(solution)/shard_map/ppermute | solution.py:392
  84.4 8.7 %collective-permute-start.24 = (bf16[24,3,512]{2,1,0:T(4,128)(2,1)S(1)}, bf16[24,3,512]{2,1,0:T(4,128)(2,1)S(1)}, u32[]{:S(2)}, u32[]{:S(2)}) collective-permute-start(bf16[24,3,512]{2,1,0:T(4,128)(2,1)S(1)} %get-tuple-element.167), channel_id=1, source_target_pairs={{0,1},{1,0},{2,3},{3,2},{4,5},{5,4},{6,7},{7,6},{8,9},{9,8},{10,11... | collective-permute-start | bytes 221192 | tf_op jit(solution)/shard_map/ppermute | solution.py:392
  (3 other events, 3.5 us)
